TPU v7x, 32 devices: a whole 2x2x4 slice. The times are simulated.
32 devices in a mesh: mem: 4 (over x, core), grid: 8 (over z, y).
Axes of the slice: x: 2, y: 2, z: 4, core: 2. Of those that a mesh axis runs over, the one named last changes fastest.
Arguments:
- hidden: bfloat16 [8, 1024, 16384], P('mem', None, 'grid'), may hold values from -6 to 6
- target: float32 [100, 16384], P(None, 'grid'), may hold values from -5 to 5
- area: float32 [16384], P('grid'), may hold values from 0.2 to 2
- var_weight: float32 [100], replicated, may hold values from 0.2 to 2
- w_inner: bfloat16 [1024, 1024], replicated, may hold values from -0.1875 to 0.1875
- b_inner: float32 [1024], replicated, may hold values from -3 to 3
- w_out: bfloat16 [100, 1024], replicated, may hold values from -0.1875 to 0.1875
- b_out: float32 [100], replicated, may hold values from -3 to 3
Outputs:
- loss: float32 [], replicated
- grad_hidden: bfloat16 [8, 1024, 16384], P('mem', None, 'grid')
- grad_inner: float32 [1024, 1024], P('grid')
- grad_out: float32 [100, 1024], replicated
All inputs are finite; a program needn't handle non-finite values.
Results may differ from a plain program's by a relative error of at most 0.0025.
The roundings to bfloat16 on the way count: a program that leaves them out, or rounds other values in their place, can miss the bound.
Values sent between devices are 32-bit elements; how exact they have to be, the bound alone decides.
No kernel may reach another device: no remote copies, remote signals or barrier semaphores. Data moves between devices by JAX's collectives and lax.ppermute only.
A program may use at most 128 MiB of HBM per device.

v0:
```python
import functools
import math

import jax
import jax.numpy as jnp
from jax import lax
from jax.experimental import pallas as pl
from jax.experimental.pallas import tpu as pltpu
from jax.sharding import PartitionSpec as P

PARTS = 4
FWD_TILE = 256
BWD_TILE = 256
EPS = 0.0004
K0 = math.sqrt(2.0 / math.pi)
K1 = K0 * 0.044715
VMEM = 56 * 1024 * 1024
NT = (((1,), (1,)), ((), ()))


def column(row, size):
    r = lax.broadcasted_iota(jnp.int32, (size, size), 0)
    c = lax.broadcasted_iota(jnp.int32, (size, size), 1)
    return jnp.sum(jnp.where(r == c, row, 0.0), axis=1, keepdims=True)


def forward_kernel(hid_ref, w_ref, b_ref, wo_ref, bo_ref, act_ref, slope_ref, f_ref, bias):
    @pl.when(pl.program_id(0) == 0)
    def _():
        for k in range(bias.shape[0] // 128):
            bias[pl.ds(k * 128, 128), :] = jnp.broadcast_to(
                column(b_ref[:, pl.ds(k * 128, 128)], 128), (128, 128)
            )

    out_bias = column(bo_ref[...], bo_ref.shape[1])
    for s in range(hid_ref.shape[2] // FWD_TILE):
        cols = pl.ds(s * FWD_TILE, FWD_TILE)
        b = jnp.concatenate([bias[...]] * (FWD_TILE // 128), axis=1)
        x = jnp.dot(w_ref[...], hid_ref[0, :, cols], preferred_element_type=jnp.float32) + b
        x2 = x * x
        u = 0.5 + 0.5 * jnp.tanh(x * (K0 + K1 * x2))
        act = (x * u).astype(jnp.bfloat16)
        act_ref[0, :, cols] = act
        slope_ref[0, :, cols] = u + (u - u * u) * (x * (2.0 * K0 + 6.0 * K1 * x2))
        f_ref[0, :, cols] = (
            jnp.dot(wo_ref[...], act, preferred_element_type=jnp.float32) + out_bias
        )


def forward(part, hidden, w_inner, b_inner, w_out, b_out):
    mloc, h, n = hidden.shape
    v = w_out.shape[0]
    p = n // PARTS
    whole = lambda m: (0, 0)
    once = pl.Buffered(1)
    return pl.pallas_call(
        forward_kernel,
        grid=(mloc,),
        in_specs=[
            pl.BlockSpec((1, h, p), lambda m: (m, 0, part)),
            pl.BlockSpec((h, h), whole, pipeline_mode=once),
            pl.BlockSpec((1, h), whole, pipeline_mode=once),
            pl.BlockSpec((v, h), whole, pipeline_mode=once),
            pl.BlockSpec((1, v), whole, pipeline_mode=once),
        ],
        out_specs=[
            pl.BlockSpec((1, h, p), lambda m: (m, 0, 0)),
            pl.BlockSpec((1, h, p), lambda m: (m, 0, 0)),
            pl.BlockSpec((1, v, p), lambda m: (m, 0, 0)),
        ],
        out_shape=[
            jax.ShapeDtypeStruct((mloc, h, p), jnp.bfloat16),
            jax.ShapeDtypeStruct((mloc, h, p), jnp.float32),
            jax.ShapeDtypeStruct((mloc, v, p), jnp.float32),
        ],
        scratch_shapes=[pltpu.VMEM((h, 128), jnp.float32)],
        compiler_params=pltpu.CompilerParams(vmem_limit_bytes=VMEM),
        cost_estimate=pl.CostEstimate(
            flops=2 * mloc * p * h * (h + v), bytes_accessed=mloc * p * h * 8 + 2 * h * h,
            transcendentals=mloc * p * h,
        ),
        name="forward_part",
    )(hidden, w_inner, b_inner, w_out, b_out)


def backward_kernel(
    first, last, dims, members,
    f_ref, fc_ref, fx_ref, fxc_ref, target_ref, area_ref, vw_ref, act_ref, slope_ref, hid_ref,
    wot_ref, wt_ref, acc_in, extra_in, gh_in, gh_ref, extra_ref, *refs,
):
    if last:
        keep_a, send_a, keep_x, send_x, acc, gf = refs
    else:
        acc, gf = refs
    step = pl.program_id(0)
    mloc, v, t = f_ref.shape
    h = wt_ref.shape[0]
    denom = members * (members - 1)
    vw = column(vw_ref[...], v)
    area = area_ref[...]
    loss = jnp.zeros((1, t), jnp.float32)
    for r0 in range(0, v, 16):
        rows = pl.ds(r0, min(16, v - r0))
        own = [f_ref[m, rows, :] for m in range(mloc)]
        others = [ref[m, rows, :] for ref in (fc_ref, fx_ref, fxc_ref) for m in range(mloc)]
        target = target_ref[rows, :]
        dsum = [None] * mloc
        obs = []
        cross = jnp.zeros_like(target)
        inner = jnp.zeros_like(target)
        near = jnp.zeros_like(target)
        n_cross = n_inner = 0

        def pair(a, b):
            d = a - b
            s = d * d + EPS
            r = lax.rsqrt(s)
            return d * r, s * r

        def add(m, value):
            dsum[m] = value if dsum[m] is None else dsum[m] + value

        for i in range(mloc):
            sl, ph = pair(own[i], target)
            obs.append(sl)
            near = near + ph
            for b in others:
                sl, ph = pair(own[i], b)
                add(i, sl)
                cross = cross + ph
                n_cross += 1
            for j in range(i + 1, mloc):
                sl, ph = pair(own[i], own[j])
                add(i, sl)
                add(j, -sl)
                inner = inner + ph
                n_inner += 1
        weight = vw[r0 : r0 + 16] * area
        for m in range(mloc):
            gf[m, rows, :] = weight * (obs[m] * (1.0 / members) - dsum[m] * (1.0 / denom))
        near = (near - 0.02 * mloc) * (1.0 / members)
        pairs = (inner - 0.02 * n_inner) + 0.5 * (cross - 0.02 * n_cross)
        loss = loss + jnp.sum(weight * (near - pairs * (1.0 / denom)), axis=0, keepdims=True)
    for m in range(mloc):
        gf[m, pl.ds(v, gf.shape[1] - v), :] = jnp.zeros((gf.shape[1] - v, t), jnp.float32)

    gp = []
    extra = None
    for m in range(mloc):
        g = gf[m].astype(jnp.bfloat16)
        ga = jnp.dot(wot_ref[...], g, preferred_element_type=jnp.float32)
        gp.append((ga * slope_ref[m]).astype(jnp.bfloat16))
        out = lax.dot_general(g, act_ref[m], NT, preferred_element_type=jnp.float32)
        extra = out if extra is None else extra + out
    gpc = jnp.concatenate(gp, axis=1)
    hidc = jnp.concatenate([hid_ref[m] for m in range(mloc)], axis=1)
    prod = lax.dot_general(gpc, hidc, NT, preferred_element_type=jnp.float32)

    @pl.when(step == 0)
    def _():
        if first:
            acc[...] = prod
            extra_ref[...] = extra
        else:
            acc[...] = acc_in[...] + prod
            extra_ref[...] = extra_in[...] + extra

    @pl.when(step > 0)
    def _():
        acc[...] += prod
        extra_ref[...] += extra

    extra_ref[pl.ds(v, 1), pl.ds(0, t)] += loss
    for m in range(mloc):
        gh_ref[m] = jnp.dot(wt_ref[...], gp[m], preferred_element_type=jnp.float32).astype(
            jnp.bfloat16
        )
    if last:
        n_hi, n_lo = dims

        @pl.when(step == pl.num_programs(0) - 1)
        def _():
            mem = lax.axis_index("mem")
            grid = lax.axis_index("grid")
            x, core = mem // 2, mem % 2
            hi, lo = grid // n_lo, grid % n_lo
            r = h // (2 * n_hi * n_lo)
            ca = keep_a.shape[3]
            cx = keep_x.shape[4]
            for dlo in range(n_lo):
                for dhi in range(n_hi):
                    g = lax.rem(hi + dhi, n_hi) * n_lo + lax.rem(lo + dlo, n_lo)
                    for c, part_a, part_x in ((core, keep_a, keep_x), (1 - core, send_a, send_x)):
                        r0 = pl.multiple_of((g * 2 + c) * r, r)
                        part_a[dlo, dhi] = acc[pl.ds(r0, r), pl.ds(0, ca)]
                        left = acc[pl.ds(r0, r), pl.ds(ca, cx)]
                        right = acc[pl.ds(r0, r), pl.ds(ca + cx, cx)]
                        part_x[0, dlo, dhi] = jnp.where(x == 0, left, right)
                        part_x[1, dlo, dhi] = jnp.where(x == 0, right, left)


def backward(part, dims, members, fields, rest, acc, extra, gh):
    target, area, vw, act, slope, hidden, wot, wt = rest
    mloc, h, n = hidden.shape
    v = target.shape[0]
    vp = wot.shape[1]
    p = n // PARTS
    t = BWD_TILE
    steps = p // t
    first, last = part == 0, part == PARTS - 1
    off = part * steps
    once = pl.Buffered(1)
    f_spec = pl.BlockSpec((mloc, v, t), lambda s: (0, 0, s))
    big = pl.BlockSpec((mloc, h, t), lambda s: (0, 0, s))
    whole = lambda s: (0, 0)
    const = lambda a: pl.BlockSpec(a.shape, whole, pipeline_mode=once)
    anyspec = pl.BlockSpec(memory_space=pl.ANY)
    placed = pl.BlockSpec((mloc, h, t), lambda s: (0, 0, off + s))
    in_specs = [f_spec] * 4 + [
        pl.BlockSpec((v, t), lambda s: (0, off + s)),
        pl.BlockSpec((1, t), lambda s: (0, off + s)),
        const(vw), big, big, placed, const(wot), const(wt),
    ]
    args = [*fields, target, area, vw, act, slope, hidden, wot, wt]
    kernel = functools.partial(backward_kernel, first, last, dims, members)
    if first:
        kernel_fn = lambda *refs: kernel(*refs[:12], None, None, None, *refs[12:])
        aliases = {}
    else:
        kernel_fn = kernel
        in_specs += [const(acc), const(extra), anyspec]
        args += [acc, extra, gh]
        aliases = {14: 0}
    out_specs = [placed, pl.BlockSpec((vp, h), whole)]
    out_shape = [
        jax.ShapeDtypeStruct(hidden.shape, jnp.bfloat16),
        jax.ShapeDtypeStruct((vp, h), jnp.float32),
    ]
    scratch = [pltpu.VMEM((mloc, vp, t), jnp.float32)]
    if last:
        n_hi, n_lo = dims
        r = h // (2 * n_hi * n_lo)
        ca = h // 2
        cx = (h - ca) // 2
        for shape in ((n_lo, n_hi, r, ca), (n_lo, n_hi, r, ca), (2, n_lo, n_hi, r, cx), (2, n_lo, n_hi, r, cx)):
            out_specs.append(pl.BlockSpec(shape, lambda s, k=len(shape): (0,) * k))
            out_shape.append(jax.ShapeDtypeStruct(shape, jnp.float32))
        scratch = [pltpu.VMEM((h, h), jnp.float32)] + scratch
    else:
        out_specs.append(pl.BlockSpec((h, h), whole))
        out_shape.append(jax.ShapeDtypeStruct((h, h), jnp.float32))
    return pl.pallas_call(
        kernel_fn,
        grid=(steps,),
        in_specs=in_specs,
        out_specs=out_specs,
        out_shape=out_shape,
        scratch_shapes=scratch,
        input_output_aliases=aliases,
        compiler_params=pltpu.CompilerParams(vmem_limit_bytes=VMEM),
        cost_estimate=pl.CostEstimate(
            flops=4 * mloc * p * h * (h + v), bytes_accessed=mloc * p * h * 10 + 10 * h * h,
            transcendentals=mloc * p * v * 8,
        ),
        name="backward_part",
    )(*args)


def shards(hidden, target, area, var_weight, w_inner, b_inner, w_out, b_out):
    mloc, h, n = hidden.shape
    n_mem = lax.axis_size("mem")
    n_grid = lax.axis_size("grid")
    members = mloc * n_mem
    npoints = n * n_grid
    v = w_out.shape[0]
    vp = 128
    n_lo = 2
    while n_lo * n_lo * 4 <= n_grid:
        n_lo *= 2
    n_hi = n_grid // n_lo

    swap_x = [(i, (i + n_mem // 2) % n_mem) for i in range(n_mem)]
    swap_core = [(i, i ^ 1) for i in range(n_mem)]

    def shift_lo(k):
        return [(a * n_lo + b, a * n_lo + (b + k) % n_lo) for a in range(n_hi) for b in range(n_lo)]

    def shift_hi(k):
        return [(a * n_lo + b, (a + k) % n_hi * n_lo + b) for a in range(n_hi) for b in range(n_lo)]

    to_x = lambda a: lax.ppermute(a, "mem", swap_x)
    to_core = lambda a: lax.ppermute(a, "mem", swap_core)
    to_lo = lambda a, k: lax.ppermute(a, "grid", shift_lo(k))
    to_hi = lambda a, k: lax.ppermute(a, "grid", shift_hi(k))

    parts = []
    for part in range(PARTS):
        parts.append(
            forward(part, hidden, w_inner, b_inner.reshape(1, h), w_out, b_out.reshape(1, v))
        )
    exchanged = []
    for act, slope, fields in parts:
        far = to_x(fields)
        exchanged.append((fields, to_core(fields), far, to_core(far)))

    w_inner, w_out, _ = lax.optimization_barrier((w_inner, w_out, parts[1][2]))
    wt = w_inner.T
    wot = jnp.pad(w_out, ((0, vp - v), (0, 0))).T
    vw, area = var_weight.reshape(1, v), area.reshape(1, n)
    acc = extra = gh = None
    for part in range(PARTS):
        act, slope, _ = parts[part]
        rest = (target, area, vw, act, slope, hidden, wot, wt)
        gh, extra, *accs = backward(
            part, (n_hi, n_lo), members, exchanged[part], rest, acc, extra, gh
        )
        acc = accs[0]
    keep_a, send_a, keep_x, send_x = accs

    core = lax.axis_index("mem") % 2
    x = lax.axis_index("mem") // 2

    def along_lo(blocks):
        total = blocks(0)
        for k in range(1, n_lo):
            total = total + to_lo(blocks(k), k)
        return total

    def along_hi(blocks):
        total = blocks[0]
        for k in range(1, n_hi):
            total = total + to_hi(blocks[k], k)
        return total

    got_a = to_core(send_a)
    got_x = to_core(send_x)
    sum_a = along_lo(lambda k: keep_a[k] + got_a[k])
    own_x = keep_x[0] + got_x[0] + to_x(keep_x[1] + got_x[1])
    sum_x = along_lo(lambda k: own_x[k])
    end_a = along_hi(sum_a)
    end_x = along_hi(sum_x)
    end_a = end_a + to_x(end_a)
    far_x = to_x(end_x)
    end_x = jnp.where(
        x == 0, jnp.concatenate([end_x, far_x], 1), jnp.concatenate([far_x, end_x], 1)
    )
    scale = 1.0 / math.sqrt(members * npoints)
    mine = jnp.concatenate([end_a, end_x], 1) * scale
    other = to_core(mine)
    grad_inner = jnp.where(
        core == 0, jnp.concatenate([mine, other], 0), jnp.concatenate([other, mine], 0)
    )
    extra = lax.psum(extra, ("mem", "grid"))
    loss = jnp.sum(extra[v]) / npoints
    return (loss, gh, grad_inner, extra[:v] * scale)


def solution(mesh):
    in_specs = (P("mem", None, "grid"), P(None, "grid"), P("grid"), P(), P(), P(), P(), P())
    out_specs = (P(), P("mem", None, "grid"), P("grid", None), P())
    return jax.shard_map(shards, mesh=mesh, in_specs=in_specs, out_specs=out_specs, check_vma=False)
```

profile of v0, /device:TPU:9, one launch (start us, length us, event | category | flops | bytes accessed | tf_op | source)
XLA Modules:
  0.0 300.2 jit_solution(12655669488090634548)
XLA Ops:
  7.2 10.4 %forward_part.7 = (bf16[2,1024,512]{2,1,0:T(8,128)(2,1)}, f32[2,1024,512]{2,1,0:T(8,128)}, f32[2,100,512]{2,1,0:T(8,128)}) custom-call(bf16[2,1024,2048]{2,1,0:T(8,128)(2,1)} %hid_ref.13, bf16[1024,1024]{1,0:T(8,128)(2,1)} %w_ref.7, f32[1,1024]{1,0:T(1,128)} %bitcast.61, bf16[100,1024]{1,0:T(8,128)(2,1)} %wo_ref.7, f32[1,100]{1,0:T(1,128)} %bitcast.65), custom_call_target="tpu_custom_call" | custom-call | flops 2357198848 | bytes 10485760 | tf_op jit(solution)/shard_map/forward_part/pallas_call | solution.py:56
  17.6 1.2 collective-permute-start.10
  18.8 1.0 collective-permute-start.9
  19.7 10.5 %forward_part.5 = (bf16[2,1024,512]{2,1,0:T(8,128)(2,1)}, f32[2,1024,512]{2,1,0:T(8,128)}, f32[2,100,512]{2,1,0:T(8,128)}) custom-call(bf16[2,1024,2048]{2,1,0:T(8,128)(2,1)} %hid_ref.13, bf16[1024,1024]{1,0:T(8,128)(2,1)} %w_ref.7, f32[1,1024]{1,0:T(1,128)} %bitcast.62, bf16[100,1024]{1,0:T(8,128)(2,1)} %wo_ref.7, f32[1,100]{1,0:T(1,128)} %bitcast.66), custom_call_target="tpu_custom_call" | custom-call | flops 2357198848 | bytes 10485760 | tf_op jit(solution)/shard_map/forward_part/pallas_call | solution.py:56
  31.0 10.5 %forward_part.6 = (bf16[2,1024,512]{2,1,0:T(8,128)(2,1)}, f32[2,1024,512]{2,1,0:T(8,128)}, f32[2,100,512]{2,1,0:T(8,128)}) custom-call(bf16[2,1024,2048]{2,1,0:T(8,128)(2,1)} %hid_ref.13, bf16[1024,1024]{1,0:T(8,128)(2,1)} %w_ref.7, f32[1,1024]{1,0:T(1,128)} %bitcast.63, bf16[100,1024]{1,0:T(8,128)(2,1)} %wo_ref.7, f32[1,100]{1,0:T(1,128)} %bitcast.67), custom_call_target="tpu_custom_call" | custom-call | flops 2357198848 | bytes 10485760 | tf_op jit(solution)/shard_map/forward_part/pallas_call | solution.py:56
  41.5 1.1 collective-permute-start.4
  42.6 2.6 copy.16
  45.4 0.7 pad_bitcast_fusion.refs_10_.wot_ref
  46.1 10.4 %forward_part.4 = (bf16[2,1024,512]{2,1,0:T(8,128)(2,1)}, f32[2,1024,512]{2,1,0:T(8,128)}, f32[2,100,512]{2,1,0:T(8,128)}) custom-call(bf16[2,1024,2048]{2,1,0:T(8,128)(2,1)} %hid_ref.13, bf16[1024,1024]{1,0:T(8,128)(2,1)} %w_ref.7, f32[1,1024]{1,0:T(1,128)} %bitcast.64, bf16[100,1024]{1,0:T(8,128)(2,1)} %wo_ref.7, f32[1,100]{1,0:T(1,128)} %bitcast.68), custom_call_target="tpu_custom_call" | custom-call | flops 2357198848 | bytes 10485760 | tf_op jit(solution)/shard_map/forward_part/pallas_call | solution.py:56
  56.5 0.6 collective-permute-start.3
  57.2 0.4 collective-permute-start.1
  57.5 0.4 collective-permute-start.8
  57.9 13.5 %backward_part.4 = (bf16[2,1024,2048]{2,1,0:T(8,128)(2,1)}, f32[128,1024]{1,0:T(8,128)}, f32[1024,1024]{1,0:T(8,128)}) custom-call(f32[2,100,512]{2,1,0:T(8,128)} %get-tuple-element.44.refs_0_, f32[2,100,512]{2,1,0:T(8,128)} %collective-permute-done.9.refs_1_, f32[2,100,512]{2,1,0:T(8,128)} %collective-permute-done.10.refs_2_, ...), custom_call_target="tpu_custom_call" | custom-call | flops 4714397696 | bytes 20971520 | tf_op jit(solution)/shard_map/backward_part/pallas_call | solution.py:252
  71.7 0.4 collective-permute-start.5
  72.2 0.8 copy-done.11
  73.0 14.8 %backward_part.5 = (bf16[2,1024,2048]{2,1,0:T(8,128)(2,1)}, f32[128,1024]{1,0:T(8,128)}, f32[1024,1024]{1,0:T(8,128)}) custom-call(f32[2,100,512]{2,1,0:T(8,128)} %get-tuple-element.36.f_ref, f32[2,100,512]{2,1,0:T(8,128)} %collective-permute-done.6.fc_ref, f32[2,100,512]{2,1,0:T(8,128)} %copy-done.7, ...), custom_call_target="tpu_custom_call", output_to_operand_aliasing={{0}: (14, {})} | custom-call | flops 4714397696 | bytes 20971520 | tf_op jit(solution)/shard_map/backward_part/pallas_call | solution.py:252
  87.8 0.7 copy-done.8
  88.7 14.8 %backward_part.6 = (bf16[2,1024,2048]{2,1,0:T(8,128)(2,1)}, f32[128,1024]{1,0:T(8,128)}, f32[1024,1024]{1,0:T(8,128)}) custom-call(f32[2,100,512]{2,1,0:T(8,128)} %get-tuple-element.39.f_ref, f32[2,100,512]{2,1,0:T(8,128)} %copy-done.8, f32[2,100,512]{2,1,0:T(8,128)} %copy-done.6, f32[2,100,512]{2,1,0:T(8,128)} %copy-done.12, ...), custom_call_target="tpu_custom_call", output_to_operand_aliasing={{0}: (14, {})} | custom-call | flops 4714397696 | bytes 20971520 | tf_op jit(solution)/shard_map/backward_part/pallas_call | solution.py:252
  103.5 0.8 copy-done.9
  104.4 16.6 %backward_part.7 = (bf16[2,1024,2048]{2,1,0:T(8,128)(2,1)}, f32[128,1024]{1,0:T(8,128)}, f32[2,4,64,512]{3,2,1,0:T(8,128)}, f32[2,4,64,512]{3,2,1,0:T(8,128)}, f...) custom-call(f32[2,100,512]{2,1,0:T(8,128)} %get-tuple-element.33.f_ref, ...), custom_call_target="tpu_custom_call", output_to_operand_aliasing={{0}: (14, {})} | custom-call | flops 4714397696 | bytes 20971520 | tf_op jit(solution)/shard_map/backward_part/pallas_call | solution.py:252
  121.1 0.4 collective-permute-start.18
  121.6 2.4 collective-permute-done.18
  124.0 1.1 fusion
  125.1 1.2 collective-permute-start.19
  126.3 1.1 fusion.3
  127.4 1.3 collective-permute-start.13
  128.7 9.6 %collective-permute-done.19 = f32[2,4,64,256]{3,2,1,0:T(8,128)S(1)} collective-permute-done((f32[2,4,64,256]{3,2,1,0:T(8,128)S(1)}, f32[2,4,64,256]{3,2,1,0:T(8,128)S(1)}, u32[]{:S(2)}, u32[]{:S(2)}) %collective-permute-start.19) | collective-permute-done | bytes 524320 | tf_op jit(solution)/shard_map/ppermute | solution.py:291
  138.3 1.1 fusion.2
  139.5 1.3 collective-permute-start.20
  141.0 1.4 collective-permute-start.14
  142.4 1.1 collective-permute-start.15
  143.4 1.4 collective-permute-start.16
  144.8 1.3 collective-permute-done.20
  146.2 1.4 collective-permute-start.21
  147.6 1.1 collective-permute-start.22
  148.7 1.4 collective-permute-start.23
  150.1 0.7 collective-permute-done.15
  150.8 7.9 %collective-permute-done.16 = f32[64,512]{1,0:T(8,128)S(1)} collective-permute-done((f32[64,512]{1,0:T(8,128)S(1)}, f32[64,512]{1,0:T(8,128)S(1)}, u32[]{:S(2)}, u32[]{:S(2)}) %collective-permute-start.16) | collective-permute-done | bytes 131104 | tf_op jit(solution)/shard_map/ppermute | solution.py:294
  158.6 1.2 collective-permute-start.17
  159.8 1.6 collective-permute-done.23
  161.4 1.2 collective-permute-start.24
  162.6 0.5 collective-permute-done.17
  163.2 1.4 collective-permute-done.24
  164.7 1.7 collective-permute-start.25
  166.4 121.1 %all-reduce.3.cloned.1.call-done = f32[128,1024]{1,0:T(8,128)} async-done(((f32[128,1024]{1,0:T(8,128)}), f32[128,1024]{1,0:T(8,128)}) %all-reduce.3.cloned.1.call-update) | async-done | bytes 524304 | tf_op jit(solution)/shard_map/psum | solution.py:353
  287.5 1.4 slice_reduce_fusion
  289.5 1.8 slice_multiply_fusion
  291.4 0.8 maximum_select_fusion
  (60 shorter events, 2.2 us)
Async XLA Ops:
  7.2 280.4 %all-reduce.3.cloned.1.call-start = ((), (), s32[]{:S(2)}) async-start(), calls=%async_computation | async-start | bytes 1048576 | tf_op jit(solution)/shard_map/psum | solution.py:353
  17.6 13.2 %collective-permute-start.10 = (f32[2,100,512]{2,1,0:T(8,128)}, f32[2,100,512]{2,1,0:T(8,128)}, u32[]{:S(2)}, u32[]{:S(2)}) collective-permute-start(f32[2,100,512]{2,1,0:T(8,128)} %get-tuple-element.44.refs_0_), channel_id=1, source_target_pairs={{0,16},{8,24},{16,0},{24,8},{1,17},{9,25},{17,1},{25,9},{2,18},{10... | collective-permute-start | bytes 1228808 | tf_op jit(solution)/shard_map/ppermute | solution.py:291
  18.8 37.7 %collective-permute-start.9 = (f32[2,100,512]{2,1,0:T(8,128)}, f32[2,100,512]{2,1,0:T(8,128)}, u32[]{:S(2)}, u32[]{:S(2)}) collective-permute-start(f32[2,100,512]{2,1,0:T(8,128)} %get-tuple-element.44.refs_0_), channel_id=1, source_target_pairs={{0,8},{8,0},{16,24},{24,16},{1,9},{9,1},{17,25},{25,17},{2,10},{10... | collective-permute-start | bytes 1228808 | tf_op jit(solution)/shard_map/ppermute | solution.py:292
  30.2 12.4 %copy-start = (bf16[1024,1024]{1,0:T(8,128)(2,1)S(1)}, bf16[1024,1024]{1,0:T(8,128)(2,1)}, u32[]{:S(2)}) copy-start(bf16[1024,1024]{1,0:T(8,128)(2,1)} %w_ref.7) | copy-start | bytes 6291460
  30.2 26.9 %collective-permute-start.7 = (f32[2,100,512]{2,1,0:T(8,128)}, f32[2,100,512]{2,1,0:T(8,128)S(1)}, u32[]{:S(2)}, u32[]{:S(2)}) collective-permute-start(f32[2,100,512]{2,1,0:T(8,128)} %get-tuple-element.36.f_ref), channel_id=1, source_target_pairs={{0,16},{8,24},{16,0},{24,8},{1,17},{9,25},{17,1},{25,9},{2,18},{10... | collective-permute-start | bytes 1228808 | tf_op jit(solution)/shard_map/ppermute | solution.py:291
  30.5 41.0 %collective-permute-start.6 = (f32[2,100,512]{2,1,0:T(8,128)}, f32[2,100,512]{2,1,0:T(8,128)}, u32[]{:S(2)}, u32[]{:S(2)}) collective-permute-start(f32[2,100,512]{2,1,0:T(8,128)} %get-tuple-element.36.f_ref), channel_id=1, source_target_pairs={{0,8},{8,0},{16,24},{24,16},{1,9},{9,1},{17,25},{25,17},{2,10},{10... | collective-permute-start | bytes 1228808 | tf_op jit(solution)/shard_map/ppermute | solution.py:292
  30.8 26.8 %collective-permute-start.11 = (f32[2,100,512]{2,1,0:T(8,128)}, f32[2,100,512]{2,1,0:T(8,128)}, u32[]{:S(2)}, u32[]{:S(2)}) collective-permute-start(f32[2,100,512]{2,1,0:T(8,128)} %collective-permute-done.10.refs_2_), channel_id=1, source_target_pairs={{0,8},{8,0},{16,24},{24,16},{1,9},{9,1},{17,25},{25,17},{2,10},{10... | collective-permute-start | bytes 1228808 | tf_op jit(solution)/shard_map/ppermute | solution.py:292
  41.5 3.7 %copy-start.1 = (bf16[100,1024]{1,0:T(8,128)(2,1)S(1)}, bf16[100,1024]{1,0:T(8,128)(2,1)}, u32[]{:S(2)}) copy-start(bf16[100,1024]{1,0:T(8,128)(2,1)} %wo_ref.7) | copy-start | bytes 614404
  41.5 30.2 %collective-permute-start.4 = (f32[2,100,512]{2,1,0:T(8,128)}, f32[2,100,512]{2,1,0:T(8,128)S(1)}, u32[]{:S(2)}, u32[]{:S(2)}) collective-permute-start(f32[2,100,512]{2,1,0:T(8,128)} %get-tuple-element.39.f_ref), channel_id=1, source_target_pairs={{0,16},{8,24},{16,0},{24,8},{1,17},{9,25},{17,1},{25,9},{2,18},{10... | collective-permute-start | bytes 1228808 | tf_op jit(solution)/shard_map/ppermute | solution.py:291
  46.1 10.4 %copy-start.5 = (f32[2,100,512]{2,1,0:T(8,128)S(1)}, f32[2,100,512]{2,1,0:T(8,128)}, u32[]{:S(2)}) copy-start(f32[2,100,512]{2,1,0:T(8,128)} %get-tuple-element.39.f_ref) | copy-start | bytes 1228804
  56.5 31.3 %collective-permute-start.3 = (f32[2,100,512]{2,1,0:T(8,128)S(1)}, f32[2,100,512]{2,1,0:T(8,128)S(1)}, u32[]{:S(2)}, u32[]{:S(2)}) collective-permute-start(f32[2,100,512]{2,1,0:T(8,128)S(1)} %copy-done.5), channel_id=1, source_target_pairs={{0,8},{8,0},{16,24},{24,16},{1,9},{9,1},{17,25},{25,17},{2,10},{10... | collective-permute-start | bytes 1228808 | tf_op jit(solution)/shard_map/ppermute | solution.py:292
  57.1 14.3 %copy-start.7 = (f32[2,100,512]{2,1,0:T(8,128)}, f32[2,100,512]{2,1,0:T(8,128)S(1)}, u32[]{:S(2)}) copy-start(f32[2,100,512]{2,1,0:T(8,128)S(1)} %collective-permute-done.7.fx_ref) | copy-start | bytes 1228804
  57.2 14.9 %collective-permute-start.1 = (f32[2,100,512]{2,1,0:T(8,128)}, f32[2,100,512]{2,1,0:T(8,128)S(1)}, u32[]{:S(2)}, u32[]{:S(2)}) collective-permute-start(f32[2,100,512]{2,1,0:T(8,128)} %get-tuple-element.33.f_ref), channel_id=1, source_target_pairs={{0,16},{8,24},{16,0},{24,8},{1,17},{9,25},{17,1},{25,9},{2,18},{10... | collective-permute-start | bytes 1228808 | tf_op jit(solution)/shard_map/ppermute | solution.py:291
  57.5 14.7 %collective-permute-start.8 = (f32[2,100,512]{2,1,0:T(8,128)S(1)}, f32[2,100,512]{2,1,0:T(8,128)S(1)}, u32[]{:S(2)}, u32[]{:S(2)}) collective-permute-start(f32[2,100,512]{2,1,0:T(8,128)S(1)} %collective-permute-done.7.fx_ref), channel_id=1, source_target_pairs={{0,8},{8,0},{16,24},{24,16},{1,9},{9,1},{17,25},{25,17},{2,10},{10... | collective-permute-start | bytes 1228808 | tf_op jit(solution)/shard_map/ppermute | solution.py:292
  57.9 13.6 %copy-start.3 = (f32[2,100,512]{2,1,0:T(8,128)S(1)}, f32[2,100,512]{2,1,0:T(8,128)}, u32[]{:S(2)}) copy-start(f32[2,100,512]{2,1,0:T(8,128)} %get-tuple-element.33.f_ref) | copy-start | bytes 1228804
  71.5 32.0 %collective-permute-start = (f32[2,100,512]{2,1,0:T(8,128)S(1)}, f32[2,100,512]{2,1,0:T(8,128)S(1)}, u32[]{:S(2)}, u32[]{:S(2)}) collective-permute-start(f32[2,100,512]{2,1,0:T(8,128)S(1)} %copy-done.3), channel_id=1, source_target_pairs={{0,8},{8,0},{16,24},{24,16},{1,9},{9,1},{17,25},{25,17},{2,10},{10... | collective-permute-start | bytes 1228808 | tf_op jit(solution)/shard_map/ppermute | solution.py:292
  71.7 16.1 %copy-start.6 = (f32[2,100,512]{2,1,0:T(8,128)}, f32[2,100,512]{2,1,0:T(8,128)S(1)}, u32[]{:S(2)}) copy-start(f32[2,100,512]{2,1,0:T(8,128)S(1)} %collective-permute-done.4.fx_ref) | copy-start | bytes 1228804
  71.7 16.1 %collective-permute-start.5 = (f32[2,100,512]{2,1,0:T(8,128)S(1)}, f32[2,100,512]{2,1,0:T(8,128)S(1)}, u32[]{:S(2)}, u32[]{:S(2)}) collective-permute-start(f32[2,100,512]{2,1,0:T(8,128)S(1)} %collective-permute-done.4.fx_ref), channel_id=1, source_target_pairs={{0,8},{8,0},{16,24},{24,16},{1,9},{9,1},{17,25},{25,17},{2,10},{10... | collective-permute-start | bytes 1228808 | tf_op jit(solution)/shard_map/ppermute | solution.py:292
  72.1 15.7 %copy-start.4 = (f32[2,100,512]{2,1,0:T(8,128)}, f32[2,100,512]{2,1,0:T(8,128)S(1)}, u32[]{:S(2)}) copy-start(f32[2,100,512]{2,1,0:T(8,128)S(1)} %collective-permute-done.1.fx_ref) | copy-start | bytes 1228804
  72.1 31.4 %collective-permute-start.2 = (f32[2,100,512]{2,1,0:T(8,128)S(1)}, f32[2,100,512]{2,1,0:T(8,128)S(1)}, u32[]{:S(2)}, u32[]{:S(2)}) collective-permute-start(f32[2,100,512]{2,1,0:T(8,128)S(1)} %collective-permute-done.1.fx_ref), channel_id=1, source_target_pairs={{0,8},{8,0},{16,24},{24,16},{1,9},{9,1},{17,25},{25,17},{2,10},{10... | collective-permute-start | bytes 1228808 | tf_op jit(solution)/shard_map/ppermute | solution.py:292
  72.2 0.8 copy-start.11
  87.8 0.8 copy-start.8
  87.8 0.9 copy-start.12
  103.5 0.8 copy-start.9
  103.5 0.9 copy-start.10
  121.1 19.8 %copy-start.2 = (f32[2,4,64,512]{3,2,1,0:T(8,128)S(1)}, f32[2,4,64,512]{3,2,1,0:T(8,128)}, u32[]{:S(2)}) copy-start(f32[2,4,64,512]{3,2,1,0:T(8,128)} %get-tuple-element.58) | copy-start | bytes 3145732
  121.1 2.9 collective-permute-start.18
  121.5 4.8 %collective-permute-start.12 = (f32[2,4,64,512]{3,2,1,0:T(8,128)}, f32[2,4,64,512]{3,2,1,0:T(8,128)S(1)}, u32[]{:S(2)}, u32[]{:S(2)}) collective-permute-start(f32[2,4,64,512]{3,2,1,0:T(8,128)} %get-tuple-element.59), channel_id=1, source_target_pairs={{0,8},{8,0},{16,24},{24,16},{1,9},{9,1},{17,25},{25,17},{2,10},{10... | collective-permute-start | bytes 3145736 | tf_op jit(solution)/shard_map/ppermute | solution.py:292
  125.1 13.2 %collective-permute-start.19 = (f32[2,4,64,256]{3,2,1,0:T(8,128)S(1)}, f32[2,4,64,256]{3,2,1,0:T(8,128)S(1)}, u32[]{:S(2)}, u32[]{:S(2)}) collective-permute-start(f32[2,4,64,256]{3,2,1,0:T(8,128)S(1)} %fusion), channel_id=1, source_target_pairs={{0,16},{8,24},{16,0},{24,8},{1,17},{9,25},{17,1},{25,9},{2,18},{10... | collective-permute-start | bytes 1572872 | tf_op jit(solution)/shard_map/ppermute | solution.py:291
  127.4 13.4 %collective-permute-start.13 = (f32[4,64,512]{2,1,0:T(8,128)S(1)}, f32[4,64,512]{2,1,0:T(8,128)S(1)}, u32[]{:S(2)}, u32[]{:S(2)}) collective-permute-start(f32[4,64,512]{2,1,0:T(8,128)S(1)} %fusion.3), channel_id=1, source_target_pairs={{0,1},{1,0},{2,3},{3,2},{4,5},{5,4},{6,7},{7,6},{8,9},{9,8},{10,11... | collective-permute-start | bytes 1572872 | tf_op jit(solution)/shard_map/ppermute | solution.py:293
  139.5 6.7 %collective-permute-start.20 = (f32[4,64,256]{2,1,0:T(8,128)S(1)}, f32[4,64,256]{2,1,0:T(8,128)S(1)}, u32[]{:S(2)}, u32[]{:S(2)}) collective-permute-start(f32[4,64,256]{2,1,0:T(8,128)S(1)} %slice_bitcast_fusion), channel_id=1, source_target_pairs={{0,1},{1,0},{2,3},{3,2},{4,5},{5,4},{6,7},{7,6},{8,9},{9,8},{10,11... | collective-permute-start | bytes 786440 | tf_op jit(solution)/shard_map/ppermute | solution.py:293
  141.0 7.7 %collective-permute-start.14 = (f32[64,512]{1,0:T(8,128)S(1)}, f32[64,512]{1,0:T(8,128)S(1)}, u32[]{:S(2)}, u32[]{:S(2)}) collective-permute-start(f32[64,512]{1,0:T(8,128)S(1)} %get-tuple-element.62), channel_id=1, source_target_pairs={{0,2},{1,3},{2,4},{3,5},{4,6},{5,7},{6,0},{7,1},{8,10},{9,11},{10,... | collective-permute-start | bytes 393224 | tf_op jit(solution)/shard_map/ppermute | solution.py:294
  142.4 8.4 %collective-permute-start.15 = (f32[64,512]{1,0:T(8,128)S(1)}, f32[64,512]{1,0:T(8,128)S(1)}, u32[]{:S(2)}, u32[]{:S(2)}) collective-permute-start(f32[64,512]{1,0:T(8,128)S(1)} %get-tuple-element.64), channel_id=1, source_target_pairs={{0,4},{1,5},{2,6},{3,7},{4,0},{5,1},{6,2},{7,3},{8,12},{9,13},{10,... | collective-permute-start | bytes 393224 | tf_op jit(solution)/shard_map/ppermute | solution.py:294
  143.4 15.2 %collective-permute-start.16 = (f32[64,512]{1,0:T(8,128)S(1)}, f32[64,512]{1,0:T(8,128)S(1)}, u32[]{:S(2)}, u32[]{:S(2)}) collective-permute-start(f32[64,512]{1,0:T(8,128)S(1)} %get-tuple-element.63), channel_id=1, source_target_pairs={{0,6},{1,7},{2,0},{3,1},{4,2},{5,3},{6,4},{7,5},{8,14},{9,15},{10,... | collective-permute-start | bytes 393224 | tf_op jit(solution)/shard_map/ppermute | solution.py:294
  146.2 13.6 %collective-permute-start.21 = (f32[64,256]{1,0:T(8,128)S(1)}, f32[64,256]{1,0:T(8,128)S(1)}, u32[]{:S(2)}, u32[]{:S(2)}) collective-permute-start(f32[64,256]{1,0:T(8,128)S(1)} %get-tuple-element.65), channel_id=1, source_target_pairs={{0,2},{1,3},{2,4},{3,5},{4,6},{5,7},{6,0},{7,1},{8,10},{9,11},{10,... | collective-permute-start | bytes 196616 | tf_op jit(solution)/shard_map/ppermute | solution.py:294
  147.6 12.2 %collective-permute-start.22 = (f32[64,256]{1,0:T(8,128)S(1)}, f32[64,256]{1,0:T(8,128)S(1)}, u32[]{:S(2)}, u32[]{:S(2)}) collective-permute-start(f32[64,256]{1,0:T(8,128)S(1)} %get-tuple-element.67), channel_id=1, source_target_pairs={{0,4},{1,5},{2,6},{3,7},{4,0},{5,1},{6,2},{7,3},{8,12},{9,13},{10,... | collective-permute-start | bytes 196616 | tf_op jit(solution)/shard_map/ppermute | solution.py:294
  148.7 12.7 %collective-permute-start.23 = (f32[64,256]{1,0:T(8,128)S(1)}, f32[64,256]{1,0:T(8,128)S(1)}, u32[]{:S(2)}, u32[]{:S(2)}) collective-permute-start(f32[64,256]{1,0:T(8,128)S(1)} %get-tuple-element.66), channel_id=1, source_target_pairs={{0,6},{1,7},{2,0},{3,1},{4,2},{5,3},{6,4},{7,5},{8,14},{9,15},{10,... | collective-permute-start | bytes 196616 | tf_op jit(solution)/shard_map/ppermute | solution.py:294
  158.6 4.5 %collective-permute-start.17 = (f32[64,512]{1,0:T(8,128)S(1)}, f32[64,512]{1,0:T(8,128)S(1)}, u32[]{:S(2)}, u32[]{:S(2)}) collective-permute-start(f32[64,512]{1,0:T(8,128)S(1)} %fusion.9), channel_id=1, source_target_pairs={{0,16},{8,24},{16,0},{24,8},{1,17},{9,25},{17,1},{25,9},{2,18},{10... | collective-permute-start | bytes 393224 | tf_op jit(solution)/shard_map/ppermute | solution.py:291
  161.4 3.2 %collective-permute-start.24 = (f32[64,256]{1,0:T(8,128)S(1)}, f32[64,256]{1,0:T(8,128)S(1)}, u32[]{:S(2)}, u32[]{:S(2)}) collective-permute-start(f32[64,256]{1,0:T(8,128)S(1)} %fusion.12), channel_id=1, source_target_pairs={{0,16},{8,24},{16,0},{24,8},{1,17},{9,25},{17,1},{25,9},{2,18},{10... | collective-permute-start | bytes 196616 | tf_op jit(solution)/shard_map/ppermute | solution.py:291
  164.7 126.7 %collective-permute-start.25 = (f32[64,1024]{1,0:T(8,128)S(1)}, f32[64,1024]{1,0:T(8,128)S(1)}, u32[]{:S(2)}, u32[]{:S(2)}) collective-permute-start(f32[64,1024]{1,0:T(8,128)S(1)} %maximum_multiply_fusion), channel_id=1, source_target_pairs={{0,8},{8,0},{16,24},{24,16},{1,9},{9,1},{17,25},{25,17},{2,10},{10... | collective-permute-start | bytes 786440 | tf_op jit(solution)/shard_map/ppermute | solution.py:292
Sparse Core Ops, SparseCore 0:
  162.7 124.7 all-reduce.2
where the time goes:
time: 304 us; the launch traced here: 300 us
  waiting for transfers between devices  147 us (48%)
  Pallas kernels  101 us (33%)
  starting transfers between devices  22.2 us (7%)
  between operations  16.1 us (5%)
  other arithmetic  7.69 us (3%)
  local copies, waits for them, and re-layouts  6.16 us (2%)
    psum x1, waiting for transfers between devices, shards(): extra = lax.psum(extra, ('mem', 'grid'))  121 us
    pallas_call x4, Pallas kernels, backward(): pl.pallas_call(kernel_fn, grid=(steps,), in_specs=in_specs, out_specs=out...  59.7 us
    pallas_call x4, Pallas kernels, forward(): pl.pallas_call(forward_kernel, grid=(mloc,), in_specs=[pl.BlockSpec((1, h...  41.7 us
    ppermute x7, waiting for transfers between devices, shards(): to_x = lambda a: lax.ppermute(a, 'mem', swap_x)  11.6 us
    ppermute x6, waiting for transfers between devices, shards(): to_hi = lambda a, k: lax.ppermute(a, 'grid', shift_hi(k))  10.2 us
    ppermute x6, starting transfers between devices, shards(): to_hi = lambda a, k: lax.ppermute(a, 'grid', shift_hi(k))  7.66 us
    ppermute x7, starting transfers between devices, shards(): to_x = lambda a: lax.ppermute(a, 'mem', swap_x)  6.42 us
  transfers between devices with their start and end apart: 27, of which 9 were waited for; matrix products, arithmetic and copies ran while one was open for 3% of the time, Pallas kernels for 25%

commit v1 on v0

--- a/solution.py
+++ b/solution.py
@@ -14,7 +14,9 @@
 EPS = 0.0004
 K0 = math.sqrt(2.0 / math.pi)
 K1 = K0 * 0.044715
-VMEM = 56 * 1024 * 1024
+SLAB = 256
+FWD_VMEM = 20 * 1024 * 1024
+BWD_VMEM = 34 * 1024 * 1024
 NT = (((1,), (1,)), ((), ()))
 
 
@@ -24,57 +26,89 @@
     return jnp.sum(jnp.where(r == c, row, 0.0), axis=1, keepdims=True)
 
 
-def forward_kernel(hid_ref, w_ref, b_ref, wo_ref, bo_ref, act_ref, slope_ref, f_ref, bias):
-    @pl.when(pl.program_id(0) == 0)
+def forward_kernel(tiles, hid_ref, w_ref, b_ref, wo_ref, bo_ref, act_ref, slope_ref, f_ref, bias, even, odd):
+    step = pl.program_id(0)
+
+    @pl.when(step == 0)
     def _():
         for k in range(bias.shape[0] // 128):
             bias[pl.ds(k * 128, 128), :] = jnp.broadcast_to(
                 column(b_ref[:, pl.ds(k * 128, 128)], 128), (128, 128)
             )
 
-    out_bias = column(bo_ref[...], bo_ref.shape[1])
-    for s in range(hid_ref.shape[2] // FWD_TILE):
-        cols = pl.ds(s * FWD_TILE, FWD_TILE)
-        b = jnp.concatenate([bias[...]] * (FWD_TILE // 128), axis=1)
-        x = jnp.dot(w_ref[...], hid_ref[0, :, cols], preferred_element_type=jnp.float32) + b
-        x2 = x * x
-        u = 0.5 + 0.5 * jnp.tanh(x * (K0 + K1 * x2))
-        act = (x * u).astype(jnp.bfloat16)
-        act_ref[0, :, cols] = act
-        slope_ref[0, :, cols] = u + (u - u * u) * (x * (2.0 * K0 + 6.0 * K1 * x2))
-        f_ref[0, :, cols] = (
-            jnp.dot(wo_ref[...], act, preferred_element_type=jnp.float32) + out_bias
-        )
+    def both(fill, drain):
+        h, t = fill.shape
+        fill[...] = jnp.dot(w_ref[...], hid_ref[0], preferred_element_type=jnp.float32)
+        out = jnp.broadcast_to(column(bo_ref[...], bo_ref.shape[1]), f_ref.shape[1:])
+        for k in range(0, h, SLAB):
+            for r in range(k, k + SLAB, 16):
+                rows = pl.ds(r, 16)
+                b = jnp.concatenate([bias[rows, :]] * (t // 128), axis=1)
+                x = drain[rows, :] + b
+                q = x * x * K1
+                th = jnp.tanh(x * (K0 + q))
+                up = 1.0 + th
+                act_ref[0, rows, :] = (x * up).astype(jnp.bfloat16)
+                slope_ref[0, rows, :] = up * (1.0 + (1.0 - th) * (x * (K0 + 3.0 * q)))
+            slab = pl.ds(k, SLAB)
+            out = out + jnp.dot(
+                wo_ref[:, slab], act_ref[0, slab, :], preferred_element_type=jnp.float32
+            )
+        f_ref[0] = out
+
+    @pl.when(step % 2 == 0)
+    def _():
+        both(even, odd)
+
+    @pl.when(step % 2 == 1)
+    def _():
+        both(odd, even)
 
 
 def forward(part, hidden, w_inner, b_inner, w_out, b_out):
     mloc, h, n = hidden.shape
     v = w_out.shape[0]
     p = n // PARTS
-    whole = lambda m: (0, 0)
+    t = FWD_TILE
+    per = p // t
+    tiles = mloc * per
+    whole = lambda s: (0, 0)
     once = pl.Buffered(1)
+
+    def ahead(s):
+        s = jnp.minimum(s, tiles - 1)
+        return (s // per, 0, part * per + s % per)
+
+    def behind(s):
+        s = jnp.maximum(s - 1, 0)
+        return (s // per, 0, s % per)
+
     return pl.pallas_call(
-        forward_kernel,
-        grid=(mloc,),
+        functools.partial(forward_kernel, tiles),
+        grid=(tiles + 1,),
         in_specs=[
-            pl.BlockSpec((1, h, p), lambda m: (m, 0, part)),
+            pl.BlockSpec((1, h, t), ahead),
             pl.BlockSpec((h, h), whole, pipeline_mode=once),
             pl.BlockSpec((1, h), whole, pipeline_mode=once),
             pl.BlockSpec((v, h), whole, pipeline_mode=once),
             pl.BlockSpec((1, v), whole, pipeline_mode=once),
         ],
         out_specs=[
-            pl.BlockSpec((1, h, p), lambda m: (m, 0, 0)),
-            pl.BlockSpec((1, h, p), lambda m: (m, 0, 0)),
-            pl.BlockSpec((1, v, p), lambda m: (m, 0, 0)),
+            pl.BlockSpec((1, h, t), behind),
+            pl.BlockSpec((1, h, t), behind),
+            pl.BlockSpec((1, v, t), behind),
         ],
         out_shape=[
             jax.ShapeDtypeStruct((mloc, h, p), jnp.bfloat16),
             jax.ShapeDtypeStruct((mloc, h, p), jnp.float32),
             jax.ShapeDtypeStruct((mloc, v, p), jnp.float32),
         ],
-        scratch_shapes=[pltpu.VMEM((h, 128), jnp.float32)],
-        compiler_params=pltpu.CompilerParams(vmem_limit_bytes=VMEM),
+        scratch_shapes=[
+            pltpu.VMEM((h, 128), jnp.float32),
+            pltpu.VMEM((h, t), jnp.float32),
+            pltpu.VMEM((h, t), jnp.float32),
+        ],
+        compiler_params=pltpu.CompilerParams(vmem_limit_bytes=FWD_VMEM),
         cost_estimate=pl.CostEstimate(
             flops=2 * mloc * p * h * (h + v), bytes_accessed=mloc * p * h * 8 + 2 * h * h,
             transcendentals=mloc * p * h,
@@ -89,9 +123,9 @@
     wot_ref, wt_ref, acc_in, extra_in, gh_in, gh_ref, extra_ref, *refs,
 ):
     if last:
-        keep_a, send_a, keep_x, send_x, acc, gf = refs
+        keep_a, send_a, keep_x, send_x, acc, gf, gp = refs
     else:
-        acc, gf = refs
+        acc, gf, gp = refs
     step = pl.program_id(0)
     mloc, v, t = f_ref.shape
     h = wt_ref.shape[0]
@@ -144,37 +178,37 @@
     for m in range(mloc):
         gf[m, pl.ds(v, gf.shape[1] - v), :] = jnp.zeros((gf.shape[1] - v, t), jnp.float32)
 
-    gp = []
-    extra = None
-    for m in range(mloc):
-        g = gf[m].astype(jnp.bfloat16)
-        ga = jnp.dot(wot_ref[...], g, preferred_element_type=jnp.float32)
-        gp.append((ga * slope_ref[m]).astype(jnp.bfloat16))
-        out = lax.dot_general(g, act_ref[m], NT, preferred_element_type=jnp.float32)
-        extra = out if extra is None else extra + out
-    gpc = jnp.concatenate(gp, axis=1)
-    hidc = jnp.concatenate([hid_ref[m] for m in range(mloc)], axis=1)
-    prod = lax.dot_general(gpc, hidc, NT, preferred_element_type=jnp.float32)
+    g = jnp.concatenate([gf[m] for m in range(mloc)], axis=1).astype(jnp.bfloat16)
+    for k in range(0, h, SLAB):
+        rows = pl.ds(k, SLAB)
+        ga = jnp.dot(wot_ref[rows, :], g, preferred_element_type=jnp.float32)
+        slope = jnp.concatenate([slope_ref[m, rows, :] for m in range(mloc)], axis=1)
+        gp[rows, :] = (ga * slope).astype(jnp.bfloat16)
+    hid = jnp.concatenate([hid_ref[m] for m in range(mloc)], axis=1)
+    act = jnp.concatenate([act_ref[m] for m in range(mloc)], axis=1)
+    extra = lax.dot_general(g, act, NT, preferred_element_type=jnp.float32)
+
+    def accumulate(base, extra_base):
+        extra_ref[...] = extra if extra_base is None else extra_base[...] + extra
+        for k in range(0, h, SLAB):
+            rows = pl.ds(k, SLAB)
+            prod = lax.dot_general(gp[rows, :], hid, NT, preferred_element_type=jnp.float32)
+            acc[rows, :] = prod if base is None else base[rows, :] + prod
 
     @pl.when(step == 0)
     def _():
-        if first:
-            acc[...] = prod
-            extra_ref[...] = extra
-        else:
-            acc[...] = acc_in[...] + prod
-            extra_ref[...] = extra_in[...] + extra
+        accumulate(acc_in, extra_in)
 
     @pl.when(step > 0)
     def _():
-        acc[...] += prod
-        extra_ref[...] += extra
+        accumulate(acc, extra_ref)
 
     extra_ref[pl.ds(v, 1), pl.ds(0, t)] += loss
-    for m in range(mloc):
-        gh_ref[m] = jnp.dot(wt_ref[...], gp[m], preferred_element_type=jnp.float32).astype(
-            jnp.bfloat16
-        )
+    for k in range(0, h, SLAB):
+        rows = pl.ds(k, SLAB)
+        out = jnp.dot(wt_ref[rows, :], gp[...], preferred_element_type=jnp.float32)
+        for m in range(mloc):
+            gh_ref[m, rows, :] = out[:, m * t : (m + 1) * t].astype(jnp.bfloat16)
     if last:
         n_hi, n_lo = dims
 
@@ -231,23 +265,26 @@
         in_specs += [const(acc), const(extra), anyspec]
         args += [acc, extra, gh]
         aliases = {14: 0}
-    out_specs = [placed, pl.BlockSpec((vp, h), whole)]
+    out_specs = [placed, pl.BlockSpec((vp, h), whole, pipeline_mode=once)]
     out_shape = [
         jax.ShapeDtypeStruct(hidden.shape, jnp.bfloat16),
         jax.ShapeDtypeStruct((vp, h), jnp.float32),
     ]
-    scratch = [pltpu.VMEM((mloc, vp, t), jnp.float32)]
+    scratch = [
+        pltpu.VMEM((mloc, vp, t), jnp.float32),
+        pltpu.VMEM((h, mloc * t), jnp.bfloat16),
+    ]
     if last:
         n_hi, n_lo = dims
         r = h // (2 * n_hi * n_lo)
         ca = h // 2
         cx = (h - ca) // 2
         for shape in ((n_lo, n_hi, r, ca), (n_lo, n_hi, r, ca), (2, n_lo, n_hi, r, cx), (2, n_lo, n_hi, r, cx)):
-            out_specs.append(pl.BlockSpec(shape, lambda s, k=len(shape): (0,) * k))
+            out_specs.append(pl.BlockSpec(shape, lambda s, k=len(shape): (0,) * k, pipeline_mode=once))
             out_shape.append(jax.ShapeDtypeStruct(shape, jnp.float32))
         scratch = [pltpu.VMEM((h, h), jnp.float32)] + scratch
     else:
-        out_specs.append(pl.BlockSpec((h, h), whole))
+        out_specs.append(pl.BlockSpec((h, h), whole, pipeline_mode=once))
         out_shape.append(jax.ShapeDtypeStruct((h, h), jnp.float32))
     return pl.pallas_call(
         kernel_fn,
@@ -257,7 +294,7 @@
         out_shape=out_shape,
         scratch_shapes=scratch,
         input_output_aliases=aliases,
-        compiler_params=pltpu.CompilerParams(vmem_limit_bytes=VMEM),
+        compiler_params=pltpu.CompilerParams(vmem_limit_bytes=BWD_VMEM),
         cost_estimate=pl.CostEstimate(
             flops=4 * mloc * p * h * (h + v), bytes_accessed=mloc * p * h * 10 + 10 * h * h,
             transcendentals=mloc * p * v * 8,
@@ -293,19 +330,20 @@
     to_lo = lambda a, k: lax.ppermute(a, "grid", shift_lo(k))
     to_hi = lambda a, k: lax.ppermute(a, "grid", shift_hi(k))
 
+    half_out = w_out * jnp.bfloat16(0.5)
     parts = []
     for part in range(PARTS):
         parts.append(
-            forward(part, hidden, w_inner, b_inner.reshape(1, h), w_out, b_out.reshape(1, v))
+            forward(part, hidden, w_inner, b_inner.reshape(1, h), half_out, b_out.reshape(1, v))
         )
     exchanged = []
     for act, slope, fields in parts:
         far = to_x(fields)
         exchanged.append((fields, to_core(fields), far, to_core(far)))
 
-    w_inner, w_out, _ = lax.optimization_barrier((w_inner, w_out, parts[1][2]))
+    w_inner, half_out, _ = lax.optimization_barrier((w_inner, half_out, parts[1][2]))
     wt = w_inner.T
-    wot = jnp.pad(w_out, ((0, vp - v), (0, 0))).T
+    wot = jnp.pad(half_out, ((0, vp - v), (0, 0))).T
     vw, area = var_weight.reshape(1, v), area.reshape(1, n)
     acc = extra = gh = None
     for part in range(PARTS):
@@ -320,6 +358,12 @@
     core = lax.axis_index("mem") % 2
     x = lax.axis_index("mem") // 2
 
+    def flips(name):
+        n, k = lax.axis_size(name), 1
+        while k < n:
+            yield [(i, i ^ k) for i in range(n)]
+            k *= 2
+
     def along_lo(blocks):
         total = blocks(0)
         for k in range(1, n_lo):
@@ -332,10 +376,18 @@
             total = total + to_hi(blocks[k], k)
         return total
 
+    half = vp // 2
+    keep_e = lax.dynamic_slice_in_dim(extra, core * half, half, 0)
+    send_e = lax.dynamic_slice_in_dim(extra, (1 - core) * half, half, 0)
     got_a = to_core(send_a)
+    got_e = to_core(send_e)
     got_x = to_core(send_x)
     sum_a = along_lo(lambda k: keep_a[k] + got_a[k])
     own_x = keep_x[0] + got_x[0] + to_x(keep_x[1] + got_x[1])
+    sum_e = keep_e + got_e
+    for perm in flips("grid"):
+        sum_e = sum_e + lax.ppermute(sum_e, "grid", perm)
+    sum_e = sum_e + to_x(sum_e)
     sum_x = along_lo(lambda k: own_x[k])
     end_a = along_hi(sum_a)
     end_x = along_hi(sum_x)
@@ -350,9 +402,12 @@
     grad_inner = jnp.where(
         core == 0, jnp.concatenate([mine, other], 0), jnp.concatenate([other, mine], 0)
     )
-    extra = lax.psum(extra, ("mem", "grid"))
+    other_e = to_core(sum_e)
+    extra = jnp.where(
+        core == 0, jnp.concatenate([sum_e, other_e], 0), jnp.concatenate([other_e, sum_e], 0)
+    )
     loss = jnp.sum(extra[v]) / npoints
-    return (loss, gh, grad_inner, extra[:v] * scale)
+    return (loss, gh, grad_inner, extra[:v] * (0.5 * scale))
 
 
 def solution(mesh):

time: 304 us -> 197 us (0.65)
  waiting for transfers between devices: 147 us -> 42.2 us
  local copies, waits for them, and re-layouts: 6.16 us -> 37.9 us
  Pallas kernels: 101 us -> 70.8 us
  between operations: 16.1 us -> 2.74 us
  starting transfers between devices: 22.2 us -> 31.9 us
    psum x1 -> x0, waiting for transfers between devices: 121 us -> none  [shards(): extra = lax.psum(extra, ('mem', 'grid'))]
    unnamed x26 -> x79, local copies, waits for them, and re-layouts: 2.61 us -> 35 us
    ppermute x0 -> x3, waiting for transfers between devices: none -> 21.7 us  [shards(): sum_e = sum_e + lax.ppermute(sum_e, 'grid', perm)]
    pallas_call x4, Pallas kernels: 59.7 us -> 42.4 us  [backward(): pl.pallas_call(kernel_fn, grid=(steps,), in_specs=in_specs, out_specs=out...]
    pallas_call x4, Pallas kernels: 41.7 us -> 28.4 us  [forward(): pl.pallas_call(functools.partial(forward_kernel, tiles), grid=(tiles + 1,...]
    ppermute x6, starting transfers between devices: 7.66 us -> 12.5 us  [shards(): to_hi = lambda a, k: lax.ppermute(a, 'grid', shift_hi(k))]
    ppermute x0 -> x3, starting transfers between devices: none -> 3.93 us  [shards(): sum_e = sum_e + lax.ppermute(sum_e, 'grid', perm)]
    ppermute x7 -> x8, waiting for transfers between devices: 11.6 us -> 8.61 us  [shards(): to_x = lambda a: lax.ppermute(a, 'mem', swap_x)]
  transfers between devices with their start and end apart: 27 -> 32, of which waited for: 9 -> 11; matrix products, arithmetic and copies ran while one was open for 3% -> 5% of each run, Pallas kernels for 25% -> 27%
where the time goes in v1:
time: 197 us; the launch traced here: 194 us
  Pallas kernels  70.8 us (36%)
  waiting for transfers between devices  42.2 us (21%)
  local copies, waits for them, and re-layouts  37.9 us (19%)
  starting transfers between devices  31.9 us (16%)
  other arithmetic  8.6 us (4%)
  between operations  2.74 us (1%)
    pallas_call x4, Pallas kernels, backward(): pl.pallas_call(kernel_fn, grid=(steps,), in_specs=in_specs, out_specs=out...  42.4 us
    unnamed x79, local copies, waits for them, and re-layouts  35 us
    pallas_call x4, Pallas kernels, forward(): pl.pallas_call(functools.partial(forward_kernel, tiles), grid=(tiles + 1,...  28.4 us
    ppermute x3, waiting for transfers between devices, shards(): sum_e = sum_e + lax.ppermute(sum_e, 'grid', perm)  21.7 us
    ppermute x6, starting transfers between devices, shards(): to_hi = lambda a, k: lax.ppermute(a, 'grid', shift_hi(k))  12.5 us
    ppermute x8, waiting for transfers between devices, shards(): to_x = lambda a: lax.ppermute(a, 'mem', swap_x)  8.61 us
    ppermute x6, waiting for transfers between devices, shards(): to_hi = lambda a, k: lax.ppermute(a, 'grid', shift_hi(k))  7.67 us
    ppermute x13, starting transfers between devices, shards(): to_core = lambda a: lax.ppermute(a, 'mem', swap_core)  6.69 us
  transfers between devices with their start and end apart: 32, of which 11 were waited for; matrix products, arithmetic and copies ran while one was open for 5% of the time, Pallas kernels for 27%

profile of v1, /device:TPU:9, one launch (start us, length us, event | category | flops | bytes accessed | tf_op | source)
XLA Modules:
  0.0 194.1 jit_solution(11515978259056823549)
XLA Ops:
  2.0 3.4 %copy-done = bf16[2,1024,2048]{2,1,0:T(8,128)(2,1)S(1)} copy-done((bf16[2,1024,2048]{2,1,0:T(8,128)(2,1)S(1)}, bf16[2,1024,2048]{2,1,0:T(8,128)(2,1)}, u32[]{:S(2)}) %copy-start) | copy-done | bytes 8388632
  5.3 1.6 copy-done.2
  8.3 7.4 %forward_part.7 = (bf16[2,1024,512]{2,1,0:T(8,128)(2,1)S(1)}, f32[2,1024,512]{2,1,0:T(8,128)S(1)}, f32[2,100,512]{2,1,0:T(8,128)}) custom-call(bf16[2,1024,2048]{2,1,0:T(8,128)(2,1)S(1)} %copy-done, bf16[1024,1024]{1,0:T(8,128)(2,1)S(1)} %copy-done.2, f32[1,1024]{1,0:T(1,128)S(1)} %bitcast.61, bf16[100,1024]{1,0:T(8,128)(2,1)S(1)} %copy.23.wo_ref, ...), custom_call_target="tpu_custom_call" | custom-call | flops 2357198848 | bytes 10485760 | tf_op jit(solution)/shard_map/forward_part/pallas_call | solution.py:86
  15.7 2.0 %copy-done.14 = f32[2,1024,512]{2,1,0:T(8,128)} copy-done((f32[2,1024,512]{2,1,0:T(8,128)}, f32[2,1024,512]{2,1,0:T(8,128)S(1)}, u32[]{:S(2)}) %copy-start.14) | copy-done | bytes 4194328
  17.7 1.3 copy-done.22
  21.1 6.8 %forward_part.5 = (bf16[2,1024,512]{2,1,0:T(8,128)(2,1)S(1)}, f32[2,1024,512]{2,1,0:T(8,128)S(1)}, f32[2,100,512]{2,1,0:T(8,128)S(1)}) custom-call(bf16[2,1024,2048]{2,1,0:T(8,128)(2,1)S(1)} %copy-done, bf16[1024,1024]{1,0:T(8,128)(2,1)S(1)} %copy-done.2, f32[1,1024]{1,0:T(1,128)S(1)} %bitcast.62, bf16[100,1024]{1,0:T(8,128)(2,1)S(1)} %copy.23.wo_ref, ...), custom_call_target="tpu_custom_call" | custom-call | flops 2357198848 | bytes 10485760 | tf_op jit(solution)/shard_map/forward_part/pallas_call | solution.py:86
  27.9 2.1 %copy-done.8 = f32[2,1024,512]{2,1,0:T(8,128)} copy-done((f32[2,1024,512]{2,1,0:T(8,128)}, f32[2,1024,512]{2,1,0:T(8,128)S(1)}, u32[]{:S(2)}) %copy-start.8) | copy-done | bytes 4194328
  30.0 1.4 copy-done.18
  32.2 6.8 %forward_part.6 = (bf16[2,1024,512]{2,1,0:T(8,128)(2,1)S(1)}, f32[2,1024,512]{2,1,0:T(8,128)S(1)}, f32[2,100,512]{2,1,0:T(8,128)S(1)}) custom-call(bf16[2,1024,2048]{2,1,0:T(8,128)(2,1)S(1)} %copy-done, bf16[1024,1024]{1,0:T(8,128)(2,1)S(1)} %copy-done.2, f32[1,1024]{1,0:T(1,128)S(1)} %bitcast.63, bf16[100,1024]{1,0:T(8,128)(2,1)S(1)} %copy.23.wo_ref, ...), custom_call_target="tpu_custom_call" | custom-call | flops 2357198848 | bytes 10485760 | tf_op jit(solution)/shard_map/forward_part/pallas_call | solution.py:86
  39.0 2.0 %copy-done.6 = f32[2,1024,512]{2,1,0:T(8,128)} copy-done((f32[2,1024,512]{2,1,0:T(8,128)}, f32[2,1024,512]{2,1,0:T(8,128)S(1)}, u32[]{:S(2)}) %copy-start.6) | copy-done | bytes 4194328
  41.0 1.4 copy-done.16
  42.4 1.2 collective-permute-start.4
  43.6 2.6 %copy.25 = bf16[1024,1024]{0,1:T(8,128)(2,1)} copy(bf16[1024,1024]{1,0:T(8,128)(2,1)S(1)} %copy-done.3) | data formatting | bytes 4194304 | tf_op jit(solution)/shard_map/optimization_barrier | solution.py:344
  46.3 3.4 %copy-done.1 = bf16[2,1024,2048]{2,1,0:T(8,128)(2,1)S(1)} copy-done((bf16[2,1024,2048]{2,1,0:T(8,128)(2,1)S(1)}, bf16[2,1024,2048]{2,1,0:T(8,128)(2,1)}, u32[]{:S(2)}) %copy-start.1) | copy-done | bytes 8388632
  49.7 7.4 %forward_part.4 = (bf16[2,1024,512]{2,1,0:T(8,128)(2,1)S(1)}, f32[2,1024,512]{2,1,0:T(8,128)S(1)}, f32[2,100,512]{2,1,0:T(8,128)}) custom-call(bf16[2,1024,2048]{2,1,0:T(8,128)(2,1)S(1)} %copy-done.1, bf16[1024,1024]{1,0:T(8,128)(2,1)S(1)} %copy-done.3, f32[1,1024]{1,0:T(1,128)S(1)} %bitcast.64, bf16[100,1024]{1,0:T(8,128)(2,1)S(1)} %copy.23.wo_ref, ...), custom_call_target="tpu_custom_call" | custom-call | flops 2357198848 | bytes 10485760 | tf_op jit(solution)/shard_map/forward_part/pallas_call | solution.py:86
  57.1 2.0 %copy-done.10 = f32[2,1024,512]{2,1,0:T(8,128)} copy-done((f32[2,1024,512]{2,1,0:T(8,128)}, f32[2,1024,512]{2,1,0:T(8,128)S(1)}, u32[]{:S(2)}) %copy-start.10) | copy-done | bytes 4194328
  59.1 1.3 copy-done.20
  61.7 10.7 %backward_part.4 = (bf16[2,1024,2048]{2,1,0:T(8,128)(2,1)}, f32[128,1024]{1,0:T(8,128)S(1)}, f32[1024,1024]{1,0:T(8,128)S(1)}) custom-call(f32[2,100,512]{2,1,0:T(8,128)} %get-tuple-element.44.refs_0_, f32[2,100,512]{2,1,0:T(8,128)} %collective-permute-done.9.refs_1_, f32[2,100,512]{2,1,0:T(8,128)} %collective-permute-done.10.refs_2_, ...), custom_call_target="tpu_custom_call" | custom-call | flops 4714397696 | bytes 20971520 | tf_op jit(solution)/shard_map/backward_part/pallas_call | solution.py:289
  72.4 2.0 %copy-done.12 = f32[1024,1024]{1,0:T(8,128)} copy-done((f32[1024,1024]{1,0:T(8,128)}, f32[1024,1024]{1,0:T(8,128)S(1)}, u32[]{:S(2)}) %copy-start.12) | copy-done | bytes 4194328
  75.0 2.2 %copy-done.13 = f32[1024,1024]{1,0:T(8,128)S(1)} copy-done((f32[1024,1024]{1,0:T(8,128)S(1)}, f32[1024,1024]{1,0:T(8,128)}, u32[]{:S(2)}) %copy-start.13) | copy-done | bytes 4194328
  77.2 10.4 %backward_part.5 = (bf16[2,1024,2048]{2,1,0:T(8,128)(2,1)}, f32[128,1024]{1,0:T(8,128)S(1)}, f32[1024,1024]{1,0:T(8,128)S(1)}) custom-call(f32[2,100,512]{2,1,0:T(8,128)S(1)} %get-tuple-element.36.f_ref, f32[2,100,512]{2,1,0:T(8,128)} %collective-permute-done.6.fc_ref, ...), custom_call_target="tpu_custom_call", output_to_operand_aliasing={{0}: (14, {})} | custom-call | flops 4714397696 | bytes 20971520 | tf_op jit(solution)/shard_map/backward_part/pallas_call | solution.py:289
  91.2 10.4 %backward_part.6 = (bf16[2,1024,2048]{2,1,0:T(8,128)(2,1)}, f32[128,1024]{1,0:T(8,128)S(1)}, f32[1024,1024]{1,0:T(8,128)S(1)}) custom-call(f32[2,100,512]{2,1,0:T(8,128)S(1)} %get-tuple-element.39.f_ref, f32[2,100,512]{2,1,0:T(8,128)S(1)} %copy-done.29, f32[2,100,512]{2,1,0:T(8,128)} %collective-permute-done.4.fx_ref, ...), custom_call_target="tpu_custom_call", output_to_operand_aliasing={{0}: (14, {})} | custom-call | flops 4714397696 | bytes 20971520 | tf_op jit(solution)/shard_map/backward_part/pallas_call | solution.py:289
  101.6 11.0 %backward_part.7 = (bf16[2,1024,2048]{2,1,0:T(8,128)(2,1)}, f32[128,1024]{1,0:T(8,128)S(1)}, f32[2,4,64,512]{3,2,1,0:T(8,128)S(1)}, f32[2,4,64,512]{3,2,1,0:T(8,...) custom-call(f32[2,100,512]{2,1,0:T(8,128)} %get-tuple-element.33.f_re, ...), custom_call_target="tpu_custom_call", output_to_operand_aliasing={{0}: (14, {})} | custom-call | flops 4714397696 | bytes 20971520 | tf_op jit(solution)/shard_map/backward_part/pallas_call | solution.py:289
  116.5 2.5 %collective-permute-done.12 = f32[64,1024]{1,0:T(8,128)S(1)} collective-permute-done((f32[64,1024]{1,0:T(8,128)S(1)}, f32[64,1024]{1,0:T(8,128)S(1)}, u32[]{:S(2)}, u32[]{:S(2)}) %collective-permute-start.12) | collective-permute-done | bytes 262176 | tf_op jit(solution)/shard_map/ppermute | solution.py:329
  119.0 1.3 collective-permute-start.13
  120.3 6.3 %collective-permute-done.13 = f32[64,1024]{1,0:T(8,128)S(1)} collective-permute-done((f32[64,1024]{1,0:T(8,128)S(1)}, f32[64,1024]{1,0:T(8,128)S(1)}, u32[]{:S(2)}, u32[]{:S(2)}) %collective-permute-start.13) | collective-permute-done | bytes 262176 | tf_op jit(solution)/shard_map/ppermute | solution.py:389
  126.9 6.4 %collective-permute-done.14 = f32[64,1024]{1,0:T(8,128)S(1)} collective-permute-done((f32[64,1024]{1,0:T(8,128)S(1)}, f32[64,1024]{1,0:T(8,128)S(1)}, u32[]{:S(2)}, u32[]{:S(2)}) %collective-permute-start.14) | collective-permute-done | bytes 262176 | tf_op jit(solution)/shard_map/ppermute | solution.py:389
  133.3 2.4 %collective-permute-start.15 = (f32[64,1024]{1,0:T(8,128)S(1)}, f32[64,1024]{1,0:T(8,128)S(1)}, u32[]{:S(2)}, u32[]{:S(2)}) collective-permute-start(f32[64,1024]{1,0:T(8,128)S(1)} %add.87), channel_id=1, source_target_pairs={{0,4},{1,5},{2,6},{3,7},{4,0},{5,1},{6,2},{7,3},{8,12},{9,13},{10,... | collective-permute-start | bytes 786440 | tf_op jit(solution)/shard_map/ppermute | solution.py:389
  135.7 1.3 fusion
  137.0 1.3 collective-permute-start.25
  138.3 8.9 %collective-permute-done.15 = f32[64,1024]{1,0:T(8,128)S(1)} collective-permute-done((f32[64,1024]{1,0:T(8,128)S(1)}, f32[64,1024]{1,0:T(8,128)S(1)}, u32[]{:S(2)}, u32[]{:S(2)}) %collective-permute-start.15) | collective-permute-done | bytes 262176 | tf_op jit(solution)/shard_map/ppermute | solution.py:389
  147.3 1.3 collective-permute-start.16
  149.7 1.3 collective-permute-start.19
  151.0 4.9 %collective-permute-done.16 = f32[64,1024]{1,0:T(8,128)} collective-permute-done((f32[64,1024]{1,0:T(8,128)S(1)}, f32[64,1024]{1,0:T(8,128)}, u32[]{:S(2)}, u32[]{:S(2)}) %collective-permute-start.16) | collective-permute-done | bytes 262176 | tf_op jit(solution)/shard_map/ppermute | solution.py:328
  156.8 1.4 collective-permute-start.17
  158.2 1.3 fusion.2
  159.5 1.3 collective-permute-start.26
  160.8 1.7 collective-permute-done.19
  162.5 1.3 fusion.5
  164.0 3.2 %collective-permute-start.21 = (f32[64,512]{1,0:T(8,128)S(1)}, f32[64,512]{1,0:T(8,128)S(1)}, u32[]{:S(2)}, u32[]{:S(2)}) collective-permute-start(f32[64,512]{1,0:T(8,128)S(1)} %get-tuple-element.64), channel_id=1, source_target_pairs={{0,4},{1,5},{2,6},{3,7},{4,0},{5,1},{6,2},{7,3},{8,12},{9,13},{10,... | collective-permute-start | bytes 393224 | tf_op jit(solution)/shard_map/ppermute | solution.py:331
  167.2 1.4 collective-permute-start.22
  168.7 2.9 %collective-permute-start.28 = (f32[64,256]{1,0:T(8,128)S(1)}, f32[64,256]{1,0:T(8,128)S(1)}, u32[]{:S(2)}, u32[]{:S(2)}) collective-permute-start(f32[64,256]{1,0:T(8,128)S(1)} %get-tuple-element.67), channel_id=1, source_target_pairs={{0,4},{1,5},{2,6},{3,7},{4,0},{5,1},{6,2},{7,3},{8,12},{9,13},{10,... | collective-permute-start | bytes 196616 | tf_op jit(solution)/shard_map/ppermute | solution.py:331
  171.6 2.2 %collective-permute-done.21 = f32[64,512]{1,0:T(8,128)S(1)} collective-permute-done((f32[64,512]{1,0:T(8,128)S(1)}, f32[64,512]{1,0:T(8,128)S(1)}, u32[]{:S(2)}, u32[]{:S(2)}) %collective-permute-start.21) | collective-permute-done | bytes 131104 | tf_op jit(solution)/shard_map/ppermute | solution.py:331
  173.8 4.9 %collective-permute-start.29 = (f32[64,256]{1,0:T(8,128)S(1)}, f32[64,256]{1,0:T(8,128)S(1)}, u32[]{:S(2)}, u32[]{:S(2)}) collective-permute-start(f32[64,256]{1,0:T(8,128)S(1)} %get-tuple-element.66), channel_id=1, source_target_pairs={{0,6},{1,7},{2,0},{3,1},{4,2},{5,3},{6,4},{7,5},{8,14},{9,15},{10,... | collective-permute-start | bytes 196616 | tf_op jit(solution)/shard_map/ppermute | solution.py:331
  178.7 3.0 %collective-permute-done.22 = f32[64,512]{1,0:T(8,128)S(1)} collective-permute-done((f32[64,512]{1,0:T(8,128)S(1)}, f32[64,512]{1,0:T(8,128)S(1)}, u32[]{:S(2)}, u32[]{:S(2)}) %collective-permute-start.22) | collective-permute-done | bytes 131104 | tf_op jit(solution)/shard_map/ppermute | solution.py:331
  182.1 2.5 %collective-permute-done.29 = f32[64,256]{1,0:T(8,128)S(1)} collective-permute-done((f32[64,256]{1,0:T(8,128)S(1)}, f32[64,256]{1,0:T(8,128)S(1)}, u32[]{:S(2)}, u32[]{:S(2)}) %collective-permute-start.29) | collective-permute-done | bytes 65568 | tf_op jit(solution)/shard_map/ppermute | solution.py:331
  185.7 3.0 %collective-permute-done.30 = f32[64,256]{1,0:T(8,128)S(1)} collective-permute-done((f32[64,256]{1,0:T(8,128)S(1)}, f32[64,256]{1,0:T(8,128)S(1)}, u32[]{:S(2)}, u32[]{:S(2)}) %collective-permute-start.30) | collective-permute-done | bytes 65568 | tf_op jit(solution)/shard_map/ppermute | solution.py:328
  188.7 1.3 collective-permute-start.31
  (130 shorter events, 21.6 us)
Async XLA Ops:
  19.0 13.0 %collective-permute-start.10 = (f32[2,100,512]{2,1,0:T(8,128)}, f32[2,100,512]{2,1,0:T(8,128)}, u32[]{:S(2)}, u32[]{:S(2)}) collective-permute-start(f32[2,100,512]{2,1,0:T(8,128)} %get-tuple-element.44.refs_0_), channel_id=1, source_target_pairs={{0,16},{8,24},{16,0},{24,8},{1,17},{9,25},{17,1},{25,9},{2,18},{10... | collective-permute-start | bytes 1228808 | tf_op jit(solution)/shard_map/ppermute | solution.py:328
  20.2 40.2 %collective-permute-start.9 = (f32[2,100,512]{2,1,0:T(8,128)}, f32[2,100,512]{2,1,0:T(8,128)}, u32[]{:S(2)}, u32[]{:S(2)}) collective-permute-start(f32[2,100,512]{2,1,0:T(8,128)} %get-tuple-element.44.refs_0_), channel_id=1, source_target_pairs={{0,8},{8,0},{16,24},{24,16},{1,9},{9,1},{17,25},{25,17},{2,10},{10... | collective-permute-start | bytes 1228808 | tf_op jit(solution)/shard_map/ppermute | solution.py:329
  31.4 12.2 %copy-start.3 = (bf16[1024,1024]{1,0:T(8,128)(2,1)S(1)}, bf16[1024,1024]{1,0:T(8,128)(2,1)}, u32[]{:S(2)}) copy-start(bf16[1024,1024]{1,0:T(8,128)(2,1)} %w_ref.7) | copy-start | bytes 6291460
  31.4 29.6 %collective-permute-start.7 = (f32[2,100,512]{2,1,0:T(8,128)S(1)}, f32[2,100,512]{2,1,0:T(8,128)}, u32[]{:S(2)}, u32[]{:S(2)}) collective-permute-start(f32[2,100,512]{2,1,0:T(8,128)S(1)} %get-tuple-element.36.f_ref), channel_id=1, source_target_pairs={{0,16},{8,24},{16,0},{24,8},{1,17},{9,25},{17,1},{25,9},{2,18},{10... | collective-permute-start | bytes 1228808 | tf_op jit(solution)/shard_map/ppermute | solution.py:328
  31.7 42.7 %collective-permute-start.6 = (f32[2,100,512]{2,1,0:T(8,128)S(1)}, f32[2,100,512]{2,1,0:T(8,128)}, u32[]{:S(2)}, u32[]{:S(2)}) collective-permute-start(f32[2,100,512]{2,1,0:T(8,128)S(1)} %get-tuple-element.36.f_ref), channel_id=1, source_target_pairs={{0,8},{8,0},{16,24},{24,16},{1,9},{9,1},{17,25},{25,17},{2,10},{10... | collective-permute-start | bytes 1228808 | tf_op jit(solution)/shard_map/ppermute | solution.py:329
  31.9 29.3 %collective-permute-start.11 = (f32[2,100,512]{2,1,0:T(8,128)}, f32[2,100,512]{2,1,0:T(8,128)}, u32[]{:S(2)}, u32[]{:S(2)}) collective-permute-start(f32[2,100,512]{2,1,0:T(8,128)} %collective-permute-done.10.refs_2_), channel_id=1, source_target_pairs={{0,8},{8,0},{16,24},{24,16},{1,9},{9,1},{17,25},{25,17},{2,10},{10... | collective-permute-start | bytes 1228808 | tf_op jit(solution)/shard_map/ppermute | solution.py:329
  42.4 3.9 %copy-start.36 = (f32[100]{0:T(128)S(1)}, f32[100]{0:T(128)}, u32[]{:S(2)}) copy-start(f32[100]{0:T(128)} %param.15) | copy-start | bytes 1204
  42.4 32.1 %collective-permute-start.4 = (f32[2,100,512]{2,1,0:T(8,128)S(1)}, f32[2,100,512]{2,1,0:T(8,128)}, u32[]{:S(2)}, u32[]{:S(2)}) collective-permute-start(f32[2,100,512]{2,1,0:T(8,128)S(1)} %get-tuple-element.39.f_ref), channel_id=1, source_target_pairs={{0,16},{8,24},{16,0},{24,8},{1,17},{9,25},{17,1},{25,9},{2,18},{10... | collective-permute-start | bytes 1228808 | tf_op jit(solution)/shard_map/ppermute | solution.py:328
  49.6 12.0 %copy-start.4 = (bf16[1024,1024]{0,1:T(8,128)(2,1)S(1)}, bf16[1024,1024]{0,1:T(8,128)(2,1)}, u32[]{:S(2)}) copy-start(bf16[1024,1024]{0,1:T(8,128)(2,1)} %copy.25) | copy-start | bytes 6291460
  49.6 12.0 %copy-start.5 = (f32[100,2048]{1,0:T(8,128)S(1)}, f32[100,2048]{1,0:T(8,128)}, u32[]{:S(2)}) copy-start(f32[100,2048]{1,0:T(8,128)} %target_ref.5) | copy-start | bytes 2457604
  49.6 12.0 %copy-start.15 = (f32[2,1024,512]{2,1,0:T(8,128)S(1)}, f32[2,1024,512]{2,1,0:T(8,128)}, u32[]{:S(2)}) copy-start(f32[2,1024,512]{2,1,0:T(8,128)} %copy-done.14) | copy-start | bytes 12582916
  49.6 12.0 %copy-start.23 = (bf16[2,1024,512]{2,1,0:T(8,128)(2,1)S(1)}, bf16[2,1024,512]{2,1,0:T(8,128)(2,1)}, u32[]{:S(2)}) copy-start(bf16[2,1024,512]{2,1,0:T(8,128)(2,1)} %copy-done.22) | copy-start | bytes 6291460
  49.7 12.0 %copy-start.32 = (f32[2048]{0:T(1024)S(1)}, f32[2048]{0:T(1024)}, u32[]{:S(2)}) copy-start(f32[2048]{0:T(1024)} %param.10) | copy-start | bytes 24580
  49.7 12.0 %copy-start.37 = (f32[100]{0:T(128)S(1)}, f32[100]{0:T(128)}, u32[]{:S(2)}) copy-start(f32[100]{0:T(128)} %param.11) | copy-start | bytes 1204
  60.4 27.2 %collective-permute-start.3 = (f32[2,100,512]{2,1,0:T(8,128)S(1)}, f32[2,100,512]{2,1,0:T(8,128)S(1)}, u32[]{:S(2)}, u32[]{:S(2)}) collective-permute-start(f32[2,100,512]{2,1,0:T(8,128)S(1)} %get-tuple-element.39.f_ref), channel_id=1, source_target_pairs={{0,8},{8,0},{16,24},{24,16},{1,9},{9,1},{17,25},{25,17},{2,10},{10... | collective-permute-start | bytes 1228808 | tf_op jit(solution)/shard_map/ppermute | solution.py:329
  61.0 13.8 %collective-permute-start.1 = (f32[2,100,512]{2,1,0:T(8,128)}, f32[2,100,512]{2,1,0:T(8,128)S(1)}, u32[]{:S(2)}, u32[]{:S(2)}) collective-permute-start(f32[2,100,512]{2,1,0:T(8,128)} %get-tuple-element.33.f_ref), channel_id=1, source_target_pairs={{0,16},{8,24},{16,0},{24,8},{1,17},{9,25},{17,1},{25,9},{2,18},{10... | collective-permute-start | bytes 1228808 | tf_op jit(solution)/shard_map/ppermute | solution.py:328
  61.3 13.7 %collective-permute-start.8 = (f32[2,100,512]{2,1,0:T(8,128)}, f32[2,100,512]{2,1,0:T(8,128)S(1)}, u32[]{:S(2)}, u32[]{:S(2)}) collective-permute-start(f32[2,100,512]{2,1,0:T(8,128)} %collective-permute-done.7.fx_ref), channel_id=1, source_target_pairs={{0,8},{8,0},{16,24},{24,16},{1,9},{9,1},{17,25},{25,17},{2,10},{10... | collective-permute-start | bytes 1228808 | tf_op jit(solution)/shard_map/ppermute | solution.py:329
  61.6 13.4 %copy-start.9 = (f32[2,1024,512]{2,1,0:T(8,128)S(1)}, f32[2,1024,512]{2,1,0:T(8,128)}, u32[]{:S(2)}) copy-start(f32[2,1024,512]{2,1,0:T(8,128)} %copy-done.8) | copy-start | bytes 12582916
  61.6 13.4 %copy-start.19 = (bf16[2,1024,512]{2,1,0:T(8,128)(2,1)S(1)}, bf16[2,1024,512]{2,1,0:T(8,128)(2,1)}, u32[]{:S(2)}) copy-start(bf16[2,1024,512]{2,1,0:T(8,128)(2,1)} %copy-done.18) | copy-start | bytes 6291460
  74.3 27.2 %collective-permute-start = (f32[2,100,512]{2,1,0:T(8,128)}, f32[2,100,512]{2,1,0:T(8,128)}, u32[]{:S(2)}, u32[]{:S(2)}) collective-permute-start(f32[2,100,512]{2,1,0:T(8,128)} %get-tuple-element.33.f_ref), channel_id=1, source_target_pairs={{0,8},{8,0},{16,24},{24,16},{1,9},{9,1},{17,25},{25,17},{2,10},{10... | collective-permute-start | bytes 1228808 | tf_op jit(solution)/shard_map/ppermute | solution.py:329
  74.5 13.9 %collective-permute-start.5 = (f32[2,100,512]{2,1,0:T(8,128)}, f32[2,100,512]{2,1,0:T(8,128)S(1)}, u32[]{:S(2)}, u32[]{:S(2)}) collective-permute-start(f32[2,100,512]{2,1,0:T(8,128)} %collective-permute-done.4.fx_ref), channel_id=1, source_target_pairs={{0,8},{8,0},{16,24},{24,16},{1,9},{9,1},{17,25},{25,17},{2,10},{10... | collective-permute-start | bytes 1228808 | tf_op jit(solution)/shard_map/ppermute | solution.py:329
  74.8 26.7 %collective-permute-start.2 = (f32[2,100,512]{2,1,0:T(8,128)S(1)}, f32[2,100,512]{2,1,0:T(8,128)}, u32[]{:S(2)}, u32[]{:S(2)}) collective-permute-start(f32[2,100,512]{2,1,0:T(8,128)S(1)} %collective-permute-done.1.fx_ref), channel_id=1, source_target_pairs={{0,8},{8,0},{16,24},{24,16},{1,9},{9,1},{17,25},{25,17},{2,10},{10... | collective-permute-start | bytes 1228808 | tf_op jit(solution)/shard_map/ppermute | solution.py:329
  77.2 11.9 %copy-start.7 = (f32[2,1024,512]{2,1,0:T(8,128)S(1)}, f32[2,1024,512]{2,1,0:T(8,128)}, u32[]{:S(2)}) copy-start(f32[2,1024,512]{2,1,0:T(8,128)} %copy-done.6) | copy-start | bytes 12582916
  77.2 11.9 %copy-start.17 = (bf16[2,1024,512]{2,1,0:T(8,128)(2,1)S(1)}, bf16[2,1024,512]{2,1,0:T(8,128)(2,1)}, u32[]{:S(2)}) copy-start(bf16[2,1024,512]{2,1,0:T(8,128)(2,1)} %copy-done.16) | copy-start | bytes 6291460
  91.2 10.4 %copy-start.11 = (f32[2,1024,512]{2,1,0:T(8,128)S(1)}, f32[2,1024,512]{2,1,0:T(8,128)}, u32[]{:S(2)}) copy-start(f32[2,1024,512]{2,1,0:T(8,128)} %copy-done.10) | copy-start | bytes 12582916
  91.2 10.4 %copy-start.21 = (bf16[2,1024,512]{2,1,0:T(8,128)(2,1)S(1)}, bf16[2,1024,512]{2,1,0:T(8,128)(2,1)}, u32[]{:S(2)}) copy-start(bf16[2,1024,512]{2,1,0:T(8,128)(2,1)} %copy-done.20) | copy-start | bytes 6291460
  115.5 33.0 %copy-start.25 = (f32[2,4,64,512]{3,2,1,0:T(8,128)S(1)}, f32[2,4,64,512]{3,2,1,0:T(8,128)}, u32[]{:S(2)}) copy-start(f32[2,4,64,512]{3,2,1,0:T(8,128)} %copy-done.24) | copy-start | bytes 3145732
  115.5 42.6 %copy-start.27 = (f32[2,2,4,64,256]{4,3,2,1,0:T(8,128)S(1)}, f32[2,2,4,64,256]{4,3,2,1,0:T(8,128)}, u32[]{:S(2)}) copy-start(f32[2,2,4,64,256]{4,3,2,1,0:T(8,128)} %copy-done.26) | copy-start | bytes 3145732
  115.5 20.2 %collective-permute-start.24 = (f32[2,2,4,64,256]{4,3,2,1,0:T(8,128)}, f32[2,2,4,64,256]{4,3,2,1,0:T(8,128)}, u32[]{:S(2)}, u32[]{:S(2)}) collective-permute-start(f32[2,2,4,64,256]{4,3,2,1,0:T(8,128)} %get-tuple-element.61), channel_id=1, source_target_pairs={{0,8},{8,0},{16,24},{24,16},{1,9},{9,1},{17,25},{25,17},{2,10},{10... | collective-permute-start | bytes 3145736 | tf_op jit(solution)/shard_map/ppermute | solution.py:329
  115.9 3.0 %collective-permute-start.12 = (f32[64,1024]{1,0:T(8,128)S(1)}, f32[64,1024]{1,0:T(8,128)S(1)}, u32[]{:S(2)}, u32[]{:S(2)}) collective-permute-start(f32[64,1024]{1,0:T(8,128)S(1)} %constant_dynamic-slice_fusion), channel_id=1, source_target_pairs={{0,8},{8,0},{16,24},{24,16},{1,9},{9,1},{17,25},{25,17},{2,10},{10... | collective-permute-start | bytes 786440 | tf_op jit(solution)/shard_map/ppermute | solution.py:329
  116.1 32.4 %collective-permute-start.18 = (f32[2,4,64,512]{3,2,1,0:T(8,128)}, f32[2,4,64,512]{3,2,1,0:T(8,128)}, u32[]{:S(2)}, u32[]{:S(2)}) collective-permute-start(f32[2,4,64,512]{3,2,1,0:T(8,128)} %copy-done.38), channel_id=1, source_target_pairs={{0,8},{8,0},{16,24},{24,16},{1,9},{9,1},{17,25},{25,17},{2,10},{10... | collective-permute-start | bytes 3145736 | tf_op jit(solution)/shard_map/ppermute | solution.py:329
  119.0 7.6 %collective-permute-start.13 = (f32[64,1024]{1,0:T(8,128)S(1)}, f32[64,1024]{1,0:T(8,128)S(1)}, u32[]{:S(2)}, u32[]{:S(2)}) collective-permute-start(f32[64,1024]{1,0:T(8,128)S(1)} %dynamic-slice_add_fusion), channel_id=1, source_target_pairs={{0,1},{1,0},{2,3},{3,2},{4,5},{5,4},{6,7},{7,6},{8,9},{9,8},{10,11... | collective-permute-start | bytes 786440 | tf_op jit(solution)/shard_map/ppermute | solution.py:389
  126.6 6.7 %collective-permute-start.14 = (f32[64,1024]{1,0:T(8,128)S(1)}, f32[64,1024]{1,0:T(8,128)S(1)}, u32[]{:S(2)}, u32[]{:S(2)}) collective-permute-start(f32[64,1024]{1,0:T(8,128)S(1)} %add.86), channel_id=1, source_target_pairs={{0,2},{1,3},{2,0},{3,1},{4,6},{5,7},{6,4},{7,5},{8,10},{9,11},{10,... | collective-permute-start | bytes 786440 | tf_op jit(solution)/shard_map/ppermute | solution.py:389
  133.3 13.9 %collective-permute-start.15 = (f32[64,1024]{1,0:T(8,128)S(1)}, f32[64,1024]{1,0:T(8,128)S(1)}, u32[]{:S(2)}, u32[]{:S(2)}) collective-permute-start(f32[64,1024]{1,0:T(8,128)S(1)} %add.87), channel_id=1, source_target_pairs={{0,4},{1,5},{2,6},{3,7},{4,0},{5,1},{6,2},{7,3},{8,12},{9,13},{10,... | collective-permute-start | bytes 786440 | tf_op jit(solution)/shard_map/ppermute | solution.py:389
  137.0 21.2 %collective-permute-start.25 = (f32[2,4,64,256]{3,2,1,0:T(8,128)S(1)}, f32[2,4,64,256]{3,2,1,0:T(8,128)}, u32[]{:S(2)}, u32[]{:S(2)}) collective-permute-start(f32[2,4,64,256]{3,2,1,0:T(8,128)S(1)} %fusion), channel_id=1, source_target_pairs={{0,16},{8,24},{16,0},{24,8},{1,17},{9,25},{17,1},{25,9},{2,18},{10... | collective-permute-start | bytes 1572872 | tf_op jit(solution)/shard_map/ppermute | solution.py:328
  147.3 8.6 %collective-permute-start.16 = (f32[64,1024]{1,0:T(8,128)S(1)}, f32[64,1024]{1,0:T(8,128)}, u32[]{:S(2)}, u32[]{:S(2)}) collective-permute-start(f32[64,1024]{1,0:T(8,128)S(1)} %add.88), channel_id=1, source_target_pairs={{0,16},{8,24},{16,0},{24,8},{1,17},{9,25},{17,1},{25,9},{2,18},{10... | collective-permute-start | bytes 786440 | tf_op jit(solution)/shard_map/ppermute | solution.py:328
  149.7 12.8 %collective-permute-start.19 = (f32[4,64,512]{2,1,0:T(8,128)S(1)}, f32[4,64,512]{2,1,0:T(8,128)}, u32[]{:S(2)}, u32[]{:S(2)}) collective-permute-start(f32[4,64,512]{2,1,0:T(8,128)S(1)} %fusion.3), channel_id=1, source_target_pairs={{0,1},{1,0},{2,3},{3,2},{4,5},{5,4},{6,7},{7,6},{8,9},{9,8},{10,11... | collective-permute-start | bytes 1572872 | tf_op jit(solution)/shard_map/ppermute | solution.py:330
  156.8 28.1 %collective-permute-start.17 = (f32[64,1024]{1,0:T(8,128)S(1)}, f32[64,1024]{1,0:T(8,128)S(1)}, u32[]{:S(2)}, u32[]{:S(2)}) collective-permute-start(f32[64,1024]{1,0:T(8,128)S(1)} %add.89), channel_id=1, source_target_pairs={{0,8},{8,0},{16,24},{24,16},{1,9},{9,1},{17,25},{25,17},{2,10},{10... | collective-permute-start | bytes 786440 | tf_op jit(solution)/shard_map/ppermute | solution.py:329
  159.5 9.0 %collective-permute-start.26 = (f32[4,64,256]{2,1,0:T(8,128)S(1)}, f32[4,64,256]{2,1,0:T(8,128)S(1)}, u32[]{:S(2)}, u32[]{:S(2)}) collective-permute-start(f32[4,64,256]{2,1,0:T(8,128)S(1)} %slice_bitcast_fusion), channel_id=1, source_target_pairs={{0,1},{1,0},{2,3},{3,2},{4,5},{5,4},{6,7},{7,6},{8,9},{9,8},{10,11... | collective-permute-start | bytes 786440 | tf_op jit(solution)/shard_map/ppermute | solution.py:330
  163.9 4.8 %collective-permute-start.20 = (f32[64,512]{1,0:T(8,128)S(1)}, f32[64,512]{1,0:T(8,128)S(1)}, u32[]{:S(2)}, u32[]{:S(2)}) collective-permute-start(f32[64,512]{1,0:T(8,128)S(1)} %get-tuple-element.62), channel_id=1, source_target_pairs={{0,2},{1,3},{2,4},{3,5},{4,6},{5,7},{6,0},{7,1},{8,10},{9,11},{10,... | collective-permute-start | bytes 393224 | tf_op jit(solution)/shard_map/ppermute | solution.py:331
  164.0 9.8 %collective-permute-start.21 = (f32[64,512]{1,0:T(8,128)S(1)}, f32[64,512]{1,0:T(8,128)S(1)}, u32[]{:S(2)}, u32[]{:S(2)}) collective-permute-start(f32[64,512]{1,0:T(8,128)S(1)} %get-tuple-element.64), channel_id=1, source_target_pairs={{0,4},{1,5},{2,6},{3,7},{4,0},{5,1},{6,2},{7,3},{8,12},{9,13},{10,... | collective-permute-start | bytes 393224 | tf_op jit(solution)/shard_map/ppermute | solution.py:331
  167.2 14.6 %collective-permute-start.22 = (f32[64,512]{1,0:T(8,128)S(1)}, f32[64,512]{1,0:T(8,128)S(1)}, u32[]{:S(2)}, u32[]{:S(2)}) collective-permute-start(f32[64,512]{1,0:T(8,128)S(1)} %get-tuple-element.63), channel_id=1, source_target_pairs={{0,6},{1,7},{2,0},{3,1},{4,2},{5,3},{6,4},{7,5},{8,14},{9,15},{10,... | collective-permute-start | bytes 393224 | tf_op jit(solution)/shard_map/ppermute | solution.py:331
  168.6 13.5 %collective-permute-start.27 = (f32[64,256]{1,0:T(8,128)S(1)}, f32[64,256]{1,0:T(8,128)S(1)}, u32[]{:S(2)}, u32[]{:S(2)}) collective-permute-start(f32[64,256]{1,0:T(8,128)S(1)} %get-tuple-element.65), channel_id=1, source_target_pairs={{0,2},{1,3},{2,4},{3,5},{4,6},{5,7},{6,0},{7,1},{8,10},{9,11},{10,... | collective-permute-start | bytes 196616 | tf_op jit(solution)/shard_map/ppermute | solution.py:331
  168.7 13.3 %collective-permute-start.28 = (f32[64,256]{1,0:T(8,128)S(1)}, f32[64,256]{1,0:T(8,128)S(1)}, u32[]{:S(2)}, u32[]{:S(2)}) collective-permute-start(f32[64,256]{1,0:T(8,128)S(1)} %get-tuple-element.67), channel_id=1, source_target_pairs={{0,4},{1,5},{2,6},{3,7},{4,0},{5,1},{6,2},{7,3},{8,12},{9,13},{10,... | collective-permute-start | bytes 196616 | tf_op jit(solution)/shard_map/ppermute | solution.py:331
  173.8 10.8 %collective-permute-start.29 = (f32[64,256]{1,0:T(8,128)S(1)}, f32[64,256]{1,0:T(8,128)S(1)}, u32[]{:S(2)}, u32[]{:S(2)}) collective-permute-start(f32[64,256]{1,0:T(8,128)S(1)} %get-tuple-element.66), channel_id=1, source_target_pairs={{0,6},{1,7},{2,0},{3,1},{4,2},{5,3},{6,4},{7,5},{8,14},{9,15},{10,... | collective-permute-start | bytes 196616 | tf_op jit(solution)/shard_map/ppermute | solution.py:331
  181.8 3.9 %collective-permute-start.23 = (f32[64,512]{1,0:T(8,128)S(1)}, f32[64,512]{1,0:T(8,128)S(1)}, u32[]{:S(2)}, u32[]{:S(2)}) collective-permute-start(f32[64,512]{1,0:T(8,128)S(1)} %fusion.9), channel_id=1, source_target_pairs={{0,16},{8,24},{16,0},{24,8},{1,17},{9,25},{17,1},{25,9},{2,18},{10... | collective-permute-start | bytes 393224 | tf_op jit(solution)/shard_map/ppermute | solution.py:328
  184.6 4.1 %collective-permute-start.30 = (f32[64,256]{1,0:T(8,128)S(1)}, f32[64,256]{1,0:T(8,128)S(1)}, u32[]{:S(2)}, u32[]{:S(2)}) collective-permute-start(f32[64,256]{1,0:T(8,128)S(1)} %fusion.12), channel_id=1, source_target_pairs={{0,16},{8,24},{16,0},{24,8},{1,17},{9,25},{17,1},{25,9},{2,18},{10... | collective-permute-start | bytes 196616 | tf_op jit(solution)/shard_map/ppermute | solution.py:328
  188.7 3.4 %collective-permute-start.31 = (f32[64,1024]{1,0:T(8,128)S(1)}, f32[64,1024]{1,0:T(8,128)S(1)}, u32[]{:S(2)}, u32[]{:S(2)}) collective-permute-start(f32[64,1024]{1,0:T(8,128)S(1)} %maximum_multiply_fusion), channel_id=1, source_target_pairs={{0,8},{8,0},{16,24},{24,16},{1,9},{9,1},{17,25},{25,17},{2,10},{10... | collective-permute-start | bytes 786440 | tf_op jit(solution)/shard_map/ppermute | solution.py:329
  (23 other events, 37.8 us)

commit v2 on v1

--- a/solution.py
+++ b/solution.py
@@ -9,14 +9,14 @@
 from jax.sharding import PartitionSpec as P
 
 PARTS = 4
-FWD_TILE = 256
+FWD_TILE = 512
 BWD_TILE = 256
 EPS = 0.0004
 K0 = math.sqrt(2.0 / math.pi)
 K1 = K0 * 0.044715
 SLAB = 256
-FWD_VMEM = 20 * 1024 * 1024
-BWD_VMEM = 34 * 1024 * 1024
+EXTRA_ROWS = 8
+VMEM = 58 * 1024 * 1024
 NT = (((1,), (1,)), ((), ()))
 
 
@@ -26,7 +26,7 @@
     return jnp.sum(jnp.where(r == c, row, 0.0), axis=1, keepdims=True)
 
 
-def forward_kernel(tiles, hid_ref, w_ref, b_ref, wo_ref, bo_ref, act_ref, slope_ref, f_ref, bias, even, odd):
+def forward_kernel(tiles, hid_ref, w_ref, b_ref, wo_ref, bo_ref, act_ref, slope_ref, f_ref, bias, half, even, odd):
     step = pl.program_id(0)
 
     @pl.when(step == 0)
@@ -35,6 +35,8 @@
             bias[pl.ds(k * 128, 128), :] = jnp.broadcast_to(
                 column(b_ref[:, pl.ds(k * 128, 128)], 128), (128, 128)
             )
+
+        half[...] = wo_ref[...] * jnp.bfloat16(0.5)
 
     def both(fill, drain):
         h, t = fill.shape
@@ -43,16 +45,18 @@
         for k in range(0, h, SLAB):
             for r in range(k, k + SLAB, 16):
                 rows = pl.ds(r, 16)
-                b = jnp.concatenate([bias[rows, :]] * (t // 128), axis=1)
-                x = drain[rows, :] + b
-                q = x * x * K1
-                th = jnp.tanh(x * (K0 + q))
-                up = 1.0 + th
-                act_ref[0, rows, :] = (x * up).astype(jnp.bfloat16)
-                slope_ref[0, rows, :] = up * (1.0 + (1.0 - th) * (x * (K0 + 3.0 * q)))
+                b = jnp.concatenate([bias[rows, :]] * 2, axis=1)
+                for c in range(0, t, 256):
+                    cols = pl.ds(c, 256)
+                    x = drain[rows, cols] + b
+                    q = x * x * K1
+                    th = jnp.tanh(x * (K0 + q))
+                    up = 1.0 + th
+                    act_ref[0, rows, cols] = (x * up).astype(jnp.bfloat16)
+                    slope_ref[0, rows, cols] = up * (1.0 + (1.0 - th) * (x * (K0 + 3.0 * q)))
             slab = pl.ds(k, SLAB)
             out = out + jnp.dot(
-                wo_ref[:, slab], act_ref[0, slab, :], preferred_element_type=jnp.float32
+                half[:, slab], act_ref[0, slab, :], preferred_element_type=jnp.float32
             )
         f_ref[0] = out
 
@@ -105,10 +109,11 @@
         ],
         scratch_shapes=[
             pltpu.VMEM((h, 128), jnp.float32),
+            pltpu.VMEM((v, h), jnp.bfloat16),
             pltpu.VMEM((h, t), jnp.float32),
             pltpu.VMEM((h, t), jnp.float32),
         ],
-        compiler_params=pltpu.CompilerParams(vmem_limit_bytes=FWD_VMEM),
+        compiler_params=pltpu.CompilerParams(vmem_limit_bytes=VMEM),
         cost_estimate=pl.CostEstimate(
             flops=2 * mloc * p * h * (h + v), bytes_accessed=mloc * p * h * 8 + 2 * h * h,
             transcendentals=mloc * p * h,
@@ -133,8 +138,8 @@
     vw = column(vw_ref[...], v)
     area = area_ref[...]
     loss = jnp.zeros((1, t), jnp.float32)
-    for r0 in range(0, v, 16):
-        rows = pl.ds(r0, min(16, v - r0))
+    for r0 in range(0, v, 8):
+        rows = pl.ds(r0, min(8, v - r0))
         own = [f_ref[m, rows, :] for m in range(mloc)]
         others = [ref[m, rows, :] for ref in (fc_ref, fx_ref, fxc_ref) for m in range(mloc)]
         target = target_ref[rows, :]
@@ -169,7 +174,7 @@
                 add(j, -sl)
                 inner = inner + ph
                 n_inner += 1
-        weight = vw[r0 : r0 + 16] * area
+        weight = vw[r0 : r0 + 8] * area
         for m in range(mloc):
             gf[m, rows, :] = weight * (obs[m] * (1.0 / members) - dsum[m] * (1.0 / denom))
         near = (near - 0.02 * mloc) * (1.0 / members)
@@ -226,7 +231,16 @@
                     g = lax.rem(hi + dhi, n_hi) * n_lo + lax.rem(lo + dlo, n_lo)
                     for c, part_a, part_x in ((core, keep_a, keep_x), (1 - core, send_a, send_x)):
                         r0 = pl.multiple_of((g * 2 + c) * r, r)
-                        part_a[dlo, dhi] = acc[pl.ds(r0, r), pl.ds(0, ca)]
+                        part_a[dlo, dhi, pl.ds(0, r), :] = acc[pl.ds(r0, r), pl.ds(0, ca)]
+                        e0 = (c * (n_hi * n_lo) + g) * EXTRA_ROWS
+                        at = pl.multiple_of(
+                            jnp.minimum(e0, extra_ref.shape[0] - EXTRA_ROWS), EXTRA_ROWS
+                        )
+                        for k in range(h // ca):
+                            e = extra_ref[pl.ds(at, EXTRA_ROWS), pl.ds(k * ca, ca)]
+                            part_a[dlo, dhi, pl.ds(r + k * EXTRA_ROWS, EXTRA_ROWS), :] = jnp.where(
+                                e0 < extra_ref.shape[0], e, 0.0
+                            )
                         left = acc[pl.ds(r0, r), pl.ds(ca, cx)]
                         right = acc[pl.ds(r0, r), pl.ds(ca + cx, cx)]
                         part_x[0, dlo, dhi] = jnp.where(x == 0, left, right)
@@ -279,7 +293,8 @@
         r = h // (2 * n_hi * n_lo)
         ca = h // 2
         cx = (h - ca) // 2
-        for shape in ((n_lo, n_hi, r, ca), (n_lo, n_hi, r, ca), (2, n_lo, n_hi, r, cx), (2, n_lo, n_hi, r, cx)):
+        ra = r + h // ca * EXTRA_ROWS
+        for shape in ((n_lo, n_hi, ra, ca), (n_lo, n_hi, ra, ca), (2, n_lo, n_hi, r, cx), (2, n_lo, n_hi, r, cx)):
             out_specs.append(pl.BlockSpec(shape, lambda s, k=len(shape): (0,) * k, pipeline_mode=once))
             out_shape.append(jax.ShapeDtypeStruct(shape, jnp.float32))
         scratch = [pltpu.VMEM((h, h), jnp.float32)] + scratch
@@ -294,7 +309,7 @@
         out_shape=out_shape,
         scratch_shapes=scratch,
         input_output_aliases=aliases,
-        compiler_params=pltpu.CompilerParams(vmem_limit_bytes=BWD_VMEM),
+        compiler_params=pltpu.CompilerParams(vmem_limit_bytes=VMEM),
         cost_estimate=pl.CostEstimate(
             flops=4 * mloc * p * h * (h + v), bytes_accessed=mloc * p * h * 10 + 10 * h * h,
             transcendentals=mloc * p * v * 8,
@@ -330,20 +345,19 @@
     to_lo = lambda a, k: lax.ppermute(a, "grid", shift_lo(k))
     to_hi = lambda a, k: lax.ppermute(a, "grid", shift_hi(k))
 
-    half_out = w_out * jnp.bfloat16(0.5)
     parts = []
     for part in range(PARTS):
         parts.append(
-            forward(part, hidden, w_inner, b_inner.reshape(1, h), half_out, b_out.reshape(1, v))
+            forward(part, hidden, w_inner, b_inner.reshape(1, h), w_out, b_out.reshape(1, v))
         )
     exchanged = []
     for act, slope, fields in parts:
         far = to_x(fields)
         exchanged.append((fields, to_core(fields), far, to_core(far)))
 
-    w_inner, half_out, _ = lax.optimization_barrier((w_inner, half_out, parts[1][2]))
+    w_inner, w_out, _ = lax.optimization_barrier((w_inner, w_out, parts[1][2]))
     wt = w_inner.T
-    wot = jnp.pad(half_out, ((0, vp - v), (0, 0))).T
+    wot = jnp.pad(w_out * jnp.bfloat16(0.5), ((0, vp - v), (0, 0))).T
     vw, area = var_weight.reshape(1, v), area.reshape(1, n)
     acc = extra = gh = None
     for part in range(PARTS):
@@ -355,14 +369,15 @@
         acc = accs[0]
     keep_a, send_a, keep_x, send_x = accs
 
-    core = lax.axis_index("mem") % 2
-    x = lax.axis_index("mem") // 2
-
-    def flips(name):
-        n, k = lax.axis_size(name), 1
-        while k < n:
-            yield [(i, i ^ k) for i in range(n)]
-            k *= 2
+
+    def gathered(block, axis, name, bit):
+        n = lax.axis_size(name)
+        other = lax.ppermute(block, name, [(i, i ^ bit) for i in range(n)])
+        return jnp.where(
+            lax.axis_index(name) & bit == 0,
+            jnp.concatenate([block, other], axis),
+            jnp.concatenate([other, block], axis),
+        )
 
     def along_lo(blocks):
         total = blocks(0)
@@ -376,36 +391,27 @@
             total = total + to_hi(blocks[k], k)
         return total
 
-    half = vp // 2
-    keep_e = lax.dynamic_slice_in_dim(extra, core * half, half, 0)
-    send_e = lax.dynamic_slice_in_dim(extra, (1 - core) * half, half, 0)
     got_a = to_core(send_a)
-    got_e = to_core(send_e)
     got_x = to_core(send_x)
     sum_a = along_lo(lambda k: keep_a[k] + got_a[k])
     own_x = keep_x[0] + got_x[0] + to_x(keep_x[1] + got_x[1])
-    sum_e = keep_e + got_e
-    for perm in flips("grid"):
-        sum_e = sum_e + lax.ppermute(sum_e, "grid", perm)
-    sum_e = sum_e + to_x(sum_e)
     sum_x = along_lo(lambda k: own_x[k])
     end_a = along_hi(sum_a)
     end_x = along_hi(sum_x)
     end_a = end_a + to_x(end_a)
-    far_x = to_x(end_x)
-    end_x = jnp.where(
-        x == 0, jnp.concatenate([end_x, far_x], 1), jnp.concatenate([far_x, end_x], 1)
+    r = h // (2 * n_grid)
+    ca = end_a.shape[1]
+    extra = jnp.concatenate(
+        [end_a[r + k : r + k + EXTRA_ROWS] for k in range(0, end_a.shape[0] - r, EXTRA_ROWS)], 1
     )
+    bit = 1
+    while bit < n_grid:
+        extra = gathered(extra, 0, "grid", bit)
+        bit *= 2
+    extra = gathered(extra, 0, "mem", 1)
+    end_x = gathered(end_x, 1, "mem", n_mem // 2)
     scale = 1.0 / math.sqrt(members * npoints)
-    mine = jnp.concatenate([end_a, end_x], 1) * scale
-    other = to_core(mine)
-    grad_inner = jnp.where(
-        core == 0, jnp.concatenate([mine, other], 0), jnp.concatenate([other, mine], 0)
-    )
-    other_e = to_core(sum_e)
-    extra = jnp.where(
-        core == 0, jnp.concatenate([sum_e, other_e], 0), jnp.concatenate([other_e, sum_e], 0)
-    )
+    grad_inner = gathered(jnp.concatenate([end_a[:r], end_x], 1) * scale, 0, "mem", 1)
     loss = jnp.sum(extra[v]) / npoints
     return (loss, gh, grad_inner, extra[:v] * (0.5 * scale))
 

time: 197 us -> 184 us (0.934)
  local copies, waits for them, and re-layouts: 37.9 us -> 6.28 us
  Pallas kernels: 70.8 us -> 100 us
  waiting for transfers between devices: 42.2 us -> 38.2 us
  other arithmetic: 8.6 us -> 5.12 us
  starting transfers between devices: 31.9 us -> 28.6 us
    unnamed x79 -> x26, local copies, waits for them, and re-layouts: 35 us -> 2.65 us
    ppermute x3 -> x6, waiting for transfers between devices: 21.7 us -> 1.46 us  [gathered(): other = lax.ppermute(block, name, [(i, i ^ bit) for i in range(n)])]
    pallas_call x4, Pallas kernels: 42.4 us -> 58.4 us  [backward(): pl.pallas_call(kernel_fn, grid=(steps,), in_specs=in_specs, out_specs=out...]
    pallas_call x4, Pallas kernels: 28.4 us -> 41.5 us  [forward(): pl.pallas_call(functools.partial(forward_kernel, tiles), grid=(tiles + 1,...]
    ppermute x6, waiting for transfers between devices: 7.67 us -> 15.9 us  [shards(): to_hi = lambda a, k: lax.ppermute(a, 'grid', shift_hi(k))]
    ppermute x3 -> x6, starting transfers between devices: 3.93 us -> 11.5 us  [gathered(): other = lax.ppermute(block, name, [(i, i ^ bit) for i in range(n)])]
    ppermute x6, starting transfers between devices: 12.5 us -> 5.34 us  [shards(): to_hi = lambda a, k: lax.ppermute(a, 'grid', shift_hi(k))]
    ppermute x8 -> x6, waiting for transfers between devices: 8.61 us -> 13.7 us  [shards(): to_x = lambda a: lax.ppermute(a, 'mem', swap_x)]
  transfers between devices with their start and end apart: 32 -> 30, of which waited for: 11 -> 10; matrix products, arithmetic and copies ran while one was open for 5% -> 4% of each run, Pallas kernels for 27% -> 41%
where the time goes in v2:
time: 184 us; the launch traced here: 181 us
  Pallas kernels  100 us (54%)
  waiting for transfers between devices  38.2 us (21%)
  starting transfers between devices  28.6 us (16%)
  local copies, waits for them, and re-layouts  6.28 us (3%)
  other arithmetic  5.12 us (3%)
  between operations  2.71 us (1%)
    pallas_call x4, Pallas kernels, backward(): pl.pallas_call(kernel_fn, grid=(steps,), in_specs=in_specs, out_specs=out...  58.4 us
    pallas_call x4, Pallas kernels, forward(): pl.pallas_call(functools.partial(forward_kernel, tiles), grid=(tiles + 1,...  41.5 us
    ppermute x6, waiting for transfers between devices, shards(): to_hi = lambda a, k: lax.ppermute(a, 'grid', shift_hi(k))  15.9 us
    ppermute x6, waiting for transfers between devices, shards(): to_x = lambda a: lax.ppermute(a, 'mem', swap_x)  13.7 us
    ppermute x6, starting transfers between devices, gathered(): other = lax.ppermute(block, name, [(i, i ^ bit) for i in range(n)])  11.5 us
    ppermute x6, starting transfers between devices, shards(): to_x = lambda a: lax.ppermute(a, 'mem', swap_x)  5.35 us
    ppermute x6, starting transfers between devices, shards(): to_hi = lambda a, k: lax.ppermute(a, 'grid', shift_hi(k))  5.34 us
    ppermute x2, waiting for transfers between devices, shards(): to_lo = lambda a, k: lax.ppermute(a, 'grid', shift_lo(k))  4.82 us
  transfers between devices with their start and end apart: 30, of which 10 were waited for; matrix products, arithmetic and copies ran while one was open for 4% of the time, Pallas kernels for 41%

profile of v2, /device:TPU:9, one launch (start us, length us, event | category | flops | bytes accessed | tf_op | source)
XLA Modules:
  0.0 180.9 jit_solution(14937312397892416063)
XLA Ops:
  0.6 10.3 %forward_part.7 = (bf16[2,1024,512]{2,1,0:T(8,128)(2,1)}, f32[2,1024,512]{2,1,0:T(8,128)}, f32[2,100,512]{2,1,0:T(8,128)}) custom-call(bf16[2,1024,2048]{2,1,0:T(8,128)(2,1)} %hid_ref.13, bf16[1024,1024]{1,0:T(8,128)(2,1)} %w_ref.7, f32[1,1024]{1,0:T(1,128)} %bitcast.61, bf16[100,1024]{1,0:T(8,128)(2,1)} %wo_ref.7, f32[1,100]{1,0:T(1,128)} %bitcast.65), custom_call_target="tpu_custom_call" | custom-call | flops 2357198848 | bytes 10485760 | tf_op jit(solution)/shard_map/forward_part/pallas_call | solution.py:90
  10.9 1.2 collective-permute-start.10
  12.1 1.0 collective-permute-start.9
  13.1 10.4 %forward_part.5 = (bf16[2,1024,512]{2,1,0:T(8,128)(2,1)}, f32[2,1024,512]{2,1,0:T(8,128)}, f32[2,100,512]{2,1,0:T(8,128)}) custom-call(bf16[2,1024,2048]{2,1,0:T(8,128)(2,1)} %hid_ref.13, bf16[1024,1024]{1,0:T(8,128)(2,1)} %w_ref.7, f32[1,1024]{1,0:T(1,128)} %bitcast.62, bf16[100,1024]{1,0:T(8,128)(2,1)} %wo_ref.7, f32[1,100]{1,0:T(1,128)} %bitcast.66), custom_call_target="tpu_custom_call" | custom-call | flops 2357198848 | bytes 10485760 | tf_op jit(solution)/shard_map/forward_part/pallas_call | solution.py:90
  24.1 10.5 %forward_part.6 = (bf16[2,1024,512]{2,1,0:T(8,128)(2,1)}, f32[2,1024,512]{2,1,0:T(8,128)}, f32[2,100,512]{2,1,0:T(8,128)}) custom-call(bf16[2,1024,2048]{2,1,0:T(8,128)(2,1)} %hid_ref.13, bf16[1024,1024]{1,0:T(8,128)(2,1)} %w_ref.7, f32[1,1024]{1,0:T(1,128)} %bitcast.63, bf16[100,1024]{1,0:T(8,128)(2,1)} %wo_ref.7, f32[1,100]{1,0:T(1,128)} %bitcast.67), custom_call_target="tpu_custom_call" | custom-call | flops 2357198848 | bytes 10485760 | tf_op jit(solution)/shard_map/forward_part/pallas_call | solution.py:90
  34.6 1.2 collective-permute-start.4
  36.0 0.5 collective-permute-start.11
  36.6 2.6 %copy.19 = bf16[1024,1024]{0,1:T(8,128)(2,1)} copy(bf16[1024,1024]{1,0:T(8,128)(2,1)S(1)} %copy-done) | data formatting | bytes 4194304 | tf_op jit(solution)/shard_map/optimization_barrier | solution.py:358
  39.2 0.8 pad_bitcast_fusion.refs_10_.wot_ref
  40.0 10.3 %forward_part.4 = (bf16[2,1024,512]{2,1,0:T(8,128)(2,1)}, f32[2,1024,512]{2,1,0:T(8,128)}, f32[2,100,512]{2,1,0:T(8,128)}) custom-call(bf16[2,1024,2048]{2,1,0:T(8,128)(2,1)} %hid_ref.13, bf16[1024,1024]{1,0:T(8,128)(2,1)} %w_ref.7, f32[1,1024]{1,0:T(1,128)} %bitcast.64, bf16[100,1024]{1,0:T(8,128)(2,1)} %wo_ref.7, f32[1,100]{1,0:T(1,128)} %bitcast.68), custom_call_target="tpu_custom_call" | custom-call | flops 2357198848 | bytes 10485760 | tf_op jit(solution)/shard_map/forward_part/pallas_call | solution.py:90
  50.7 0.7 collective-permute-start.8
  51.4 13.1 %backward_part.4 = (bf16[2,1024,2048]{2,1,0:T(8,128)(2,1)}, f32[128,1024]{1,0:T(8,128)}, f32[1024,1024]{1,0:T(8,128)}) custom-call(f32[2,100,512]{2,1,0:T(8,128)} %get-tuple-element.43.refs_0_, f32[2,100,512]{2,1,0:T(8,128)} %collective-permute-done.9.refs_1_, f32[2,100,512]{2,1,0:T(8,128)} %collective-permute-done.10.refs_2_, ...), custom_call_target="tpu_custom_call" | custom-call | flops 4714397696 | bytes 20971520 | tf_op jit(solution)/shard_map/backward_part/pallas_call | solution.py:304
  64.7 0.5 collective-permute-start.5
  65.3 0.8 copy-done.11
  66.1 14.6 %backward_part.5 = (bf16[2,1024,2048]{2,1,0:T(8,128)(2,1)}, f32[128,1024]{1,0:T(8,128)}, f32[1024,1024]{1,0:T(8,128)}) custom-call(f32[2,100,512]{2,1,0:T(8,128)} %get-tuple-element.35.f_ref, f32[2,100,512]{2,1,0:T(8,128)} %collective-permute-done.6.fc_ref, f32[2,100,512]{2,1,0:T(8,128)} %collective-permute-done.7.fx_ref, ...), custom_call_target="tpu_custom_call", output_to_operand_aliasing={{0}: (14, {})} | custom-call | flops 4714397696 | bytes 20971520 | tf_op jit(solution)/shard_map/backward_part/pallas_call | solution.py:304
  80.7 0.7 copy-done.8
  81.7 14.3 %backward_part.6 = (bf16[2,1024,2048]{2,1,0:T(8,128)(2,1)}, f32[128,1024]{1,0:T(8,128)}, f32[1024,1024]{1,0:T(8,128)}) custom-call(f32[2,100,512]{2,1,0:T(8,128)} %get-tuple-element.38.f_ref, f32[2,100,512]{2,1,0:T(8,128)} %copy-done.8, f32[2,100,512]{2,1,0:T(8,128)} %copy-done.6, f32[2,100,512]{2,1,0:T(8,128)} %copy-done.12, ...), custom_call_target="tpu_custom_call", output_to_operand_aliasing={{0}: (14, {})} | custom-call | flops 4714397696 | bytes 20971520 | tf_op jit(solution)/shard_map/backward_part/pallas_call | solution.py:304
  96.0 0.8 copy-done.9
  96.9 16.4 %backward_part.7 = (bf16[2,1024,2048]{2,1,0:T(8,128)(2,1)}, f32[128,1024]{1,0:T(8,128)}, f32[2,4,80,512]{3,2,1,0:T(8,128)}, f32[2,4,80,512]{3,2,1,0:T(8,128)}, f...) custom-call(f32[2,100,512]{2,1,0:T(8,128)} %get-tuple-element.32.f_ref, ...), custom_call_target="tpu_custom_call", output_to_operand_aliasing={{0}: (14, {})} | custom-call | flops 4714397696 | bytes 20971520 | tf_op jit(solution)/shard_map/backward_part/pallas_call | solution.py:304
  113.3 0.4 collective-permute-start.22
  113.9 2.4 %collective-permute-done.22 = f32[2,2,4,64,256]{4,3,2,1,0:T(8,128)S(1)} collective-permute-done((f32[2,2,4,64,256]{4,3,2,1,0:T(8,128)}, f32[2,2,4,64,256]{4,3,2,1,0:T(8,128)S(1)}, u32[]{:S(2)}, u32[]{:S(2)}) %collective-permute-start.22) | collective-permute-done | bytes 1048608 | tf_op jit(solution)/shard_map/ppermute | solution.py:344
  116.2 1.1 fusion.3
  117.4 1.2 collective-permute-start.23
  118.6 1.2 fusion
  119.8 1.3 collective-permute-start.13
  121.1 9.5 %collective-permute-done.23 = f32[2,4,64,256]{3,2,1,0:T(8,128)S(1)} collective-permute-done((f32[2,4,64,256]{3,2,1,0:T(8,128)S(1)}, f32[2,4,64,256]{3,2,1,0:T(8,128)S(1)}, u32[]{:S(2)}, u32[]{:S(2)}) %collective-permute-start.23) | collective-permute-done | bytes 524320 | tf_op jit(solution)/shard_map/ppermute | solution.py:343
  130.7 4.8 %collective-permute-done.13 = f32[4,80,512]{2,1,0:T(8,128)S(1)} collective-permute-done((f32[4,80,512]{2,1,0:T(8,128)S(1)}, f32[4,80,512]{2,1,0:T(8,128)S(1)}, u32[]{:S(2)}, u32[]{:S(2)}) %collective-permute-start.13) | collective-permute-done | bytes 655392 | tf_op jit(solution)/shard_map/ppermute | solution.py:345
  135.8 1.4 collective-permute-start.14
  137.1 1.1 collective-permute-start.15
  138.2 1.4 collective-permute-start.16
  139.6 1.3 collective-permute-start.24
  140.9 8.7 %collective-permute-done.15 = f32[80,512]{1,0:T(8,128)S(1)} collective-permute-done((f32[80,512]{1,0:T(8,128)S(1)}, f32[80,512]{1,0:T(8,128)S(1)}, u32[]{:S(2)}, u32[]{:S(2)}) %collective-permute-start.15) | collective-permute-done | bytes 163872 | tf_op jit(solution)/shard_map/ppermute | solution.py:346
  149.6 3.7 %collective-permute-done.16 = f32[80,512]{1,0:T(8,128)S(1)} collective-permute-done((f32[80,512]{1,0:T(8,128)S(1)}, f32[80,512]{1,0:T(8,128)S(1)}, u32[]{:S(2)}, u32[]{:S(2)}) %collective-permute-start.16) | collective-permute-done | bytes 163872 | tf_op jit(solution)/shard_map/ppermute | solution.py:346
  153.4 1.1 collective-permute-start.17
  154.5 4.2 %collective-permute-done.17 = f32[80,512]{1,0:T(8,128)S(1)} collective-permute-done((f32[80,512]{1,0:T(8,128)S(1)}, f32[80,512]{1,0:T(8,128)S(1)}, u32[]{:S(2)}, u32[]{:S(2)}) %collective-permute-start.17) | collective-permute-done | bytes 163872 | tf_op jit(solution)/shard_map/ppermute | solution.py:343
  158.8 1.3 collective-permute-start.18
  160.2 1.4 collective-permute-start.27
  161.6 2.2 %collective-permute-start.19 = (f32[16,1024]{1,0:T(8,128)S(1)}, f32[16,1024]{1,0:T(8,128)S(1)}, u32[]{:S(2)}, u32[]{:S(2)}) collective-permute-start(f32[16,1024]{1,0:T(8,128)S(1)} %maximum_select_fusion.5), channel_id=1, source_target_pairs={{0,2},{1,3},{2,0},{3,1},{4,6},{5,7},{6,4},{7,5},{8,10},{9,11},{10,... | collective-permute-start | bytes 196616 | tf_op jit(solution)/shard_map/ppermute | solution.py:375
  163.9 1.1 collective-permute-done.26
  164.9 2.4 %collective-permute-done.27 = f32[64,256]{1,0:T(8,128)S(1)} collective-permute-done((f32[64,256]{1,0:T(8,128)S(1)}, f32[64,256]{1,0:T(8,128)S(1)}, u32[]{:S(2)}, u32[]{:S(2)}) %collective-permute-start.27) | collective-permute-done | bytes 65568 | tf_op jit(solution)/shard_map/ppermute | solution.py:346
  167.3 1.1 collective-permute-start.28
  168.4 1.0 collective-permute-start.20
  169.4 1.1 collective-permute-done.28
  170.6 3.0 %collective-permute-start.29 = (f32[64,1024]{1,0:T(8,128)S(1)}, f32[64,1024]{1,0:T(8,128)S(1)}, u32[]{:S(2)}, u32[]{:S(2)}) collective-permute-start(f32[64,1024]{1,0:T(8,128)S(1)} %maximum_multiply_fusion), channel_id=1, source_target_pairs={{0,8},{8,0},{16,24},{24,16},{1,9},{9,1},{17,25},{25,17},{2,10},{10... | collective-permute-start | bytes 786440 | tf_op jit(solution)/shard_map/ppermute | solution.py:375
  173.6 3.0 %collective-permute-start.21 = (f32[64,1024]{1,0:T(8,128)S(1)}, f32[64,1024]{1,0:T(8,128)S(1)}, u32[]{:S(2)}, u32[]{:S(2)}) collective-permute-start(f32[64,1024]{1,0:T(8,128)S(1)} %maximum_select_fusion.2), channel_id=1, source_target_pairs={{0,8},{8,0},{16,24},{24,16},{1,9},{9,1},{17,25},{25,17},{2,10},{10... | collective-permute-start | bytes 786440 | tf_op jit(solution)/shard_map/ppermute | solution.py:375
  176.6 0.8 maximum_select_fusion.1
  177.8 0.8 slice_multiply_fusion
  178.6 0.6 slice_reduce_fusion
  (73 shorter events, 3.0 us)
Async XLA Ops:
  10.9 25.1 %collective-permute-start.10 = (f32[2,100,512]{2,1,0:T(8,128)}, f32[2,100,512]{2,1,0:T(8,128)}, u32[]{:S(2)}, u32[]{:S(2)}) collective-permute-start(f32[2,100,512]{2,1,0:T(8,128)} %get-tuple-element.43.refs_0_), channel_id=1, source_target_pairs={{0,16},{8,24},{16,0},{24,8},{1,17},{9,25},{17,1},{25,9},{2,18},{10... | collective-permute-start | bytes 1228808 | tf_op jit(solution)/shard_map/ppermute | solution.py:343
  12.1 38.1 %collective-permute-start.9 = (f32[2,100,512]{2,1,0:T(8,128)}, f32[2,100,512]{2,1,0:T(8,128)}, u32[]{:S(2)}, u32[]{:S(2)}) collective-permute-start(f32[2,100,512]{2,1,0:T(8,128)} %get-tuple-element.43.refs_0_), channel_id=1, source_target_pairs={{0,8},{8,0},{16,24},{24,16},{1,9},{9,1},{17,25},{25,17},{2,10},{10... | collective-permute-start | bytes 1228808 | tf_op jit(solution)/shard_map/ppermute | solution.py:344
  23.5 12.3 %copy-start.1 = (bf16[100,1024]{1,0:T(8,128)(2,1)S(1)}, bf16[100,1024]{1,0:T(8,128)(2,1)}, u32[]{:S(2)}) copy-start(bf16[100,1024]{1,0:T(8,128)(2,1)} %wo_ref.7) | copy-start | bytes 614404
  23.5 26.8 %collective-permute-start.7 = (f32[2,100,512]{2,1,0:T(8,128)}, f32[2,100,512]{2,1,0:T(8,128)}, u32[]{:S(2)}, u32[]{:S(2)}) collective-permute-start(f32[2,100,512]{2,1,0:T(8,128)} %get-tuple-element.35.f_ref), channel_id=1, source_target_pairs={{0,16},{8,24},{16,0},{24,8},{1,17},{9,25},{17,1},{25,9},{2,18},{10... | collective-permute-start | bytes 1228808 | tf_op jit(solution)/shard_map/ppermute | solution.py:343
  23.8 40.8 %collective-permute-start.6 = (f32[2,100,512]{2,1,0:T(8,128)}, f32[2,100,512]{2,1,0:T(8,128)}, u32[]{:S(2)}, u32[]{:S(2)}) collective-permute-start(f32[2,100,512]{2,1,0:T(8,128)} %get-tuple-element.35.f_ref), channel_id=1, source_target_pairs={{0,8},{8,0},{16,24},{24,16},{1,9},{9,1},{17,25},{25,17},{2,10},{10... | collective-permute-start | bytes 1228808 | tf_op jit(solution)/shard_map/ppermute | solution.py:344
  24.1 12.4 %copy-start = (bf16[1024,1024]{1,0:T(8,128)(2,1)S(1)}, bf16[1024,1024]{1,0:T(8,128)(2,1)}, u32[]{:S(2)}) copy-start(bf16[1024,1024]{1,0:T(8,128)(2,1)} %w_ref.7) | copy-start | bytes 6291460
  34.6 30.1 %collective-permute-start.4 = (f32[2,100,512]{2,1,0:T(8,128)}, f32[2,100,512]{2,1,0:T(8,128)S(1)}, u32[]{:S(2)}, u32[]{:S(2)}) collective-permute-start(f32[2,100,512]{2,1,0:T(8,128)} %get-tuple-element.38.f_ref), channel_id=1, source_target_pairs={{0,16},{8,24},{16,0},{24,8},{1,17},{9,25},{17,1},{25,9},{2,18},{10... | collective-permute-start | bytes 1228808 | tf_op jit(solution)/shard_map/ppermute | solution.py:343
  36.0 14.7 %collective-permute-start.11 = (f32[2,100,512]{2,1,0:T(8,128)}, f32[2,100,512]{2,1,0:T(8,128)}, u32[]{:S(2)}, u32[]{:S(2)}) collective-permute-start(f32[2,100,512]{2,1,0:T(8,128)} %collective-permute-done.10.refs_2_), channel_id=1, source_target_pairs={{0,8},{8,0},{16,24},{24,16},{1,9},{9,1},{17,25},{25,17},{2,10},{10... | collective-permute-start | bytes 1228808 | tf_op jit(solution)/shard_map/ppermute | solution.py:344
  40.0 10.3 %copy-start.5 = (f32[2,100,512]{2,1,0:T(8,128)S(1)}, f32[2,100,512]{2,1,0:T(8,128)}, u32[]{:S(2)}) copy-start(f32[2,100,512]{2,1,0:T(8,128)} %get-tuple-element.38.f_ref) | copy-start | bytes 1228804
  50.3 30.4 %collective-permute-start.3 = (f32[2,100,512]{2,1,0:T(8,128)S(1)}, f32[2,100,512]{2,1,0:T(8,128)S(1)}, u32[]{:S(2)}, u32[]{:S(2)}) collective-permute-start(f32[2,100,512]{2,1,0:T(8,128)S(1)} %copy-done.5), channel_id=1, source_target_pairs={{0,8},{8,0},{16,24},{24,16},{1,9},{9,1},{17,25},{25,17},{2,10},{10... | collective-permute-start | bytes 1228808 | tf_op jit(solution)/shard_map/ppermute | solution.py:344
  50.4 14.8 %collective-permute-start.1 = (f32[2,100,512]{2,1,0:T(8,128)}, f32[2,100,512]{2,1,0:T(8,128)S(1)}, u32[]{:S(2)}, u32[]{:S(2)}) collective-permute-start(f32[2,100,512]{2,1,0:T(8,128)} %get-tuple-element.32.f_ref), channel_id=1, source_target_pairs={{0,16},{8,24},{16,0},{24,8},{1,17},{9,25},{17,1},{25,9},{2,18},{10... | collective-permute-start | bytes 1228808 | tf_op jit(solution)/shard_map/ppermute | solution.py:343
  50.7 14.6 %collective-permute-start.8 = (f32[2,100,512]{2,1,0:T(8,128)}, f32[2,100,512]{2,1,0:T(8,128)S(1)}, u32[]{:S(2)}, u32[]{:S(2)}) collective-permute-start(f32[2,100,512]{2,1,0:T(8,128)} %collective-permute-done.7.fx_ref), channel_id=1, source_target_pairs={{0,8},{8,0},{16,24},{24,16},{1,9},{9,1},{17,25},{25,17},{2,10},{10... | collective-permute-start | bytes 1228808 | tf_op jit(solution)/shard_map/ppermute | solution.py:344
  51.4 13.2 %copy-start.4 = (f32[2,100,512]{2,1,0:T(8,128)S(1)}, f32[2,100,512]{2,1,0:T(8,128)}, u32[]{:S(2)}) copy-start(f32[2,100,512]{2,1,0:T(8,128)} %get-tuple-element.32.f_ref) | copy-start | bytes 1228804
  64.6 31.4 %collective-permute-start = (f32[2,100,512]{2,1,0:T(8,128)S(1)}, f32[2,100,512]{2,1,0:T(8,128)S(1)}, u32[]{:S(2)}, u32[]{:S(2)}) collective-permute-start(f32[2,100,512]{2,1,0:T(8,128)S(1)} %copy-done.4), channel_id=1, source_target_pairs={{0,8},{8,0},{16,24},{24,16},{1,9},{9,1},{17,25},{25,17},{2,10},{10... | collective-permute-start | bytes 1228808 | tf_op jit(solution)/shard_map/ppermute | solution.py:344
  64.7 16.0 %copy-start.6 = (f32[2,100,512]{2,1,0:T(8,128)}, f32[2,100,512]{2,1,0:T(8,128)S(1)}, u32[]{:S(2)}) copy-start(f32[2,100,512]{2,1,0:T(8,128)S(1)} %collective-permute-done.4.fx_ref) | copy-start | bytes 1228804
  64.7 16.0 %collective-permute-start.5 = (f32[2,100,512]{2,1,0:T(8,128)S(1)}, f32[2,100,512]{2,1,0:T(8,128)S(1)}, u32[]{:S(2)}, u32[]{:S(2)}) collective-permute-start(f32[2,100,512]{2,1,0:T(8,128)S(1)} %collective-permute-done.4.fx_ref), channel_id=1, source_target_pairs={{0,8},{8,0},{16,24},{24,16},{1,9},{9,1},{17,25},{25,17},{2,10},{10... | collective-permute-start | bytes 1228808 | tf_op jit(solution)/shard_map/ppermute | solution.py:344
  65.2 15.5 %copy-start.7 = (f32[2,100,512]{2,1,0:T(8,128)}, f32[2,100,512]{2,1,0:T(8,128)S(1)}, u32[]{:S(2)}) copy-start(f32[2,100,512]{2,1,0:T(8,128)S(1)} %collective-permute-done.1.fx_ref) | copy-start | bytes 1228804
  65.2 30.9 %collective-permute-start.2 = (f32[2,100,512]{2,1,0:T(8,128)S(1)}, f32[2,100,512]{2,1,0:T(8,128)S(1)}, u32[]{:S(2)}, u32[]{:S(2)}) collective-permute-start(f32[2,100,512]{2,1,0:T(8,128)S(1)} %collective-permute-done.1.fx_ref), channel_id=1, source_target_pairs={{0,8},{8,0},{16,24},{24,16},{1,9},{9,1},{17,25},{25,17},{2,10},{10... | collective-permute-start | bytes 1228808 | tf_op jit(solution)/shard_map/ppermute | solution.py:344
  65.3 0.8 copy-start.11
  80.7 0.8 copy-start.8
  80.7 0.9 copy-start.12
  96.0 0.8 copy-start.9
  96.0 0.9 copy-start.10
  113.3 17.3 %copy-start.3 = (f32[2,2,4,64,256]{4,3,2,1,0:T(8,128)S(1)}, f32[2,2,4,64,256]{4,3,2,1,0:T(8,128)}, u32[]{:S(2)}) copy-start(f32[2,2,4,64,256]{4,3,2,1,0:T(8,128)} %get-tuple-element.58) | copy-start | bytes 3145732
  113.3 2.9 %collective-permute-start.22 = (f32[2,2,4,64,256]{4,3,2,1,0:T(8,128)}, f32[2,2,4,64,256]{4,3,2,1,0:T(8,128)S(1)}, u32[]{:S(2)}, u32[]{:S(2)}) collective-permute-start(f32[2,2,4,64,256]{4,3,2,1,0:T(8,128)} %get-tuple-element.59), channel_id=1, source_target_pairs={{0,8},{8,0},{16,24},{24,16},{1,9},{9,1},{17,25},{25,17},{2,10},{10... | collective-permute-start | bytes 3145736 | tf_op jit(solution)/shard_map/ppermute | solution.py:344
  113.7 4.9 %collective-permute-start.12 = (f32[2,4,80,512]{3,2,1,0:T(8,128)}, f32[2,4,80,512]{3,2,1,0:T(8,128)S(1)}, u32[]{:S(2)}, u32[]{:S(2)}) collective-permute-start(f32[2,4,80,512]{3,2,1,0:T(8,128)} %get-tuple-element.56), channel_id=1, source_target_pairs={{0,8},{8,0},{16,24},{24,16},{1,9},{9,1},{17,25},{25,17},{2,10},{10... | collective-permute-start | bytes 3932168 | tf_op jit(solution)/shard_map/ppermute | solution.py:344
  117.4 18.2 %copy-start.2 = (f32[2,4,80,512]{3,2,1,0:T(8,128)S(1)}, f32[2,4,80,512]{3,2,1,0:T(8,128)}, u32[]{:S(2)}) copy-start(f32[2,4,80,512]{3,2,1,0:T(8,128)} %get-tuple-element.55) | copy-start | bytes 3932164
  117.4 13.2 %collective-permute-start.23 = (f32[2,4,64,256]{3,2,1,0:T(8,128)S(1)}, f32[2,4,64,256]{3,2,1,0:T(8,128)S(1)}, u32[]{:S(2)}, u32[]{:S(2)}) collective-permute-start(f32[2,4,64,256]{3,2,1,0:T(8,128)S(1)} %fusion.3), channel_id=1, source_target_pairs={{0,16},{8,24},{16,0},{24,8},{1,17},{9,25},{17,1},{25,9},{2,18},{10... | collective-permute-start | bytes 1572872 | tf_op jit(solution)/shard_map/ppermute | solution.py:343
  119.8 15.7 %collective-permute-start.13 = (f32[4,80,512]{2,1,0:T(8,128)S(1)}, f32[4,80,512]{2,1,0:T(8,128)S(1)}, u32[]{:S(2)}, u32[]{:S(2)}) collective-permute-start(f32[4,80,512]{2,1,0:T(8,128)S(1)} %fusion), channel_id=1, source_target_pairs={{0,1},{1,0},{2,3},{3,2},{4,5},{5,4},{6,7},{7,6},{8,9},{9,8},{10,11... | collective-permute-start | bytes 1966088 | tf_op jit(solution)/shard_map/ppermute | solution.py:345
  135.8 5.2 %collective-permute-start.14 = (f32[80,512]{1,0:T(8,128)S(1)}, f32[80,512]{1,0:T(8,128)S(1)}, u32[]{:S(2)}, u32[]{:S(2)}) collective-permute-start(f32[80,512]{1,0:T(8,128)S(1)} %get-tuple-element.60), channel_id=1, source_target_pairs={{0,2},{1,3},{2,4},{3,5},{4,6},{5,7},{6,0},{7,1},{8,10},{9,11},{10,... | collective-permute-start | bytes 491528 | tf_op jit(solution)/shard_map/ppermute | solution.py:346
  137.1 12.5 %collective-permute-start.15 = (f32[80,512]{1,0:T(8,128)S(1)}, f32[80,512]{1,0:T(8,128)S(1)}, u32[]{:S(2)}, u32[]{:S(2)}) collective-permute-start(f32[80,512]{1,0:T(8,128)S(1)} %get-tuple-element.62), channel_id=1, source_target_pairs={{0,4},{1,5},{2,6},{3,7},{4,0},{5,1},{6,2},{7,3},{8,12},{9,13},{10,... | collective-permute-start | bytes 491528 | tf_op jit(solution)/shard_map/ppermute | solution.py:346
  138.2 15.1 %collective-permute-start.16 = (f32[80,512]{1,0:T(8,128)S(1)}, f32[80,512]{1,0:T(8,128)S(1)}, u32[]{:S(2)}, u32[]{:S(2)}) collective-permute-start(f32[80,512]{1,0:T(8,128)S(1)} %get-tuple-element.61), channel_id=1, source_target_pairs={{0,6},{1,7},{2,0},{3,1},{4,2},{5,3},{6,4},{7,5},{8,14},{9,15},{10,... | collective-permute-start | bytes 491528 | tf_op jit(solution)/shard_map/ppermute | solution.py:346
  139.6 14.8 %collective-permute-start.24 = (f32[4,64,256]{2,1,0:T(8,128)S(1)}, f32[4,64,256]{2,1,0:T(8,128)S(1)}, u32[]{:S(2)}, u32[]{:S(2)}) collective-permute-start(f32[4,64,256]{2,1,0:T(8,128)S(1)} %slice_bitcast_fusion), channel_id=1, source_target_pairs={{0,1},{1,0},{2,3},{3,2},{4,5},{5,4},{6,7},{7,6},{8,9},{9,8},{10,11... | collective-permute-start | bytes 786440 | tf_op jit(solution)/shard_map/ppermute | solution.py:345
  153.4 5.3 %collective-permute-start.17 = (f32[80,512]{1,0:T(8,128)S(1)}, f32[80,512]{1,0:T(8,128)S(1)}, u32[]{:S(2)}, u32[]{:S(2)}) collective-permute-start(f32[80,512]{1,0:T(8,128)S(1)} %fusion.9), channel_id=1, source_target_pairs={{0,16},{8,24},{16,0},{24,8},{1,17},{9,25},{17,1},{25,9},{2,18},{10... | collective-permute-start | bytes 491528 | tf_op jit(solution)/shard_map/ppermute | solution.py:343
  158.8 2.8 %collective-permute-start.18 = (f32[8,1024]{1,0:T(8,128)S(1)}, f32[8,1024]{1,0:T(8,128)S(1)}, u32[]{:S(2)}, u32[]{:S(2)}) collective-permute-start(f32[8,1024]{1,0:T(8,128)S(1)} %pad_maximum_fusion), channel_id=1, source_target_pairs={{0,1},{1,0},{2,3},{3,2},{4,5},{5,4},{6,7},{7,6},{8,9},{9,8},{10,11... | collective-permute-start | bytes 98312 | tf_op jit(solution)/shard_map/ppermute | solution.py:375
  160.1 3.8 %collective-permute-start.25 = (f32[64,256]{1,0:T(8,128)S(1)}, f32[64,256]{1,0:T(8,128)S(1)}, u32[]{:S(2)}, u32[]{:S(2)}) collective-permute-start(f32[64,256]{1,0:T(8,128)S(1)} %get-tuple-element.63), channel_id=1, source_target_pairs={{0,2},{1,3},{2,4},{3,5},{4,6},{5,7},{6,0},{7,1},{8,10},{9,11},{10,... | collective-permute-start | bytes 196616 | tf_op jit(solution)/shard_map/ppermute | solution.py:346
  160.2 4.8 %collective-permute-start.26 = (f32[64,256]{1,0:T(8,128)S(1)}, f32[64,256]{1,0:T(8,128)S(1)}, u32[]{:S(2)}, u32[]{:S(2)}) collective-permute-start(f32[64,256]{1,0:T(8,128)S(1)} %get-tuple-element.65), channel_id=1, source_target_pairs={{0,4},{1,5},{2,6},{3,7},{4,0},{5,1},{6,2},{7,3},{8,12},{9,13},{10,... | collective-permute-start | bytes 196616 | tf_op jit(solution)/shard_map/ppermute | solution.py:346
  160.2 7.1 %collective-permute-start.27 = (f32[64,256]{1,0:T(8,128)S(1)}, f32[64,256]{1,0:T(8,128)S(1)}, u32[]{:S(2)}, u32[]{:S(2)}) collective-permute-start(f32[64,256]{1,0:T(8,128)S(1)} %get-tuple-element.64), channel_id=1, source_target_pairs={{0,6},{1,7},{2,0},{3,1},{4,2},{5,3},{6,4},{7,5},{8,14},{9,15},{10,... | collective-permute-start | bytes 196616 | tf_op jit(solution)/shard_map/ppermute | solution.py:346
  161.6 6.8 %collective-permute-start.19 = (f32[16,1024]{1,0:T(8,128)S(1)}, f32[16,1024]{1,0:T(8,128)S(1)}, u32[]{:S(2)}, u32[]{:S(2)}) collective-permute-start(f32[16,1024]{1,0:T(8,128)S(1)} %maximum_select_fusion.5), channel_id=1, source_target_pairs={{0,2},{1,3},{2,0},{3,1},{4,6},{5,7},{6,4},{7,5},{8,10},{9,11},{10,... | collective-permute-start | bytes 196616 | tf_op jit(solution)/shard_map/ppermute | solution.py:375
  167.3 3.2 %collective-permute-start.28 = (f32[64,256]{1,0:T(8,128)S(1)}, f32[64,256]{1,0:T(8,128)S(1)}, u32[]{:S(2)}, u32[]{:S(2)}) collective-permute-start(f32[64,256]{1,0:T(8,128)S(1)} %fusion.12), channel_id=1, source_target_pairs={{0,16},{8,24},{16,0},{24,8},{1,17},{9,25},{17,1},{25,9},{2,18},{10... | collective-permute-start | bytes 196616 | tf_op jit(solution)/shard_map/ppermute | solution.py:375
  168.4 5.1 %collective-permute-start.20 = (f32[32,1024]{1,0:T(8,128)S(1)}, f32[32,1024]{1,0:T(8,128)S(1)}, u32[]{:S(2)}, u32[]{:S(2)}) collective-permute-start(f32[32,1024]{1,0:T(8,128)S(1)} %maximum_select_fusion.3), channel_id=1, source_target_pairs={{0,4},{1,5},{2,6},{3,7},{4,0},{5,1},{6,2},{7,3},{8,12},{9,13},{10,... | collective-permute-start | bytes 393224 | tf_op jit(solution)/shard_map/ppermute | solution.py:375
  170.6 6.0 %collective-permute-start.29 = (f32[64,1024]{1,0:T(8,128)S(1)}, f32[64,1024]{1,0:T(8,128)S(1)}, u32[]{:S(2)}, u32[]{:S(2)}) collective-permute-start(f32[64,1024]{1,0:T(8,128)S(1)} %maximum_multiply_fusion), channel_id=1, source_target_pairs={{0,8},{8,0},{16,24},{24,16},{1,9},{9,1},{17,25},{25,17},{2,10},{10... | collective-permute-start | bytes 786440 | tf_op jit(solution)/shard_map/ppermute | solution.py:375
  173.6 4.2 %collective-permute-start.21 = (f32[64,1024]{1,0:T(8,128)S(1)}, f32[64,1024]{1,0:T(8,128)S(1)}, u32[]{:S(2)}, u32[]{:S(2)}) collective-permute-start(f32[64,1024]{1,0:T(8,128)S(1)} %maximum_select_fusion.2), channel_id=1, source_target_pairs={{0,8},{8,0},{16,24},{24,16},{1,9},{9,1},{17,25},{25,17},{2,10},{10... | collective-permute-start | bytes 786440 | tf_op jit(solution)/shard_map/ppermute | solution.py:375

commit v3 on v2

--- a/solution.py
+++ b/solution.py
@@ -8,13 +8,12 @@
 from jax.experimental.pallas import tpu as pltpu
 from jax.sharding import PartitionSpec as P
 
-PARTS = 4
-FWD_TILE = 512
-BWD_TILE = 256
+EIGHTHS = (3, 3, 2)
+TILE = 256
 EPS = 0.0004
 K0 = math.sqrt(2.0 / math.pi)
 K1 = K0 * 0.044715
-SLAB = 256
+SLAB = 512
 EXTRA_ROWS = 8
 VMEM = 58 * 1024 * 1024
 NT = (((1,), (1,)), ((), ()))
@@ -26,7 +25,14 @@
     return jnp.sum(jnp.where(r == c, row, 0.0), axis=1, keepdims=True)
 
 
-def forward_kernel(tiles, hid_ref, w_ref, b_ref, wo_ref, bo_ref, act_ref, slope_ref, f_ref, bias, half, even, odd):
+def field_rows(v, mloc, m, r0):
+    full = v // 8 * 8
+    if r0 < full:
+        return pl.ds(m * full + r0, 8)
+    return pl.ds(mloc * full + m * (v - full), v - full)
+
+
+def forward_kernel(mloc, hid_ref, w_ref, b_ref, wo_ref, bo_ref, act_ref, slope_ref, f_ref, bias, half, even, odd):
     step = pl.program_id(0)
 
     @pl.when(step == 0)
@@ -38,57 +44,56 @@
 
         half[...] = wo_ref[...] * jnp.bfloat16(0.5)
 
-    def both(fill, drain):
+    def both(m, fill, drain):
         h, t = fill.shape
-        fill[...] = jnp.dot(w_ref[...], hid_ref[0], preferred_element_type=jnp.float32)
-        out = jnp.broadcast_to(column(bo_ref[...], bo_ref.shape[1]), f_ref.shape[1:])
+        out = jnp.broadcast_to(column(bo_ref[...], bo_ref.shape[1]), (bo_ref.shape[1], t))
         for k in range(0, h, SLAB):
+            slab = pl.ds(k, SLAB)
+            fill[slab, :] = jnp.dot(
+                w_ref[slab, :], hid_ref[0], preferred_element_type=jnp.float32
+            )
             for r in range(k, k + SLAB, 16):
                 rows = pl.ds(r, 16)
-                b = jnp.concatenate([bias[rows, :]] * 2, axis=1)
-                for c in range(0, t, 256):
-                    cols = pl.ds(c, 256)
-                    x = drain[rows, cols] + b
-                    q = x * x * K1
-                    th = jnp.tanh(x * (K0 + q))
-                    up = 1.0 + th
-                    act_ref[0, rows, cols] = (x * up).astype(jnp.bfloat16)
-                    slope_ref[0, rows, cols] = up * (1.0 + (1.0 - th) * (x * (K0 + 3.0 * q)))
-            slab = pl.ds(k, SLAB)
+                x = drain[rows, :] + jnp.concatenate([bias[rows, :]] * (t // 128), axis=1)
+                q = x * x * K1
+                th = jnp.tanh(x * (K0 + q))
+                up = 1.0 + th
+                act_ref[0, rows, :] = (x * up).astype(jnp.bfloat16)
+                slope_ref[0, rows, :] = up * (1.0 + (1.0 - th) * (x * (K0 + 3.0 * q)))
             out = out + jnp.dot(
                 half[:, slab], act_ref[0, slab, :], preferred_element_type=jnp.float32
             )
-        f_ref[0] = out
+        for r0 in range(0, out.shape[0], 8):
+            f_ref[field_rows(out.shape[0], mloc, m, r0), :] = out[r0 : r0 + 8]
 
     @pl.when(step % 2 == 0)
     def _():
-        both(even, odd)
+        both(1, even, odd)
 
     @pl.when(step % 2 == 1)
     def _():
-        both(odd, even)
-
-
-def forward(part, hidden, w_inner, b_inner, w_out, b_out):
+        both(0, odd, even)
+
+
+def forward(start, p, hidden, w_inner, b_inner, w_out, b_out):
     mloc, h, n = hidden.shape
     v = w_out.shape[0]
-    p = n // PARTS
-    t = FWD_TILE
-    per = p // t
-    tiles = mloc * per
+    t = TILE
+    tiles = mloc * (p // t)
+    assert mloc == 2
     whole = lambda s: (0, 0)
     once = pl.Buffered(1)
 
     def ahead(s):
         s = jnp.minimum(s, tiles - 1)
-        return (s // per, 0, part * per + s % per)
+        return (s % mloc, 0, start // t + s // mloc)
 
     def behind(s):
         s = jnp.maximum(s - 1, 0)
-        return (s // per, 0, s % per)
+        return (s % mloc, 0, s // mloc)
 
     return pl.pallas_call(
-        functools.partial(forward_kernel, tiles),
+        functools.partial(forward_kernel, mloc),
         grid=(tiles + 1,),
         in_specs=[
             pl.BlockSpec((1, h, t), ahead),
@@ -100,12 +105,12 @@
         out_specs=[
             pl.BlockSpec((1, h, t), behind),
             pl.BlockSpec((1, h, t), behind),
-            pl.BlockSpec((1, v, t), behind),
+            pl.BlockSpec((mloc * v, t), lambda s: (0, behind(s)[2])),
         ],
         out_shape=[
             jax.ShapeDtypeStruct((mloc, h, p), jnp.bfloat16),
             jax.ShapeDtypeStruct((mloc, h, p), jnp.float32),
-            jax.ShapeDtypeStruct((mloc, v, p), jnp.float32),
+            jax.ShapeDtypeStruct((mloc * v, p), jnp.float32),
         ],
         scratch_shapes=[
             pltpu.VMEM((h, 128), jnp.float32),
@@ -125,23 +130,35 @@
 def backward_kernel(
     first, last, dims, members,
     f_ref, fc_ref, fx_ref, fxc_ref, target_ref, area_ref, vw_ref, act_ref, slope_ref, hid_ref,
-    wot_ref, wt_ref, acc_in, extra_in, gh_in, gh_ref, extra_ref, *refs,
+    wot_ref, acc_in, extra_in, gp_ref, extra_ref, *refs,
 ):
     if last:
-        keep_a, send_a, keep_x, send_x, acc, gf, gp = refs
+        keep_a, send_a, keep_x, send_x, acc, *refs = refs
     else:
-        acc, gf, gp = refs
+        acc, *refs = refs
+    gf, gp, *refs = refs
     step = pl.program_id(0)
-    mloc, v, t = f_ref.shape
-    h = wt_ref.shape[0]
+    mloc, _, t = hid_ref.shape
+    v = target_ref.shape[0]
+    h = wot_ref.shape[0]
+    final = step == pl.num_programs(0) - 1
+    if not first:
+        earlier, sem = refs
+        fetch = pltpu.make_async_copy(acc_in, earlier, sem)
+
+        @pl.when(step == 0)
+        def _():
+            fetch.start()
+
     denom = members * (members - 1)
     vw = column(vw_ref[...], v)
     area = area_ref[...]
     loss = jnp.zeros((1, t), jnp.float32)
     for r0 in range(0, v, 8):
         rows = pl.ds(r0, min(8, v - r0))
-        own = [f_ref[m, rows, :] for m in range(mloc)]
-        others = [ref[m, rows, :] for ref in (fc_ref, fx_ref, fxc_ref) for m in range(mloc)]
+        places = [field_rows(v, mloc, m, r0) for m in range(mloc)]
+        own = [f_ref[place, :] for place in places]
+        others = [ref[place, :] for ref in (fc_ref, fx_ref, fxc_ref) for place in places]
         target = target_ref[rows, :]
         dsum = [None] * mloc
         obs = []
@@ -184,11 +201,13 @@
         gf[m, pl.ds(v, gf.shape[1] - v), :] = jnp.zeros((gf.shape[1] - v, t), jnp.float32)
 
     g = jnp.concatenate([gf[m] for m in range(mloc)], axis=1).astype(jnp.bfloat16)
-    for k in range(0, h, SLAB):
-        rows = pl.ds(k, SLAB)
+    for k in range(0, h, 256):
+        rows = pl.ds(k, 256)
         ga = jnp.dot(wot_ref[rows, :], g, preferred_element_type=jnp.float32)
-        slope = jnp.concatenate([slope_ref[m, rows, :] for m in range(mloc)], axis=1)
-        gp[rows, :] = (ga * slope).astype(jnp.bfloat16)
+        for m in range(mloc):
+            piece = (ga[:, m * t : (m + 1) * t] * slope_ref[m, rows, :]).astype(jnp.bfloat16)
+            gp[rows, pl.ds(m * t, t)] = piece
+            gp_ref[m, rows, :] = piece
     hid = jnp.concatenate([hid_ref[m] for m in range(mloc)], axis=1)
     act = jnp.concatenate([act_ref[m] for m in range(mloc)], axis=1)
     extra = lax.dot_general(g, act, NT, preferred_element_type=jnp.float32)
@@ -202,22 +221,25 @@
 
     @pl.when(step == 0)
     def _():
-        accumulate(acc_in, extra_in)
+        accumulate(None, extra_in)
 
     @pl.when(step > 0)
     def _():
         accumulate(acc, extra_ref)
 
     extra_ref[pl.ds(v, 1), pl.ds(0, t)] += loss
-    for k in range(0, h, SLAB):
-        rows = pl.ds(k, SLAB)
-        out = jnp.dot(wt_ref[rows, :], gp[...], preferred_element_type=jnp.float32)
-        for m in range(mloc):
-            gh_ref[m, rows, :] = out[:, m * t : (m + 1) * t].astype(jnp.bfloat16)
+    if not first:
+
+        @pl.when(final)
+        def _():
+            fetch.wait()
+            if not last:
+                acc[...] += earlier[...]
+
     if last:
         n_hi, n_lo = dims
 
-        @pl.when(step == pl.num_programs(0) - 1)
+        @pl.when(final)
         def _():
             mem = lax.axis_index("mem")
             grid = lax.axis_index("grid")
@@ -231,7 +253,8 @@
                     g = lax.rem(hi + dhi, n_hi) * n_lo + lax.rem(lo + dlo, n_lo)
                     for c, part_a, part_x in ((core, keep_a, keep_x), (1 - core, send_a, send_x)):
                         r0 = pl.multiple_of((g * 2 + c) * r, r)
-                        part_a[dlo, dhi, pl.ds(0, r), :] = acc[pl.ds(r0, r), pl.ds(0, ca)]
+                        total = acc[pl.ds(r0, r), :] + earlier[pl.ds(r0, r), :]
+                        part_a[dlo, dhi, pl.ds(0, r), :] = total[:, :ca]
                         e0 = (c * (n_hi * n_lo) + g) * EXTRA_ROWS
                         at = pl.multiple_of(
                             jnp.minimum(e0, extra_ref.shape[0] - EXTRA_ROWS), EXTRA_ROWS
@@ -241,53 +264,50 @@
                             part_a[dlo, dhi, pl.ds(r + k * EXTRA_ROWS, EXTRA_ROWS), :] = jnp.where(
                                 e0 < extra_ref.shape[0], e, 0.0
                             )
-                        left = acc[pl.ds(r0, r), pl.ds(ca, cx)]
-                        right = acc[pl.ds(r0, r), pl.ds(ca + cx, cx)]
+                        left = total[:, ca : ca + cx]
+                        right = total[:, ca + cx :]
                         part_x[0, dlo, dhi] = jnp.where(x == 0, left, right)
                         part_x[1, dlo, dhi] = jnp.where(x == 0, right, left)
 
 
-def backward(part, dims, members, fields, rest, acc, extra, gh):
-    target, area, vw, act, slope, hidden, wot, wt = rest
+def backward(start, p, first, last, dims, members, fields, rest, acc, extra):
+    target, area, vw, act, slope, hidden, wot = rest
     mloc, h, n = hidden.shape
     v = target.shape[0]
     vp = wot.shape[1]
-    p = n // PARTS
-    t = BWD_TILE
-    steps = p // t
-    first, last = part == 0, part == PARTS - 1
-    off = part * steps
+    t = TILE
+    off = start // t
     once = pl.Buffered(1)
-    f_spec = pl.BlockSpec((mloc, v, t), lambda s: (0, 0, s))
+    f_spec = pl.BlockSpec((mloc * v, t), lambda s: (0, s))
     big = pl.BlockSpec((mloc, h, t), lambda s: (0, 0, s))
     whole = lambda s: (0, 0)
     const = lambda a: pl.BlockSpec(a.shape, whole, pipeline_mode=once)
-    anyspec = pl.BlockSpec(memory_space=pl.ANY)
-    placed = pl.BlockSpec((mloc, h, t), lambda s: (0, 0, off + s))
     in_specs = [f_spec] * 4 + [
         pl.BlockSpec((v, t), lambda s: (0, off + s)),
         pl.BlockSpec((1, t), lambda s: (0, off + s)),
-        const(vw), big, big, placed, const(wot), const(wt),
+        const(vw), big, big,
+        pl.BlockSpec((mloc, h, t), lambda s: (0, 0, off + s)),
+        const(wot),
     ]
-    args = [*fields, target, area, vw, act, slope, hidden, wot, wt]
+    args = [*fields, target, area, vw, act, slope, hidden, wot]
     kernel = functools.partial(backward_kernel, first, last, dims, members)
     if first:
-        kernel_fn = lambda *refs: kernel(*refs[:12], None, None, None, *refs[12:])
-        aliases = {}
+        kernel_fn = lambda *refs: kernel(*refs[:11], None, None, *refs[11:])
     else:
         kernel_fn = kernel
-        in_specs += [const(acc), const(extra), anyspec]
-        args += [acc, extra, gh]
-        aliases = {14: 0}
-    out_specs = [placed, pl.BlockSpec((vp, h), whole, pipeline_mode=once)]
+        in_specs += [pl.BlockSpec(memory_space=pl.ANY), const(extra)]
+        args += [acc, extra]
+    out_specs = [big, pl.BlockSpec((vp, h), whole, pipeline_mode=once)]
     out_shape = [
-        jax.ShapeDtypeStruct(hidden.shape, jnp.bfloat16),
+        jax.ShapeDtypeStruct((mloc, h, p), jnp.bfloat16),
         jax.ShapeDtypeStruct((vp, h), jnp.float32),
     ]
     scratch = [
         pltpu.VMEM((mloc, vp, t), jnp.float32),
         pltpu.VMEM((h, mloc * t), jnp.bfloat16),
     ]
+    if not first:
+        scratch += [pltpu.VMEM((h, h), jnp.float32), pltpu.SemaphoreType.DMA]
     if last:
         n_hi, n_lo = dims
         r = h // (2 * n_hi * n_lo)
@@ -295,7 +315,9 @@
         cx = (h - ca) // 2
         ra = r + h // ca * EXTRA_ROWS
         for shape in ((n_lo, n_hi, ra, ca), (n_lo, n_hi, ra, ca), (2, n_lo, n_hi, r, cx), (2, n_lo, n_hi, r, cx)):
-            out_specs.append(pl.BlockSpec(shape, lambda s, k=len(shape): (0,) * k, pipeline_mode=once))
+            out_specs.append(
+                pl.BlockSpec(shape, lambda s, k=len(shape): (0,) * k, pipeline_mode=once)
+            )
             out_shape.append(jax.ShapeDtypeStruct(shape, jnp.float32))
         scratch = [pltpu.VMEM((h, h), jnp.float32)] + scratch
     else:
@@ -303,18 +325,51 @@
         out_shape.append(jax.ShapeDtypeStruct((h, h), jnp.float32))
     return pl.pallas_call(
         kernel_fn,
-        grid=(steps,),
+        grid=(p // t,),
         in_specs=in_specs,
         out_specs=out_specs,
         out_shape=out_shape,
         scratch_shapes=scratch,
-        input_output_aliases=aliases,
         compiler_params=pltpu.CompilerParams(vmem_limit_bytes=VMEM),
         cost_estimate=pl.CostEstimate(
-            flops=4 * mloc * p * h * (h + v), bytes_accessed=mloc * p * h * 10 + 10 * h * h,
+            flops=2 * mloc * p * h * (h + 2 * v), bytes_accessed=mloc * p * h * 10 + 10 * h * h,
             transcendentals=mloc * p * v * 8,
         ),
         name="backward_part",
+    )(*args)
+
+
+def input_kernel(wt_ref, gp_ref, *refs):
+    refs[-1][0] = jnp.dot(wt_ref[...], gp_ref[0], preferred_element_type=jnp.float32).astype(
+        jnp.bfloat16
+    )
+
+
+def input_gradient(start, p, n, wt, gp, gh):
+    mloc, h, _ = gp.shape
+    t = TILE
+    off = start // t
+    in_specs = [
+        pl.BlockSpec((h, h), lambda m, s: (0, 0), pipeline_mode=pl.Buffered(1)),
+        pl.BlockSpec((1, h, t), lambda m, s: (m, 0, s)),
+    ]
+    args = [wt, gp]
+    if gh is not None:
+        in_specs.append(pl.BlockSpec(memory_space=pl.ANY))
+        args.append(gh)
+    return pl.pallas_call(
+        input_kernel,
+        grid=(mloc, p // t),
+        in_specs=in_specs,
+        out_specs=pl.BlockSpec((1, h, t), lambda m, s: (m, 0, off + s)),
+        out_shape=jax.ShapeDtypeStruct((mloc, h, n), jnp.bfloat16),
+        input_output_aliases={} if gh is None else {2: 0},
+        compiler_params=pltpu.CompilerParams(vmem_limit_bytes=VMEM),
+        cost_estimate=pl.CostEstimate(
+            flops=2 * mloc * p * h * h, bytes_accessed=mloc * p * h * 4 + 2 * h * h,
+            transcendentals=0,
+        ),
+        name="grad_hidden_part",
     )(*args)
 
 
@@ -345,11 +400,13 @@
     to_lo = lambda a, k: lax.ppermute(a, "grid", shift_lo(k))
     to_hi = lambda a, k: lax.ppermute(a, "grid", shift_hi(k))
 
-    parts = []
-    for part in range(PARTS):
-        parts.append(
-            forward(part, hidden, w_inner, b_inner.reshape(1, h), w_out, b_out.reshape(1, v))
-        )
+    unit = n // sum(EIGHTHS)
+    starts = [unit * sum(EIGHTHS[:k]) for k in range(len(EIGHTHS))]
+    spans = [(start, unit * size) for start, size in zip(starts, EIGHTHS)]
+    parts = [
+        forward(start, p, hidden, w_inner, b_inner.reshape(1, h), w_out, b_out.reshape(1, v))
+        for start, p in spans
+    ]
     exchanged = []
     for act, slope, fields in parts:
         far = to_x(fields)
@@ -360,15 +417,20 @@
     wot = jnp.pad(w_out * jnp.bfloat16(0.5), ((0, vp - v), (0, 0))).T
     vw, area = var_weight.reshape(1, v), area.reshape(1, n)
     acc = extra = gh = None
-    for part in range(PARTS):
-        act, slope, _ = parts[part]
-        rest = (target, area, vw, act, slope, hidden, wot, wt)
-        gh, extra, *accs = backward(
-            part, (n_hi, n_lo), members, exchanged[part], rest, acc, extra, gh
+    grad_pre = []
+    for k, (start, p) in enumerate(spans):
+        act, slope, _ = parts[k]
+        first, last = k == 0, k == len(spans) - 1
+        gp, extra, *accs = backward(
+            start, p, first, last, (n_hi, n_lo), members, exchanged[k],
+            (target, area, vw, act, slope, hidden, wot), acc, extra,
         )
+        grad_pre.append(gp)
         acc = accs[0]
     keep_a, send_a, keep_x, send_x = accs
-
+    wt, _ = lax.optimization_barrier((wt, extra))
+    for (start, p), gp in zip(spans, grad_pre):
+        gh = input_gradient(start, p, n, wt, gp, gh)
 
     def gathered(block, axis, name, bit):
         n = lax.axis_size(name)

time: 184 us -> 174 us (0.946)
  waiting for transfers between devices: 38.2 us -> 27.5 us
  Pallas kernels: 100 us -> 96.4 us
  other arithmetic: 5.12 us -> 7.42 us
    ppermute x6, waiting for transfers between devices: 15.9 us -> 9.29 us  [shards(): to_hi = lambda a, k: lax.ppermute(a, 'grid', shift_hi(k))]
    pallas_call x8 -> x9, Pallas kernels: 100 us -> 96.4 us  [the longest x3 41.3 us: backward(): pl.pallas_call(kernel_fn, grid=(p // t,), in_specs=in_specs, out_specs=ou...]
    ppermute x10 -> x8, waiting for transfers between devices: 2.38 us -> 0.02 us  [shards(): to_core = lambda a: lax.ppermute(a, 'mem', swap_core)]
    ppermute x2, waiting for transfers between devices: 4.82 us -> 2.73 us  [shards(): to_lo = lambda a, k: lax.ppermute(a, 'grid', shift_lo(k))]
    ppermute x10 -> x8, starting transfers between devices: 3.83 us -> 5.7 us  [shards(): to_core = lambda a: lax.ppermute(a, 'mem', swap_core)]
    ppermute x6 -> x5, starting transfers between devices: 5.35 us -> 5.97 us  [shards(): to_x = lambda a: lax.ppermute(a, 'mem', swap_x)]
    ppermute x6 -> x5, waiting for transfers between devices: 13.7 us -> 13.9 us  [shards(): to_x = lambda a: lax.ppermute(a, 'mem', swap_x)]
  transfers between devices with their start and end apart: 30 -> 27, of which waited for: 10 -> 11; matrix products, arithmetic and copies ran while one was open for 4% -> 6% of each run, Pallas kernels for 41% -> 42%
where the time goes in v3:
time: 174 us; the launch traced here: 170 us
  Pallas kernels  96.4 us (55%)
  starting transfers between devices  30.2 us (17%)
  waiting for transfers between devices  27.5 us (16%)
  other arithmetic  7.42 us (4%)
  local copies, waits for them, and re-layouts  6.1 us (4%)
  between operations  2.69 us (2%)
    pallas_call x3, Pallas kernels, backward(): pl.pallas_call(kernel_fn, grid=(p // t,), in_specs=in_specs, out_specs=ou...  41.3 us
    pallas_call x3, Pallas kernels, forward(): pl.pallas_call(functools.partial(forward_kernel, mloc), grid=(tiles + 1,)...  33 us
    pallas_call x3, Pallas kernels, input_gradient(): pl.pallas_call(input_kernel, grid=(mloc, p // t), in_specs=in_specs, out_...  22.1 us
    ppermute x5, waiting for transfers between devices, shards(): to_x = lambda a: lax.ppermute(a, 'mem', swap_x)  13.9 us
    ppermute x6, starting transfers between devices, gathered(): other = lax.ppermute(block, name, [(i, i ^ bit) for i in range(n)])  10.6 us
    ppermute x6, waiting for transfers between devices, shards(): to_hi = lambda a, k: lax.ppermute(a, 'grid', shift_hi(k))  9.29 us
    ppermute x5, starting transfers between devices, shards(): to_x = lambda a: lax.ppermute(a, 'mem', swap_x)  5.97 us
    ppermute x8, starting transfers between devices, shards(): to_core = lambda a: lax.ppermute(a, 'mem', swap_core)  5.7 us
  transfers between devices with their start and end apart: 27, of which 11 were waited for; matrix products, arithmetic and copies ran while one was open for 6% of the time, Pallas kernels for 42%

profile of v3, /device:TPU:9, one launch (start us, length us, event | category | flops | bytes accessed | tf_op | source)
XLA Modules:
  0.0 170.3 jit_solution(15534380982433079664)
XLA Ops:
  0.6 11.9 %forward_part.5 = (bf16[2,1024,768]{2,1,0:T(8,128)(2,1)}, f32[2,1024,768]{2,1,0:T(8,128)}, f32[200,768]{1,0:T(8,128)}) custom-call(bf16[2,1024,2048]{2,1,0:T(8,128)(2,1)} %hid_ref.9, bf16[1024,1024]{1,0:T(8,128)(2,1)} %w_ref.5, f32[1,1024]{1,0:T(1,128)} %bitcast.62, bf16[100,1024]{1,0:T(8,128)(2,1)} %wo_ref.5, f32[1,100]{1,0:T(1,128)} %bitcast.65), custom_call_target="tpu_custom_call" | custom-call | flops 3535798272 | bytes 14680064 | tf_op jit(solution)/shard_map/forward_part/pallas_call | solution.py:95
  12.6 1.2 collective-permute-start.7
  13.8 11.8 %forward_part.4 = (bf16[2,1024,768]{2,1,0:T(8,128)(2,1)}, f32[2,1024,768]{2,1,0:T(8,128)}, f32[200,768]{1,0:T(8,128)}) custom-call(bf16[2,1024,2048]{2,1,0:T(8,128)(2,1)} %hid_ref.9, bf16[1024,1024]{1,0:T(8,128)(2,1)} %w_ref.5, f32[1,1024]{1,0:T(1,128)} %bitcast.63, bf16[100,1024]{1,0:T(8,128)(2,1)} %wo_ref.5, f32[1,100]{1,0:T(1,128)} %bitcast.66), custom_call_target="tpu_custom_call" | custom-call | flops 3535798272 | bytes 14680064 | tf_op jit(solution)/shard_map/forward_part/pallas_call | solution.py:95
  25.9 1.2 collective-permute-start.6
  27.5 1.6 collective-permute-start.8
  29.2 9.2 %forward_part.3 = (bf16[2,1024,512]{2,1,0:T(8,128)(2,1)}, f32[2,1024,512]{2,1,0:T(8,128)}, f32[200,512]{1,0:T(8,128)}) custom-call(bf16[2,1024,2048]{2,1,0:T(8,128)(2,1)} %hid_ref.9, bf16[1024,1024]{1,0:T(8,128)(2,1)} %w_ref.5, f32[1,1024]{1,0:T(1,128)} %bitcast.64, bf16[100,1024]{1,0:T(8,128)(2,1)} %wo_ref.5, f32[1,100]{1,0:T(1,128)} %bitcast.67), custom_call_target="tpu_custom_call" | custom-call | flops 2357198848 | bytes 10485760 | tf_op jit(solution)/shard_map/forward_part/pallas_call | solution.py:95
  38.4 2.2 %collective-permute-start.1 = (f32[200,512]{1,0:T(8,128)}, f32[200,512]{1,0:T(8,128)}, u32[]{:S(2)}, u32[]{:S(2)}) collective-permute-start(f32[200,512]{1,0:T(8,128)} %get-tuple-element.26.f_ref), channel_id=1, source_target_pairs={{0,16},{8,24},{16,0},{24,8},{1,17},{9,25},{17,1},{25,9},{2,18},{10... | collective-permute-start | bytes 1228808 | tf_op jit(solution)/shard_map/ppermute | solution.py:398
  41.2 1.0 collective-permute-start.5
  42.3 0.8 pad_bitcast_fusion.refs_10_.wot_ref
  43.0 7.5 %collective-permute-done.1.fx_ref = f32[200,512]{1,0:T(8,128)} collective-permute-done((f32[200,512]{1,0:T(8,128)}, f32[200,512]{1,0:T(8,128)}, u32[]{:S(2)}, u32[]{:S(2)}) %collective-permute-start.1) | collective-permute-done | bytes 409632 | tf_op jit(solution)/shard_map/ppermute | solution.py:398
  51.4 0.8 copy-done.8
  52.1 14.1 %backward_part.3 = (bf16[2,1024,768]{2,1,0:T(8,128)(2,1)}, f32[128,1024]{1,0:T(8,128)}, f32[1024,1024]{1,0:T(8,128)}) custom-call(f32[200,768]{1,0:T(8,128)} %get-tuple-element.33.refs_0_, f32[200,768]{1,0:T(8,128)} %copy-done.8, f32[200,768]{1,0:T(8,128)} %copy-done.7, f32[200,768]{1,0:T(8,128)} %collective-permute-done.8.refs_3_, f32[100,2048]{1,0:T(8,128)} %target_ref.3, ...), custom_call_target="tpu_custom_call" | custom-call | flops 3850371072 | bytes 26214400 | tf_op jit(solution)/shard_map/backward_part/pallas_call | solution.py:326
  66.3 0.8 copy-done.9
  67.1 15.0 %backward_part.4 = (bf16[2,1024,768]{2,1,0:T(8,128)(2,1)}, f32[128,1024]{1,0:T(8,128)}, f32[1024,1024]{1,0:T(8,128)}) custom-call(f32[200,768]{1,0:T(8,128)} %get-tuple-element.29.f_ref, f32[200,768]{1,0:T(8,128)} %collective-permute-done.3.fc_ref, f32[200,768]{1,0:T(8,128)} %copy-done.5, f32[200,768]{1,0:T(8,128)} %copy-done.9, f32[100,2048]{1,0:T(8,128)} %target_ref.3, ...), custom_call_target="tpu_custom_call" | custom-call | flops 3850371072 | bytes 26214400 | tf_op jit(solution)/shard_map/backward_part/pallas_call | solution.py:326
  82.2 0.7 copy-done.10
  83.1 12.1 %backward_part.5 = (bf16[2,1024,512]{2,1,0:T(8,128)(2,1)}, f32[128,1024]{1,0:T(8,128)}, f32[2,4,80,512]{3,2,1,0:T(8,128)}, f32[2,4,80,512]{3,2,1,0:T(8,128)}, f3...) custom-call(f32[200,512]{1,0:T(8,128)} %get-tuple-element.26.f_ref, f32[200,512]{1,0:T(8,128)} %copy-done.10, ...), custom_call_target="tpu_custom_call" | custom-call | flops 2566914048 | bytes 20971520 | tf_op jit(solution)/shard_map/backward_part/pallas_call | solution.py:326
  95.8 2.6 %copy.18 = bf16[1024,1024]{0,1:T(8,128)(2,1)} copy(bf16[1024,1024]{1,0:T(8,128)(2,1)S(1)} %copy-done) | data formatting | bytes 4194304 | tf_op jit(solution)/shard_map/optimization_barrier | solution.py:415
  98.4 1.3 fusion.3
  99.6 1.5 collective-permute-start.20
  101.2 1.2 fusion
  102.4 1.3 collective-permute-start.10
  103.7 8.1 %grad_hidden_part.3.refs_0_ = bf16[2,1024,2048]{2,1,0:T(8,128)(2,1)} custom-call(bf16[1024,1024]{1,0:T(8,128)(2,1)} %bitcast.53, bf16[2,1024,768]{2,1,0:T(8,128)(2,1)} %get-tuple-element.45.gp_ref), custom_call_target="tpu_custom_call" | custom-call | flops 3221225472 | bytes 8388608 | tf_op jit(solution)/shard_map/grad_hidden_part/pallas_call | solution.py:360
  111.8 1.4 collective-permute-done.20
  113.2 1.1 fusion.5
  114.4 1.3 collective-permute-start.21
  115.7 2.7 %collective-permute-done.10 = f32[4,80,512]{2,1,0:T(8,128)S(1)} collective-permute-done((f32[4,80,512]{2,1,0:T(8,128)S(1)}, f32[4,80,512]{2,1,0:T(8,128)S(1)}, u32[]{:S(2)}, u32[]{:S(2)}) %collective-permute-start.10) | collective-permute-done | bytes 655392 | tf_op jit(solution)/shard_map/ppermute | solution.py:400
  118.4 1.3 fusion.2
  119.7 1.4 collective-permute-start.11
  121.1 1.1 collective-permute-start.12
  122.2 1.3 collective-permute-start.13
  123.6 8.0 %grad_hidden_part.4.refs_0_ = bf16[2,1024,2048]{2,1,0:T(8,128)(2,1)} custom-call(bf16[1024,1024]{1,0:T(8,128)(2,1)} %bitcast.54, bf16[2,1024,768]{2,1,0:T(8,128)(2,1)} %get-tuple-element.44.gp_ref, bf16[2,1024,2048]{2,1,0:T(8,128)(2,1)} %grad_hidden_part.3.refs_0_), custom_call_target="tpu_custom_call", output_to_operand_aliasing={{}: (2, {})} | custom-call | flops 3221225472 | bytes 8388608 | tf_op jit(solution)/shard_map/grad_hidden_part/pallas_call | solution.py:360
  131.6 1.5 collective-permute-done.12
  133.1 4.3 %collective-permute-done.13 = f32[80,512]{1,0:T(8,128)S(1)} collective-permute-done((f32[80,512]{1,0:T(8,128)S(1)}, f32[80,512]{1,0:T(8,128)S(1)}, u32[]{:S(2)}, u32[]{:S(2)}) %collective-permute-start.13) | collective-permute-done | bytes 163872 | tf_op jit(solution)/shard_map/ppermute | solution.py:401
  137.5 0.7 collective-permute-start.14
  138.2 4.6 %collective-permute-done.14 = f32[80,512]{1,0:T(8,128)S(1)} collective-permute-done((f32[80,512]{1,0:T(8,128)S(1)}, f32[80,512]{1,0:T(8,128)S(1)}, u32[]{:S(2)}, u32[]{:S(2)}) %collective-permute-start.14) | collective-permute-done | bytes 163872 | tf_op jit(solution)/shard_map/ppermute | solution.py:398
  142.9 1.2 collective-permute-start.15
  144.2 1.4 collective-permute-start.24
  145.7 2.1 %collective-permute-start.16 = (f32[16,1024]{1,0:T(8,128)S(1)}, f32[16,1024]{1,0:T(8,128)S(1)}, u32[]{:S(2)}, u32[]{:S(2)}) collective-permute-start(f32[16,1024]{1,0:T(8,128)S(1)} %maximum_select_fusion.5), channel_id=1, source_target_pairs={{0,2},{1,3},{2,0},{3,1},{4,6},{5,7},{6,4},{7,5},{8,10},{9,11},{10,... | collective-permute-start | bytes 196616 | tf_op jit(solution)/shard_map/ppermute | solution.py:437
  147.8 1.1 collective-permute-done.23
  148.9 2.4 %collective-permute-done.24 = f32[64,256]{1,0:T(8,128)S(1)} collective-permute-done((f32[64,256]{1,0:T(8,128)S(1)}, f32[64,256]{1,0:T(8,128)S(1)}, u32[]{:S(2)}, u32[]{:S(2)}) %collective-permute-start.24) | collective-permute-done | bytes 65568 | tf_op jit(solution)/shard_map/ppermute | solution.py:401
  151.3 0.7 collective-permute-start.25
  152.0 1.0 collective-permute-start.17
  153.0 1.5 collective-permute-done.25
  154.6 3.0 %collective-permute-start.26 = (f32[64,1024]{1,0:T(8,128)S(1)}, f32[64,1024]{1,0:T(8,128)S(1)}, u32[]{:S(2)}, u32[]{:S(2)}) collective-permute-start(f32[64,1024]{1,0:T(8,128)S(1)} %maximum_multiply_fusion), channel_id=1, source_target_pairs={{0,8},{8,0},{16,24},{24,16},{1,9},{9,1},{17,25},{25,17},{2,10},{10... | collective-permute-start | bytes 786440 | tf_op jit(solution)/shard_map/ppermute | solution.py:437
  157.5 2.7 %collective-permute-start.18 = (f32[64,1024]{1,0:T(8,128)S(1)}, f32[64,1024]{1,0:T(8,128)S(1)}, u32[]{:S(2)}, u32[]{:S(2)}) collective-permute-start(f32[64,1024]{1,0:T(8,128)S(1)} %maximum_select_fusion.2), channel_id=1, source_target_pairs={{0,8},{8,0},{16,24},{24,16},{1,9},{9,1},{17,25},{25,17},{2,10},{10... | collective-permute-start | bytes 786440 | tf_op jit(solution)/shard_map/ppermute | solution.py:437
  160.2 6.0 %grad_hidden_part.5 = bf16[2,1024,2048]{2,1,0:T(8,128)(2,1)} custom-call(bf16[1024,1024]{1,0:T(8,128)(2,1)} %bitcast.55, bf16[2,1024,512]{2,1,0:T(8,128)(2,1)} %get-tuple-element.43.gp_ref, bf16[2,1024,2048]{2,1,0:T(8,128)(2,1)} %grad_hidden_part.4.refs_0_), custom_call_target="tpu_custom_call", output_to_operand_aliasing={{}: (2, {})} | custom-call | flops 2147483648 | bytes 6291456 | tf_op jit(solution)/shard_map/grad_hidden_part/pallas_call | solution.py:360
  166.2 0.8 maximum_select_fusion.1
  167.1 0.8 slice_multiply_fusion
  (66 shorter events, 4.1 us)
Async XLA Ops:
  12.6 13.4 %copy-start.6 = (f32[200,768]{1,0:T(8,128)S(1)}, f32[200,768]{1,0:T(8,128)}, u32[]{:S(2)}) copy-start(f32[200,768]{1,0:T(8,128)} %get-tuple-element.33.refs_0_) | copy-start | bytes 1843204
  12.6 15.0 %collective-permute-start.7 = (f32[200,768]{1,0:T(8,128)}, f32[200,768]{1,0:T(8,128)S(1)}, u32[]{:S(2)}, u32[]{:S(2)}) collective-permute-start(f32[200,768]{1,0:T(8,128)} %get-tuple-element.33.refs_0_), channel_id=1, source_target_pairs={{0,16},{8,24},{16,0},{24,8},{1,17},{9,25},{17,1},{25,9},{2,18},{10... | collective-permute-start | bytes 1843208 | tf_op jit(solution)/shard_map/ppermute | solution.py:398
  25.6 14.9 %copy-start.4 = (f32[200,768]{1,0:T(8,128)S(1)}, f32[200,768]{1,0:T(8,128)}, u32[]{:S(2)}) copy-start(f32[200,768]{1,0:T(8,128)} %get-tuple-element.29.f_ref) | copy-start | bytes 1843204
  25.6 15.4 %copy-start.3 = (bf16[100,1024]{1,0:T(8,128)(2,1)S(1)}, bf16[100,1024]{1,0:T(8,128)(2,1)}, u32[]{:S(2)}) copy-start(bf16[100,1024]{1,0:T(8,128)(2,1)} %wo_ref.5) | copy-start | bytes 614404
  25.6 15.6 %collective-permute-start.4 = (f32[200,768]{1,0:T(8,128)}, f32[200,768]{1,0:T(8,128)S(1)}, u32[]{:S(2)}, u32[]{:S(2)}) collective-permute-start(f32[200,768]{1,0:T(8,128)} %get-tuple-element.29.f_ref), channel_id=1, source_target_pairs={{0,16},{8,24},{16,0},{24,8},{1,17},{9,25},{17,1},{25,9},{2,18},{10... | collective-permute-start | bytes 1843208 | tf_op jit(solution)/shard_map/ppermute | solution.py:398
  25.9 25.3 %collective-permute-start.6 = (f32[200,768]{1,0:T(8,128)S(1)}, f32[200,768]{1,0:T(8,128)S(1)}, u32[]{:S(2)}, u32[]{:S(2)}) collective-permute-start(f32[200,768]{1,0:T(8,128)S(1)} %copy-done.6), channel_id=1, source_target_pairs={{0,8},{8,0},{16,24},{24,16},{1,9},{9,1},{17,25},{25,17},{2,10},{10... | collective-permute-start | bytes 1843208 | tf_op jit(solution)/shard_map/ppermute | solution.py:399
  27.5 10.8 %copy-start.7 = (f32[200,768]{1,0:T(8,128)}, f32[200,768]{1,0:T(8,128)S(1)}, u32[]{:S(2)}) copy-start(f32[200,768]{1,0:T(8,128)S(1)} %collective-permute-done.7.refs_2_) | copy-start | bytes 1843204
  27.5 23.8 %collective-permute-start.8 = (f32[200,768]{1,0:T(8,128)S(1)}, f32[200,768]{1,0:T(8,128)}, u32[]{:S(2)}, u32[]{:S(2)}) collective-permute-start(f32[200,768]{1,0:T(8,128)S(1)} %collective-permute-done.7.refs_2_), channel_id=1, source_target_pairs={{0,8},{8,0},{16,24},{24,16},{1,9},{9,1},{17,25},{25,17},{2,10},{10... | collective-permute-start | bytes 1843208 | tf_op jit(solution)/shard_map/ppermute | solution.py:399
  38.4 12.2 %collective-permute-start.1 = (f32[200,512]{1,0:T(8,128)}, f32[200,512]{1,0:T(8,128)}, u32[]{:S(2)}, u32[]{:S(2)}) collective-permute-start(f32[200,512]{1,0:T(8,128)} %get-tuple-element.26.f_ref), channel_id=1, source_target_pairs={{0,16},{8,24},{16,0},{24,8},{1,17},{9,25},{17,1},{25,9},{2,18},{10... | collective-permute-start | bytes 1228808 | tf_op jit(solution)/shard_map/ppermute | solution.py:398
  40.5 25.7 %collective-permute-start.3 = (f32[200,768]{1,0:T(8,128)S(1)}, f32[200,768]{1,0:T(8,128)}, u32[]{:S(2)}, u32[]{:S(2)}) collective-permute-start(f32[200,768]{1,0:T(8,128)S(1)} %copy-done.4), channel_id=1, source_target_pairs={{0,8},{8,0},{16,24},{24,16},{1,9},{9,1},{17,25},{25,17},{2,10},{10... | collective-permute-start | bytes 1843208 | tf_op jit(solution)/shard_map/ppermute | solution.py:399
  41.2 25.0 %copy-start.5 = (f32[200,768]{1,0:T(8,128)}, f32[200,768]{1,0:T(8,128)S(1)}, u32[]{:S(2)}) copy-start(f32[200,768]{1,0:T(8,128)S(1)} %collective-permute-done.4.fx_ref) | copy-start | bytes 1843204
  41.2 25.0 %collective-permute-start.5 = (f32[200,768]{1,0:T(8,128)S(1)}, f32[200,768]{1,0:T(8,128)S(1)}, u32[]{:S(2)}, u32[]{:S(2)}) collective-permute-start(f32[200,768]{1,0:T(8,128)S(1)} %collective-permute-done.4.fx_ref), channel_id=1, source_target_pairs={{0,8},{8,0},{16,24},{24,16},{1,9},{9,1},{17,25},{25,17},{2,10},{10... | collective-permute-start | bytes 1843208 | tf_op jit(solution)/shard_map/ppermute | solution.py:399
  50.6 31.6 %collective-permute-start = (f32[200,512]{1,0:T(8,128)}, f32[200,512]{1,0:T(8,128)S(1)}, u32[]{:S(2)}, u32[]{:S(2)}) collective-permute-start(f32[200,512]{1,0:T(8,128)} %get-tuple-element.26.f_ref), channel_id=1, source_target_pairs={{0,8},{8,0},{16,24},{24,16},{1,9},{9,1},{17,25},{25,17},{2,10},{10... | collective-permute-start | bytes 1228808 | tf_op jit(solution)/shard_map/ppermute | solution.py:399
  51.3 0.9 copy-start.8
  51.3 30.9 %collective-permute-start.2 = (f32[200,512]{1,0:T(8,128)}, f32[200,512]{1,0:T(8,128)S(1)}, u32[]{:S(2)}, u32[]{:S(2)}) collective-permute-start(f32[200,512]{1,0:T(8,128)} %collective-permute-done.1.fx_ref), channel_id=1, source_target_pairs={{0,8},{8,0},{16,24},{24,16},{1,9},{9,1},{17,25},{25,17},{2,10},{10... | collective-permute-start | bytes 1228808 | tf_op jit(solution)/shard_map/ppermute | solution.py:399
  66.3 0.8 copy-start.9
  82.2 0.8 copy-start.10
  82.2 0.9 copy-start.11
  83.1 12.7 %copy-start = (bf16[1024,1024]{1,0:T(8,128)(2,1)S(1)}, bf16[1024,1024]{1,0:T(8,128)(2,1)}, u32[]{:S(2)}) copy-start(bf16[1024,1024]{1,0:T(8,128)(2,1)} %w_ref.5) | copy-start | bytes 6291460
  95.2 6.0 %copy-start.1 = (f32[2,4,80,512]{3,2,1,0:T(8,128)S(1)}, f32[2,4,80,512]{3,2,1,0:T(8,128)}, u32[]{:S(2)}) copy-start(f32[2,4,80,512]{3,2,1,0:T(8,128)} %get-tuple-element.40) | copy-start | bytes 3932164
  95.2 3.1 %collective-permute-start.19 = (f32[2,2,4,64,256]{4,3,2,1,0:T(8,128)}, f32[2,2,4,64,256]{4,3,2,1,0:T(8,128)}, u32[]{:S(2)}, u32[]{:S(2)}) collective-permute-start(f32[2,2,4,64,256]{4,3,2,1,0:T(8,128)} %get-tuple-element.47), channel_id=1, source_target_pairs={{0,8},{8,0},{16,24},{24,16},{1,9},{9,1},{17,25},{25,17},{2,10},{10... | collective-permute-start | bytes 3145736 | tf_op jit(solution)/shard_map/ppermute | solution.py:399
  95.3 5.9 %collective-permute-start.9 = (f32[2,4,80,512]{3,2,1,0:T(8,128)}, f32[2,4,80,512]{3,2,1,0:T(8,128)}, u32[]{:S(2)}, u32[]{:S(2)}) collective-permute-start(f32[2,4,80,512]{3,2,1,0:T(8,128)} %get-tuple-element.41), channel_id=1, source_target_pairs={{0,8},{8,0},{16,24},{24,16},{1,9},{9,1},{17,25},{25,17},{2,10},{10... | collective-permute-start | bytes 3932168 | tf_op jit(solution)/shard_map/ppermute | solution.py:399
  99.6 13.6 %collective-permute-start.20 = (f32[2,4,64,256]{3,2,1,0:T(8,128)S(1)}, f32[2,4,64,256]{3,2,1,0:T(8,128)S(1)}, u32[]{:S(2)}, u32[]{:S(2)}) collective-permute-start(f32[2,4,64,256]{3,2,1,0:T(8,128)S(1)} %fusion.3), channel_id=1, source_target_pairs={{0,16},{8,24},{16,0},{24,8},{1,17},{9,25},{17,1},{25,9},{2,18},{10... | collective-permute-start | bytes 1572872 | tf_op jit(solution)/shard_map/ppermute | solution.py:398
  102.4 16.0 %collective-permute-start.10 = (f32[4,80,512]{2,1,0:T(8,128)S(1)}, f32[4,80,512]{2,1,0:T(8,128)S(1)}, u32[]{:S(2)}, u32[]{:S(2)}) collective-permute-start(f32[4,80,512]{2,1,0:T(8,128)S(1)} %fusion), channel_id=1, source_target_pairs={{0,1},{1,0},{2,3},{3,2},{4,5},{5,4},{6,7},{7,6},{8,9},{9,8},{10,11... | collective-permute-start | bytes 1966088 | tf_op jit(solution)/shard_map/ppermute | solution.py:400
  103.7 9.5 %copy-start.2 = (f32[2,2,4,64,256]{4,3,2,1,0:T(8,128)S(1)}, f32[2,2,4,64,256]{4,3,2,1,0:T(8,128)}, u32[]{:S(2)}) copy-start(f32[2,2,4,64,256]{4,3,2,1,0:T(8,128)} %get-tuple-element.46) | copy-start | bytes 3145732
  114.4 23.8 %collective-permute-start.21 = (f32[4,64,256]{2,1,0:T(8,128)S(1)}, f32[4,64,256]{2,1,0:T(8,128)S(1)}, u32[]{:S(2)}, u32[]{:S(2)}) collective-permute-start(f32[4,64,256]{2,1,0:T(8,128)S(1)} %slice_bitcast_fusion), channel_id=1, source_target_pairs={{0,1},{1,0},{2,3},{3,2},{4,5},{5,4},{6,7},{7,6},{8,9},{9,8},{10,11... | collective-permute-start | bytes 786440 | tf_op jit(solution)/shard_map/ppermute | solution.py:400
  119.7 11.9 %collective-permute-start.11 = (f32[80,512]{1,0:T(8,128)S(1)}, f32[80,512]{1,0:T(8,128)S(1)}, u32[]{:S(2)}, u32[]{:S(2)}) collective-permute-start(f32[80,512]{1,0:T(8,128)S(1)} %get-tuple-element.48), channel_id=1, source_target_pairs={{0,2},{1,3},{2,4},{3,5},{4,6},{5,7},{6,0},{7,1},{8,10},{9,11},{10,... | collective-permute-start | bytes 491528 | tf_op jit(solution)/shard_map/ppermute | solution.py:401
  121.1 12.0 %collective-permute-start.12 = (f32[80,512]{1,0:T(8,128)S(1)}, f32[80,512]{1,0:T(8,128)S(1)}, u32[]{:S(2)}, u32[]{:S(2)}) collective-permute-start(f32[80,512]{1,0:T(8,128)S(1)} %get-tuple-element.50), channel_id=1, source_target_pairs={{0,4},{1,5},{2,6},{3,7},{4,0},{5,1},{6,2},{7,3},{8,12},{9,13},{10,... | collective-permute-start | bytes 491528 | tf_op jit(solution)/shard_map/ppermute | solution.py:401
  122.2 15.2 %collective-permute-start.13 = (f32[80,512]{1,0:T(8,128)S(1)}, f32[80,512]{1,0:T(8,128)S(1)}, u32[]{:S(2)}, u32[]{:S(2)}) collective-permute-start(f32[80,512]{1,0:T(8,128)S(1)} %get-tuple-element.49), channel_id=1, source_target_pairs={{0,6},{1,7},{2,0},{3,1},{4,2},{5,3},{6,4},{7,5},{8,14},{9,15},{10,... | collective-permute-start | bytes 491528 | tf_op jit(solution)/shard_map/ppermute | solution.py:401
  137.5 5.3 %collective-permute-start.14 = (f32[80,512]{1,0:T(8,128)S(1)}, f32[80,512]{1,0:T(8,128)S(1)}, u32[]{:S(2)}, u32[]{:S(2)}) collective-permute-start(f32[80,512]{1,0:T(8,128)S(1)} %fusion.9), channel_id=1, source_target_pairs={{0,16},{8,24},{16,0},{24,8},{1,17},{9,25},{17,1},{25,9},{2,18},{10... | collective-permute-start | bytes 491528 | tf_op jit(solution)/shard_map/ppermute | solution.py:398
  142.9 2.8 %collective-permute-start.15 = (f32[8,1024]{1,0:T(8,128)S(1)}, f32[8,1024]{1,0:T(8,128)S(1)}, u32[]{:S(2)}, u32[]{:S(2)}) collective-permute-start(f32[8,1024]{1,0:T(8,128)S(1)} %pad_maximum_fusion), channel_id=1, source_target_pairs={{0,1},{1,0},{2,3},{3,2},{4,5},{5,4},{6,7},{7,6},{8,9},{9,8},{10,11... | collective-permute-start | bytes 98312 | tf_op jit(solution)/shard_map/ppermute | solution.py:437
  144.1 3.8 %collective-permute-start.22 = (f32[64,256]{1,0:T(8,128)S(1)}, f32[64,256]{1,0:T(8,128)S(1)}, u32[]{:S(2)}, u32[]{:S(2)}) collective-permute-start(f32[64,256]{1,0:T(8,128)S(1)} %get-tuple-element.51), channel_id=1, source_target_pairs={{0,2},{1,3},{2,4},{3,5},{4,6},{5,7},{6,0},{7,1},{8,10},{9,11},{10,... | collective-permute-start | bytes 196616 | tf_op jit(solution)/shard_map/ppermute | solution.py:401
  144.1 4.8 %collective-permute-start.23 = (f32[64,256]{1,0:T(8,128)S(1)}, f32[64,256]{1,0:T(8,128)S(1)}, u32[]{:S(2)}, u32[]{:S(2)}) collective-permute-start(f32[64,256]{1,0:T(8,128)S(1)} %get-tuple-element.53), channel_id=1, source_target_pairs={{0,4},{1,5},{2,6},{3,7},{4,0},{5,1},{6,2},{7,3},{8,12},{9,13},{10,... | collective-permute-start | bytes 196616 | tf_op jit(solution)/shard_map/ppermute | solution.py:401
  144.2 7.1 %collective-permute-start.24 = (f32[64,256]{1,0:T(8,128)S(1)}, f32[64,256]{1,0:T(8,128)S(1)}, u32[]{:S(2)}, u32[]{:S(2)}) collective-permute-start(f32[64,256]{1,0:T(8,128)S(1)} %get-tuple-element.52), channel_id=1, source_target_pairs={{0,6},{1,7},{2,0},{3,1},{4,2},{5,3},{6,4},{7,5},{8,14},{9,15},{10,... | collective-permute-start | bytes 196616 | tf_op jit(solution)/shard_map/ppermute | solution.py:401
  145.7 6.3 %collective-permute-start.16 = (f32[16,1024]{1,0:T(8,128)S(1)}, f32[16,1024]{1,0:T(8,128)S(1)}, u32[]{:S(2)}, u32[]{:S(2)}) collective-permute-start(f32[16,1024]{1,0:T(8,128)S(1)} %maximum_select_fusion.5), channel_id=1, source_target_pairs={{0,2},{1,3},{2,0},{3,1},{4,6},{5,7},{6,4},{7,5},{8,10},{9,11},{10,... | collective-permute-start | bytes 196616 | tf_op jit(solution)/shard_map/ppermute | solution.py:437
  151.3 3.2 %collective-permute-start.25 = (f32[64,256]{1,0:T(8,128)S(1)}, f32[64,256]{1,0:T(8,128)S(1)}, u32[]{:S(2)}, u32[]{:S(2)}) collective-permute-start(f32[64,256]{1,0:T(8,128)S(1)} %fusion.12), channel_id=1, source_target_pairs={{0,16},{8,24},{16,0},{24,8},{1,17},{9,25},{17,1},{25,9},{2,18},{10... | collective-permute-start | bytes 196616 | tf_op jit(solution)/shard_map/ppermute | solution.py:437
  152.0 5.5 %collective-permute-start.17 = (f32[32,1024]{1,0:T(8,128)S(1)}, f32[32,1024]{1,0:T(8,128)S(1)}, u32[]{:S(2)}, u32[]{:S(2)}) collective-permute-start(f32[32,1024]{1,0:T(8,128)S(1)} %maximum_select_fusion.3), channel_id=1, source_target_pairs={{0,4},{1,5},{2,6},{3,7},{4,0},{5,1},{6,2},{7,3},{8,12},{9,13},{10,... | collective-permute-start | bytes 393224 | tf_op jit(solution)/shard_map/ppermute | solution.py:437
  154.6 11.7 %collective-permute-start.26 = (f32[64,1024]{1,0:T(8,128)S(1)}, f32[64,1024]{1,0:T(8,128)S(1)}, u32[]{:S(2)}, u32[]{:S(2)}) collective-permute-start(f32[64,1024]{1,0:T(8,128)S(1)} %maximum_multiply_fusion), channel_id=1, source_target_pairs={{0,8},{8,0},{16,24},{24,16},{1,9},{9,1},{17,25},{25,17},{2,10},{10... | collective-permute-start | bytes 786440 | tf_op jit(solution)/shard_map/ppermute | solution.py:437
  157.5 9.5 %collective-permute-start.18 = (f32[64,1024]{1,0:T(8,128)S(1)}, f32[64,1024]{1,0:T(8,128)S(1)}, u32[]{:S(2)}, u32[]{:S(2)}) collective-permute-start(f32[64,1024]{1,0:T(8,128)S(1)} %maximum_select_fusion.2), channel_id=1, source_target_pairs={{0,8},{8,0},{16,24},{24,16},{1,9},{9,1},{17,25},{25,17},{2,10},{10... | collective-permute-start | bytes 786440 | tf_op jit(solution)/shard_map/ppermute | solution.py:437

commit v4 on v3

--- a/solution.py
+++ b/solution.py
@@ -58,8 +58,9 @@
                 q = x * x * K1
                 th = jnp.tanh(x * (K0 + q))
                 up = 1.0 + th
-                act_ref[0, rows, :] = (x * up).astype(jnp.bfloat16)
-                slope_ref[0, rows, :] = up * (1.0 + (1.0 - th) * (x * (K0 + 3.0 * q)))
+                act = x * up
+                act_ref[0, rows, :] = act.astype(jnp.bfloat16)
+                slope_ref[0, rows, :] = up + act * ((1.0 - th) * (K0 + 3.0 * q))
             out = out + jnp.dot(
                 half[:, slab], act_ref[0, slab, :], preferred_element_type=jnp.float32
             )
@@ -136,7 +137,7 @@
         keep_a, send_a, keep_x, send_x, acc, *refs = refs
     else:
         acc, *refs = refs
-    gf, gp, *refs = refs
+    gf, *refs = refs
     step = pl.program_id(0)
     mloc, _, t = hid_ref.shape
     v = target_ref.shape[0]
@@ -206,8 +207,7 @@
         ga = jnp.dot(wot_ref[rows, :], g, preferred_element_type=jnp.float32)
         for m in range(mloc):
             piece = (ga[:, m * t : (m + 1) * t] * slope_ref[m, rows, :]).astype(jnp.bfloat16)
-            gp[rows, pl.ds(m * t, t)] = piece
-            gp_ref[m, rows, :] = piece
+            gp_ref[rows, pl.ds(m * t, t)] = piece
     hid = jnp.concatenate([hid_ref[m] for m in range(mloc)], axis=1)
     act = jnp.concatenate([act_ref[m] for m in range(mloc)], axis=1)
     extra = lax.dot_general(g, act, NT, preferred_element_type=jnp.float32)
@@ -216,7 +216,7 @@
         extra_ref[...] = extra if extra_base is None else extra_base[...] + extra
         for k in range(0, h, SLAB):
             rows = pl.ds(k, SLAB)
-            prod = lax.dot_general(gp[rows, :], hid, NT, preferred_element_type=jnp.float32)
+            prod = lax.dot_general(gp_ref[rows, :], hid, NT, preferred_element_type=jnp.float32)
             acc[rows, :] = prod if base is None else base[rows, :] + prod
 
     @pl.when(step == 0)
@@ -255,7 +255,8 @@
                         r0 = pl.multiple_of((g * 2 + c) * r, r)
                         total = acc[pl.ds(r0, r), :] + earlier[pl.ds(r0, r), :]
                         part_a[dlo, dhi, pl.ds(0, r), :] = total[:, :ca]
-                        e0 = (c * (n_hi * n_lo) + g) * EXTRA_ROWS
+                        e0 = dhi * n_lo + lax.rem(lo + dlo, n_lo)
+                        e0 = (c * (n_hi * n_lo) + e0) * EXTRA_ROWS
                         at = pl.multiple_of(
                             jnp.minimum(e0, extra_ref.shape[0] - EXTRA_ROWS), EXTRA_ROWS
                         )
@@ -297,15 +298,15 @@
         kernel_fn = kernel
         in_specs += [pl.BlockSpec(memory_space=pl.ANY), const(extra)]
         args += [acc, extra]
-    out_specs = [big, pl.BlockSpec((vp, h), whole, pipeline_mode=once)]
+    out_specs = [
+        pl.BlockSpec((h, mloc * t), lambda s: (0, s)),
+        pl.BlockSpec((vp, h), whole, pipeline_mode=once),
+    ]
     out_shape = [
-        jax.ShapeDtypeStruct((mloc, h, p), jnp.bfloat16),
+        jax.ShapeDtypeStruct((h, mloc * p), jnp.bfloat16),
         jax.ShapeDtypeStruct((vp, h), jnp.float32),
     ]
-    scratch = [
-        pltpu.VMEM((mloc, vp, t), jnp.float32),
-        pltpu.VMEM((h, mloc * t), jnp.bfloat16),
-    ]
+    scratch = [pltpu.VMEM((mloc, vp, t), jnp.float32)]
     if not first:
         scratch += [pltpu.VMEM((h, h), jnp.float32), pltpu.SemaphoreType.DMA]
     if last:
@@ -340,18 +341,22 @@
 
 
 def input_kernel(wt_ref, gp_ref, *refs):
-    refs[-1][0] = jnp.dot(wt_ref[...], gp_ref[0], preferred_element_type=jnp.float32).astype(
-        jnp.bfloat16
-    )
+    mloc, h, t = refs[-1].shape
+    for k in range(0, h, SLAB):
+        rows = pl.ds(k, SLAB)
+        out = jnp.dot(wt_ref[rows, :], gp_ref[...], preferred_element_type=jnp.float32)
+        for m in range(mloc):
+            refs[-1][m, rows, :] = out[:, m * t : (m + 1) * t].astype(jnp.bfloat16)
 
 
 def input_gradient(start, p, n, wt, gp, gh):
-    mloc, h, _ = gp.shape
+    h = gp.shape[0]
+    mloc = gp.shape[1] // p
     t = TILE
     off = start // t
     in_specs = [
-        pl.BlockSpec((h, h), lambda m, s: (0, 0), pipeline_mode=pl.Buffered(1)),
-        pl.BlockSpec((1, h, t), lambda m, s: (m, 0, s)),
+        pl.BlockSpec((h, h), lambda s: (0, 0), pipeline_mode=pl.Buffered(1)),
+        pl.BlockSpec((h, mloc * t), lambda s: (0, s)),
     ]
     args = [wt, gp]
     if gh is not None:
@@ -359,18 +364,21 @@
         args.append(gh)
     return pl.pallas_call(
         input_kernel,
-        grid=(mloc, p // t),
+        grid=(p // t,),
         in_specs=in_specs,
-        out_specs=pl.BlockSpec((1, h, t), lambda m, s: (m, 0, off + s)),
+        out_specs=pl.BlockSpec((mloc, h, t), lambda s: (0, 0, off + s)),
         out_shape=jax.ShapeDtypeStruct((mloc, h, n), jnp.bfloat16),
         input_output_aliases={} if gh is None else {2: 0},
         compiler_params=pltpu.CompilerParams(vmem_limit_bytes=VMEM),
         cost_estimate=pl.CostEstimate(
-            flops=2 * mloc * p * h * h, bytes_accessed=mloc * p * h * 4 + 2 * h * h,
-            transcendentals=0,
+            flops=2 * h * h, bytes_accessed=2 * h * h, transcendentals=0
         ),
         name="grad_hidden_part",
     )(*args)
+
+
+def after(value, *others):
+    return lax.optimization_barrier((value,) + others)[0]
 
 
 def shards(hidden, target, area, var_weight, w_inner, b_inner, w_out, b_out):
@@ -407,30 +415,27 @@
         forward(start, p, hidden, w_inner, b_inner.reshape(1, h), w_out, b_out.reshape(1, v))
         for start, p in spans
     ]
-    exchanged = []
-    for act, slope, fields in parts:
-        far = to_x(fields)
-        exchanged.append((fields, to_core(fields), far, to_core(far)))
-
-    w_inner, w_out, _ = lax.optimization_barrier((w_inner, w_out, parts[1][2]))
-    wt = w_inner.T
+    far = [to_x(fields) for _, _, fields in parts]
+    near = [to_core(fields) for _, _, fields in parts]
+    w_out = after(w_out, parts[1][2])
     wot = jnp.pad(w_out * jnp.bfloat16(0.5), ((0, vp - v), (0, 0))).T
     vw, area = var_weight.reshape(1, v), area.reshape(1, n)
     acc = extra = gh = None
     grad_pre = []
     for k, (start, p) in enumerate(spans):
-        act, slope, _ = parts[k]
+        act, slope, fields = parts[k]
         first, last = k == 0, k == len(spans) - 1
+        if k >= 2:
+            far[k] = after(far[k], grad_pre[k - 2])
         gp, extra, *accs = backward(
-            start, p, first, last, (n_hi, n_lo), members, exchanged[k],
+            start, p, first, last, (n_hi, n_lo), members,
+            (fields, near[k], far[k], to_core(far[k])),
             (target, area, vw, act, slope, hidden, wot), acc, extra,
         )
         grad_pre.append(gp)
         acc = accs[0]
     keep_a, send_a, keep_x, send_x = accs
-    wt, _ = lax.optimization_barrier((wt, extra))
-    for (start, p), gp in zip(spans, grad_pre):
-        gh = input_gradient(start, p, n, wt, gp, gh)
+    wt = after(w_inner, extra).T
 
     def gathered(block, axis, name, bit):
         n = lax.axis_size(name)
@@ -441,39 +446,58 @@
             jnp.concatenate([other, block], axis),
         )
 
-    def along_lo(blocks):
-        total = blocks(0)
-        for k in range(1, n_lo):
-            total = total + to_lo(blocks(k), k)
-        return total
-
-    def along_hi(blocks):
-        total = blocks[0]
-        for k in range(1, n_hi):
-            total = total + to_hi(blocks[k], k)
-        return total
-
+    def along_lo(blocks, own):
+        return sum([to_lo(blocks[k], k) for k in range(1, n_lo)], own[0])
+
+    def beside(k, gh, start_after, wait_for):
+        gh = input_gradient(*spans[k], n, wt, after(grad_pre[k], start_after), gh)
+        return lax.optimization_barrier((gh, wait_for))
+
+    r = h // (2 * n_grid)
+    ca, cx = keep_a.shape[-1], keep_x.shape[-1]
+    got_x = to_core(send_x)
     got_a = to_core(send_a)
-    got_x = to_core(send_x)
-    sum_a = along_lo(lambda k: keep_a[k] + got_a[k])
-    own_x = keep_x[0] + got_x[0] + to_x(keep_x[1] + got_x[1])
-    sum_x = along_lo(lambda k: own_x[k])
-    end_a = along_hi(sum_a)
-    end_x = along_hi(sum_x)
-    end_a = end_a + to_x(end_a)
-    r = h // (2 * n_grid)
-    ca = end_a.shape[1]
-    extra = jnp.concatenate(
-        [end_a[r + k : r + k + EXTRA_ROWS] for k in range(0, end_a.shape[0] - r, EXTRA_ROWS)], 1
-    )
+    from_x = to_x(keep_x[1] + got_x[1])
+    here_a = [keep_a[k] + got_a[k] for k in range(n_lo)]
+    sum_a = along_lo(here_a, here_a)
+    gh, keep_x = beside(0, gh, here_a[1], keep_x)
+    own_x = keep_x[0] + got_x[0] + from_x
+    own_x = [own_x[k] for k in range(n_lo)]
+    gh, last_x = beside(2, gh, own_x[1], own_x[0])
+    sum_x = along_lo(own_x, [last_x])
+    pieces = [
+        jnp.concatenate([sum_a[k, :r, c : c + cx] for c in range(0, ca, cx)] + [sum_x[k]], 0)
+        for k in range(n_hi)
+    ]
+    from_hi = [to_hi(pieces[k], k) for k in range(1, n_hi)]
+    gh, own = beside(1, gh, pieces[1], pieces[0])
+
+    extra = sum_a[:, r:]
+    extra = extra + to_x(extra)
+    bit = n_lo
+    while bit < n_grid:
+        extra = extra + lax.ppermute(extra, "grid", [(i, i ^ bit) for i in range(n_grid)])
+        bit *= 2
+
+    total = after(sum(from_hi, own), extra)
+    far = to_x(total)
+    extra = extra[None]
     bit = 1
-    while bit < n_grid:
+    while bit < n_lo:
         extra = gathered(extra, 0, "grid", bit)
         bit *= 2
-    extra = gathered(extra, 0, "mem", 1)
-    end_x = gathered(end_x, 1, "mem", n_mem // 2)
+    extra = gathered(extra[None], 0, "mem", 1)
+    extra = extra.reshape(2, n_lo, n_hi, h // ca, EXTRA_ROWS, ca).transpose(0, 2, 1, 4, 3, 5)
+    extra = extra.reshape(2 * n_grid * EXTRA_ROWS, h)
+
+    done = h // cx // 2 * r
+    both = total[:done] + far[:done]
+    left, right = total[done:], far[done:]
+    x = lax.axis_index("mem") // 2
+    ends = [both[k : k + r] for k in range(0, done, r)]
+    ends += [jnp.where(x == 0, left, right), jnp.where(x == 0, right, left)]
     scale = 1.0 / math.sqrt(members * npoints)
-    grad_inner = gathered(jnp.concatenate([end_a[:r], end_x], 1) * scale, 0, "mem", 1)
+    grad_inner = gathered(jnp.concatenate(ends, 1) * scale, 0, "mem", 1)
     loss = jnp.sum(extra[v]) / npoints
     return (loss, gh, grad_inner, extra[:v] * (0.5 * scale))
 

time: 174 us -> 163 us (0.937); the launches traced: 170 us -> 162 us
  waiting for transfers between devices: 27.5 us -> 21.6 us
  Pallas kernels: 96.4 us -> 93.4 us
    ppermute x5 -> x6, waiting for transfers between devices: 13.9 us -> 1.4 us  [shards(): to_x = lambda a: lax.ppermute(a, 'mem', swap_x)]
    ppermute x0 -> x2, waiting for transfers between devices: none -> 11.4 us  [shards(): lax.ppermute(extra, 'grid', [(i, i ^ bit) for i in range(n_grid)])]
    ppermute x6 -> x3, waiting for transfers between devices: 9.29 us -> 0.01 us  [shards(): to_hi = lambda a, k: lax.ppermute(a, 'grid', shift_hi(k))]
    ppermute x8, waiting for transfers between devices: 0.02 us -> 2.85 us  [shards(): to_core = lambda a: lax.ppermute(a, 'mem', swap_core)]
    pallas_call x3, Pallas kernels: 22.1 us -> 19.6 us  [input_gradient(): pl.pallas_call(input_kernel, grid=(p // t,), in_specs=in_specs, out_specs...]
    ppermute x2, waiting for transfers between devices: 2.73 us -> 4.91 us  [shards(): to_lo = lambda a, k: lax.ppermute(a, 'grid', shift_lo(k))]
    ppermute x6 -> x3, starting transfers between devices: 10.6 us -> 8.68 us  [gathered(): other = lax.ppermute(block, name, [(i, i ^ bit) for i in range(n)])]
    unnamed x24 -> x28, local copies, waits for them, and re-layouts: 2.5 us -> 3.66 us
  transfers between devices with their start and end apart: 27 -> 24, of which waited for: 11 -> 7; matrix products, arithmetic and copies ran while one was open for 6% -> 6% of each run, Pallas kernels for 42% -> 43%
where the time goes in v4:
time: 163 us; the launch traced here: 162 us
  Pallas kernels  93.4 us (57%)
  starting transfers between devices  28.8 us (18%)
  waiting for transfers between devices  21.6 us (13%)
  other arithmetic  8.15 us (5%)
  local copies, waits for them, and re-layouts  7.3 us (4%)
  between operations  2.73 us (2%)
    pallas_call x3, Pallas kernels, backward(): pl.pallas_call(kernel_fn, grid=(p // t,), in_specs=in_specs, out_specs=ou...  41.3 us
    pallas_call x3, Pallas kernels, forward(): pl.pallas_call(functools.partial(forward_kernel, mloc), grid=(tiles + 1,)...  32.6 us
    pallas_call x3, Pallas kernels, input_gradient(): pl.pallas_call(input_kernel, grid=(p // t,), in_specs=in_specs, out_specs...  19.6 us
    ppermute x2, waiting for transfers between devices, shards(): lax.ppermute(extra, 'grid', [(i, i ^ bit) for i in range(n_grid)])  11.4 us
    ppermute x3, starting transfers between devices, gathered(): other = lax.ppermute(block, name, [(i, i ^ bit) for i in range(n)])  8.68 us
    ppermute x6, starting transfers between devices, shards(): to_x = lambda a: lax.ppermute(a, 'mem', swap_x)  6.8 us
    ppermute x8, starting transfers between devices, shards(): to_core = lambda a: lax.ppermute(a, 'mem', swap_core)  5.28 us
    ppermute x3, starting transfers between devices, shards(): to_hi = lambda a, k: lax.ppermute(a, 'grid', shift_hi(k))  5.14 us
  transfers between devices with their start and end apart: 24, of which 7 were waited for; matrix products, arithmetic and copies ran while one was open for 6% of the time, Pallas kernels for 43%

profile of v4, /device:TPU:9, one launch (start us, length us, event | category | flops | bytes accessed | tf_op | source)
XLA Modules:
  0.0 162.0 jit_solution(10514139085065209373)
XLA Ops:
  0.6 11.7 %forward_part.4 = (bf16[2,1024,768]{2,1,0:T(8,128)(2,1)}, f32[2,1024,768]{2,1,0:T(8,128)}, f32[200,768]{1,0:T(8,128)}) custom-call(bf16[2,1024,2048]{2,1,0:T(8,128)(2,1)} %hid_ref.9, bf16[1024,1024]{1,0:T(8,128)(2,1)} %w_ref.5, f32[1,1024]{1,0:T(1,128)} %bitcast.73, bf16[100,1024]{1,0:T(8,128)(2,1)} %wo_ref.5, f32[1,100]{1,0:T(1,128)} %bitcast.76), custom_call_target="tpu_custom_call" | custom-call | flops 3535798272 | bytes 14680064 | tf_op jit(solution)/shard_map/forward_part/pallas_call | solution.py:96
  12.4 1.2 collective-permute-start.3
  13.6 11.7 %forward_part.5 = (bf16[2,1024,768]{2,1,0:T(8,128)(2,1)}, f32[2,1024,768]{2,1,0:T(8,128)}, f32[200,768]{1,0:T(8,128)}) custom-call(bf16[2,1024,2048]{2,1,0:T(8,128)(2,1)} %hid_ref.9, bf16[1024,1024]{1,0:T(8,128)(2,1)} %w_ref.5, f32[1,1024]{1,0:T(1,128)} %bitcast.74, bf16[100,1024]{1,0:T(8,128)(2,1)} %wo_ref.5, f32[1,100]{1,0:T(1,128)} %bitcast.77), custom_call_target="tpu_custom_call" | custom-call | flops 3535798272 | bytes 14680064 | tf_op jit(solution)/shard_map/forward_part/pallas_call | solution.py:96
  25.3 0.3 collective-permute-start.7
  25.6 1.2 collective-permute-start.2
  26.8 0.5 collective-permute-done.3.refs_2_
  27.3 1.8 %collective-permute-start.4 = (f32[200,768]{1,0:T(8,128)S(1)}, f32[200,768]{1,0:T(8,128)}, u32[]{:S(2)}, u32[]{:S(2)}) collective-permute-start(f32[200,768]{1,0:T(8,128)S(1)} %collective-permute-done.3.refs_2_), channel_id=1, source_target_pairs={{0,8},{8,0},{16,24},{24,16},{1,9},{9,1},{17,25},{25,17},{2,10},{10... | collective-permute-start | bytes 1843208 | tf_op jit(solution)/shard_map/ppermute | solution.py:407
  29.1 9.1 %forward_part.3 = (bf16[2,1024,512]{2,1,0:T(8,128)(2,1)}, f32[2,1024,512]{2,1,0:T(8,128)}, f32[200,512]{1,0:T(8,128)}) custom-call(bf16[2,1024,2048]{2,1,0:T(8,128)(2,1)} %hid_ref.9, bf16[1024,1024]{1,0:T(8,128)(2,1)} %w_ref.5, f32[1,1024]{1,0:T(1,128)} %bitcast.75, bf16[100,1024]{1,0:T(8,128)(2,1)} %wo_ref.5, f32[1,100]{1,0:T(1,128)} %bitcast.78), custom_call_target="tpu_custom_call" | custom-call | flops 2357198848 | bytes 10485760 | tf_op jit(solution)/shard_map/forward_part/pallas_call | solution.py:96
  38.3 2.2 %collective-permute-start.1 = (f32[200,512]{1,0:T(8,128)}, f32[200,512]{1,0:T(8,128)}, u32[]{:S(2)}, u32[]{:S(2)}) collective-permute-start(f32[200,512]{1,0:T(8,128)} %get-tuple-element.36.f_ref), channel_id=1, source_target_pairs={{0,16},{8,24},{16,0},{24,8},{1,17},{9,25},{17,1},{25,9},{2,18},{10... | collective-permute-start | bytes 1228808 | tf_op jit(solution)/shard_map/ppermute | solution.py:406
  40.7 1.4 collective-permute-start.8
  42.1 0.8 pad_bitcast_fusion.refs_10_.wot_ref
  42.9 0.7 copy-done.10
  43.7 14.1 %backward_part.3 = (bf16[1024,1536]{1,0:T(8,128)(2,1)}, f32[128,1024]{1,0:T(8,128)}, f32[1024,1024]{1,0:T(8,128)}) custom-call(f32[200,768]{1,0:T(8,128)} %get-tuple-element.37.refs_0_, f32[200,768]{1,0:T(8,128)} %copy-done.10, f32[200,768]{1,0:T(8,128)} %copy-done.9, f32[200,768]{1,0:T(8,128)} %collective-permute-done.4.refs_3_, f32[100,2048]{1,0:T(8,128)} %target_ref.3, ...), custom_call_target="tpu_custom_call" | custom-call | flops 3850371072 | bytes 26214400 | tf_op jit(solution)/shard_map/backward_part/pallas_call | solution.py:327
  58.0 0.8 copy-done.8
  58.8 0.2 copy-done.11
  59.0 15.0 %backward_part.4 = (bf16[1024,1536]{1,0:T(8,128)(2,1)}, f32[128,1024]{1,0:T(8,128)}, f32[1024,1024]{1,0:T(8,128)}) custom-call(f32[200,768]{1,0:T(8,128)} %get-tuple-element.40.f_ref, f32[200,768]{1,0:T(8,128)} %copy-done.8, f32[200,768]{1,0:T(8,128)} %copy-done.6, f32[200,768]{1,0:T(8,128)} %copy-done.11, f32[100,2048]{1,0:T(8,128)} %target_ref.3, ...), custom_call_target="tpu_custom_call" | custom-call | flops 3850371072 | bytes 26214400 | tf_op jit(solution)/shard_map/backward_part/pallas_call | solution.py:327
  74.1 0.7 copy-done.12
  75.0 12.1 %backward_part.5 = (bf16[1024,1024]{1,0:T(8,128)(2,1)}, f32[128,1024]{1,0:T(8,128)}, f32[2,4,80,512]{3,2,1,0:T(8,128)}, f32[2,4,80,512]{3,2,1,0:T(8,128)}, f32[2...) custom-call(f32[200,512]{1,0:T(8,128)} %get-tuple-element.36.f_ref, f32[200,512]{1,0:T(8,128)} %copy-done.12, ...), custom_call_target="tpu_custom_call" | custom-call | flops 2566914048 | bytes 20971520 | tf_op jit(solution)/shard_map/backward_part/pallas_call | solution.py:327
  87.1 0.5 collective-permute-start.16
  87.7 2.8 %collective-permute-done.16 = f32[2,2,4,64,256]{4,3,2,1,0:T(8,128)S(1)} collective-permute-done((f32[2,2,4,64,256]{4,3,2,1,0:T(8,128)}, f32[2,2,4,64,256]{4,3,2,1,0:T(8,128)S(1)}, u32[]{:S(2)}, u32[]{:S(2)}) %collective-permute-start.16) | collective-permute-done | bytes 1048608 | tf_op jit(solution)/shard_map/ppermute | solution.py:407
  90.5 1.0 copy-done.3
  91.5 1.9 %fusion.3 = f32[2,4,64,256]{3,2,1,0:T(8,128)} fusion(f32[2,2,4,64,256]{4,3,2,1,0:T(8,128)S(1)} %collective-permute-done.16, f32[2,2,4,64,256]{4,3,2,1,0:T(8,128)} %get-tuple-element.58), kind=kLoop, calls=%fused_computation.6 | loop fusion | flops 131072 | bytes 1572864 | tf_op jit(solution)/shard_map/add | solution.py:460
  93.4 1.2 collective-permute-start.17
  94.6 2.6 %copy.20 = bf16[1024,1024]{0,1:T(8,128)(2,1)} copy(bf16[1024,1024]{1,0:T(8,128)(2,1)S(1)} %copy-done) | data formatting | bytes 4194304 | tf_op jit(solution)/shard_map/optimization_barrier | solution.py:381
  97.2 1.2 fusion
  98.4 1.3 collective-permute-start.10
  99.7 7.1 %grad_hidden_part.3.refs_0_ = bf16[2,1024,2048]{2,1,0:T(8,128)(2,1)} custom-call(bf16[1024,1024]{1,0:T(8,128)(2,1)} %bitcast.56, bf16[1024,1536]{1,0:T(8,128)(2,1)} %get-tuple-element.56.gp_ref), custom_call_target="tpu_custom_call" | custom-call | flops 2097152 | bytes 2097152 | tf_op jit(solution)/shard_map/grad_hidden_part/pallas_call | solution.py:365
  106.9 1.1 fusion.5
  108.1 1.3 collective-permute-start.18
  109.4 5.4 %grad_hidden_part.4.refs_0_ = bf16[2,1024,2048]{2,1,0:T(8,128)(2,1)} custom-call(bf16[1024,1024]{1,0:T(8,128)(2,1)} %bitcast.57, bf16[1024,1024]{1,0:T(8,128)(2,1)} %get-tuple-element.60.gp_ref, bf16[2,1024,2048]{2,1,0:T(8,128)(2,1)} %grad_hidden_part.3.refs_0_), custom_call_target="tpu_custom_call", output_to_operand_aliasing={{}: (2, {})} | custom-call | flops 2097152 | bytes 2097152 | tf_op jit(solution)/shard_map/grad_hidden_part/pallas_call | solution.py:365
  114.8 4.9 %collective-permute-done.18 = f32[4,64,256]{2,1,0:T(8,128)S(1)} collective-permute-done((f32[4,64,256]{2,1,0:T(8,128)S(1)}, f32[4,64,256]{2,1,0:T(8,128)S(1)}, u32[]{:S(2)}, u32[]{:S(2)}) %collective-permute-start.18) | collective-permute-done | bytes 262176 | tf_op jit(solution)/shard_map/ppermute | solution.py:408
  119.8 1.3 fusion.2
  121.1 0.3 collective-permute-start.11
  121.4 2.5 %collective-permute-start.20 = (f32[192,256]{1,0:T(8,128)S(1)}, f32[192,256]{1,0:T(8,128)S(1)}, u32[]{:S(2)}, u32[]{:S(2)}) collective-permute-start(f32[192,256]{1,0:T(8,128)S(1)} %pad_maximum_fusion.2), channel_id=1, source_target_pairs={{0,4},{1,5},{2,6},{3,7},{4,0},{5,1},{6,2},{7,3},{8,12},{9,13},{10,... | collective-permute-start | bytes 589832 | tf_op jit(solution)/shard_map/ppermute | solution.py:409
  124.1 0.8 collective-permute-done.11
  125.0 0.3 collective-permute-start.12
  125.3 2.5 %collective-permute-start.19 = (f32[192,256]{1,0:T(8,128)S(1)}, f32[192,256]{1,0:T(8,128)S(1)}, u32[]{:S(2)}, u32[]{:S(2)}) collective-permute-start(f32[192,256]{1,0:T(8,128)S(1)} %pad_maximum_fusion), channel_id=1, source_target_pairs={{0,2},{1,3},{2,4},{3,5},{4,6},{5,7},{6,0},{7,1},{8,10},{9,11},{10,... | collective-permute-start | bytes 589832 | tf_op jit(solution)/shard_map/ppermute | solution.py:409
  127.7 6.6 %collective-permute-done.12 = f32[4,16,512]{2,1,0:T(8,128)S(1)} collective-permute-done((f32[4,16,512]{2,1,0:T(8,128)S(1)}, f32[4,16,512]{2,1,0:T(8,128)S(1)}, u32[]{:S(2)}, u32[]{:S(2)}) %collective-permute-start.12) | collective-permute-done | bytes 131104 | tf_op jit(solution)/shard_map/ppermute | solution.py:479
  134.4 7.0 %grad_hidden_part.5 = bf16[2,1024,2048]{2,1,0:T(8,128)(2,1)} custom-call(bf16[1024,1024]{1,0:T(8,128)(2,1)} %bitcast.58, bf16[1024,1536]{1,0:T(8,128)(2,1)} %get-tuple-element.63.gp_ref, bf16[2,1024,2048]{2,1,0:T(8,128)(2,1)} %grad_hidden_part.4.refs_0_), custom_call_target="tpu_custom_call", output_to_operand_aliasing={{}: (2, {})} | custom-call | flops 2097152 | bytes 2097152 | tf_op jit(solution)/shard_map/grad_hidden_part/pallas_call | solution.py:365
  141.5 4.8 %collective-permute-done.13 = f32[4,16,512]{2,1,0:T(8,128)S(1)} collective-permute-done((f32[4,16,512]{2,1,0:T(8,128)S(1)}, f32[4,16,512]{2,1,0:T(8,128)S(1)}, u32[]{:S(2)}, u32[]{:S(2)}) %collective-permute-start.13) | collective-permute-done | bytes 131104 | tf_op jit(solution)/shard_map/ppermute | solution.py:479
  146.3 1.2 collective-permute-start.14
  147.6 1.6 collective-permute-start.22
  149.2 1.0 collective-permute-done.14
  150.2 5.3 %collective-permute-start.15 = (f32[1,2,4,16,512]{4,3,2,1,0:T(8,128)S(1)}, f32[1,2,4,16,512]{4,3,2,1,0:T(8,128)S(1)}, u32[]{:S(2)}, u32[]{:S(2)}) collective-permute-start(f32[1,2,4,16,512]{4,3,2,1,0:T(8,128)S(1)} %maximum_select_fusion.3), channel_id=1, source_target_pairs={{0,8},{8,0},{16,24},{24,16},{1,9},{9,1},{17,25},{25,17},{2,10},{10... | collective-permute-start | bytes 786440 | tf_op jit(solution)/shard_map/ppermute | solution.py:442
  155.6 2.3 %collective-permute-start.23 = (f32[64,1024]{1,0:T(8,128)S(1)}, f32[64,1024]{1,0:T(8,128)S(1)}, u32[]{:S(2)}, u32[]{:S(2)}) collective-permute-start(f32[64,1024]{1,0:T(8,128)S(1)} %maximum_multiply_fusion), channel_id=1, source_target_pairs={{0,8},{8,0},{16,24},{24,16},{1,9},{9,1},{17,25},{25,17},{2,10},{10... | collective-permute-start | bytes 786440 | tf_op jit(solution)/shard_map/ppermute | solution.py:442
  158.0 0.6 slice_reduce_fusion
  159.2 0.8 slice_multiply_fusion
  160.0 0.8 maximum_select_fusion.1
  (69 shorter events, 1.6 us)
Async XLA Ops:
  12.4 13.2 %copy-start.7 = (f32[200,768]{1,0:T(8,128)S(1)}, f32[200,768]{1,0:T(8,128)}, u32[]{:S(2)}) copy-start(f32[200,768]{1,0:T(8,128)} %get-tuple-element.37.refs_0_) | copy-start | bytes 1843204
  12.4 15.0 %collective-permute-start.3 = (f32[200,768]{1,0:T(8,128)}, f32[200,768]{1,0:T(8,128)S(1)}, u32[]{:S(2)}, u32[]{:S(2)}) collective-permute-start(f32[200,768]{1,0:T(8,128)} %get-tuple-element.37.refs_0_), channel_id=1, source_target_pairs={{0,16},{8,24},{16,0},{24,8},{1,17},{9,25},{17,1},{25,9},{2,18},{10... | collective-permute-start | bytes 1843208 | tf_op jit(solution)/shard_map/ppermute | solution.py:406
  25.3 15.1 %copy-start.5 = (bf16[100,1024]{1,0:T(8,128)(2,1)S(1)}, bf16[100,1024]{1,0:T(8,128)(2,1)}, u32[]{:S(2)}) copy-start(bf16[100,1024]{1,0:T(8,128)(2,1)} %wo_ref.5) | copy-start | bytes 614404
  25.3 15.3 %collective-permute-start.7 = (f32[200,768]{1,0:T(8,128)}, f32[200,768]{1,0:T(8,128)S(1)}, u32[]{:S(2)}, u32[]{:S(2)}) collective-permute-start(f32[200,768]{1,0:T(8,128)} %get-tuple-element.40.f_ref), channel_id=1, source_target_pairs={{0,16},{8,24},{16,0},{24,8},{1,17},{9,25},{17,1},{25,9},{2,18},{10... | collective-permute-start | bytes 1843208 | tf_op jit(solution)/shard_map/ppermute | solution.py:406
  25.6 17.3 %collective-permute-start.2 = (f32[200,768]{1,0:T(8,128)S(1)}, f32[200,768]{1,0:T(8,128)S(1)}, u32[]{:S(2)}, u32[]{:S(2)}) collective-permute-start(f32[200,768]{1,0:T(8,128)S(1)} %copy-done.7), channel_id=1, source_target_pairs={{0,8},{8,0},{16,24},{24,16},{1,9},{9,1},{17,25},{25,17},{2,10},{10... | collective-permute-start | bytes 1843208 | tf_op jit(solution)/shard_map/ppermute | solution.py:407
  27.3 11.0 %copy-start.9 = (f32[200,768]{1,0:T(8,128)}, f32[200,768]{1,0:T(8,128)S(1)}, u32[]{:S(2)}) copy-start(f32[200,768]{1,0:T(8,128)S(1)} %collective-permute-done.3.refs_2_) | copy-start | bytes 1843204
  27.3 15.6 %collective-permute-start.4 = (f32[200,768]{1,0:T(8,128)S(1)}, f32[200,768]{1,0:T(8,128)}, u32[]{:S(2)}, u32[]{:S(2)}) collective-permute-start(f32[200,768]{1,0:T(8,128)S(1)} %collective-permute-done.3.refs_2_), channel_id=1, source_target_pairs={{0,8},{8,0},{16,24},{24,16},{1,9},{9,1},{17,25},{25,17},{2,10},{10... | collective-permute-start | bytes 1843208 | tf_op jit(solution)/shard_map/ppermute | solution.py:407
  29.1 28.8 %collective-permute-start.6 = (f32[200,768]{1,0:T(8,128)}, f32[200,768]{1,0:T(8,128)S(1)}, u32[]{:S(2)}, u32[]{:S(2)}) collective-permute-start(f32[200,768]{1,0:T(8,128)} %get-tuple-element.40.f_ref), channel_id=1, source_target_pairs={{0,8},{8,0},{16,24},{24,16},{1,9},{9,1},{17,25},{25,17},{2,10},{10... | collective-permute-start | bytes 1843208 | tf_op jit(solution)/shard_map/ppermute | solution.py:407
  38.3 19.5 %collective-permute-start.1 = (f32[200,512]{1,0:T(8,128)}, f32[200,512]{1,0:T(8,128)}, u32[]{:S(2)}, u32[]{:S(2)}) collective-permute-start(f32[200,512]{1,0:T(8,128)} %get-tuple-element.36.f_ref), channel_id=1, source_target_pairs={{0,16},{8,24},{16,0},{24,8},{1,17},{9,25},{17,1},{25,9},{2,18},{10... | collective-permute-start | bytes 1228808 | tf_op jit(solution)/shard_map/ppermute | solution.py:406
  40.6 17.1 %copy-start.6 = (f32[200,768]{1,0:T(8,128)}, f32[200,768]{1,0:T(8,128)S(1)}, u32[]{:S(2)}) copy-start(f32[200,768]{1,0:T(8,128)S(1)} %collective-permute-done.7.fx_ref) | copy-start | bytes 1843204
  40.7 17.3 %collective-permute-start.8 = (f32[200,768]{1,0:T(8,128)S(1)}, f32[200,768]{1,0:T(8,128)S(1)}, u32[]{:S(2)}, u32[]{:S(2)}) collective-permute-start(f32[200,768]{1,0:T(8,128)S(1)} %collective-permute-done.7.fx_ref), channel_id=1, source_target_pairs={{0,8},{8,0},{16,24},{24,16},{1,9},{9,1},{17,25},{25,17},{2,10},{10... | collective-permute-start | bytes 1843208 | tf_op jit(solution)/shard_map/ppermute | solution.py:407
  42.8 0.8 copy-start.10
  42.8 31.2 %collective-permute-start = (f32[200,512]{1,0:T(8,128)}, f32[200,512]{1,0:T(8,128)S(1)}, u32[]{:S(2)}, u32[]{:S(2)}) collective-permute-start(f32[200,512]{1,0:T(8,128)} %get-tuple-element.36.f_ref), channel_id=1, source_target_pairs={{0,8},{8,0},{16,24},{24,16},{1,9},{9,1},{17,25},{25,17},{2,10},{10... | collective-permute-start | bytes 1228808 | tf_op jit(solution)/shard_map/ppermute | solution.py:407
  57.8 16.3 %collective-permute-start.5 = (f32[200,512]{1,0:T(8,128)}, f32[200,512]{1,0:T(8,128)S(1)}, u32[]{:S(2)}, u32[]{:S(2)}) collective-permute-start(f32[200,512]{1,0:T(8,128)} %collective-permute-done.1.fx_ref), channel_id=1, source_target_pairs={{0,8},{8,0},{16,24},{24,16},{1,9},{9,1},{17,25},{25,17},{2,10},{10... | collective-permute-start | bytes 1228808 | tf_op jit(solution)/shard_map/ppermute | solution.py:407
  58.0 0.8 copy-start.8
  58.0 1.0 copy-start.11
  74.1 0.8 copy-start.12
  74.1 0.9 copy-start.13
  75.0 19.6 %copy-start = (bf16[1024,1024]{1,0:T(8,128)(2,1)S(1)}, bf16[1024,1024]{1,0:T(8,128)(2,1)}, u32[]{:S(2)}) copy-start(bf16[1024,1024]{1,0:T(8,128)(2,1)} %w_ref.5) | copy-start | bytes 6291460
  87.1 10.1 %copy-start.1 = (f32[2,4,80,512]{3,2,1,0:T(8,128)S(1)}, f32[2,4,80,512]{3,2,1,0:T(8,128)}, u32[]{:S(2)}) copy-start(f32[2,4,80,512]{3,2,1,0:T(8,128)} %get-tuple-element.52) | copy-start | bytes 3932164
  87.1 3.4 %collective-permute-start.16 = (f32[2,2,4,64,256]{4,3,2,1,0:T(8,128)}, f32[2,2,4,64,256]{4,3,2,1,0:T(8,128)S(1)}, u32[]{:S(2)}, u32[]{:S(2)}) collective-permute-start(f32[2,2,4,64,256]{4,3,2,1,0:T(8,128)} %get-tuple-element.59), channel_id=1, source_target_pairs={{0,8},{8,0},{16,24},{24,16},{1,9},{9,1},{17,25},{25,17},{2,10},{10... | collective-permute-start | bytes 3145736 | tf_op jit(solution)/shard_map/ppermute | solution.py:407
  87.6 9.6 %collective-permute-start.9 = (f32[2,4,80,512]{3,2,1,0:T(8,128)}, f32[2,4,80,512]{3,2,1,0:T(8,128)}, u32[]{:S(2)}, u32[]{:S(2)}) collective-permute-start(f32[2,4,80,512]{3,2,1,0:T(8,128)} %get-tuple-element.53), channel_id=1, source_target_pairs={{0,8},{8,0},{16,24},{24,16},{1,9},{9,1},{17,25},{25,17},{2,10},{10... | collective-permute-start | bytes 3932168 | tf_op jit(solution)/shard_map/ppermute | solution.py:407
  90.5 1.0 copy-start.3
  93.4 13.5 %collective-permute-start.17 = (f32[2,4,64,256]{3,2,1,0:T(8,128)}, f32[2,4,64,256]{3,2,1,0:T(8,128)}, u32[]{:S(2)}, u32[]{:S(2)}) collective-permute-start(f32[2,4,64,256]{3,2,1,0:T(8,128)} %fusion.3), channel_id=1, source_target_pairs={{0,16},{8,24},{16,0},{24,8},{1,17},{9,25},{17,1},{25,9},{2,18},{10... | collective-permute-start | bytes 1572872 | tf_op jit(solution)/shard_map/ppermute | solution.py:406
  98.4 21.4 %collective-permute-start.10 = (f32[4,80,512]{2,1,0:T(8,128)S(1)}, f32[4,80,512]{2,1,0:T(8,128)S(1)}, u32[]{:S(2)}, u32[]{:S(2)}) collective-permute-start(f32[4,80,512]{2,1,0:T(8,128)S(1)} %fusion), channel_id=1, source_target_pairs={{0,1},{1,0},{2,3},{3,2},{4,5},{5,4},{6,7},{7,6},{8,9},{9,8},{10,11... | collective-permute-start | bytes 1966088 | tf_op jit(solution)/shard_map/ppermute | solution.py:408
  99.7 7.2 %copy-start.2 = (f32[2,2,4,64,256]{4,3,2,1,0:T(8,128)S(1)}, f32[2,2,4,64,256]{4,3,2,1,0:T(8,128)}, u32[]{:S(2)}) copy-start(f32[2,2,4,64,256]{4,3,2,1,0:T(8,128)} %get-tuple-element.58) | copy-start | bytes 3145732
  99.7 7.2 %copy-start.4 = (f32[2,2,4,64,256]{4,3,2,1,0:T(8,128)S(1)}, f32[2,2,4,64,256]{4,3,2,1,0:T(8,128)}, u32[]{:S(2)}) copy-start(f32[2,2,4,64,256]{4,3,2,1,0:T(8,128)} %copy-done.3) | copy-start | bytes 3145732
  108.1 11.6 %collective-permute-start.18 = (f32[4,64,256]{2,1,0:T(8,128)S(1)}, f32[4,64,256]{2,1,0:T(8,128)S(1)}, u32[]{:S(2)}, u32[]{:S(2)}) collective-permute-start(f32[4,64,256]{2,1,0:T(8,128)S(1)} %get-tuple-element.77), channel_id=1, source_target_pairs={{0,1},{1,0},{2,3},{3,2},{4,5},{5,4},{6,7},{7,6},{8,9},{9,8},{10,11... | collective-permute-start | bytes 786440 | tf_op jit(solution)/shard_map/ppermute | solution.py:408
  121.1 3.9 %collective-permute-start.11 = (f32[4,16,512]{2,1,0:T(8,128)S(1)}, f32[4,16,512]{2,1,0:T(8,128)S(1)}, u32[]{:S(2)}, u32[]{:S(2)}) collective-permute-start(f32[4,16,512]{2,1,0:T(8,128)S(1)} %slice.126), channel_id=1, source_target_pairs={{0,16},{8,24},{16,0},{24,8},{1,17},{9,25},{17,1},{25,9},{2,18},{10... | collective-permute-start | bytes 393224 | tf_op jit(solution)/shard_map/ppermute | solution.py:406
  121.4 26.0 %collective-permute-start.20 = (f32[192,256]{1,0:T(8,128)S(1)}, f32[192,256]{1,0:T(8,128)S(1)}, u32[]{:S(2)}, u32[]{:S(2)}) collective-permute-start(f32[192,256]{1,0:T(8,128)S(1)} %pad_maximum_fusion.2), channel_id=1, source_target_pairs={{0,4},{1,5},{2,6},{3,7},{4,0},{5,1},{6,2},{7,3},{8,12},{9,13},{10,... | collective-permute-start | bytes 589832 | tf_op jit(solution)/shard_map/ppermute | solution.py:409
  123.9 23.6 %collective-permute-start.21 = (f32[192,256]{1,0:T(8,128)S(1)}, f32[192,256]{1,0:T(8,128)S(1)}, u32[]{:S(2)}, u32[]{:S(2)}) collective-permute-start(f32[192,256]{1,0:T(8,128)S(1)} %pad_maximum_fusion.3), channel_id=1, source_target_pairs={{0,6},{1,7},{2,0},{3,1},{4,2},{5,3},{6,4},{7,5},{8,14},{9,15},{10,... | collective-permute-start | bytes 589832 | tf_op jit(solution)/shard_map/ppermute | solution.py:409
  125.0 9.3 %collective-permute-start.12 = (f32[4,16,512]{2,1,0:T(8,128)S(1)}, f32[4,16,512]{2,1,0:T(8,128)S(1)}, u32[]{:S(2)}, u32[]{:S(2)}) collective-permute-start(f32[4,16,512]{2,1,0:T(8,128)S(1)} %slice_add_fusion.5), channel_id=1, source_target_pairs={{0,2},{1,3},{2,0},{3,1},{4,6},{5,7},{6,4},{7,5},{8,10},{9,11},{10,... | collective-permute-start | bytes 393224 | tf_op jit(solution)/shard_map/ppermute | solution.py:479
  125.3 22.2 %collective-permute-start.19 = (f32[192,256]{1,0:T(8,128)S(1)}, f32[192,256]{1,0:T(8,128)S(1)}, u32[]{:S(2)}, u32[]{:S(2)}) collective-permute-start(f32[192,256]{1,0:T(8,128)S(1)} %pad_maximum_fusion), channel_id=1, source_target_pairs={{0,2},{1,3},{2,4},{3,5},{4,6},{5,7},{6,0},{7,1},{8,10},{9,11},{10,... | collective-permute-start | bytes 589832 | tf_op jit(solution)/shard_map/ppermute | solution.py:409
  134.3 12.0 %collective-permute-start.13 = (f32[4,16,512]{2,1,0:T(8,128)S(1)}, f32[4,16,512]{2,1,0:T(8,128)S(1)}, u32[]{:S(2)}, u32[]{:S(2)}) collective-permute-start(f32[4,16,512]{2,1,0:T(8,128)S(1)} %add.63), channel_id=1, source_target_pairs={{0,4},{1,5},{2,6},{3,7},{4,0},{5,1},{6,2},{7,3},{8,12},{9,13},{10,... | collective-permute-start | bytes 393224 | tf_op jit(solution)/shard_map/ppermute | solution.py:479
  146.3 3.9 %collective-permute-start.14 = (f32[1,4,16,512]{3,2,1,0:T(8,128)S(1)}, f32[1,4,16,512]{3,2,1,0:T(8,128)S(1)}, u32[]{:S(2)}, u32[]{:S(2)}) collective-permute-start(f32[1,4,16,512]{3,2,1,0:T(8,128)S(1)} %bitcast.61), channel_id=1, source_target_pairs={{0,1},{1,0},{2,3},{3,2},{4,5},{5,4},{6,7},{7,6},{8,9},{9,8},{10,11... | collective-permute-start | bytes 393224 | tf_op jit(solution)/shard_map/ppermute | solution.py:442
  147.6 8.0 %collective-permute-start.22 = (f32[192,256]{1,0:T(8,128)S(1)}, f32[192,256]{1,0:T(8,128)S(1)}, u32[]{:S(2)}, u32[]{:S(2)}) collective-permute-start(f32[192,256]{1,0:T(8,128)S(1)} %add_add_fusion), channel_id=1, source_target_pairs={{0,16},{8,24},{16,0},{24,8},{1,17},{9,25},{17,1},{25,9},{2,18},{10... | collective-permute-start | bytes 589832 | tf_op jit(solution)/shard_map/ppermute | solution.py:406
  150.2 7.7 %collective-permute-start.15 = (f32[1,2,4,16,512]{4,3,2,1,0:T(8,128)S(1)}, f32[1,2,4,16,512]{4,3,2,1,0:T(8,128)S(1)}, u32[]{:S(2)}, u32[]{:S(2)}) collective-permute-start(f32[1,2,4,16,512]{4,3,2,1,0:T(8,128)S(1)} %maximum_select_fusion.3), channel_id=1, source_target_pairs={{0,8},{8,0},{16,24},{24,16},{1,9},{9,1},{17,25},{25,17},{2,10},{10... | collective-permute-start | bytes 786440 | tf_op jit(solution)/shard_map/ppermute | solution.py:442
  155.6 4.4 %collective-permute-start.23 = (f32[64,1024]{1,0:T(8,128)S(1)}, f32[64,1024]{1,0:T(8,128)S(1)}, u32[]{:S(2)}, u32[]{:S(2)}) collective-permute-start(f32[64,1024]{1,0:T(8,128)S(1)} %maximum_multiply_fusion), channel_id=1, source_target_pairs={{0,8},{8,0},{16,24},{24,16},{1,9},{9,1},{17,25},{25,17},{2,10},{10... | collective-permute-start | bytes 786440 | tf_op jit(solution)/shard_map/ppermute | solution.py:442

commit v5 on v4

--- a/solution.py
+++ b/solution.py
@@ -15,7 +15,7 @@
 K1 = K0 * 0.044715
 SLAB = 512
 EXTRA_ROWS = 8
-VMEM = 58 * 1024 * 1024
+VMEM = 8 * 1024 * 1024
 NT = (((1,), (1,)), ((), ()))
 
 
@@ -43,6 +43,8 @@
             )
 
         half[...] = wo_ref[...] * jnp.bfloat16(0.5)
+
+    tile = lax.max(step - 1, 0) // mloc
 
     def both(m, fill, drain):
         h, t = fill.shape
@@ -59,10 +61,10 @@
                 th = jnp.tanh(x * (K0 + q))
                 up = 1.0 + th
                 act = x * up
-                act_ref[0, rows, :] = act.astype(jnp.bfloat16)
-                slope_ref[0, rows, :] = up + act * ((1.0 - th) * (K0 + 3.0 * q))
+                act_ref[tile, m, rows, :] = act.astype(jnp.bfloat16)
+                slope_ref[tile, m, rows, :] = up + act * ((1.0 - th) * (K0 + 3.0 * q))
             out = out + jnp.dot(
-                half[:, slab], act_ref[0, slab, :], preferred_element_type=jnp.float32
+                half[:, slab], act_ref[tile, m, slab, :], preferred_element_type=jnp.float32
             )
         for r0 in range(0, out.shape[0], 8):
             f_ref[field_rows(out.shape[0], mloc, m, r0), :] = out[r0 : r0 + 8]
@@ -89,10 +91,8 @@
         s = jnp.minimum(s, tiles - 1)
         return (s % mloc, 0, start // t + s // mloc)
 
-    def behind(s):
-        s = jnp.maximum(s - 1, 0)
-        return (s % mloc, 0, s // mloc)
-
+    shape = (p // t, mloc, h, t)
+    held = pl.BlockSpec(shape, lambda s: (0, 0, 0, 0))
     return pl.pallas_call(
         functools.partial(forward_kernel, mloc),
         grid=(tiles + 1,),
@@ -104,13 +104,13 @@
             pl.BlockSpec((1, v), whole, pipeline_mode=once),
         ],
         out_specs=[
-            pl.BlockSpec((1, h, t), behind),
-            pl.BlockSpec((1, h, t), behind),
-            pl.BlockSpec((mloc * v, t), lambda s: (0, behind(s)[2])),
+            held,
+            held,
+            pl.BlockSpec((mloc * v, t), lambda s: (0, jnp.maximum(s - 1, 0) // mloc)),
         ],
         out_shape=[
-            jax.ShapeDtypeStruct((mloc, h, p), jnp.bfloat16),
-            jax.ShapeDtypeStruct((mloc, h, p), jnp.float32),
+            pltpu.VMEM(shape, jnp.bfloat16),
+            pltpu.VMEM(shape, jnp.float32),
             jax.ShapeDtypeStruct((mloc * v, p), jnp.float32),
         ],
         scratch_shapes=[
@@ -133,24 +133,14 @@
     f_ref, fc_ref, fx_ref, fxc_ref, target_ref, area_ref, vw_ref, act_ref, slope_ref, hid_ref,
     wot_ref, acc_in, extra_in, gp_ref, extra_ref, *refs,
 ):
+    acc, *refs = refs
     if last:
-        keep_a, send_a, keep_x, send_x, acc, *refs = refs
-    else:
-        acc, *refs = refs
-    gf, *refs = refs
+        keep_a, send_a, keep_x, send_x, *refs = refs
+    (gf,) = refs
     step = pl.program_id(0)
     mloc, _, t = hid_ref.shape
     v = target_ref.shape[0]
     h = wot_ref.shape[0]
-    final = step == pl.num_programs(0) - 1
-    if not first:
-        earlier, sem = refs
-        fetch = pltpu.make_async_copy(acc_in, earlier, sem)
-
-        @pl.when(step == 0)
-        def _():
-            fetch.start()
-
     denom = members * (members - 1)
     vw = column(vw_ref[...], v)
     area = area_ref[...]
@@ -206,40 +196,32 @@
         rows = pl.ds(k, 256)
         ga = jnp.dot(wot_ref[rows, :], g, preferred_element_type=jnp.float32)
         for m in range(mloc):
-            piece = (ga[:, m * t : (m + 1) * t] * slope_ref[m, rows, :]).astype(jnp.bfloat16)
-            gp_ref[rows, pl.ds(m * t, t)] = piece
+            piece = (ga[:, m * t : (m + 1) * t] * slope_ref[step, m, rows, :]).astype(jnp.bfloat16)
+            gp_ref[step, rows, pl.ds(m * t, t)] = piece
     hid = jnp.concatenate([hid_ref[m] for m in range(mloc)], axis=1)
-    act = jnp.concatenate([act_ref[m] for m in range(mloc)], axis=1)
+    act = jnp.concatenate([act_ref[step, m] for m in range(mloc)], axis=1)
     extra = lax.dot_general(g, act, NT, preferred_element_type=jnp.float32)
 
     def accumulate(base, extra_base):
         extra_ref[...] = extra if extra_base is None else extra_base[...] + extra
         for k in range(0, h, SLAB):
             rows = pl.ds(k, SLAB)
-            prod = lax.dot_general(gp_ref[rows, :], hid, NT, preferred_element_type=jnp.float32)
+            prod = lax.dot_general(gp_ref[step, rows, :], hid, NT, preferred_element_type=jnp.float32)
             acc[rows, :] = prod if base is None else base[rows, :] + prod
 
     @pl.when(step == 0)
     def _():
-        accumulate(None, extra_in)
+        accumulate(acc_in, extra_in)
 
     @pl.when(step > 0)
     def _():
         accumulate(acc, extra_ref)
 
     extra_ref[pl.ds(v, 1), pl.ds(0, t)] += loss
-    if not first:
-
-        @pl.when(final)
-        def _():
-            fetch.wait()
-            if not last:
-                acc[...] += earlier[...]
-
     if last:
         n_hi, n_lo = dims
 
-        @pl.when(final)
+        @pl.when(step == pl.num_programs(0) - 1)
         def _():
             mem = lax.axis_index("mem")
             grid = lax.axis_index("grid")
@@ -253,7 +235,7 @@
                     g = lax.rem(hi + dhi, n_hi) * n_lo + lax.rem(lo + dlo, n_lo)
                     for c, part_a, part_x in ((core, keep_a, keep_x), (1 - core, send_a, send_x)):
                         r0 = pl.multiple_of((g * 2 + c) * r, r)
-                        total = acc[pl.ds(r0, r), :] + earlier[pl.ds(r0, r), :]
+                        total = acc[pl.ds(r0, r), :]
                         part_a[dlo, dhi, pl.ds(0, r), :] = total[:, :ca]
                         e0 = dhi * n_lo + lax.rem(lo + dlo, n_lo)
                         e0 = (c * (n_hi * n_lo) + e0) * EXTRA_ROWS
@@ -280,57 +262,49 @@
     off = start // t
     once = pl.Buffered(1)
     f_spec = pl.BlockSpec((mloc * v, t), lambda s: (0, s))
-    big = pl.BlockSpec((mloc, h, t), lambda s: (0, 0, s))
     whole = lambda s: (0, 0)
     const = lambda a: pl.BlockSpec(a.shape, whole, pipeline_mode=once)
+    held = lambda a: pl.BlockSpec(a.shape, lambda s: (0,) * len(a.shape))
     in_specs = [f_spec] * 4 + [
         pl.BlockSpec((v, t), lambda s: (0, off + s)),
         pl.BlockSpec((1, t), lambda s: (0, off + s)),
-        const(vw), big, big,
+        const(vw), held(act), held(slope),
         pl.BlockSpec((mloc, h, t), lambda s: (0, 0, off + s)),
         const(wot),
     ]
+    act, slope = (pltpu.with_memory_space_constraint(a, pltpu.VMEM) for a in (act, slope))
     args = [*fields, target, area, vw, act, slope, hidden, wot]
     kernel = functools.partial(backward_kernel, first, last, dims, members)
     if first:
         kernel_fn = lambda *refs: kernel(*refs[:11], None, None, *refs[11:])
+        aliases = {}
     else:
         kernel_fn = kernel
-        in_specs += [pl.BlockSpec(memory_space=pl.ANY), const(extra)]
+        in_specs += [held(acc), const(extra)]
         args += [acc, extra]
-    out_specs = [
-        pl.BlockSpec((h, mloc * t), lambda s: (0, s)),
-        pl.BlockSpec((vp, h), whole, pipeline_mode=once),
+        aliases = {11: 2}
+    out_shape = [
+        pltpu.VMEM((p // t, h, mloc * t), jnp.bfloat16),
+        jax.ShapeDtypeStruct((vp, h), jnp.float32),
+        pltpu.VMEM((h, h), jnp.float32),
     ]
-    out_shape = [
-        jax.ShapeDtypeStruct((h, mloc * p), jnp.bfloat16),
-        jax.ShapeDtypeStruct((vp, h), jnp.float32),
-    ]
-    scratch = [pltpu.VMEM((mloc, vp, t), jnp.float32)]
-    if not first:
-        scratch += [pltpu.VMEM((h, h), jnp.float32), pltpu.SemaphoreType.DMA]
     if last:
         n_hi, n_lo = dims
         r = h // (2 * n_hi * n_lo)
         ca = h // 2
         cx = (h - ca) // 2
         ra = r + h // ca * EXTRA_ROWS
-        for shape in ((n_lo, n_hi, ra, ca), (n_lo, n_hi, ra, ca), (2, n_lo, n_hi, r, cx), (2, n_lo, n_hi, r, cx)):
-            out_specs.append(
-                pl.BlockSpec(shape, lambda s, k=len(shape): (0,) * k, pipeline_mode=once)
-            )
-            out_shape.append(jax.ShapeDtypeStruct(shape, jnp.float32))
-        scratch = [pltpu.VMEM((h, h), jnp.float32)] + scratch
-    else:
-        out_specs.append(pl.BlockSpec((h, h), whole, pipeline_mode=once))
-        out_shape.append(jax.ShapeDtypeStruct((h, h), jnp.float32))
+        out_shape += [pltpu.VMEM((n_lo, n_hi, ra, ca), jnp.float32)] * 2
+        out_shape += [pltpu.VMEM((2, n_lo, n_hi, r, cx), jnp.float32)] * 2
+    out_specs = [held(a) for a in out_shape]
     return pl.pallas_call(
         kernel_fn,
         grid=(p // t,),
         in_specs=in_specs,
         out_specs=out_specs,
         out_shape=out_shape,
-        scratch_shapes=scratch,
+        scratch_shapes=[pltpu.VMEM((mloc, vp, t), jnp.float32)],
+        input_output_aliases=aliases,
         compiler_params=pltpu.CompilerParams(vmem_limit_bytes=VMEM),
         cost_estimate=pl.CostEstimate(
             flops=2 * mloc * p * h * (h + 2 * v), bytes_accessed=mloc * p * h * 10 + 10 * h * h,
@@ -344,19 +318,19 @@
     mloc, h, t = refs[-1].shape
     for k in range(0, h, SLAB):
         rows = pl.ds(k, SLAB)
-        out = jnp.dot(wt_ref[rows, :], gp_ref[...], preferred_element_type=jnp.float32)
+        out = jnp.dot(wt_ref[rows, :], gp_ref[pl.program_id(0)], preferred_element_type=jnp.float32)
         for m in range(mloc):
             refs[-1][m, rows, :] = out[:, m * t : (m + 1) * t].astype(jnp.bfloat16)
 
 
 def input_gradient(start, p, n, wt, gp, gh):
-    h = gp.shape[0]
-    mloc = gp.shape[1] // p
+    steps, h, width = gp.shape
     t = TILE
+    mloc = width // t
     off = start // t
     in_specs = [
         pl.BlockSpec((h, h), lambda s: (0, 0), pipeline_mode=pl.Buffered(1)),
-        pl.BlockSpec((h, mloc * t), lambda s: (0, s)),
+        pl.BlockSpec(gp.shape, lambda s: (0, 0, 0)),
     ]
     args = [wt, gp]
     if gh is not None:
@@ -364,7 +338,7 @@
         args.append(gh)
     return pl.pallas_call(
         input_kernel,
-        grid=(p // t,),
+        grid=(steps,),
         in_specs=in_specs,
         out_specs=pl.BlockSpec((mloc, h, t), lambda s: (0, 0, off + s)),
         out_shape=jax.ShapeDtypeStruct((mloc, h, n), jnp.bfloat16),
@@ -408,6 +382,7 @@
     to_lo = lambda a, k: lax.ppermute(a, "grid", shift_lo(k))
     to_hi = lambda a, k: lax.ppermute(a, "grid", shift_hi(k))
 
+    hidden = pltpu.with_memory_space_constraint(hidden, pltpu.HBM)
     unit = n // sum(EIGHTHS)
     starts = [unit * sum(EIGHTHS[:k]) for k in range(len(EIGHTHS))]
     spans = [(start, unit * size) for start, size in zip(starts, EIGHTHS)]
@@ -427,13 +402,12 @@
         first, last = k == 0, k == len(spans) - 1
         if k >= 2:
             far[k] = after(far[k], grad_pre[k - 2])
-        gp, extra, *accs = backward(
+        gp, extra, acc, *accs = backward(
             start, p, first, last, (n_hi, n_lo), members,
             (fields, near[k], far[k], to_core(far[k])),
             (target, area, vw, act, slope, hidden, wot), acc, extra,
         )
         grad_pre.append(gp)
-        acc = accs[0]
     keep_a, send_a, keep_x, send_x = accs
     wt = after(w_inner, extra).T
 

time: 163 us -> 166 us (1.018)
  Pallas kernels: 93.4 us -> 67.4 us
  local copies, waits for them, and re-layouts: 7.3 us -> 31.6 us
  waiting for transfers between devices: 21.6 us -> 27.8 us
  starting transfers between devices: 28.8 us -> 26.6 us
    unnamed x28 -> x62, local copies, waits for them, and re-layouts: 3.66 us -> 28.3 us
    pallas_call x3, Pallas kernels: 41.3 us -> 27.8 us  [backward(): pl.pallas_call(kernel_fn, grid=(p // t,), in_specs=in_specs, out_specs=ou...]
    pallas_call x3, Pallas kernels: 19.6 us -> 13 us  [input_gradient(): pl.pallas_call(input_kernel, grid=(steps,), in_specs=in_specs, out_specs=...]
    pallas_call x3, Pallas kernels: 32.6 us -> 26.6 us  [forward(): pl.pallas_call(functools.partial(forward_kernel, mloc), grid=(tiles + 1,)...]
    ppermute x6, starting transfers between devices: 6.8 us -> 4.03 us  [shards(): to_x = lambda a: lax.ppermute(a, 'mem', swap_x)]
    ppermute x6, waiting for transfers between devices: 1.4 us -> 3.47 us  [shards(): to_x = lambda a: lax.ppermute(a, 'mem', swap_x)]
  transfers between devices with their start and end apart: 24 -> 24, of which waited for: 7 -> 7; matrix products, arithmetic and copies ran while one was open for 6% -> 6% of each run, Pallas kernels for 43% -> 30%
where the time goes in v5:
time: 166 us; the launch traced here: 165 us
  Pallas kernels  67.4 us (41%)
  local copies, waits for them, and re-layouts  31.6 us (19%)
  waiting for transfers between devices  27.8 us (17%)
  starting transfers between devices  26.6 us (16%)
  other arithmetic  9.02 us (5%)
  between operations  2.83 us (2%)
    unnamed x62, local copies, waits for them, and re-layouts  28.3 us
    pallas_call x3, Pallas kernels, backward(): pl.pallas_call(kernel_fn, grid=(p // t,), in_specs=in_specs, out_specs=ou...  27.8 us
    pallas_call x3, Pallas kernels, forward(): pl.pallas_call(functools.partial(forward_kernel, mloc), grid=(tiles + 1,)...  26.6 us
    ppermute x2, waiting for transfers between devices, shards(): lax.ppermute(extra, 'grid', [(i, i ^ bit) for i in range(n_grid)])  13 us
    pallas_call x3, Pallas kernels, input_gradient(): pl.pallas_call(input_kernel, grid=(steps,), in_specs=in_specs, out_specs=...  13 us
    ppermute x3, starting transfers between devices, gathered(): other = lax.ppermute(block, name, [(i, i ^ bit) for i in range(n)])  8.42 us
    ppermute x2, waiting for transfers between devices, shards(): to_lo = lambda a, k: lax.ppermute(a, 'grid', shift_lo(k))  6.38 us
    ppermute x8, starting transfers between devices, shards(): to_core = lambda a: lax.ppermute(a, 'mem', swap_core)  6.14 us
  transfers between devices with their start and end apart: 24, of which 7 were waited for; matrix products, arithmetic and copies ran while one was open for 6% of the time, Pallas kernels for 30%

profile of v5, /device:TPU:9, one launch (start us, length us, event | category | flops | bytes accessed | tf_op | source)
XLA Modules:
  0.0 165.2 jit_solution(10760639751207044955)
XLA Ops:
  0.6 1.6 copy-done
  4.5 9.6 %forward_part.4 = (bf16[3,2,1024,256]{3,2,1,0:T(8,128)(2,1)S(1)}, f32[3,2,1024,256]{3,2,1,0:T(8,128)S(1)}, f32[200,768]{1,0:T(8,128)}) custom-call(bf16[2,1024,2048]{2,1,0:T(8,128)(2,1)} %hid_ref.9, bf16[1024,1024]{1,0:T(8,128)(2,1)S(1)} %copy-done, f32[1,1024]{1,0:T(1,128)S(1)} %bitcast.67, bf16[100,1024]{1,0:T(8,128)(2,1)S(1)} %copy-done.21, ...), custom_call_target="tpu_custom_call" | custom-call | flops 3535798272 | bytes 14680064 | tf_op jit(solution)/shard_map/forward_part/pallas_call | solution.py:96
  14.1 2.6 %copy-done.3 = f32[3,2,1024,256]{3,2,1,0:T(8,128)} copy-done((f32[3,2,1024,256]{3,2,1,0:T(8,128)}, f32[3,2,1024,256]{3,2,1,0:T(8,128)S(1)}, u32[]{:S(2)}) %copy-start.3) | copy-done | bytes 6291480
  16.7 1.6 copy-done.13
  18.3 1.2 collective-permute-start.3
  19.6 9.6 %forward_part.5 = (bf16[3,2,1024,256]{3,2,1,0:T(8,128)(2,1)S(1)}, f32[3,2,1024,256]{3,2,1,0:T(8,128)S(1)}, f32[200,768]{1,0:T(8,128)}) custom-call(bf16[2,1024,2048]{2,1,0:T(8,128)(2,1)} %hid_ref.9, bf16[1024,1024]{1,0:T(8,128)(2,1)S(1)} %copy-done, f32[1,1024]{1,0:T(1,128)S(1)} %bitcast.68, bf16[100,1024]{1,0:T(8,128)(2,1)S(1)} %copy-done.21, ...), custom_call_target="tpu_custom_call" | custom-call | flops 3535798272 | bytes 14680064 | tf_op jit(solution)/shard_map/forward_part/pallas_call | solution.py:96
  29.2 2.7 %copy-done.2 = f32[3,2,1024,256]{3,2,1,0:T(8,128)} copy-done((f32[3,2,1024,256]{3,2,1,0:T(8,128)}, f32[3,2,1024,256]{3,2,1,0:T(8,128)S(1)}, u32[]{:S(2)}) %copy-start.2) | copy-done | bytes 6291480
  31.9 1.7 %copy-done.11 = bf16[3,2,1024,256]{3,2,1,0:T(8,128)(2,1)} copy-done((bf16[3,2,1024,256]{3,2,1,0:T(8,128)(2,1)}, bf16[3,2,1024,256]{3,2,1,0:T(8,128)(2,1)S(1)}, u32[]{:S(2)}) %copy-start.11) | copy-done | bytes 3145752
  34.0 1.2 collective-permute-start.2
  35.7 7.4 %forward_part.3 = (bf16[2,2,1024,256]{3,2,1,0:T(8,128)(2,1)S(1)}, f32[2,2,1024,256]{3,2,1,0:T(8,128)S(1)}, f32[200,512]{1,0:T(8,128)}) custom-call(bf16[2,1024,2048]{2,1,0:T(8,128)(2,1)} %hid_ref.9, bf16[1024,1024]{1,0:T(8,128)(2,1)S(1)} %copy-done, f32[1,1024]{1,0:T(1,128)S(1)} %bitcast.69, bf16[100,1024]{1,0:T(8,128)(2,1)S(1)} %copy-done.21, ...), custom_call_target="tpu_custom_call" | custom-call | flops 2357198848 | bytes 10485760 | tf_op jit(solution)/shard_map/forward_part/pallas_call | solution.py:96
  43.1 2.1 %copy-done.5 = f32[2,2,1024,256]{3,2,1,0:T(8,128)} copy-done((f32[2,2,1024,256]{3,2,1,0:T(8,128)}, f32[2,2,1024,256]{3,2,1,0:T(8,128)S(1)}, u32[]{:S(2)}) %copy-start.5) | copy-done | bytes 4194328
  45.2 1.2 collective-permute-start.1
  46.6 1.8 %collective-permute-done.7.fx_ref = f32[200,768]{1,0:T(8,128)} collective-permute-done((f32[200,768]{1,0:T(8,128)}, f32[200,768]{1,0:T(8,128)}, u32[]{:S(2)}, u32[]{:S(2)}) %collective-permute-start.7) | collective-permute-done | bytes 614432 | tf_op jit(solution)/shard_map/ppermute | solution.py:380
  48.4 3.3 %collective-permute-start.8 = (f32[200,768]{1,0:T(8,128)}, f32[200,768]{1,0:T(8,128)S(1)}, u32[]{:S(2)}, u32[]{:S(2)}) collective-permute-start(f32[200,768]{1,0:T(8,128)} %collective-permute-done.7.fx_ref), channel_id=1, source_target_pairs={{0,8},{8,0},{16,24},{24,16},{1,9},{9,1},{17,25},{25,17},{2,10},{10... | collective-permute-start | bytes 1843208 | tf_op jit(solution)/shard_map/ppermute | solution.py:381
  52.0 2.9 %copy-done.4 = f32[3,2,1024,256]{3,2,1,0:T(8,128)S(1)} copy-done((f32[3,2,1024,256]{3,2,1,0:T(8,128)S(1)}, f32[3,2,1024,256]{3,2,1,0:T(8,128)}, u32[]{:S(2)}) %copy-start.4) | copy-done | bytes 6291480
  54.9 2.0 %copy-done.14 = bf16[3,2,1024,256]{3,2,1,0:T(8,128)(2,1)S(1)} copy-done((bf16[3,2,1024,256]{3,2,1,0:T(8,128)(2,1)S(1)}, bf16[3,2,1024,256]{3,2,1,0:T(8,128)(2,1)}, u32[]{:S(2)}) %copy-start.14) | copy-done | bytes 3145752
  56.9 9.6 %backward_part.3 = (bf16[3,1024,512]{2,1,0:T(8,128)(2,1)S(1)}, f32[128,1024]{1,0:T(8,128)S(1)}, f32[1024,1024]{1,0:T(8,128)S(1)}) custom-call(f32[200,768]{1,0:T(8,128)} %get-tuple-element.37.refs_0_, f32[200,768]{1,0:T(8,128)} %collective-permute-done.2.refs_1_, f32[200,768]{1,0:T(8,128)} %collective-permute-done.3.refs_2_, ...), custom_call_target="tpu_custom_call" | custom-call | flops 3850371072 | bytes 26214400 | tf_op jit(solution)/shard_map/backward_part/pallas_call | solution.py:300
  66.6 1.7 %copy-done.9 = bf16[3,1024,512]{2,1,0:T(8,128)(2,1)} copy-done((bf16[3,1024,512]{2,1,0:T(8,128)(2,1)}, bf16[3,1024,512]{2,1,0:T(8,128)(2,1)S(1)}, u32[]{:S(2)}) %copy-start.9) | copy-done | bytes 3145752
  68.8 9.9 %backward_part.4 = (bf16[3,1024,512]{2,1,0:T(8,128)(2,1)S(1)}, f32[128,1024]{1,0:T(8,128)S(1)}, f32[1024,1024]{1,0:T(8,128)S(1)}) custom-call(f32[200,768]{1,0:T(8,128)} %get-tuple-element.40.f_ref, f32[200,768]{1,0:T(8,128)} %collective-permute-done.6.fc_ref, f32[200,768]{1,0:T(8,128)} %collective-permute-done.7.fx_ref, ...), custom_call_target="tpu_custom_call", output_to_operand_aliasing={{2}: (11, {})} | custom-call | flops 3850371072 | bytes 26214400 | tf_op jit(solution)/shard_map/backward_part/pallas_call | solution.py:300
  78.7 1.6 copy-done.7
  80.3 8.3 %backward_part.5 = (bf16[2,1024,512]{2,1,0:T(8,128)(2,1)S(1)}, f32[128,1024]{1,0:T(8,128)}, f32[1024,1024]{1,0:T(8,128)S(1)}, f32[2,4,80,512]{3,2,1,0:T(8,128)S(...) custom-call(f32[200,512]{1,0:T(8,128)} %get-tuple-element.36.f_ref, ...), custom_call_target="tpu_custom_call", output_to_operand_aliasing={{2}: (11, {})} | custom-call | flops 2566914048 | bytes 20971520 | tf_op jit(solution)/shard_map/backward_part/pallas_call | solution.py:300
  88.6 1.4 copy-done.15
  90.5 3.4 %collective-permute-done.16 = f32[2,2,4,64,256]{4,3,2,1,0:T(8,128)S(1)} collective-permute-done((f32[2,2,4,64,256]{4,3,2,1,0:T(8,128)S(1)}, f32[2,2,4,64,256]{4,3,2,1,0:T(8,128)S(1)}, u32[]{:S(2)}, u32[]{:S(2)}) %collective-permute-start.16) | collective-permute-done | bytes 1048608 | tf_op jit(solution)/shard_map/ppermute | solution.py:381
  93.9 1.0 fusion.3
  95.1 3.0 %copy.22 = bf16[1024,1024]{0,1:T(8,128)(2,1)S(1)} copy(bf16[1024,1024]{1,0:T(8,128)(2,1)} %w_ref.5) | data formatting | bytes 4194304 | tf_op jit(solution)/shard_map/optimization_barrier | solution.py:355
  98.1 1.2 fusion
  99.3 1.3 collective-permute-start.10
  100.6 1.9 %copy-done.10 = bf16[3,1024,512]{2,1,0:T(8,128)(2,1)S(1)} copy-done((bf16[3,1024,512]{2,1,0:T(8,128)(2,1)S(1)}, bf16[3,1024,512]{2,1,0:T(8,128)(2,1)}, u32[]{:S(2)}) %copy-start.10) | copy-done | bytes 3145752
  102.5 4.7 %grad_hidden_part.3.refs_0_ = bf16[2,1024,2048]{2,1,0:T(8,128)(2,1)} custom-call(bf16[1024,1024]{1,0:T(8,128)(2,1)S(1)} %bitcast.56, bf16[3,1024,512]{2,1,0:T(8,128)(2,1)S(1)} %copy-done.10), custom_call_target="tpu_custom_call" | custom-call | flops 2097152 | bytes 2097152 | tf_op jit(solution)/shard_map/grad_hidden_part/pallas_call | solution.py:339
  107.2 1.6 collective-permute-done.17
  108.8 1.1 fusion.5
  110.0 1.3 collective-permute-start.18
  111.3 3.5 %grad_hidden_part.4.refs_0_ = bf16[2,1024,2048]{2,1,0:T(8,128)(2,1)} custom-call(bf16[1024,1024]{1,0:T(8,128)(2,1)S(1)} %bitcast.57, bf16[2,1024,512]{2,1,0:T(8,128)(2,1)S(1)} %copy-done.16, bf16[2,1024,2048]{2,1,0:T(8,128)(2,1)} %grad_hidden_part.3.refs_0_), custom_call_target="tpu_custom_call", output_to_operand_aliasing={{}: (2, {})} | custom-call | flops 2097152 | bytes 2097152 | tf_op jit(solution)/shard_map/grad_hidden_part/pallas_call | solution.py:339
  114.8 6.4 %collective-permute-done.18 = f32[4,64,256]{2,1,0:T(8,128)S(1)} collective-permute-done((f32[4,64,256]{2,1,0:T(8,128)S(1)}, f32[4,64,256]{2,1,0:T(8,128)S(1)}, u32[]{:S(2)}, u32[]{:S(2)}) %collective-permute-start.18) | collective-permute-done | bytes 262176 | tf_op jit(solution)/shard_map/ppermute | solution.py:382
  121.2 1.3 fusion.2
  122.6 1.2 collective-permute-start.11
  123.8 2.4 %collective-permute-start.20 = (f32[192,256]{1,0:T(8,128)S(1)}, f32[192,256]{1,0:T(8,128)S(1)}, u32[]{:S(2)}, u32[]{:S(2)}) collective-permute-start(f32[192,256]{1,0:T(8,128)S(1)} %pad_maximum_fusion.2), channel_id=1, source_target_pairs={{0,4},{1,5},{2,6},{3,7},{4,0},{5,1},{6,2},{7,3},{8,12},{9,13},{10,... | collective-permute-start | bytes 589832 | tf_op jit(solution)/shard_map/ppermute | solution.py:383
  126.5 1.1 collective-permute-start.12
  127.6 1.6 collective-permute-start.19
  129.2 7.6 %collective-permute-done.12 = f32[4,16,512]{2,1,0:T(8,128)S(1)} collective-permute-done((f32[4,16,512]{2,1,0:T(8,128)S(1)}, f32[4,16,512]{2,1,0:T(8,128)S(1)}, u32[]{:S(2)}, u32[]{:S(2)}) %collective-permute-start.12) | collective-permute-done | bytes 131104 | tf_op jit(solution)/shard_map/ppermute | solution.py:453
  137.0 1.9 %copy-done.8 = bf16[3,1024,512]{2,1,0:T(8,128)(2,1)S(1)} copy-done((bf16[3,1024,512]{2,1,0:T(8,128)(2,1)S(1)}, bf16[3,1024,512]{2,1,0:T(8,128)(2,1)}, u32[]{:S(2)}) %copy-start.8) | copy-done | bytes 3145752
  138.8 4.7 %grad_hidden_part.5 = bf16[2,1024,2048]{2,1,0:T(8,128)(2,1)} custom-call(bf16[1024,1024]{1,0:T(8,128)(2,1)S(1)} %bitcast.58, bf16[3,1024,512]{2,1,0:T(8,128)(2,1)S(1)} %copy-done.8, bf16[2,1024,2048]{2,1,0:T(8,128)(2,1)} %grad_hidden_part.4.refs_0_), custom_call_target="tpu_custom_call", output_to_operand_aliasing={{}: (2, {})} | custom-call | flops 2097152 | bytes 2097152 | tf_op jit(solution)/shard_map/grad_hidden_part/pallas_call | solution.py:339
  143.6 5.4 %collective-permute-done.13 = f32[4,16,512]{2,1,0:T(8,128)} collective-permute-done((f32[4,16,512]{2,1,0:T(8,128)S(1)}, f32[4,16,512]{2,1,0:T(8,128)}, u32[]{:S(2)}, u32[]{:S(2)}) %collective-permute-start.13) | collective-permute-done | bytes 131104 | tf_op jit(solution)/shard_map/ppermute | solution.py:453
  149.9 1.3 collective-permute-start.14
  151.2 1.0 add_add_fusion
  152.3 1.5 collective-permute-done.14
  153.8 3.9 %collective-permute-start.15 = (f32[1,2,4,16,512]{4,3,2,1,0:T(8,128)S(1)}, f32[1,2,4,16,512]{4,3,2,1,0:T(8,128)S(1)}, u32[]{:S(2)}, u32[]{:S(2)}) collective-permute-start(f32[1,2,4,16,512]{4,3,2,1,0:T(8,128)S(1)} %maximum_select_fusion.3), channel_id=1, source_target_pairs={{0,8},{8,0},{16,24},{24,16},{1,9},{9,1},{17,25},{25,17},{2,10},{10... | collective-permute-start | bytes 786440 | tf_op jit(solution)/shard_map/ppermute | solution.py:416
  157.8 3.2 %collective-permute-start.23 = (f32[64,1024]{1,0:T(8,128)S(1)}, f32[64,1024]{1,0:T(8,128)S(1)}, u32[]{:S(2)}, u32[]{:S(2)}) collective-permute-start(f32[64,1024]{1,0:T(8,128)S(1)} %maximum_multiply_fusion), channel_id=1, source_target_pairs={{0,8},{8,0},{16,24},{24,16},{1,9},{9,1},{17,25},{25,17},{2,10},{10... | collective-permute-start | bytes 786440 | tf_op jit(solution)/shard_map/ppermute | solution.py:416
  (104 shorter events, 8.8 us)
Async XLA Ops:
  14.1 2.6 %copy-start.3 = (f32[3,2,1024,256]{3,2,1,0:T(8,128)}, f32[3,2,1024,256]{3,2,1,0:T(8,128)S(1)}, u32[]{:S(2)}) copy-start(f32[3,2,1024,256]{3,2,1,0:T(8,128)S(1)} %get-tuple-element.39.refs_8_) | copy-start | bytes 18874372
  16.7 1.6 copy-start.13
  18.3 16.9 %collective-permute-start.3 = (f32[200,768]{1,0:T(8,128)}, f32[200,768]{1,0:T(8,128)}, u32[]{:S(2)}, u32[]{:S(2)}) collective-permute-start(f32[200,768]{1,0:T(8,128)} %get-tuple-element.37.refs_0_), channel_id=1, source_target_pairs={{0,16},{8,24},{16,0},{24,8},{1,17},{9,25},{17,1},{25,9},{2,18},{10... | collective-permute-start | bytes 1843208 | tf_op jit(solution)/shard_map/ppermute | solution.py:380
  29.2 2.7 %copy-start.2 = (f32[3,2,1024,256]{3,2,1,0:T(8,128)}, f32[3,2,1024,256]{3,2,1,0:T(8,128)S(1)}, u32[]{:S(2)}) copy-start(f32[3,2,1024,256]{3,2,1,0:T(8,128)S(1)} %get-tuple-element.47.slope_ref) | copy-start | bytes 18874372
  31.9 1.7 %copy-start.11 = (bf16[3,2,1024,256]{3,2,1,0:T(8,128)(2,1)}, bf16[3,2,1024,256]{3,2,1,0:T(8,128)(2,1)S(1)}, u32[]{:S(2)}) copy-start(bf16[3,2,1024,256]{3,2,1,0:T(8,128)(2,1)S(1)} %get-tuple-element.46.act_ref) | copy-start | bytes 9437188
  33.6 12.8 %copy-start.22 = (bf16[100,1024]{1,0:T(8,128)(2,1)S(1)}, bf16[100,1024]{1,0:T(8,128)(2,1)}, u32[]{:S(2)}) copy-start(bf16[100,1024]{1,0:T(8,128)(2,1)} %wo_ref.5) | copy-start | bytes 614404
  33.6 18.3 %copy-start.1 = (f32[100,2048]{1,0:T(8,128)S(1)}, f32[100,2048]{1,0:T(8,128)}, u32[]{:S(2)}) copy-start(f32[100,2048]{1,0:T(8,128)} %target_ref.3) | copy-start | bytes 2457604
  33.6 18.3 %copy-start.23 = (f32[2048]{0:T(1024)S(1)}, f32[2048]{0:T(1024)}, u32[]{:S(2)}) copy-start(f32[2048]{0:T(1024)} %param.10) | copy-start | bytes 24580
  33.7 18.3 %copy-start.24 = (f32[100]{0:T(128)S(1)}, f32[100]{0:T(128)}, u32[]{:S(2)}) copy-start(f32[100]{0:T(128)} %param.11) | copy-start | bytes 1204
  33.7 14.8 %collective-permute-start.7 = (f32[200,768]{1,0:T(8,128)}, f32[200,768]{1,0:T(8,128)}, u32[]{:S(2)}, u32[]{:S(2)}) collective-permute-start(f32[200,768]{1,0:T(8,128)} %get-tuple-element.40.f_ref), channel_id=1, source_target_pairs={{0,16},{8,24},{16,0},{24,8},{1,17},{9,25},{17,1},{25,9},{2,18},{10... | collective-permute-start | bytes 1843208 | tf_op jit(solution)/shard_map/ppermute | solution.py:380
  34.0 17.9 %collective-permute-start.2 = (f32[200,768]{1,0:T(8,128)}, f32[200,768]{1,0:T(8,128)}, u32[]{:S(2)}, u32[]{:S(2)}) collective-permute-start(f32[200,768]{1,0:T(8,128)} %get-tuple-element.37.refs_0_), channel_id=1, source_target_pairs={{0,8},{8,0},{16,24},{24,16},{1,9},{9,1},{17,25},{25,17},{2,10},{10... | collective-permute-start | bytes 1843208 | tf_op jit(solution)/shard_map/ppermute | solution.py:381
  35.2 16.7 %collective-permute-start.4 = (f32[200,768]{1,0:T(8,128)}, f32[200,768]{1,0:T(8,128)}, u32[]{:S(2)}, u32[]{:S(2)}) collective-permute-start(f32[200,768]{1,0:T(8,128)} %collective-permute-done.3.refs_2_), channel_id=1, source_target_pairs={{0,8},{8,0},{16,24},{24,16},{1,9},{9,1},{17,25},{25,17},{2,10},{10... | collective-permute-start | bytes 1843208 | tf_op jit(solution)/shard_map/ppermute | solution.py:381
  35.2 33.5 %collective-permute-start.6 = (f32[200,768]{1,0:T(8,128)}, f32[200,768]{1,0:T(8,128)}, u32[]{:S(2)}, u32[]{:S(2)}) collective-permute-start(f32[200,768]{1,0:T(8,128)} %get-tuple-element.40.f_ref), channel_id=1, source_target_pairs={{0,8},{8,0},{16,24},{24,16},{1,9},{9,1},{17,25},{25,17},{2,10},{10... | collective-permute-start | bytes 1843208 | tf_op jit(solution)/shard_map/ppermute | solution.py:381
  43.1 2.1 %copy-start.5 = (f32[2,2,1024,256]{3,2,1,0:T(8,128)}, f32[2,2,1024,256]{3,2,1,0:T(8,128)S(1)}, u32[]{:S(2)}) copy-start(f32[2,2,1024,256]{3,2,1,0:T(8,128)S(1)} %get-tuple-element.45.slope_ref) | copy-start | bytes 12582916
  45.2 23.1 %collective-permute-start.1 = (f32[200,512]{1,0:T(8,128)}, f32[200,512]{1,0:T(8,128)}, u32[]{:S(2)}, u32[]{:S(2)}) collective-permute-start(f32[200,512]{1,0:T(8,128)} %get-tuple-element.36.f_ref), channel_id=1, source_target_pairs={{0,16},{8,24},{16,0},{24,8},{1,17},{9,25},{17,1},{25,9},{2,18},{10... | collective-permute-start | bytes 1228808 | tf_op jit(solution)/shard_map/ppermute | solution.py:380
  48.4 20.3 %collective-permute-start.8 = (f32[200,768]{1,0:T(8,128)}, f32[200,768]{1,0:T(8,128)S(1)}, u32[]{:S(2)}, u32[]{:S(2)}) collective-permute-start(f32[200,768]{1,0:T(8,128)} %collective-permute-done.7.fx_ref), channel_id=1, source_target_pairs={{0,8},{8,0},{16,24},{24,16},{1,9},{9,1},{17,25},{25,17},{2,10},{10... | collective-permute-start | bytes 1843208 | tf_op jit(solution)/shard_map/ppermute | solution.py:381
  51.9 28.4 %collective-permute-start = (f32[200,512]{1,0:T(8,128)}, f32[200,512]{1,0:T(8,128)S(1)}, u32[]{:S(2)}, u32[]{:S(2)}) collective-permute-start(f32[200,512]{1,0:T(8,128)} %get-tuple-element.36.f_ref), channel_id=1, source_target_pairs={{0,8},{8,0},{16,24},{24,16},{1,9},{9,1},{17,25},{25,17},{2,10},{10... | collective-permute-start | bytes 1228808 | tf_op jit(solution)/shard_map/ppermute | solution.py:381
  52.0 16.8 %slice-start = ((s8[6291456]{0:T(1024)(128)(4,1)}), s8[4194304]{0:T(1024)(128)(4,1)S(1)}, s32[]{:S(2)}) async-start(s8[6291456]{0:T(1024)(128)(4,1)} %bitcast.59), calls=%async_computation | async-start | bytes 8388608
  52.0 2.9 %copy-start.4 = (f32[3,2,1024,256]{3,2,1,0:T(8,128)S(1)}, f32[3,2,1024,256]{3,2,1,0:T(8,128)}, u32[]{:S(2)}) copy-start(f32[3,2,1024,256]{3,2,1,0:T(8,128)} %copy-done.3) | copy-start | bytes 18874372
  54.9 2.0 %copy-start.14 = (bf16[3,2,1024,256]{3,2,1,0:T(8,128)(2,1)S(1)}, bf16[3,2,1024,256]{3,2,1,0:T(8,128)(2,1)}, u32[]{:S(2)}) copy-start(bf16[3,2,1024,256]{3,2,1,0:T(8,128)(2,1)} %copy-done.13) | copy-start | bytes 9437188
  56.9 11.8 %slice-start.1 = ((s8[6291456]{0:T(1024)(128)(4,1)}), s8[2097152]{0:T(1024)(128)(4,1)S(1)}, s32[]{:S(2)}) async-start(s8[6291456]{0:T(1024)(128)(4,1)} %bitcast.59), calls=%async_computation.1 | async-start | bytes 4194304
  56.9 11.9 %copy-start.12 = (bf16[3,2,1024,256]{3,2,1,0:T(8,128)(2,1)S(1)}, bf16[3,2,1024,256]{3,2,1,0:T(8,128)(2,1)}, u32[]{:S(2)}) copy-start(bf16[3,2,1024,256]{3,2,1,0:T(8,128)(2,1)} %copy-done.11) | copy-start | bytes 9437188
  66.6 1.7 %copy-start.9 = (bf16[3,1024,512]{2,1,0:T(8,128)(2,1)}, bf16[3,1024,512]{2,1,0:T(8,128)(2,1)S(1)}, u32[]{:S(2)}) copy-start(bf16[3,1024,512]{2,1,0:T(8,128)(2,1)S(1)} %get-tuple-element.56.gp_ref) | copy-start | bytes 9437188
  68.3 12.0 %collective-permute-start.5 = (f32[200,512]{1,0:T(8,128)}, f32[200,512]{1,0:T(8,128)S(1)}, u32[]{:S(2)}, u32[]{:S(2)}) collective-permute-start(f32[200,512]{1,0:T(8,128)} %collective-permute-done.1.fx_ref), channel_id=1, source_target_pairs={{0,8},{8,0},{16,24},{24,16},{1,9},{9,1},{17,25},{25,17},{2,10},{10... | collective-permute-start | bytes 1228808 | tf_op jit(solution)/shard_map/ppermute | solution.py:381
  68.8 11.5 %copy-start.6 = (f32[2,2,1024,256]{3,2,1,0:T(8,128)S(1)}, f32[2,2,1024,256]{3,2,1,0:T(8,128)}, u32[]{:S(2)}) copy-start(f32[2,2,1024,256]{3,2,1,0:T(8,128)} %copy-done.5) | copy-start | bytes 12582916
  90.0 4.9 %copy-start.17 = (f32[2,4,80,512]{3,2,1,0:T(8,128)}, f32[2,4,80,512]{3,2,1,0:T(8,128)S(1)}, u32[]{:S(2)}) copy-start(f32[2,4,80,512]{3,2,1,0:T(8,128)S(1)} %get-tuple-element.52) | copy-start | bytes 3932164
  90.0 4.9 %copy-start.19 = (f32[2,2,4,64,256]{4,3,2,1,0:T(8,128)}, f32[2,2,4,64,256]{4,3,2,1,0:T(8,128)S(1)}, u32[]{:S(2)}) copy-start(f32[2,2,4,64,256]{4,3,2,1,0:T(8,128)S(1)} %get-tuple-element.58) | copy-start | bytes 3145732
  90.0 3.9 %collective-permute-start.16 = (f32[2,2,4,64,256]{4,3,2,1,0:T(8,128)S(1)}, f32[2,2,4,64,256]{4,3,2,1,0:T(8,128)S(1)}, u32[]{:S(2)}, u32[]{:S(2)}) collective-permute-start(f32[2,2,4,64,256]{4,3,2,1,0:T(8,128)S(1)} %get-tuple-element.59), channel_id=1, source_target_pairs={{0,8},{8,0},{16,24},{24,16},{1,9},{9,1},{17,25},{25,17},{2,10},{10... | collective-permute-start | bytes 3145736 | tf_op jit(solution)/shard_map/ppermute | solution.py:381
  90.0 8.0 %collective-permute-start.9 = (f32[2,4,80,512]{3,2,1,0:T(8,128)}, f32[2,4,80,512]{3,2,1,0:T(8,128)}, u32[]{:S(2)}, u32[]{:S(2)}) collective-permute-start(f32[2,4,80,512]{3,2,1,0:T(8,128)} %get-tuple-element.53), channel_id=1, source_target_pairs={{0,8},{8,0},{16,24},{24,16},{1,9},{9,1},{17,25},{25,17},{2,10},{10... | collective-permute-start | bytes 3932168 | tf_op jit(solution)/shard_map/ppermute | solution.py:381
  95.1 13.7 %collective-permute-start.17 = (f32[2,4,64,256]{3,2,1,0:T(8,128)}, f32[2,4,64,256]{3,2,1,0:T(8,128)}, u32[]{:S(2)}, u32[]{:S(2)}) collective-permute-start(f32[2,4,64,256]{3,2,1,0:T(8,128)} %fusion.3), channel_id=1, source_target_pairs={{0,16},{8,24},{16,0},{24,8},{1,17},{9,25},{17,1},{25,9},{2,18},{10... | collective-permute-start | bytes 1572872 | tf_op jit(solution)/shard_map/ppermute | solution.py:380
  95.1 3.0 %copy-start.18 = (f32[2,4,80,512]{3,2,1,0:T(8,128)S(1)}, f32[2,4,80,512]{3,2,1,0:T(8,128)}, u32[]{:S(2)}) copy-start(f32[2,4,80,512]{3,2,1,0:T(8,128)} %copy-done.17) | copy-start | bytes 3932164
  99.3 21.9 %collective-permute-start.10 = (f32[4,80,512]{2,1,0:T(8,128)S(1)}, f32[4,80,512]{2,1,0:T(8,128)S(1)}, u32[]{:S(2)}, u32[]{:S(2)}) collective-permute-start(f32[4,80,512]{2,1,0:T(8,128)S(1)} %fusion), channel_id=1, source_target_pairs={{0,1},{1,0},{2,3},{3,2},{4,5},{5,4},{6,7},{7,6},{8,9},{9,8},{10,11... | collective-permute-start | bytes 1966088 | tf_op jit(solution)/shard_map/ppermute | solution.py:382
  100.6 1.9 %copy-start.10 = (bf16[3,1024,512]{2,1,0:T(8,128)(2,1)S(1)}, bf16[3,1024,512]{2,1,0:T(8,128)(2,1)}, u32[]{:S(2)}) copy-start(bf16[3,1024,512]{2,1,0:T(8,128)(2,1)} %copy-done.9) | copy-start | bytes 9437188
  102.5 6.3 %copy-start.20 = (f32[2,2,4,64,256]{4,3,2,1,0:T(8,128)S(1)}, f32[2,2,4,64,256]{4,3,2,1,0:T(8,128)}, u32[]{:S(2)}) copy-start(f32[2,2,4,64,256]{4,3,2,1,0:T(8,128)} %copy-done.19) | copy-start | bytes 3145732
  102.5 6.3 %copy-start.28 = (f32[2,2,4,64,256]{4,3,2,1,0:T(8,128)S(1)}, f32[2,2,4,64,256]{4,3,2,1,0:T(8,128)}, u32[]{:S(2)}) copy-start(f32[2,2,4,64,256]{4,3,2,1,0:T(8,128)} %copy-done.27) | copy-start | bytes 3145732
  107.2 4.1 %copy-start.16 = (bf16[2,1024,512]{2,1,0:T(8,128)(2,1)S(1)}, bf16[2,1024,512]{2,1,0:T(8,128)(2,1)}, u32[]{:S(2)}) copy-start(bf16[2,1024,512]{2,1,0:T(8,128)(2,1)} %copy-done.15) | copy-start | bytes 6291460
  110.0 11.2 %collective-permute-start.18 = (f32[4,64,256]{2,1,0:T(8,128)S(1)}, f32[4,64,256]{2,1,0:T(8,128)S(1)}, u32[]{:S(2)}, u32[]{:S(2)}) collective-permute-start(f32[4,64,256]{2,1,0:T(8,128)S(1)} %get-tuple-element.77), channel_id=1, source_target_pairs={{0,1},{1,0},{2,3},{3,2},{4,5},{5,4},{6,7},{7,6},{8,9},{9,8},{10,11... | collective-permute-start | bytes 786440 | tf_op jit(solution)/shard_map/ppermute | solution.py:382
  122.6 3.9 %collective-permute-start.11 = (f32[4,16,512]{2,1,0:T(8,128)S(1)}, f32[4,16,512]{2,1,0:T(8,128)S(1)}, u32[]{:S(2)}, u32[]{:S(2)}) collective-permute-start(f32[4,16,512]{2,1,0:T(8,128)S(1)} %slice.126), channel_id=1, source_target_pairs={{0,16},{8,24},{16,0},{24,8},{1,17},{9,25},{17,1},{25,9},{2,18},{10... | collective-permute-start | bytes 393224 | tf_op jit(solution)/shard_map/ppermute | solution.py:380
  123.8 27.4 %collective-permute-start.20 = (f32[192,256]{1,0:T(8,128)S(1)}, f32[192,256]{1,0:T(8,128)S(1)}, u32[]{:S(2)}, u32[]{:S(2)}) collective-permute-start(f32[192,256]{1,0:T(8,128)S(1)} %pad_maximum_fusion.2), channel_id=1, source_target_pairs={{0,4},{1,5},{2,6},{3,7},{4,0},{5,1},{6,2},{7,3},{8,12},{9,13},{10,... | collective-permute-start | bytes 589832 | tf_op jit(solution)/shard_map/ppermute | solution.py:383
  126.2 25.0 %collective-permute-start.21 = (f32[192,256]{1,0:T(8,128)S(1)}, f32[192,256]{1,0:T(8,128)S(1)}, u32[]{:S(2)}, u32[]{:S(2)}) collective-permute-start(f32[192,256]{1,0:T(8,128)S(1)} %pad_maximum_fusion.3), channel_id=1, source_target_pairs={{0,6},{1,7},{2,0},{3,1},{4,2},{5,3},{6,4},{7,5},{8,14},{9,15},{10,... | collective-permute-start | bytes 589832 | tf_op jit(solution)/shard_map/ppermute | solution.py:383
  126.5 10.3 %collective-permute-start.12 = (f32[4,16,512]{2,1,0:T(8,128)S(1)}, f32[4,16,512]{2,1,0:T(8,128)S(1)}, u32[]{:S(2)}, u32[]{:S(2)}) collective-permute-start(f32[4,16,512]{2,1,0:T(8,128)S(1)} %slice_add_fusion.5), channel_id=1, source_target_pairs={{0,2},{1,3},{2,0},{3,1},{4,6},{5,7},{6,4},{7,5},{8,10},{9,11},{10,... | collective-permute-start | bytes 393224 | tf_op jit(solution)/shard_map/ppermute | solution.py:453
  127.6 23.6 %collective-permute-start.19 = (f32[192,256]{1,0:T(8,128)S(1)}, f32[192,256]{1,0:T(8,128)}, u32[]{:S(2)}, u32[]{:S(2)}) collective-permute-start(f32[192,256]{1,0:T(8,128)S(1)} %pad_maximum_fusion), channel_id=1, source_target_pairs={{0,2},{1,3},{2,4},{3,5},{4,6},{5,7},{6,0},{7,1},{8,10},{9,11},{10,... | collective-permute-start | bytes 589832 | tf_op jit(solution)/shard_map/ppermute | solution.py:383
  136.9 12.1 %collective-permute-start.13 = (f32[4,16,512]{2,1,0:T(8,128)S(1)}, f32[4,16,512]{2,1,0:T(8,128)}, u32[]{:S(2)}, u32[]{:S(2)}) collective-permute-start(f32[4,16,512]{2,1,0:T(8,128)S(1)} %add.63), channel_id=1, source_target_pairs={{0,4},{1,5},{2,6},{3,7},{4,0},{5,1},{6,2},{7,3},{8,12},{9,13},{10,... | collective-permute-start | bytes 393224 | tf_op jit(solution)/shard_map/ppermute | solution.py:453
  137.0 1.9 %copy-start.8 = (bf16[3,1024,512]{2,1,0:T(8,128)(2,1)S(1)}, bf16[3,1024,512]{2,1,0:T(8,128)(2,1)}, u32[]{:S(2)}) copy-start(bf16[3,1024,512]{2,1,0:T(8,128)(2,1)} %copy-done.7) | copy-start | bytes 9437188
  149.9 3.9 %collective-permute-start.14 = (f32[1,4,16,512]{3,2,1,0:T(8,128)S(1)}, f32[1,4,16,512]{3,2,1,0:T(8,128)S(1)}, u32[]{:S(2)}, u32[]{:S(2)}) collective-permute-start(f32[1,4,16,512]{3,2,1,0:T(8,128)S(1)} %bitcast.75), channel_id=1, source_target_pairs={{0,1},{1,0},{2,3},{3,2},{4,5},{5,4},{6,7},{7,6},{8,9},{9,8},{10,11... | collective-permute-start | bytes 393224 | tf_op jit(solution)/shard_map/ppermute | solution.py:416
  152.2 5.5 %collective-permute-start.22 = (f32[192,256]{1,0:T(8,128)S(1)}, f32[192,256]{1,0:T(8,128)S(1)}, u32[]{:S(2)}, u32[]{:S(2)}) collective-permute-start(f32[192,256]{1,0:T(8,128)S(1)} %add_add_fusion), channel_id=1, source_target_pairs={{0,16},{8,24},{16,0},{24,8},{1,17},{9,25},{17,1},{25,9},{2,18},{10... | collective-permute-start | bytes 589832 | tf_op jit(solution)/shard_map/ppermute | solution.py:380
  153.8 7.2 %collective-permute-start.15 = (f32[1,2,4,16,512]{4,3,2,1,0:T(8,128)S(1)}, f32[1,2,4,16,512]{4,3,2,1,0:T(8,128)S(1)}, u32[]{:S(2)}, u32[]{:S(2)}) collective-permute-start(f32[1,2,4,16,512]{4,3,2,1,0:T(8,128)S(1)} %maximum_select_fusion.3), channel_id=1, source_target_pairs={{0,8},{8,0},{16,24},{24,16},{1,9},{9,1},{17,25},{25,17},{2,10},{10... | collective-permute-start | bytes 786440 | tf_op jit(solution)/shard_map/ppermute | solution.py:416
  157.8 5.4 %collective-permute-start.23 = (f32[64,1024]{1,0:T(8,128)S(1)}, f32[64,1024]{1,0:T(8,128)S(1)}, u32[]{:S(2)}, u32[]{:S(2)}) collective-permute-start(f32[64,1024]{1,0:T(8,128)S(1)} %maximum_multiply_fusion), channel_id=1, source_target_pairs={{0,8},{8,0},{16,24},{24,16},{1,9},{9,1},{17,25},{25,17},{2,10},{10... | collective-permute-start | bytes 786440 | tf_op jit(solution)/shard_map/ppermute | solution.py:416
  (7 other events, 8.0 us)

commit v6 on v5

--- a/solution.py
+++ b/solution.py
@@ -233,24 +233,28 @@
             for dlo in range(n_lo):
                 for dhi in range(n_hi):
                     g = lax.rem(hi + dhi, n_hi) * n_lo + lax.rem(lo + dlo, n_lo)
+                    block = dhi * n_lo + lax.rem(lo + dlo, n_lo)
                     for c, part_a, part_x in ((core, keep_a, keep_x), (1 - core, send_a, send_x)):
                         r0 = pl.multiple_of((g * 2 + c) * r, r)
                         total = acc[pl.ds(r0, r), :]
-                        part_a[dlo, dhi, pl.ds(0, r), :] = total[:, :ca]
-                        e0 = dhi * n_lo + lax.rem(lo + dlo, n_lo)
-                        e0 = (c * (n_hi * n_lo) + e0) * EXTRA_ROWS
+                        part_a[dlo, dhi] = total[:, :ca]
+                        e0 = (c * (n_hi * n_lo) + block) * EXTRA_ROWS
                         at = pl.multiple_of(
                             jnp.minimum(e0, extra_ref.shape[0] - EXTRA_ROWS), EXTRA_ROWS
                         )
-                        for k in range(h // ca):
-                            e = extra_ref[pl.ds(at, EXTRA_ROWS), pl.ds(k * ca, ca)]
-                            part_a[dlo, dhi, pl.ds(r + k * EXTRA_ROWS, EXTRA_ROWS), :] = jnp.where(
-                                e0 < extra_ref.shape[0], e, 0.0
+                        e = jnp.where(
+                            e0 < extra_ref.shape[0], extra_ref[pl.ds(at, EXTRA_ROWS), :], 0.0
+                        )
+                        for d in range(2):
+                            own = x == 0 if d == 0 else x == 1
+                            part_x[d, dlo, dhi, pl.ds(0, r), :] = jnp.where(
+                                own, total[:, ca : ca + cx], total[:, ca + cx :]
                             )
-                        left = total[:, ca : ca + cx]
-                        right = total[:, ca + cx :]
-                        part_x[0, dlo, dhi] = jnp.where(x == 0, left, right)
-                        part_x[1, dlo, dhi] = jnp.where(x == 0, right, left)
+                            side = jnp.where(own, e[:, : h // 2], e[:, h // 2 :])
+                            for k in range(h // 2 // cx):
+                                part_x[d, dlo, dhi, pl.ds(r + k * EXTRA_ROWS, EXTRA_ROWS), :] = (
+                                    side[:, k * cx : (k + 1) * cx]
+                                )
 
 
 def backward(start, p, first, last, dims, members, fields, rest, acc, extra):
@@ -293,9 +297,9 @@
         r = h // (2 * n_hi * n_lo)
         ca = h // 2
         cx = (h - ca) // 2
-        ra = r + h // ca * EXTRA_ROWS
-        out_shape += [pltpu.VMEM((n_lo, n_hi, ra, ca), jnp.float32)] * 2
-        out_shape += [pltpu.VMEM((2, n_lo, n_hi, r, cx), jnp.float32)] * 2
+        rx = r + h // 2 // cx * EXTRA_ROWS
+        out_shape += [pltpu.VMEM((n_lo, n_hi, r, ca), jnp.float32)] * 2
+        out_shape += [pltpu.VMEM((2, n_lo, n_hi, rx, cx), jnp.float32)] * 2
     out_specs = [held(a) for a in out_shape]
     return pl.pallas_call(
         kernel_fn,
@@ -312,6 +316,38 @@
         ),
         name="backward_part",
     )(*args)
+
+
+def transposes_kernel(w_ref, wo_ref, wt_ref, wot_ref):
+    wt_ref[...] = w_ref[...].astype(jnp.float32).T.astype(jnp.bfloat16)
+
+    @pl.when(pl.program_id(0) == 0)
+    def _():
+        v, h = wo_ref.shape
+        rows = jnp.concatenate(
+            [wo_ref[...].astype(jnp.float32) * 0.5, jnp.zeros((wot_ref.shape[1] - v, h), jnp.float32)], 0
+        )
+        wot_ref[...] = rows.T.astype(jnp.bfloat16)
+
+
+def transposes(w_inner, w_out, vp):
+    v, h = w_out.shape
+    t = TILE
+    return pl.pallas_call(
+        transposes_kernel,
+        grid=(h // t,),
+        in_specs=[
+            pl.BlockSpec((t, h), lambda s: (s, 0)),
+            pl.BlockSpec((v, h), lambda s: (0, 0)),
+        ],
+        out_specs=[
+            pl.BlockSpec((h, t), lambda s: (0, s)),
+            pl.BlockSpec((h, vp), lambda s: (0, 0)),
+        ],
+        out_shape=[pltpu.VMEM((h, h), jnp.bfloat16), pltpu.VMEM((h, vp), jnp.bfloat16)],
+        compiler_params=pltpu.CompilerParams(vmem_limit_bytes=VMEM),
+        name="transposes",
+    )(w_inner, w_out)
 
 
 def input_kernel(wt_ref, gp_ref, *refs):
@@ -382,18 +418,27 @@
     to_lo = lambda a, k: lax.ppermute(a, "grid", shift_lo(k))
     to_hi = lambda a, k: lax.ppermute(a, "grid", shift_hi(k))
 
-    hidden = pltpu.with_memory_space_constraint(hidden, pltpu.HBM)
+    mem, grid = lax.axis_index("mem"), lax.axis_index("grid")
+    at_zero = {("mem", bit): mem & bit == 0 for bit in (1, n_mem // 2)}
+    bit = 1
+    while bit < n_lo:
+        at_zero["grid", bit] = grid & bit == 0
+        bit *= 2
+    hidden, at_zero = lax.optimization_barrier((hidden, at_zero))
+    hidden, w_out, b_inner, b_out = (
+        pltpu.with_memory_space_constraint(a, pltpu.HBM)
+        for a in (hidden, w_out, b_inner.reshape(1, h), b_out.reshape(1, v))
+    )
     unit = n // sum(EIGHTHS)
     starts = [unit * sum(EIGHTHS[:k]) for k in range(len(EIGHTHS))]
     spans = [(start, unit * size) for start, size in zip(starts, EIGHTHS)]
     parts = [
-        forward(start, p, hidden, w_inner, b_inner.reshape(1, h), w_out, b_out.reshape(1, v))
+        forward(start, p, hidden, w_inner, b_inner, w_out, b_out)
         for start, p in spans
     ]
     far = [to_x(fields) for _, _, fields in parts]
     near = [to_core(fields) for _, _, fields in parts]
-    w_out = after(w_out, parts[1][2])
-    wot = jnp.pad(w_out * jnp.bfloat16(0.5), ((0, vp - v), (0, 0))).T
+    wt, wot = transposes(after(w_inner, parts[-1][2]), w_out, vp)
     vw, area = var_weight.reshape(1, v), area.reshape(1, n)
     acc = extra = gh = None
     grad_pre = []
@@ -409,13 +454,15 @@
         )
         grad_pre.append(gp)
     keep_a, send_a, keep_x, send_x = accs
-    wt = after(w_inner, extra).T
 
     def gathered(block, axis, name, bit):
         n = lax.axis_size(name)
         other = lax.ppermute(block, name, [(i, i ^ bit) for i in range(n)])
+        return ordered(block, other, axis, name, bit)
+
+    def ordered(block, other, axis, name, bit):
         return jnp.where(
-            lax.axis_index(name) & bit == 0,
+            at_zero[name, bit],
             jnp.concatenate([block, other], axis),
             jnp.concatenate([other, block], axis),
         )
@@ -439,39 +486,34 @@
     own_x = [own_x[k] for k in range(n_lo)]
     gh, last_x = beside(2, gh, own_x[1], own_x[0])
     sum_x = along_lo(own_x, [last_x])
+    extra = sum_x[:, r:].reshape(-1, cx)
     pieces = [
-        jnp.concatenate([sum_a[k, :r, c : c + cx] for c in range(0, ca, cx)] + [sum_x[k]], 0)
+        jnp.concatenate(
+            [sum_a[k][:, c : c + cx] for c in range(0, ca, cx)] + [sum_x[k, :r], extra], 0
+        )
         for k in range(n_hi)
     ]
     from_hi = [to_hi(pieces[k], k) for k in range(1, n_hi)]
     gh, own = beside(1, gh, pieces[1], pieces[0])
-
-    extra = sum_a[:, r:]
-    extra = extra + to_x(extra)
-    bit = n_lo
-    while bit < n_grid:
-        extra = extra + lax.ppermute(extra, "grid", [(i, i ^ bit) for i in range(n_grid)])
-        bit *= 2
-
-    total = after(sum(from_hi, own), extra)
+    total = sum(from_hi, own)
     far = to_x(total)
+
+    na, nx = ca // cx * r, (ca // cx + 1) * r
+    both = total[:na] + far[:na]
+    ends = [both[k : k + r] for k in range(0, na, r)]
+    ends.append(ordered(total[na:nx], far[na:nx], 1, "mem", n_mem // 2))
+    scale = 1.0 / math.sqrt(members * npoints)
+    grad_inner = gathered(jnp.concatenate(ends, 1) * scale, 0, "mem", 1)
+
+    extra = ordered(total[nx:][None], far[nx:][None], 0, "mem", n_mem // 2)
     extra = extra[None]
     bit = 1
     while bit < n_lo:
         extra = gathered(extra, 0, "grid", bit)
         bit *= 2
     extra = gathered(extra[None], 0, "mem", 1)
-    extra = extra.reshape(2, n_lo, n_hi, h // ca, EXTRA_ROWS, ca).transpose(0, 2, 1, 4, 3, 5)
-    extra = extra.reshape(2 * n_grid * EXTRA_ROWS, h)
-
-    done = h // cx // 2 * r
-    both = total[:done] + far[:done]
-    left, right = total[done:], far[done:]
-    x = lax.axis_index("mem") // 2
-    ends = [both[k : k + r] for k in range(0, done, r)]
-    ends += [jnp.where(x == 0, left, right), jnp.where(x == 0, right, left)]
-    scale = 1.0 / math.sqrt(members * npoints)
-    grad_inner = gathered(jnp.concatenate(ends, 1) * scale, 0, "mem", 1)
+    extra = extra.reshape(2, n_lo, 2, n_hi, h // 2 // cx, EXTRA_ROWS, cx)
+    extra = extra.transpose(0, 3, 1, 5, 2, 4, 6).reshape(2 * n_grid * EXTRA_ROWS, h)
     loss = jnp.sum(extra[v]) / npoints
     return (loss, gh, grad_inner, extra[:v] * (0.5 * scale))
 

time: 166 us -> 153 us (0.922)
  local copies, waits for them, and re-layouts: 31.6 us -> 1.83 us
  waiting for transfers between devices: 27.8 us -> 55.8 us
  other arithmetic: 9.02 us -> 3.09 us
  starting transfers between devices: 26.6 us -> 22.1 us
    unnamed x62 -> x8, local copies, waits for them, and re-layouts: 28.3 us -> 1.6 us
    ppermute x6 -> x5, waiting for transfers between devices: 3.47 us -> 24.9 us  [shards(): to_x = lambda a: lax.ppermute(a, 'mem', swap_x)]
    ppermute x3, waiting for transfers between devices: 0.01 us -> 17.4 us  [shards(): to_hi = lambda a, k: lax.ppermute(a, 'grid', shift_hi(k))]
    ppermute x2 -> x0, waiting for transfers between devices: 13 us -> none  [shards(): lax.ppermute(extra, 'grid', [(i, i ^ bit) for i in range(n_grid)])]
    ppermute x2, waiting for transfers between devices: 6.38 us -> 9.72 us  [shards(): to_lo = lambda a, k: lax.ppermute(a, 'grid', shift_lo(k))]
    optimization_barrier x2 -> x0, local copies, waits for them, and re-layouts: 3.13 us -> none  [after(): return lax.optimization_barrier((value,) + others)[0]]
    ppermute x3, starting transfers between devices: 8.42 us -> 5.53 us  [gathered(): other = lax.ppermute(block, name, [(i, i ^ bit) for i in range(n)])]
    pallas_call x0 -> x1, Pallas kernels: none -> 2.19 us  [transposes(): pl.pallas_call(transposes_kernel, grid=(h // t,), in_specs=[pl.BlockSpec(...]
  transfers between devices with their start and end apart: 24 -> 21, of which waited for: 7 -> 12; matrix products, arithmetic and copies ran while one was open for 6% -> 1% of each run, Pallas kernels for 30% -> 33%
where the time goes in v6:
time: 153 us; the launch traced here: 152 us
  Pallas kernels  67 us (44%)
  waiting for transfers between devices  55.8 us (36%)
  starting transfers between devices  22.1 us (14%)
  other arithmetic  3.09 us (2%)
  between operations  2.72 us (2%)
  local copies, waits for them, and re-layouts  1.83 us (1%)
    pallas_call x3, Pallas kernels, backward(): pl.pallas_call(kernel_fn, grid=(p // t,), in_specs=in_specs, out_specs=ou...  26.8 us
    pallas_call x3, Pallas kernels, forward(): pl.pallas_call(functools.partial(forward_kernel, mloc), grid=(tiles + 1,)...  25 us
    ppermute x5, waiting for transfers between devices, shards(): to_x = lambda a: lax.ppermute(a, 'mem', swap_x)  24.9 us
    ppermute x3, waiting for transfers between devices, shards(): to_hi = lambda a, k: lax.ppermute(a, 'grid', shift_hi(k))  17.4 us
    pallas_call x3, Pallas kernels, input_gradient(): pl.pallas_call(input_kernel, grid=(steps,), in_specs=in_specs, out_specs=...  13 us
    ppermute x2, waiting for transfers between devices, shards(): to_lo = lambda a, k: lax.ppermute(a, 'grid', shift_lo(k))  9.72 us
    ppermute x8, starting transfers between devices, shards(): to_core = lambda a: lax.ppermute(a, 'mem', swap_core)  6.63 us
    ppermute x3, starting transfers between devices, gathered(): other = lax.ppermute(block, name, [(i, i ^ bit) for i in range(n)])  5.53 us
  transfers between devices with their start and end apart: 21, of which 12 were waited for; matrix products, arithmetic and copies ran while one was open for 1% of the time, Pallas kernels for 33%

profile of v6, /device:TPU:9, one launch (start us, length us, event | category | flops | bytes accessed | tf_op | source)
XLA Modules:
  0.0 152.5 jit_solution(12671989592709954276)
XLA Ops:
  0.7 1.6 %copy-done = bf16[1024,1024]{1,0:T(8,128)(2,1)S(1)} copy-done((bf16[1024,1024]{1,0:T(8,128)(2,1)S(1)}, bf16[1024,1024]{1,0:T(8,128)(2,1)}, u32[]{:S(2)}) %copy-start) | copy-done | bytes 2097176
  2.2 9.1 %forward_part.5 = (bf16[3,2,1024,256]{3,2,1,0:T(8,128)(2,1)S(1)}, f32[3,2,1024,256]{3,2,1,0:T(8,128)S(1)}, f32[200,768]{1,0:T(8,128)S(1)}) custom-call(bf16[2,1024,2048]{2,1,0:T(8,128)(2,1)} %hid_ref.4, bf16[1024,1024]{1,0:T(8,128)(2,1)S(1)} %copy-done, f32[1,1024]{1,0:T(1,128)} %bitcast.67, bf16[100,1024]{1,0:T(8,128)(2,1)} %wo_ref.7, f32[1,100]{1,0:T(1,128)} %bitcast.70), custom_call_target="tpu_custom_call" | custom-call | flops 3535798272 | bytes 14680064 | tf_op jit(solution)/shard_map/forward_part/pallas_call | solution.py:96
  11.3 1.3 collective-permute-start.4
  12.6 9.1 %forward_part.4 = (bf16[3,2,1024,256]{3,2,1,0:T(8,128)(2,1)S(1)}, f32[3,2,1024,256]{3,2,1,0:T(8,128)S(1)}, f32[200,768]{1,0:T(8,128)S(1)}) custom-call(bf16[2,1024,2048]{2,1,0:T(8,128)(2,1)} %hid_ref.4, bf16[1024,1024]{1,0:T(8,128)(2,1)S(1)} %copy-done, f32[1,1024]{1,0:T(1,128)} %bitcast.68, bf16[100,1024]{1,0:T(8,128)(2,1)} %wo_ref.7, f32[1,100]{1,0:T(1,128)} %bitcast.71), custom_call_target="tpu_custom_call" | custom-call | flops 3535798272 | bytes 14680064 | tf_op jit(solution)/shard_map/forward_part/pallas_call | solution.py:96
  21.7 0.3 collective-permute-start.1
  22.0 1.2 collective-permute-start.3
  23.3 2.8 %collective-permute-done.4.refs_2_ = f32[200,768]{1,0:T(8,128)S(1)} collective-permute-done((f32[200,768]{1,0:T(8,128)S(1)}, f32[200,768]{1,0:T(8,128)S(1)}, u32[]{:S(2)}, u32[]{:S(2)}) %collective-permute-start.4) | collective-permute-done | bytes 614432 | tf_op jit(solution)/shard_map/ppermute | solution.py:416
  26.1 2.7 %collective-permute-start.5 = (f32[200,768]{1,0:T(8,128)S(1)}, f32[200,768]{1,0:T(8,128)S(1)}, u32[]{:S(2)}, u32[]{:S(2)}) collective-permute-start(f32[200,768]{1,0:T(8,128)S(1)} %collective-permute-done.4.refs_2_), channel_id=1, source_target_pairs={{0,8},{8,0},{16,24},{24,16},{1,9},{9,1},{17,25},{25,17},{2,10},{10... | collective-permute-start | bytes 1843208 | tf_op jit(solution)/shard_map/ppermute | solution.py:417
  28.8 10.5 %collective-permute-done.1.fx_ref = f32[200,768]{1,0:T(8,128)S(1)} collective-permute-done((f32[200,768]{1,0:T(8,128)S(1)}, f32[200,768]{1,0:T(8,128)S(1)}, u32[]{:S(2)}, u32[]{:S(2)}) %collective-permute-start.1) | collective-permute-done | bytes 614432 | tf_op jit(solution)/shard_map/ppermute | solution.py:416
  39.3 1.5 %collective-permute-start.2 = (f32[200,768]{1,0:T(8,128)S(1)}, f32[200,768]{1,0:T(8,128)S(1)}, u32[]{:S(2)}, u32[]{:S(2)}) collective-permute-start(f32[200,768]{1,0:T(8,128)S(1)} %collective-permute-done.1.fx_ref), channel_id=1, source_target_pairs={{0,8},{8,0},{16,24},{24,16},{1,9},{9,1},{17,25},{25,17},{2,10},{10... | collective-permute-start | bytes 1843208 | tf_op jit(solution)/shard_map/ppermute | solution.py:417
  40.8 6.9 %forward_part.3 = (bf16[2,2,1024,256]{3,2,1,0:T(8,128)(2,1)S(1)}, f32[2,2,1024,256]{3,2,1,0:T(8,128)S(1)}, f32[200,512]{1,0:T(8,128)S(1)}) custom-call(bf16[2,1024,2048]{2,1,0:T(8,128)(2,1)} %hid_ref.4, bf16[1024,1024]{1,0:T(8,128)(2,1)S(1)} %copy-done, f32[1,1024]{1,0:T(1,128)} %bitcast.69, bf16[100,1024]{1,0:T(8,128)(2,1)} %wo_ref.7, f32[1,100]{1,0:T(1,128)} %bitcast.72), custom_call_target="tpu_custom_call" | custom-call | flops 2357198848 | bytes 10485760 | tf_op jit(solution)/shard_map/forward_part/pallas_call | solution.py:96
  47.7 1.3 collective-permute-start.7
  48.9 2.2 %transposes.1 = (bf16[1024,1024]{1,0:T(8,128)(2,1)S(1)}, bf16[1024,128]{1,0:T(8,128)(2,1)S(1)}) custom-call(bf16[1024,1024]{1,0:T(8,128)(2,1)S(1)} %copy-done, bf16[100,1024]{1,0:T(8,128)(2,1)} %wo_ref.7), custom_call_target="tpu_custom_call" | custom-call | tf_op jit(solution)/shard_map/transposes/pallas_call | solution.py:336
  51.2 0.3 collective-permute-start.6
  51.5 9.4 %backward_part.3 = (bf16[3,1024,512]{2,1,0:T(8,128)(2,1)S(1)}, f32[128,1024]{1,0:T(8,128)S(1)}, f32[1024,1024]{1,0:T(8,128)S(1)}) custom-call(f32[200,768]{1,0:T(8,128)S(1)} %get-tuple-element.52.refs_0_, f32[200,768]{1,0:T(8,128)S(1)} %collective-permute-done.3.refs_1_, f32[200,768]{1,0:T(8,128)S(1)} %collective-permute-done.4.refs_2_, ...), custom_call_target="tpu_custom_call" | custom-call | flops 3850371072 | bytes 26214400 | tf_op jit(solution)/shard_map/backward_part/pallas_call | solution.py:304
  60.9 0.3 collective-permute-start.8
  61.2 9.6 %backward_part.4 = (bf16[3,1024,512]{2,1,0:T(8,128)(2,1)S(1)}, f32[128,1024]{1,0:T(8,128)S(1)}, f32[1024,1024]{1,0:T(8,128)S(1)}) custom-call(f32[200,768]{1,0:T(8,128)S(1)} %get-tuple-element.48.f_ref, f32[200,768]{1,0:T(8,128)S(1)} %collective-permute-done.fc_ref, f32[200,768]{1,0:T(8,128)S(1)} %collective-permute-done.1.fx_ref, ...), custom_call_target="tpu_custom_call", output_to_operand_aliasing={{2}: (11, {})} | custom-call | flops 3850371072 | bytes 26214400 | tf_op jit(solution)/shard_map/backward_part/pallas_call | solution.py:304
  70.8 7.8 %backward_part.5 = (bf16[2,1024,512]{2,1,0:T(8,128)(2,1)S(1)}, f32[128,1024]{1,0:T(8,128)}, f32[1024,1024]{1,0:T(8,128)S(1)}, f32[2,4,64,512]{3,2,1,0:T(8,128)S(...) custom-call(f32[200,512]{1,0:T(8,128)S(1)} %get-tuple-element.45.f_r, ...), custom_call_target="tpu_custom_call", output_to_operand_aliasing={{2}: (11, {})} | custom-call | flops 2566914048 | bytes 20971520 | tf_op jit(solution)/shard_map/backward_part/pallas_call | solution.py:304
  78.7 0.3 collective-permute-start.9
  78.9 0.2 collective-permute-start.11
  79.2 2.1 %collective-permute-done.9 = f32[2,4,64,512]{3,2,1,0:T(8,128)S(1)} collective-permute-done((f32[2,4,64,512]{3,2,1,0:T(8,128)S(1)}, f32[2,4,64,512]{3,2,1,0:T(8,128)S(1)}, u32[]{:S(2)}, u32[]{:S(2)}) %collective-permute-start.9) | collective-permute-done | bytes 1048608 | tf_op jit(solution)/shard_map/ppermute | solution.py:417
  81.4 1.3 collective-permute-start.10
  82.7 0.5 collective-permute-done.11
  83.3 0.3 collective-permute-start.12
  83.6 4.7 %grad_hidden_part.3.refs_0_ = bf16[2,1024,2048]{2,1,0:T(8,128)(2,1)} custom-call(bf16[1024,1024]{1,0:T(8,128)(2,1)S(1)} %get-tuple-element.47.wt_ref, bf16[3,1024,512]{2,1,0:T(8,128)(2,1)S(1)} %get-tuple-element.67.gp_ref), custom_call_target="tpu_custom_call" | custom-call | flops 2097152 | bytes 2097152 | tf_op jit(solution)/shard_map/grad_hidden_part/pallas_call | solution.py:375
  88.4 6.4 %collective-permute-done.10 = f32[4,64,512]{2,1,0:T(8,128)S(1)} collective-permute-done((f32[4,64,512]{2,1,0:T(8,128)S(1)}, f32[4,64,512]{2,1,0:T(8,128)S(1)}, u32[]{:S(2)}, u32[]{:S(2)}) %collective-permute-start.10) | collective-permute-done | bytes 524320 | tf_op jit(solution)/shard_map/ppermute | solution.py:418
  94.7 0.2 fusion.5
  95.0 4.5 %collective-permute-done.12 = f32[2,4,80,256]{3,2,1,0:T(8,128)S(1)} collective-permute-done((f32[2,4,80,256]{3,2,1,0:T(8,128)S(1)}, f32[2,4,80,256]{3,2,1,0:T(8,128)S(1)}, u32[]{:S(2)}, u32[]{:S(2)}) %collective-permute-start.12) | collective-permute-done | bytes 655392 | tf_op jit(solution)/shard_map/ppermute | solution.py:416
  99.4 0.1 fusion.2
  99.6 1.3 collective-permute-start.13
  101.0 3.5 %grad_hidden_part.4.refs_0_ = bf16[2,1024,2048]{2,1,0:T(8,128)(2,1)} custom-call(bf16[1024,1024]{1,0:T(8,128)(2,1)S(1)} %get-tuple-element.47.wt_ref, bf16[2,1024,512]{2,1,0:T(8,128)(2,1)S(1)} %get-tuple-element.71.gp_ref, bf16[2,1024,2048]{2,1,0:T(8,128)(2,1)} %grad_hidden_part.3.refs_0_), custom_call_target="tpu_custom_call", output_to_operand_aliasing={{}: (2, {})} | custom-call | flops 2097152 | bytes 2097152 | tf_op jit(solution)/shard_map/grad_hidden_part/pallas_call | solution.py:375
  104.5 3.3 %collective-permute-done.13 = f32[4,80,256]{2,1,0:T(8,128)S(1)} collective-permute-done((f32[4,80,256]{2,1,0:T(8,128)S(1)}, f32[4,80,256]{2,1,0:T(8,128)S(1)}, u32[]{:S(2)}, u32[]{:S(2)}) %collective-permute-start.13) | collective-permute-done | bytes 327712 | tf_op jit(solution)/shard_map/ppermute | solution.py:418
  108.0 1.4 collective-permute-start.14
  109.3 1.1 collective-permute-start.15
  110.4 1.4 collective-permute-start.16
  111.8 4.7 %grad_hidden_part.5 = bf16[2,1024,2048]{2,1,0:T(8,128)(2,1)} custom-call(bf16[1024,1024]{1,0:T(8,128)(2,1)S(1)} %get-tuple-element.47.wt_ref, bf16[3,1024,512]{2,1,0:T(8,128)(2,1)S(1)} %get-tuple-element.74.gp_ref, bf16[2,1024,2048]{2,1,0:T(8,128)(2,1)} %grad_hidden_part.4.refs_0_), custom_call_target="tpu_custom_call", output_to_operand_aliasing={{}: (2, {})} | custom-call | flops 2097152 | bytes 2097152 | tf_op jit(solution)/shard_map/grad_hidden_part/pallas_call | solution.py:375
  116.6 13.2 %collective-permute-done.15 = f32[256,256]{1,0:T(8,128)S(1)} collective-permute-done((f32[256,256]{1,0:T(8,128)S(1)}, f32[256,256]{1,0:T(8,128)S(1)}, u32[]{:S(2)}, u32[]{:S(2)}) %collective-permute-start.15) | collective-permute-done | bytes 262176 | tf_op jit(solution)/shard_map/ppermute | solution.py:419
  129.8 4.2 %collective-permute-done.16 = f32[256,256]{1,0:T(8,128)S(1)} collective-permute-done((f32[256,256]{1,0:T(8,128)S(1)}, f32[256,256]{1,0:T(8,128)S(1)}, u32[]{:S(2)}, u32[]{:S(2)}) %collective-permute-start.16) | collective-permute-done | bytes 262176 | tf_op jit(solution)/shard_map/ppermute | solution.py:419
  134.1 0.3 collective-permute-start.17
  134.4 7.1 %collective-permute-done.17 = f32[256,256]{1,0:T(8,128)S(1)} collective-permute-done((f32[256,256]{1,0:T(8,128)S(1)}, f32[256,256]{1,0:T(8,128)S(1)}, u32[]{:S(2)}, u32[]{:S(2)}) %collective-permute-start.17) | collective-permute-done | bytes 262176 | tf_op jit(solution)/shard_map/ppermute | solution.py:416
  141.6 1.3 collective-permute-start.18
  142.9 1.7 %collective-permute-start.20 = (f32[64,1024]{1,0:T(8,128)S(1)}, f32[64,1024]{1,0:T(8,128)S(1)}, u32[]{:S(2)}, u32[]{:S(2)}) collective-permute-start(f32[64,1024]{1,0:T(8,128)S(1)} %maximum_multiply_fusion), channel_id=1, source_target_pairs={{0,8},{8,0},{16,24},{24,16},{1,9},{9,1},{17,25},{25,17},{2,10},{10... | collective-permute-start | bytes 786440 | tf_op jit(solution)/shard_map/ppermute | solution.py:460
  144.6 0.8 collective-permute-done.18
  145.5 2.6 %collective-permute-start.19 = (f32[1,2,2,64,256]{4,3,2,1,0:T(8,128)S(1)}, f32[1,2,2,64,256]{4,3,2,1,0:T(8,128)S(1)}, u32[]{:S(2)}, u32[]{:S(2)}) collective-permute-start(f32[1,2,2,64,256]{4,3,2,1,0:T(8,128)S(1)} %maximum_select_fusion.3), channel_id=1, source_target_pairs={{0,8},{8,0},{16,24},{24,16},{1,9},{9,1},{17,25},{25,17},{2,10},{10... | collective-permute-start | bytes 786440 | tf_op jit(solution)/shard_map/ppermute | solution.py:460
  148.1 0.8 maximum_select_fusion.1
  149.0 0.3 collective-permute-done.19
  149.3 0.8 slice_multiply_fusion
  150.1 0.6 slice_reduce_fusion
  (41 shorter events, 0.8 us)
Async XLA Ops:
  0.6 1.6 %copy-start = (bf16[1024,1024]{1,0:T(8,128)(2,1)S(1)}, bf16[1024,1024]{1,0:T(8,128)(2,1)}, u32[]{:S(2)}) copy-start(bf16[1024,1024]{1,0:T(8,128)(2,1)} %w_ref.6) | copy-start | bytes 6291460
  11.3 14.8 %collective-permute-start.4 = (f32[200,768]{1,0:T(8,128)S(1)}, f32[200,768]{1,0:T(8,128)S(1)}, u32[]{:S(2)}, u32[]{:S(2)}) collective-permute-start(f32[200,768]{1,0:T(8,128)S(1)} %get-tuple-element.52.refs_0_), channel_id=1, source_target_pairs={{0,16},{8,24},{16,0},{24,8},{1,17},{9,25},{17,1},{25,9},{2,18},{10... | collective-permute-start | bytes 1843208 | tf_op jit(solution)/shard_map/ppermute | solution.py:416
  21.7 29.8 %copy-start.1 = (f32[100,2048]{1,0:T(8,128)S(1)}, f32[100,2048]{1,0:T(8,128)}, u32[]{:S(2)}) copy-start(f32[100,2048]{1,0:T(8,128)} %target_ref.3) | copy-start | bytes 2457604
  21.7 29.8 %copy-start.2 = (f32[2048]{0:T(1024)S(1)}, f32[2048]{0:T(1024)}, u32[]{:S(2)}) copy-start(f32[2048]{0:T(1024)} %param.10) | copy-start | bytes 24580
  21.7 29.8 %copy-start.3 = (f32[100]{0:T(128)S(1)}, f32[100]{0:T(128)}, u32[]{:S(2)}) copy-start(f32[100]{0:T(128)} %param.11) | copy-start | bytes 1204
  21.7 17.6 %collective-permute-start.1 = (f32[200,768]{1,0:T(8,128)S(1)}, f32[200,768]{1,0:T(8,128)S(1)}, u32[]{:S(2)}, u32[]{:S(2)}) collective-permute-start(f32[200,768]{1,0:T(8,128)S(1)} %get-tuple-element.48.f_ref), channel_id=1, source_target_pairs={{0,16},{8,24},{16,0},{24,8},{1,17},{9,25},{17,1},{25,9},{2,18},{10... | collective-permute-start | bytes 1843208 | tf_op jit(solution)/shard_map/ppermute | solution.py:416
  22.0 29.1 %collective-permute-start.3 = (f32[200,768]{1,0:T(8,128)S(1)}, f32[200,768]{1,0:T(8,128)S(1)}, u32[]{:S(2)}, u32[]{:S(2)}) collective-permute-start(f32[200,768]{1,0:T(8,128)S(1)} %get-tuple-element.52.refs_0_), channel_id=1, source_target_pairs={{0,8},{8,0},{16,24},{24,16},{1,9},{9,1},{17,25},{25,17},{2,10},{10... | collective-permute-start | bytes 1843208 | tf_op jit(solution)/shard_map/ppermute | solution.py:417
  26.1 25.4 %collective-permute-start.5 = (f32[200,768]{1,0:T(8,128)S(1)}, f32[200,768]{1,0:T(8,128)S(1)}, u32[]{:S(2)}, u32[]{:S(2)}) collective-permute-start(f32[200,768]{1,0:T(8,128)S(1)} %collective-permute-done.4.refs_2_), channel_id=1, source_target_pairs={{0,8},{8,0},{16,24},{24,16},{1,9},{9,1},{17,25},{25,17},{2,10},{10... | collective-permute-start | bytes 1843208 | tf_op jit(solution)/shard_map/ppermute | solution.py:417
  28.8 32.4 %collective-permute-start = (f32[200,768]{1,0:T(8,128)S(1)}, f32[200,768]{1,0:T(8,128)S(1)}, u32[]{:S(2)}, u32[]{:S(2)}) collective-permute-start(f32[200,768]{1,0:T(8,128)S(1)} %get-tuple-element.48.f_ref), channel_id=1, source_target_pairs={{0,8},{8,0},{16,24},{24,16},{1,9},{9,1},{17,25},{25,17},{2,10},{10... | collective-permute-start | bytes 1843208 | tf_op jit(solution)/shard_map/ppermute | solution.py:417
  39.3 22.0 %collective-permute-start.2 = (f32[200,768]{1,0:T(8,128)S(1)}, f32[200,768]{1,0:T(8,128)S(1)}, u32[]{:S(2)}, u32[]{:S(2)}) collective-permute-start(f32[200,768]{1,0:T(8,128)S(1)} %collective-permute-done.1.fx_ref), channel_id=1, source_target_pairs={{0,8},{8,0},{16,24},{24,16},{1,9},{9,1},{17,25},{25,17},{2,10},{10... | collective-permute-start | bytes 1843208 | tf_op jit(solution)/shard_map/ppermute | solution.py:417
  47.7 13.3 %collective-permute-start.7 = (f32[200,512]{1,0:T(8,128)S(1)}, f32[200,512]{1,0:T(8,128)S(1)}, u32[]{:S(2)}, u32[]{:S(2)}) collective-permute-start(f32[200,512]{1,0:T(8,128)S(1)} %get-tuple-element.45.f_ref), channel_id=1, source_target_pairs={{0,16},{8,24},{16,0},{24,8},{1,17},{9,25},{17,1},{25,9},{2,18},{10... | collective-permute-start | bytes 1228808 | tf_op jit(solution)/shard_map/ppermute | solution.py:416
  51.2 19.6 %collective-permute-start.6 = (f32[200,512]{1,0:T(8,128)S(1)}, f32[200,512]{1,0:T(8,128)S(1)}, u32[]{:S(2)}, u32[]{:S(2)}) collective-permute-start(f32[200,512]{1,0:T(8,128)S(1)} %get-tuple-element.45.f_ref), channel_id=1, source_target_pairs={{0,8},{8,0},{16,24},{24,16},{1,9},{9,1},{17,25},{25,17},{2,10},{10... | collective-permute-start | bytes 1228808 | tf_op jit(solution)/shard_map/ppermute | solution.py:417
  60.9 9.9 %collective-permute-start.8 = (f32[200,512]{1,0:T(8,128)S(1)}, f32[200,512]{1,0:T(8,128)S(1)}, u32[]{:S(2)}, u32[]{:S(2)}) collective-permute-start(f32[200,512]{1,0:T(8,128)S(1)} %collective-permute-done.7.fx_ref), channel_id=1, source_target_pairs={{0,8},{8,0},{16,24},{24,16},{1,9},{9,1},{17,25},{25,17},{2,10},{10... | collective-permute-start | bytes 1228808 | tf_op jit(solution)/shard_map/ppermute | solution.py:417
  78.7 2.7 %collective-permute-start.9 = (f32[2,4,64,512]{3,2,1,0:T(8,128)S(1)}, f32[2,4,64,512]{3,2,1,0:T(8,128)S(1)}, u32[]{:S(2)}, u32[]{:S(2)}) collective-permute-start(f32[2,4,64,512]{3,2,1,0:T(8,128)S(1)} %get-tuple-element.65), channel_id=1, source_target_pairs={{0,8},{8,0},{16,24},{24,16},{1,9},{9,1},{17,25},{25,17},{2,10},{10... | collective-permute-start | bytes 3145736 | tf_op jit(solution)/shard_map/ppermute | solution.py:417
  78.9 4.3 %collective-permute-start.11 = (f32[2,2,4,80,256]{4,3,2,1,0:T(8,128)S(1)}, f32[2,2,4,80,256]{4,3,2,1,0:T(8,128)S(1)}, u32[]{:S(2)}, u32[]{:S(2)}) collective-permute-start(f32[2,2,4,80,256]{4,3,2,1,0:T(8,128)S(1)} %get-tuple-element.70), channel_id=1, source_target_pairs={{0,8},{8,0},{16,24},{24,16},{1,9},{9,1},{17,25},{25,17},{2,10},{10... | collective-permute-start | bytes 3932168 | tf_op jit(solution)/shard_map/ppermute | solution.py:417
  81.4 13.3 %collective-permute-start.10 = (f32[4,64,512]{2,1,0:T(8,128)S(1)}, f32[4,64,512]{2,1,0:T(8,128)S(1)}, u32[]{:S(2)}, u32[]{:S(2)}) collective-permute-start(f32[4,64,512]{2,1,0:T(8,128)S(1)} %fusion.3), channel_id=1, source_target_pairs={{0,1},{1,0},{2,3},{3,2},{4,5},{5,4},{6,7},{7,6},{8,9},{9,8},{10,11... | collective-permute-start | bytes 1572872 | tf_op jit(solution)/shard_map/ppermute | solution.py:418
  83.3 16.1 %collective-permute-start.12 = (f32[2,4,80,256]{3,2,1,0:T(8,128)S(1)}, f32[2,4,80,256]{3,2,1,0:T(8,128)S(1)}, u32[]{:S(2)}, u32[]{:S(2)}) collective-permute-start(f32[2,4,80,256]{3,2,1,0:T(8,128)S(1)} %fusion), channel_id=1, source_target_pairs={{0,16},{8,24},{16,0},{24,8},{1,17},{9,25},{17,1},{25,9},{2,18},{10... | collective-permute-start | bytes 1966088 | tf_op jit(solution)/shard_map/ppermute | solution.py:416
  99.6 8.2 %collective-permute-start.13 = (f32[4,80,256]{2,1,0:T(8,128)S(1)}, f32[4,80,256]{2,1,0:T(8,128)S(1)}, u32[]{:S(2)}, u32[]{:S(2)}) collective-permute-start(f32[4,80,256]{2,1,0:T(8,128)S(1)} %get-tuple-element.79), channel_id=1, source_target_pairs={{0,1},{1,0},{2,3},{3,2},{4,5},{5,4},{6,7},{7,6},{8,9},{9,8},{10,11... | collective-permute-start | bytes 983048 | tf_op jit(solution)/shard_map/ppermute | solution.py:418
  108.0 8.6 %collective-permute-start.14 = (f32[256,256]{1,0:T(8,128)S(1)}, f32[256,256]{1,0:T(8,128)S(1)}, u32[]{:S(2)}, u32[]{:S(2)}) collective-permute-start(f32[256,256]{1,0:T(8,128)S(1)} %get-tuple-element.107), channel_id=1, source_target_pairs={{0,2},{1,3},{2,4},{3,5},{4,6},{5,7},{6,0},{7,1},{8,10},{9,11},{10,... | collective-permute-start | bytes 786440 | tf_op jit(solution)/shard_map/ppermute | solution.py:419
  109.3 20.5 %collective-permute-start.15 = (f32[256,256]{1,0:T(8,128)S(1)}, f32[256,256]{1,0:T(8,128)S(1)}, u32[]{:S(2)}, u32[]{:S(2)}) collective-permute-start(f32[256,256]{1,0:T(8,128)S(1)} %get-tuple-element.105), channel_id=1, source_target_pairs={{0,4},{1,5},{2,6},{3,7},{4,0},{5,1},{6,2},{7,3},{8,12},{9,13},{10,... | collective-permute-start | bytes 786440 | tf_op jit(solution)/shard_map/ppermute | solution.py:419
  110.4 23.6 %collective-permute-start.16 = (f32[256,256]{1,0:T(8,128)S(1)}, f32[256,256]{1,0:T(8,128)S(1)}, u32[]{:S(2)}, u32[]{:S(2)}) collective-permute-start(f32[256,256]{1,0:T(8,128)S(1)} %get-tuple-element.106), channel_id=1, source_target_pairs={{0,6},{1,7},{2,0},{3,1},{4,2},{5,3},{6,4},{7,5},{8,14},{9,15},{10,... | collective-permute-start | bytes 786440 | tf_op jit(solution)/shard_map/ppermute | solution.py:419
  134.1 7.4 %collective-permute-start.17 = (f32[256,256]{1,0:T(8,128)S(1)}, f32[256,256]{1,0:T(8,128)S(1)}, u32[]{:S(2)}, u32[]{:S(2)}) collective-permute-start(f32[256,256]{1,0:T(8,128)S(1)} %add_add_fusion), channel_id=1, source_target_pairs={{0,16},{8,24},{16,0},{24,8},{1,17},{9,25},{17,1},{25,9},{2,18},{10... | collective-permute-start | bytes 786440 | tf_op jit(solution)/shard_map/ppermute | solution.py:416
  141.6 3.9 %collective-permute-start.18 = (f32[1,2,64,256]{3,2,1,0:T(8,128)S(1)}, f32[1,2,64,256]{3,2,1,0:T(8,128)S(1)}, u32[]{:S(2)}, u32[]{:S(2)}) collective-permute-start(f32[1,2,64,256]{3,2,1,0:T(8,128)S(1)} %maximum_select_fusion.5), channel_id=1, source_target_pairs={{0,1},{1,0},{2,3},{3,2},{4,5},{5,4},{6,7},{7,6},{8,9},{9,8},{10,11... | collective-permute-start | bytes 393224 | tf_op jit(solution)/shard_map/ppermute | solution.py:460
  142.9 5.2 %collective-permute-start.20 = (f32[64,1024]{1,0:T(8,128)S(1)}, f32[64,1024]{1,0:T(8,128)S(1)}, u32[]{:S(2)}, u32[]{:S(2)}) collective-permute-start(f32[64,1024]{1,0:T(8,128)S(1)} %maximum_multiply_fusion), channel_id=1, source_target_pairs={{0,8},{8,0},{16,24},{24,16},{1,9},{9,1},{17,25},{25,17},{2,10},{10... | collective-permute-start | bytes 786440 | tf_op jit(solution)/shard_map/ppermute | solution.py:460
  145.5 3.7 %collective-permute-start.19 = (f32[1,2,2,64,256]{4,3,2,1,0:T(8,128)S(1)}, f32[1,2,2,64,256]{4,3,2,1,0:T(8,128)S(1)}, u32[]{:S(2)}, u32[]{:S(2)}) collective-permute-start(f32[1,2,2,64,256]{4,3,2,1,0:T(8,128)S(1)} %maximum_select_fusion.3), channel_id=1, source_target_pairs={{0,8},{8,0},{16,24},{24,16},{1,9},{9,1},{17,25},{25,17},{2,10},{10... | collective-permute-start | bytes 786440 | tf_op jit(solution)/shard_map/ppermute | solution.py:460

commit v7 on v6

--- a/solution.py
+++ b/solution.py
@@ -8,7 +8,7 @@
 from jax.experimental.pallas import tpu as pltpu
 from jax.sharding import PartitionSpec as P
 
-EIGHTHS = (3, 3, 2)
+EIGHTHS = (2, 3, 3)
 TILE = 256
 EPS = 0.0004
 K0 = math.sqrt(2.0 / math.pi)
@@ -121,8 +121,7 @@
         ],
         compiler_params=pltpu.CompilerParams(vmem_limit_bytes=VMEM),
         cost_estimate=pl.CostEstimate(
-            flops=2 * mloc * p * h * (h + v), bytes_accessed=mloc * p * h * 8 + 2 * h * h,
-            transcendentals=mloc * p * h,
+            flops=2 * h * h, bytes_accessed=2 * h * h, transcendentals=0
         ),
         name="forward_part",
     )(hidden, w_inner, b_inner, w_out, b_out)
@@ -135,7 +134,7 @@
 ):
     acc, *refs = refs
     if last:
-        keep_a, send_a, keep_x, send_x, *refs = refs
+        keep_x, send_x, keep_y, send_y, *refs = refs
     (gf,) = refs
     step = pl.program_id(0)
     mloc, _, t = hid_ref.shape
@@ -228,16 +227,14 @@
             x, core = mem // 2, mem % 2
             hi, lo = grid // n_lo, grid % n_lo
             r = h // (2 * n_hi * n_lo)
-            ca = keep_a.shape[3]
             cx = keep_x.shape[4]
             for dlo in range(n_lo):
                 for dhi in range(n_hi):
                     g = lax.rem(hi + dhi, n_hi) * n_lo + lax.rem(lo + dlo, n_lo)
                     block = dhi * n_lo + lax.rem(lo + dlo, n_lo)
-                    for c, part_a, part_x in ((core, keep_a, keep_x), (1 - core, send_a, send_x)):
+                    for c, to_x, to_y in ((core, keep_x, keep_y), (1 - core, send_x, send_y)):
                         r0 = pl.multiple_of((g * 2 + c) * r, r)
                         total = acc[pl.ds(r0, r), :]
-                        part_a[dlo, dhi] = total[:, :ca]
                         e0 = (c * (n_hi * n_lo) + block) * EXTRA_ROWS
                         at = pl.multiple_of(
                             jnp.minimum(e0, extra_ref.shape[0] - EXTRA_ROWS), EXTRA_ROWS
@@ -245,16 +242,12 @@
                         e = jnp.where(
                             e0 < extra_ref.shape[0], extra_ref[pl.ds(at, EXTRA_ROWS), :], 0.0
                         )
-                        for d in range(2):
-                            own = x == 0 if d == 0 else x == 1
-                            part_x[d, dlo, dhi, pl.ds(0, r), :] = jnp.where(
-                                own, total[:, ca : ca + cx], total[:, ca + cx :]
-                            )
-                            side = jnp.where(own, e[:, : h // 2], e[:, h // 2 :])
-                            for k in range(h // 2 // cx):
-                                part_x[d, dlo, dhi, pl.ds(r + k * EXTRA_ROWS, EXTRA_ROWS), :] = (
-                                    side[:, k * cx : (k + 1) * cx]
-                                )
+                        for values, rows in ((total, pl.ds(0, r)), (e, pl.ds(r, EXTRA_ROWS))):
+                            q = [values[:, k * cx : (k + 1) * cx] for k in range(4)]
+                            for d in range(2):
+                                own = x == d
+                                to_x[d, dlo, dhi, rows, :] = jnp.where(own, q[0], q[1])
+                                to_y[dlo, d, dhi, rows, :] = jnp.where(own, q[2], q[3])
 
 
 def backward(start, p, first, last, dims, members, fields, rest, acc, extra):
@@ -295,11 +288,9 @@
     if last:
         n_hi, n_lo = dims
         r = h // (2 * n_hi * n_lo)
-        ca = h // 2
-        cx = (h - ca) // 2
-        rx = r + h // 2 // cx * EXTRA_ROWS
-        out_shape += [pltpu.VMEM((n_lo, n_hi, r, ca), jnp.float32)] * 2
-        out_shape += [pltpu.VMEM((2, n_lo, n_hi, rx, cx), jnp.float32)] * 2
+        cx = h // 4
+        out_shape += [pltpu.VMEM((2, n_lo, n_hi, r + EXTRA_ROWS, cx), jnp.float32)] * 2
+        out_shape += [pltpu.VMEM((n_lo, 2, n_hi, r + EXTRA_ROWS, cx), jnp.float32)] * 2
     out_specs = [held(a) for a in out_shape]
     return pl.pallas_call(
         kernel_fn,
@@ -311,8 +302,7 @@
         input_output_aliases=aliases,
         compiler_params=pltpu.CompilerParams(vmem_limit_bytes=VMEM),
         cost_estimate=pl.CostEstimate(
-            flops=2 * mloc * p * h * (h + 2 * v), bytes_accessed=mloc * p * h * 10 + 10 * h * h,
-            transcendentals=mloc * p * v * 8,
+            flops=2 * h * h, bytes_accessed=2 * h * h, transcendentals=0
         ),
         name="backward_part",
     )(*args)
@@ -346,6 +336,7 @@
         ],
         out_shape=[pltpu.VMEM((h, h), jnp.bfloat16), pltpu.VMEM((h, vp), jnp.bfloat16)],
         compiler_params=pltpu.CompilerParams(vmem_limit_bytes=VMEM),
+        cost_estimate=pl.CostEstimate(flops=2 * h, bytes_accessed=2 * h, transcendentals=0),
         name="transposes",
     )(w_inner, w_out)
 
@@ -432,10 +423,11 @@
     unit = n // sum(EIGHTHS)
     starts = [unit * sum(EIGHTHS[:k]) for k in range(len(EIGHTHS))]
     spans = [(start, unit * size) for start, size in zip(starts, EIGHTHS)]
-    parts = [
-        forward(start, p, hidden, w_inner, b_inner, w_out, b_out)
-        for start, p in spans
-    ]
+    parts = []
+    for start, p in spans:
+        if parts:
+            b_out = after(b_out, parts[-1][2])
+        parts.append(forward(start, p, hidden, w_inner, b_inner, w_out, b_out))
     far = [to_x(fields) for _, _, fields in parts]
     near = [to_core(fields) for _, _, fields in parts]
     wt, wot = transposes(after(w_inner, parts[-1][2]), w_out, vp)
@@ -445,15 +437,15 @@
     for k, (start, p) in enumerate(spans):
         act, slope, fields = parts[k]
         first, last = k == 0, k == len(spans) - 1
-        if k >= 2:
-            far[k] = after(far[k], grad_pre[k - 2])
+        if k:
+            far[k] = after(far[k], parts[-1][2] if k == 1 else grad_pre[k - 2])
         gp, extra, acc, *accs = backward(
             start, p, first, last, (n_hi, n_lo), members,
             (fields, near[k], far[k], to_core(far[k])),
             (target, area, vw, act, slope, hidden, wot), acc, extra,
         )
         grad_pre.append(gp)
-    keep_a, send_a, keep_x, send_x = accs
+    keep_x, send_x, keep_y, send_y = accs
 
     def gathered(block, axis, name, bit):
         n = lax.axis_size(name)
@@ -467,53 +459,46 @@
             jnp.concatenate([other, block], axis),
         )
 
-    def along_lo(blocks, own):
-        return sum([to_lo(blocks[k], k) for k in range(1, n_lo)], own[0])
-
     def beside(k, gh, start_after, wait_for):
         gh = input_gradient(*spans[k], n, wt, after(grad_pre[k], start_after), gh)
         return lax.optimization_barrier((gh, wait_for))
 
-    r = h // (2 * n_grid)
-    ca, cx = keep_a.shape[-1], keep_x.shape[-1]
+    r, cx = h // (2 * n_grid), keep_x.shape[-1]
+    others = range(1, n_lo)
     got_x = to_core(send_x)
-    got_a = to_core(send_a)
-    from_x = to_x(keep_x[1] + got_x[1])
-    here_a = [keep_a[k] + got_a[k] for k in range(n_lo)]
-    sum_a = along_lo(here_a, here_a)
-    gh, keep_x = beside(0, gh, here_a[1], keep_x)
+    got_y = to_core(send_y)
+    out_x = keep_x[1] + got_x[1]
+    out_y = [keep_y[k] + got_y[k] for k in others]
+    from_x = to_x(out_x)
+    from_y = [to_lo(out_y[k - 1], k) for k in others]
+    gh, (keep_x, keep_y) = beside(0, gh, (out_x, out_y), (keep_x, keep_y))
     own_x = keep_x[0] + got_x[0] + from_x
-    own_x = [own_x[k] for k in range(n_lo)]
-    gh, last_x = beside(2, gh, own_x[1], own_x[0])
-    sum_x = along_lo(own_x, [last_x])
-    extra = sum_x[:, r:].reshape(-1, cx)
-    pieces = [
-        jnp.concatenate(
-            [sum_a[k][:, c : c + cx] for c in range(0, ca, cx)] + [sum_x[k, :r], extra], 0
-        )
-        for k in range(n_hi)
-    ]
+    own_y = sum(from_y, keep_y[0] + got_y[0])
+    own_x, own_y = [own_x[k] for k in range(n_lo)], [own_y[k] for k in range(2)]
+    from_y = [to_lo(own_x[k], k) for k in others]
+    from_x = to_x(own_y[1])
+    gh, (own_x, own_y) = beside(2, gh, (own_x[1:], own_y[1]), (own_x[0], own_y[0]))
+    sums = [sum(from_y, own_x), own_y + from_x]
+
+    extra = [part[:, r:].reshape(-1, cx) for part in sums]
+    pieces = [jnp.concatenate([part[k, :r] for part in sums] + extra, 0) for k in range(n_hi)]
     from_hi = [to_hi(pieces[k], k) for k in range(1, n_hi)]
-    gh, own = beside(1, gh, pieces[1], pieces[0])
+    gh, own = beside(1, gh, pieces[1:], pieces[0])
     total = sum(from_hi, own)
     far = to_x(total)
 
-    na, nx = ca // cx * r, (ca // cx + 1) * r
-    both = total[:na] + far[:na]
-    ends = [both[k : k + r] for k in range(0, na, r)]
-    ends.append(ordered(total[na:nx], far[na:nx], 1, "mem", n_mem // 2))
     scale = 1.0 / math.sqrt(members * npoints)
-    grad_inner = gathered(jnp.concatenate(ends, 1) * scale, 0, "mem", 1)
-
-    extra = ordered(total[nx:][None], far[nx:][None], 0, "mem", n_mem // 2)
-    extra = extra[None]
+    halves = [ordered(total[k : k + r], far[k : k + r], 1, "mem", n_mem // 2) for k in (0, r)]
+    grad_inner = gathered(jnp.concatenate(halves, 1) * scale, 0, "mem", 1)
+
+    extra = ordered(total[2 * r :][None], far[2 * r :][None], 0, "mem", n_mem // 2)[None]
     bit = 1
     while bit < n_lo:
         extra = gathered(extra, 0, "grid", bit)
         bit *= 2
     extra = gathered(extra[None], 0, "mem", 1)
-    extra = extra.reshape(2, n_lo, 2, n_hi, h // 2 // cx, EXTRA_ROWS, cx)
-    extra = extra.transpose(0, 3, 1, 5, 2, 4, 6).reshape(2 * n_grid * EXTRA_ROWS, h)
+    extra = extra.reshape(2, n_lo, 2, 2, n_hi, EXTRA_ROWS, cx)
+    extra = extra.transpose(0, 4, 1, 5, 3, 2, 6).reshape(2 * n_grid * EXTRA_ROWS, h)
     loss = jnp.sum(extra[v]) / npoints
     return (loss, gh, grad_inner, extra[:v] * (0.5 * scale))
 

time: 153 us -> 134 us (0.88)
  waiting for transfers between devices: 55.8 us -> 36.1 us
    ppermute x2, waiting for transfers between devices: 9.72 us -> 1.02 us  [shards(): to_lo = lambda a, k: lax.ppermute(a, 'grid', shift_lo(k))]
    ppermute x5 -> x6, waiting for transfers between devices: 24.9 us -> 18.7 us  [shards(): to_x = lambda a: lax.ppermute(a, 'mem', swap_x)]
    ppermute x3, waiting for transfers between devices: 17.4 us -> 11.8 us  [shards(): to_hi = lambda a, k: lax.ppermute(a, 'grid', shift_hi(k))]
    ppermute x5 -> x6, starting transfers between devices: 3.54 us -> 3.85 us  [shards(): to_x = lambda a: lax.ppermute(a, 'mem', swap_x)]
  transfers between devices with their start and end apart: 21 -> 22, of which waited for: 12 -> 12; matrix products, arithmetic and copies ran while one was open for 1% -> 1% of each run, Pallas kernels for 33% -> 37%
where the time goes in v7:
time: 134 us
  Pallas kernels  67 us (50%)
  waiting for transfers between devices  36.1 us (27%)
  starting transfers between devices  23.2 us (17%)
  other arithmetic  3 us (2%)
  between operations  2.72 us (2%)
  local copies, waits for them, and re-layouts  1.83 us (1%)
    pallas_call x3, Pallas kernels, backward(): pl.pallas_call(kernel_fn, grid=(p // t,), in_specs=in_specs, out_specs=ou...  26.8 us
    pallas_call x3, Pallas kernels, forward(): pl.pallas_call(functools.partial(forward_kernel, mloc), grid=(tiles + 1,)...  25 us
    ppermute x6, waiting for transfers between devices, shards(): to_x = lambda a: lax.ppermute(a, 'mem', swap_x)  18.7 us
    pallas_call x3, Pallas kernels, input_gradient(): pl.pallas_call(input_kernel, grid=(steps,), in_specs=in_specs, out_specs=...  13 us
    ppermute x3, waiting for transfers between devices, shards(): to_hi = lambda a, k: lax.ppermute(a, 'grid', shift_hi(k))  11.8 us
    ppermute x8, starting transfers between devices, shards(): to_core = lambda a: lax.ppermute(a, 'mem', swap_core)  7.26 us
    ppermute x3, starting transfers between devices, gathered(): other = lax.ppermute(block, name, [(i, i ^ bit) for i in range(n)])  5.61 us
    ppermute x6, starting transfers between devices, shards(): to_x = lambda a: lax.ppermute(a, 'mem', swap_x)  3.85 us
  transfers between devices with their start and end apart: 22, of which 12 were waited for; matrix products, arithmetic and copies ran while one was open for 1% of the time, Pallas kernels for 37%

profile of v7, /device:TPU:9, one launch (start us, length us, event | category | flops | bytes accessed | tf_op | source)
XLA Modules:
  0.0 133.8 jit_solution(10740390722144719064)
XLA Ops:
  0.7 1.6 %copy-done = bf16[1024,1024]{1,0:T(8,128)(2,1)S(1)} copy-done((bf16[1024,1024]{1,0:T(8,128)(2,1)S(1)}, bf16[1024,1024]{1,0:T(8,128)(2,1)}, u32[]{:S(2)}) %copy-start) | copy-done | bytes 2097176
  2.2 6.8 %forward_part.3 = (bf16[2,2,1024,256]{3,2,1,0:T(8,128)(2,1)S(1)}, f32[2,2,1024,256]{3,2,1,0:T(8,128)S(1)}, f32[200,512]{1,0:T(8,128)S(1)}) custom-call(bf16[2,1024,2048]{2,1,0:T(8,128)(2,1)} %hid_ref.4, bf16[1024,1024]{1,0:T(8,128)(2,1)S(1)} %copy-done, f32[1,1024]{1,0:T(1,128)} %bitcast.73, bf16[100,1024]{1,0:T(8,128)(2,1)} %wo_ref.7, f32[1,100]{1,0:T(1,128)} %bitcast.76), custom_call_target="tpu_custom_call" | custom-call | flops 2097152 | bytes 2097152 | tf_op jit(solution)/shard_map/forward_part/pallas_call | solution.py:96
  9.1 1.3 collective-permute-start.4
  10.4 9.1 %forward_part.4 = (bf16[3,2,1024,256]{3,2,1,0:T(8,128)(2,1)S(1)}, f32[3,2,1024,256]{3,2,1,0:T(8,128)S(1)}, f32[200,768]{1,0:T(8,128)S(1)}) custom-call(bf16[2,1024,2048]{2,1,0:T(8,128)(2,1)} %hid_ref.4, bf16[1024,1024]{1,0:T(8,128)(2,1)S(1)} %copy-done, f32[1,1024]{1,0:T(1,128)} %bitcast.74, bf16[100,1024]{1,0:T(8,128)(2,1)} %wo_ref.7, f32[1,100]{1,0:T(1,128)} %bitcast.77), custom_call_target="tpu_custom_call" | custom-call | flops 2097152 | bytes 2097152 | tf_op jit(solution)/shard_map/forward_part/pallas_call | solution.py:96
  19.4 0.3 collective-permute-start.1
  19.8 9.1 %forward_part.5 = (bf16[3,2,1024,256]{3,2,1,0:T(8,128)(2,1)S(1)}, f32[3,2,1024,256]{3,2,1,0:T(8,128)S(1)}, f32[200,768]{1,0:T(8,128)S(1)}) custom-call(bf16[2,1024,2048]{2,1,0:T(8,128)(2,1)} %hid_ref.4, bf16[1024,1024]{1,0:T(8,128)(2,1)S(1)} %copy-done, f32[1,1024]{1,0:T(1,128)} %bitcast.75, bf16[100,1024]{1,0:T(8,128)(2,1)} %wo_ref.7, f32[1,100]{1,0:T(1,128)} %bitcast.78), custom_call_target="tpu_custom_call" | custom-call | flops 2097152 | bytes 2097152 | tf_op jit(solution)/shard_map/forward_part/pallas_call | solution.py:96
  28.9 1.3 collective-permute-start.7
  30.2 1.5 %collective-permute-start.3 = (f32[200,512]{1,0:T(8,128)S(1)}, f32[200,512]{1,0:T(8,128)S(1)}, u32[]{:S(2)}, u32[]{:S(2)}) collective-permute-start(f32[200,512]{1,0:T(8,128)S(1)} %get-tuple-element.50.refs_0_), channel_id=1, source_target_pairs={{0,8},{8,0},{16,24},{24,16},{1,9},{9,1},{17,25},{25,17},{2,10},{10... | collective-permute-start | bytes 1228808 | tf_op jit(solution)/shard_map/ppermute | solution.py:408
  31.7 0.5 collective-permute-start
  32.2 2.2 %transposes.1 = (bf16[1024,1024]{1,0:T(8,128)(2,1)S(1)}, bf16[1024,128]{1,0:T(8,128)(2,1)S(1)}) custom-call(bf16[1024,1024]{1,0:T(8,128)(2,1)S(1)} %copy-done, bf16[100,1024]{1,0:T(8,128)(2,1)} %wo_ref.7), custom_call_target="tpu_custom_call" | custom-call | flops 2048 | bytes 2048 | tf_op jit(solution)/shard_map/transposes/pallas_call | solution.py:326
  34.4 2.8 %collective-permute-start.6 = (f32[200,768]{1,0:T(8,128)S(1)}, f32[200,768]{1,0:T(8,128)S(1)}, u32[]{:S(2)}, u32[]{:S(2)}) collective-permute-start(f32[200,768]{1,0:T(8,128)S(1)} %get-tuple-element.54.f_ref), channel_id=1, source_target_pairs={{0,8},{8,0},{16,24},{24,16},{1,9},{9,1},{17,25},{25,17},{2,10},{10... | collective-permute-start | bytes 1843208 | tf_op jit(solution)/shard_map/ppermute | solution.py:408
  37.3 6.6 %backward_part.3 = (bf16[2,1024,512]{2,1,0:T(8,128)(2,1)S(1)}, f32[128,1024]{1,0:T(8,128)S(1)}, f32[1024,1024]{1,0:T(8,128)S(1)}) custom-call(f32[200,512]{1,0:T(8,128)S(1)} %get-tuple-element.50.refs_0_, f32[200,512]{1,0:T(8,128)S(1)} %collective-permute-done.3.refs_1_, f32[200,512]{1,0:T(8,128)S(1)} %collective-permute-done.4.refs_2_, ...), custom_call_target="tpu_custom_call" | custom-call | flops 2097152 | bytes 2097152 | tf_op jit(solution)/shard_map/backward_part/pallas_call | solution.py:295
  43.9 3.1 %collective-permute-done.7.fx_ref = f32[200,768]{1,0:T(8,128)S(1)} collective-permute-done((f32[200,768]{1,0:T(8,128)S(1)}, f32[200,768]{1,0:T(8,128)S(1)}, u32[]{:S(2)}, u32[]{:S(2)}) %collective-permute-start.7) | collective-permute-done | bytes 614432 | tf_op jit(solution)/shard_map/ppermute | solution.py:407
  47.1 1.9 %collective-permute-start.8 = (f32[200,768]{1,0:T(8,128)S(1)}, f32[200,768]{1,0:T(8,128)S(1)}, u32[]{:S(2)}, u32[]{:S(2)}) collective-permute-start(f32[200,768]{1,0:T(8,128)S(1)} %collective-permute-done.7.fx_ref), channel_id=1, source_target_pairs={{0,8},{8,0},{16,24},{24,16},{1,9},{9,1},{17,25},{25,17},{2,10},{10... | collective-permute-start | bytes 1843208 | tf_op jit(solution)/shard_map/ppermute | solution.py:408
  49.0 9.6 %backward_part.4 = (bf16[3,1024,512]{2,1,0:T(8,128)(2,1)S(1)}, f32[128,1024]{1,0:T(8,128)S(1)}, f32[1024,1024]{1,0:T(8,128)S(1)}) custom-call(f32[200,768]{1,0:T(8,128)S(1)} %get-tuple-element.52.f_ref, f32[200,768]{1,0:T(8,128)S(1)} %collective-permute-done.fc_ref, f32[200,768]{1,0:T(8,128)S(1)} %collective-permute-done.1.fx_ref, ...), custom_call_target="tpu_custom_call", output_to_operand_aliasing={{2}: (11, {})} | custom-call | flops 2097152 | bytes 2097152 | tf_op jit(solution)/shard_map/backward_part/pallas_call | solution.py:295
  58.5 10.6 %backward_part.5 = (bf16[3,1024,512]{2,1,0:T(8,128)(2,1)S(1)}, f32[128,1024]{1,0:T(8,128)}, f32[1024,1024]{1,0:T(8,128)S(1)}, f32[2,2,4,72,256]{4,3,2,1,0:T(8,12...) custom-call(f32[200,768]{1,0:T(8,128)S(1)} %get-tuple-element.54.f_r, ...), custom_call_target="tpu_custom_call", output_to_operand_aliasing={{2}: (11, {})} | custom-call | flops 2097152 | bytes 2097152 | tf_op jit(solution)/shard_map/backward_part/pallas_call | solution.py:295
  69.1 0.2 collective-permute-start.9
  69.3 0.3 collective-permute-start.10
  69.6 2.3 %collective-permute-done.9 = f32[2,2,4,72,256]{4,3,2,1,0:T(8,128)S(1)} collective-permute-done((f32[2,2,4,72,256]{4,3,2,1,0:T(8,128)S(1)}, f32[2,2,4,72,256]{4,3,2,1,0:T(8,128)S(1)}, u32[]{:S(2)}, u32[]{:S(2)}) %collective-permute-start.9) | collective-permute-done | bytes 1179680 | tf_op jit(solution)/shard_map/ppermute | solution.py:408
  72.1 0.3 collective-permute-start.11
  72.4 1.3 collective-permute-done.10
  73.7 1.3 collective-permute-start.12
  75.1 3.5 %grad_hidden_part.3.refs_0_ = bf16[2,1024,2048]{2,1,0:T(8,128)(2,1)} custom-call(bf16[1024,1024]{1,0:T(8,128)(2,1)S(1)} %get-tuple-element.56.wt_ref, bf16[2,1024,512]{2,1,0:T(8,128)(2,1)S(1)} %get-tuple-element.77.gp_ref), custom_call_target="tpu_custom_call" | custom-call | flops 2097152 | bytes 2097152 | tf_op jit(solution)/shard_map/grad_hidden_part/pallas_call | solution.py:366
  78.5 8.3 %collective-permute-done.11 = f32[2,4,72,256]{3,2,1,0:T(8,128)S(1)} collective-permute-done((f32[2,4,72,256]{3,2,1,0:T(8,128)S(1)}, f32[2,4,72,256]{3,2,1,0:T(8,128)S(1)}, u32[]{:S(2)}, u32[]{:S(2)}) %collective-permute-start.11) | collective-permute-done | bytes 589856 | tf_op jit(solution)/shard_map/ppermute | solution.py:407
  86.9 0.1 fusion.3
  87.0 1.3 collective-permute-start.13
  88.3 0.2 collective-permute-done.12
  88.5 0.1 fusion.1
  88.7 0.3 collective-permute-start.14
  89.0 4.7 %grad_hidden_part.4.refs_0_ = bf16[2,1024,2048]{2,1,0:T(8,128)(2,1)} custom-call(bf16[1024,1024]{1,0:T(8,128)(2,1)S(1)} %get-tuple-element.56.wt_ref, bf16[3,1024,512]{2,1,0:T(8,128)(2,1)S(1)} %get-tuple-element.80.gp_ref, bf16[2,1024,2048]{2,1,0:T(8,128)(2,1)} %grad_hidden_part.3.refs_0_), custom_call_target="tpu_custom_call", output_to_operand_aliasing={{}: (2, {})} | custom-call | flops 2097152 | bytes 2097152 | tf_op jit(solution)/shard_map/grad_hidden_part/pallas_call | solution.py:366
  93.8 0.8 collective-permute-done.13
  94.7 1.5 %collective-permute-done.14 = f32[4,72,256]{2,1,0:T(8,128)S(1)} collective-permute-done((f32[4,72,256]{2,1,0:T(8,128)S(1)}, f32[4,72,256]{2,1,0:T(8,128)S(1)}, u32[]{:S(2)}, u32[]{:S(2)}) %collective-permute-start.14) | collective-permute-done | bytes 294944 | tf_op jit(solution)/shard_map/ppermute | solution.py:407
  96.3 1.4 %collective-permute-start.15 = (f32[192,256]{1,0:T(8,128)S(1)}, f32[192,256]{1,0:T(8,128)S(1)}, u32[]{:S(2)}, u32[]{:S(2)}) collective-permute-start(f32[192,256]{1,0:T(8,128)S(1)} %get-tuple-element.111), channel_id=1, source_target_pairs={{0,2},{1,3},{2,4},{3,5},{4,6},{5,7},{6,0},{7,1},{8,10},{9,11},{10,... | collective-permute-start | bytes 589832 | tf_op jit(solution)/shard_map/ppermute | solution.py:410
  97.7 1.1 collective-permute-start.16
  98.8 1.4 %collective-permute-start.17 = (f32[192,256]{1,0:T(8,128)S(1)}, f32[192,256]{1,0:T(8,128)S(1)}, u32[]{:S(2)}, u32[]{:S(2)}) collective-permute-start(f32[192,256]{1,0:T(8,128)S(1)} %get-tuple-element.110), channel_id=1, source_target_pairs={{0,6},{1,7},{2,0},{3,1},{4,2},{5,3},{6,4},{7,5},{8,14},{9,15},{10,... | collective-permute-start | bytes 589832 | tf_op jit(solution)/shard_map/ppermute | solution.py:410
  100.2 4.8 %grad_hidden_part.5 = bf16[2,1024,2048]{2,1,0:T(8,128)(2,1)} custom-call(bf16[1024,1024]{1,0:T(8,128)(2,1)S(1)} %get-tuple-element.56.wt_ref, bf16[3,1024,512]{2,1,0:T(8,128)(2,1)S(1)} %get-tuple-element.84.gp_ref, bf16[2,1024,2048]{2,1,0:T(8,128)(2,1)} %grad_hidden_part.4.refs_0_), custom_call_target="tpu_custom_call", output_to_operand_aliasing={{}: (2, {})} | custom-call | flops 2097152 | bytes 2097152 | tf_op jit(solution)/shard_map/grad_hidden_part/pallas_call | solution.py:366
  105.0 7.7 %collective-permute-done.16 = f32[192,256]{1,0:T(8,128)S(1)} collective-permute-done((f32[192,256]{1,0:T(8,128)S(1)}, f32[192,256]{1,0:T(8,128)S(1)}, u32[]{:S(2)}, u32[]{:S(2)}) %collective-permute-start.16) | collective-permute-done | bytes 196640 | tf_op jit(solution)/shard_map/ppermute | solution.py:410
  112.7 4.0 %collective-permute-done.17 = f32[192,256]{1,0:T(8,128)S(1)} collective-permute-done((f32[192,256]{1,0:T(8,128)S(1)}, f32[192,256]{1,0:T(8,128)S(1)}, u32[]{:S(2)}, u32[]{:S(2)}) %collective-permute-start.17) | collective-permute-done | bytes 196640 | tf_op jit(solution)/shard_map/ppermute | solution.py:410
  116.8 0.3 collective-permute-start.18
  117.1 5.7 %collective-permute-done.18 = f32[192,256]{1,0:T(8,128)S(1)} collective-permute-done((f32[192,256]{1,0:T(8,128)S(1)}, f32[192,256]{1,0:T(8,128)S(1)}, u32[]{:S(2)}, u32[]{:S(2)}) %collective-permute-start.18) | collective-permute-done | bytes 196640 | tf_op jit(solution)/shard_map/ppermute | solution.py:407
  122.9 1.4 %collective-permute-start.19 = (f32[1,2,64,256]{3,2,1,0:T(8,128)S(1)}, f32[1,2,64,256]{3,2,1,0:T(8,128)S(1)}, u32[]{:S(2)}, u32[]{:S(2)}) collective-permute-start(f32[1,2,64,256]{3,2,1,0:T(8,128)S(1)} %maximum_select_fusion.5), channel_id=1, source_target_pairs={{0,1},{1,0},{2,3},{3,2},{4,5},{5,4},{6,7},{7,6},{8,9},{9,8},{10,11... | collective-permute-start | bytes 393224 | tf_op jit(solution)/shard_map/ppermute | solution.py:452
  124.3 1.7 %collective-permute-start.21 = (f32[64,1024]{1,0:T(8,128)S(1)}, f32[64,1024]{1,0:T(8,128)S(1)}, u32[]{:S(2)}, u32[]{:S(2)}) collective-permute-start(f32[64,1024]{1,0:T(8,128)S(1)} %maximum_multiply_fusion), channel_id=1, source_target_pairs={{0,8},{8,0},{16,24},{24,16},{1,9},{9,1},{17,25},{25,17},{2,10},{10... | collective-permute-start | bytes 786440 | tf_op jit(solution)/shard_map/ppermute | solution.py:452
  126.0 0.8 collective-permute-done.19
  126.8 2.6 %collective-permute-start.20 = (f32[1,2,2,64,256]{4,3,2,1,0:T(8,128)S(1)}, f32[1,2,2,64,256]{4,3,2,1,0:T(8,128)S(1)}, u32[]{:S(2)}, u32[]{:S(2)}) collective-permute-start(f32[1,2,2,64,256]{4,3,2,1,0:T(8,128)S(1)} %maximum_select_fusion.3), channel_id=1, source_target_pairs={{0,8},{8,0},{16,24},{24,16},{1,9},{9,1},{17,25},{25,17},{2,10},{10... | collective-permute-start | bytes 786440 | tf_op jit(solution)/shard_map/ppermute | solution.py:452
  129.4 0.8 maximum_select_fusion.1
  130.2 0.3 collective-permute-done.20
  130.6 0.8 slice_multiply_fusion
  131.4 0.6 slice_reduce_fusion
  (42 shorter events, 0.8 us)
Async XLA Ops:
  0.6 1.6 %copy-start = (bf16[1024,1024]{1,0:T(8,128)(2,1)S(1)}, bf16[1024,1024]{1,0:T(8,128)(2,1)}, u32[]{:S(2)}) copy-start(bf16[1024,1024]{1,0:T(8,128)(2,1)} %w_ref.6) | copy-start | bytes 6291460
  9.1 22.6 %collective-permute-start.4 = (f32[200,512]{1,0:T(8,128)S(1)}, f32[200,512]{1,0:T(8,128)S(1)}, u32[]{:S(2)}, u32[]{:S(2)}) collective-permute-start(f32[200,512]{1,0:T(8,128)S(1)} %get-tuple-element.50.refs_0_), channel_id=1, source_target_pairs={{0,16},{8,24},{16,0},{24,8},{1,17},{9,25},{17,1},{25,9},{2,18},{10... | collective-permute-start | bytes 1228808 | tf_op jit(solution)/shard_map/ppermute | solution.py:407
  19.4 15.0 %collective-permute-start.1 = (f32[200,768]{1,0:T(8,128)S(1)}, f32[200,768]{1,0:T(8,128)S(1)}, u32[]{:S(2)}, u32[]{:S(2)}) collective-permute-start(f32[200,768]{1,0:T(8,128)S(1)} %get-tuple-element.52.f_ref), channel_id=1, source_target_pairs={{0,16},{8,24},{16,0},{24,8},{1,17},{9,25},{17,1},{25,9},{2,18},{10... | collective-permute-start | bytes 1843208 | tf_op jit(solution)/shard_map/ppermute | solution.py:407
  28.8 8.4 %copy-start.1 = (f32[100,2048]{1,0:T(8,128)S(1)}, f32[100,2048]{1,0:T(8,128)}, u32[]{:S(2)}) copy-start(f32[100,2048]{1,0:T(8,128)} %target_ref.3) | copy-start | bytes 2457604
  28.9 8.4 %copy-start.2 = (f32[2048]{0:T(1024)S(1)}, f32[2048]{0:T(1024)}, u32[]{:S(2)}) copy-start(f32[2048]{0:T(1024)} %param.10) | copy-start | bytes 24580
  28.9 8.4 %copy-start.3 = (f32[100]{0:T(128)S(1)}, f32[100]{0:T(128)}, u32[]{:S(2)}) copy-start(f32[100]{0:T(128)} %param.11) | copy-start | bytes 1204
  28.9 18.2 %collective-permute-start.7 = (f32[200,768]{1,0:T(8,128)S(1)}, f32[200,768]{1,0:T(8,128)S(1)}, u32[]{:S(2)}, u32[]{:S(2)}) collective-permute-start(f32[200,768]{1,0:T(8,128)S(1)} %get-tuple-element.54.f_ref), channel_id=1, source_target_pairs={{0,16},{8,24},{16,0},{24,8},{1,17},{9,25},{17,1},{25,9},{2,18},{10... | collective-permute-start | bytes 1843208 | tf_op jit(solution)/shard_map/ppermute | solution.py:407
  30.2 7.1 %collective-permute-start.3 = (f32[200,512]{1,0:T(8,128)S(1)}, f32[200,512]{1,0:T(8,128)S(1)}, u32[]{:S(2)}, u32[]{:S(2)}) collective-permute-start(f32[200,512]{1,0:T(8,128)S(1)} %get-tuple-element.50.refs_0_), channel_id=1, source_target_pairs={{0,8},{8,0},{16,24},{24,16},{1,9},{9,1},{17,25},{25,17},{2,10},{10... | collective-permute-start | bytes 1228808 | tf_op jit(solution)/shard_map/ppermute | solution.py:408
  31.7 5.6 %collective-permute-start.5 = (f32[200,512]{1,0:T(8,128)S(1)}, f32[200,512]{1,0:T(8,128)S(1)}, u32[]{:S(2)}, u32[]{:S(2)}) collective-permute-start(f32[200,512]{1,0:T(8,128)S(1)} %collective-permute-done.4.refs_2_), channel_id=1, source_target_pairs={{0,8},{8,0},{16,24},{24,16},{1,9},{9,1},{17,25},{25,17},{2,10},{10... | collective-permute-start | bytes 1228808 | tf_op jit(solution)/shard_map/ppermute | solution.py:408
  31.7 17.3 %collective-permute-start = (f32[200,768]{1,0:T(8,128)S(1)}, f32[200,768]{1,0:T(8,128)S(1)}, u32[]{:S(2)}, u32[]{:S(2)}) collective-permute-start(f32[200,768]{1,0:T(8,128)S(1)} %get-tuple-element.52.f_ref), channel_id=1, source_target_pairs={{0,8},{8,0},{16,24},{24,16},{1,9},{9,1},{17,25},{25,17},{2,10},{10... | collective-permute-start | bytes 1843208 | tf_op jit(solution)/shard_map/ppermute | solution.py:408
  34.4 24.1 %collective-permute-start.6 = (f32[200,768]{1,0:T(8,128)S(1)}, f32[200,768]{1,0:T(8,128)S(1)}, u32[]{:S(2)}, u32[]{:S(2)}) collective-permute-start(f32[200,768]{1,0:T(8,128)S(1)} %get-tuple-element.54.f_ref), channel_id=1, source_target_pairs={{0,8},{8,0},{16,24},{24,16},{1,9},{9,1},{17,25},{25,17},{2,10},{10... | collective-permute-start | bytes 1843208 | tf_op jit(solution)/shard_map/ppermute | solution.py:408
  37.3 11.7 %collective-permute-start.2 = (f32[200,768]{1,0:T(8,128)S(1)}, f32[200,768]{1,0:T(8,128)S(1)}, u32[]{:S(2)}, u32[]{:S(2)}) collective-permute-start(f32[200,768]{1,0:T(8,128)S(1)} %collective-permute-done.1.fx_ref), channel_id=1, source_target_pairs={{0,8},{8,0},{16,24},{24,16},{1,9},{9,1},{17,25},{25,17},{2,10},{10... | collective-permute-start | bytes 1843208 | tf_op jit(solution)/shard_map/ppermute | solution.py:408
  47.1 11.4 %collective-permute-start.8 = (f32[200,768]{1,0:T(8,128)S(1)}, f32[200,768]{1,0:T(8,128)S(1)}, u32[]{:S(2)}, u32[]{:S(2)}) collective-permute-start(f32[200,768]{1,0:T(8,128)S(1)} %collective-permute-done.7.fx_ref), channel_id=1, source_target_pairs={{0,8},{8,0},{16,24},{24,16},{1,9},{9,1},{17,25},{25,17},{2,10},{10... | collective-permute-start | bytes 1843208 | tf_op jit(solution)/shard_map/ppermute | solution.py:408
  69.1 2.8 %collective-permute-start.9 = (f32[2,2,4,72,256]{4,3,2,1,0:T(8,128)S(1)}, f32[2,2,4,72,256]{4,3,2,1,0:T(8,128)S(1)}, u32[]{:S(2)}, u32[]{:S(2)}) collective-permute-start(f32[2,2,4,72,256]{4,3,2,1,0:T(8,128)S(1)} %get-tuple-element.74), channel_id=1, source_target_pairs={{0,8},{8,0},{16,24},{24,16},{1,9},{9,1},{17,25},{25,17},{2,10},{10... | collective-permute-start | bytes 3538952 | tf_op jit(solution)/shard_map/ppermute | solution.py:408
  69.3 4.3 %collective-permute-start.10 = (f32[2,2,4,72,256]{4,3,2,1,0:T(8,128)S(1)}, f32[2,2,4,72,256]{4,3,2,1,0:T(8,128)S(1)}, u32[]{:S(2)}, u32[]{:S(2)}) collective-permute-start(f32[2,2,4,72,256]{4,3,2,1,0:T(8,128)S(1)} %get-tuple-element.76), channel_id=1, source_target_pairs={{0,8},{8,0},{16,24},{24,16},{1,9},{9,1},{17,25},{25,17},{2,10},{10... | collective-permute-start | bytes 3538952 | tf_op jit(solution)/shard_map/ppermute | solution.py:408
  72.1 14.8 %collective-permute-start.11 = (f32[2,4,72,256]{3,2,1,0:T(8,128)S(1)}, f32[2,4,72,256]{3,2,1,0:T(8,128)S(1)}, u32[]{:S(2)}, u32[]{:S(2)}) collective-permute-start(f32[2,4,72,256]{3,2,1,0:T(8,128)S(1)} %fusion.5), channel_id=1, source_target_pairs={{0,16},{8,24},{16,0},{24,8},{1,17},{9,25},{17,1},{25,9},{2,18},{10... | collective-permute-start | bytes 1769480 | tf_op jit(solution)/shard_map/ppermute | solution.py:407
  73.7 14.8 %collective-permute-start.12 = (f32[2,4,72,256]{3,2,1,0:T(8,128)S(1)}, f32[2,4,72,256]{3,2,1,0:T(8,128)S(1)}, u32[]{:S(2)}, u32[]{:S(2)}) collective-permute-start(f32[2,4,72,256]{3,2,1,0:T(8,128)S(1)} %fusion.4), channel_id=1, source_target_pairs={{0,1},{1,0},{2,3},{3,2},{4,5},{5,4},{6,7},{7,6},{8,9},{9,8},{10,11... | collective-permute-start | bytes 1769480 | tf_op jit(solution)/shard_map/ppermute | solution.py:409
  87.0 7.6 %collective-permute-start.13 = (f32[4,72,256]{2,1,0:T(8,128)S(1)}, f32[4,72,256]{2,1,0:T(8,128)S(1)}, u32[]{:S(2)}, u32[]{:S(2)}) collective-permute-start(f32[4,72,256]{2,1,0:T(8,128)S(1)} %get-tuple-element.91), channel_id=1, source_target_pairs={{0,1},{1,0},{2,3},{3,2},{4,5},{5,4},{6,7},{7,6},{8,9},{9,8},{10,11... | collective-permute-start | bytes 884744 | tf_op jit(solution)/shard_map/ppermute | solution.py:409
  88.7 7.5 %collective-permute-start.14 = (f32[4,72,256]{2,1,0:T(8,128)S(1)}, f32[4,72,256]{2,1,0:T(8,128)S(1)}, u32[]{:S(2)}, u32[]{:S(2)}) collective-permute-start(f32[4,72,256]{2,1,0:T(8,128)S(1)} %get-tuple-element.89), channel_id=1, source_target_pairs={{0,16},{8,24},{16,0},{24,8},{1,17},{9,25},{17,1},{25,9},{2,18},{10... | collective-permute-start | bytes 884744 | tf_op jit(solution)/shard_map/ppermute | solution.py:407
  96.3 8.6 %collective-permute-start.15 = (f32[192,256]{1,0:T(8,128)S(1)}, f32[192,256]{1,0:T(8,128)S(1)}, u32[]{:S(2)}, u32[]{:S(2)}) collective-permute-start(f32[192,256]{1,0:T(8,128)S(1)} %get-tuple-element.111), channel_id=1, source_target_pairs={{0,2},{1,3},{2,4},{3,5},{4,6},{5,7},{6,0},{7,1},{8,10},{9,11},{10,... | collective-permute-start | bytes 589832 | tf_op jit(solution)/shard_map/ppermute | solution.py:410
  97.7 15.0 %collective-permute-start.16 = (f32[192,256]{1,0:T(8,128)S(1)}, f32[192,256]{1,0:T(8,128)S(1)}, u32[]{:S(2)}, u32[]{:S(2)}) collective-permute-start(f32[192,256]{1,0:T(8,128)S(1)} %get-tuple-element.109), channel_id=1, source_target_pairs={{0,4},{1,5},{2,6},{3,7},{4,0},{5,1},{6,2},{7,3},{8,12},{9,13},{10,... | collective-permute-start | bytes 589832 | tf_op jit(solution)/shard_map/ppermute | solution.py:410
  98.8 17.9 %collective-permute-start.17 = (f32[192,256]{1,0:T(8,128)S(1)}, f32[192,256]{1,0:T(8,128)S(1)}, u32[]{:S(2)}, u32[]{:S(2)}) collective-permute-start(f32[192,256]{1,0:T(8,128)S(1)} %get-tuple-element.110), channel_id=1, source_target_pairs={{0,6},{1,7},{2,0},{3,1},{4,2},{5,3},{6,4},{7,5},{8,14},{9,15},{10,... | collective-permute-start | bytes 589832 | tf_op jit(solution)/shard_map/ppermute | solution.py:410
  116.8 6.0 %collective-permute-start.18 = (f32[192,256]{1,0:T(8,128)S(1)}, f32[192,256]{1,0:T(8,128)S(1)}, u32[]{:S(2)}, u32[]{:S(2)}) collective-permute-start(f32[192,256]{1,0:T(8,128)S(1)} %add_add_fusion), channel_id=1, source_target_pairs={{0,16},{8,24},{16,0},{24,8},{1,17},{9,25},{17,1},{25,9},{2,18},{10... | collective-permute-start | bytes 589832 | tf_op jit(solution)/shard_map/ppermute | solution.py:407
  122.9 3.9 %collective-permute-start.19 = (f32[1,2,64,256]{3,2,1,0:T(8,128)S(1)}, f32[1,2,64,256]{3,2,1,0:T(8,128)S(1)}, u32[]{:S(2)}, u32[]{:S(2)}) collective-permute-start(f32[1,2,64,256]{3,2,1,0:T(8,128)S(1)} %maximum_select_fusion.5), channel_id=1, source_target_pairs={{0,1},{1,0},{2,3},{3,2},{4,5},{5,4},{6,7},{7,6},{8,9},{9,8},{10,11... | collective-permute-start | bytes 393224 | tf_op jit(solution)/shard_map/ppermute | solution.py:452
  124.3 5.1 %collective-permute-start.21 = (f32[64,1024]{1,0:T(8,128)S(1)}, f32[64,1024]{1,0:T(8,128)S(1)}, u32[]{:S(2)}, u32[]{:S(2)}) collective-permute-start(f32[64,1024]{1,0:T(8,128)S(1)} %maximum_multiply_fusion), channel_id=1, source_target_pairs={{0,8},{8,0},{16,24},{24,16},{1,9},{9,1},{17,25},{25,17},{2,10},{10... | collective-permute-start | bytes 786440 | tf_op jit(solution)/shard_map/ppermute | solution.py:452
  126.8 3.7 %collective-permute-start.20 = (f32[1,2,2,64,256]{4,3,2,1,0:T(8,128)S(1)}, f32[1,2,2,64,256]{4,3,2,1,0:T(8,128)S(1)}, u32[]{:S(2)}, u32[]{:S(2)}) collective-permute-start(f32[1,2,2,64,256]{4,3,2,1,0:T(8,128)S(1)} %maximum_select_fusion.3), channel_id=1, source_target_pairs={{0,8},{8,0},{16,24},{24,16},{1,9},{9,1},{17,25},{25,17},{2,10},{10... | collective-permute-start | bytes 786440 | tf_op jit(solution)/shard_map/ppermute | solution.py:452

commit v8 on v7

--- a/solution.py
+++ b/solution.py
@@ -8,7 +8,7 @@
 from jax.experimental.pallas import tpu as pltpu
 from jax.sharding import PartitionSpec as P
 
-EIGHTHS = (2, 3, 3)
+EIGHTHS = (2, 2, 2, 2)
 TILE = 256
 EPS = 0.0004
 K0 = math.sqrt(2.0 / math.pi)
@@ -54,8 +54,8 @@
             fill[slab, :] = jnp.dot(
                 w_ref[slab, :], hid_ref[0], preferred_element_type=jnp.float32
             )
-            for r in range(k, k + SLAB, 16):
-                rows = pl.ds(r, 16)
+            for r in range(k, k + SLAB, 32):
+                rows = pl.ds(r, 32)
                 x = drain[rows, :] + jnp.concatenate([bias[rows, :]] * (t // 128), axis=1)
                 q = x * x * K1
                 th = jnp.tanh(x * (K0 + q))
@@ -425,9 +425,12 @@
     spans = [(start, unit * size) for start, size in zip(starts, EIGHTHS)]
     parts = []
     for start, p in spans:
+        w = w_inner
         if parts:
             b_out = after(b_out, parts[-1][2])
-        parts.append(forward(start, p, hidden, w_inner, b_inner, w_out, b_out))
+        else:
+            w = pltpu.with_memory_space_constraint(w_inner, pltpu.HBM)
+        parts.append(forward(start, p, hidden, w, b_inner, w_out, b_out))
     far = [to_x(fields) for _, _, fields in parts]
     near = [to_core(fields) for _, _, fields in parts]
     wt, wot = transposes(after(w_inner, parts[-1][2]), w_out, vp)
@@ -472,6 +475,7 @@
     from_x = to_x(out_x)
     from_y = [to_lo(out_y[k - 1], k) for k in others]
     gh, (keep_x, keep_y) = beside(0, gh, (out_x, out_y), (keep_x, keep_y))
+    gh, (keep_x, keep_y) = beside(1, gh, (out_x, out_y), (keep_x, keep_y))
     own_x = keep_x[0] + got_x[0] + from_x
     own_y = sum(from_y, keep_y[0] + got_y[0])
     own_x, own_y = [own_x[k] for k in range(n_lo)], [own_y[k] for k in range(2)]
@@ -483,7 +487,7 @@
     extra = [part[:, r:].reshape(-1, cx) for part in sums]
     pieces = [jnp.concatenate([part[k, :r] for part in sums] + extra, 0) for k in range(n_hi)]
     from_hi = [to_hi(pieces[k], k) for k in range(1, n_hi)]
-    gh, own = beside(1, gh, pieces[1:], pieces[0])
+    gh, own = beside(3, gh, pieces[1:], pieces[0])
     total = sum(from_hi, own)
     far = to_x(total)
 

time: 134 us -> 134 us (level)
  waiting for transfers between devices: 36.1 us -> 28.8 us
  Pallas kernels: 67 us -> 72.7 us
  starting transfers between devices: 23.2 us -> 25.6 us
  local copies, waits for them, and re-layouts: 1.83 us -> 0.25 us
    ppermute x6 -> x7, waiting for transfers between devices: 18.7 us -> 11.3 us  [shards(): to_x = lambda a: lax.ppermute(a, 'mem', swap_x)]
    ppermute x6 -> x7, starting transfers between devices: 3.85 us -> 8.12 us  [shards(): to_x = lambda a: lax.ppermute(a, 'mem', swap_x)]
    pallas_call x3 -> x4, Pallas kernels: 25 us -> 28.3 us  [forward(): pl.pallas_call(functools.partial(forward_kernel, mloc), grid=(tiles + 1,)...]
    ppermute x8 -> x10, starting transfers between devices: 7.26 us -> 5.57 us  [shards(): to_core = lambda a: lax.ppermute(a, 'mem', swap_core)]
    unnamed x8, local copies, waits for them, and re-layouts: 1.6 us -> 0.02 us
    pallas_call x3 -> x4, Pallas kernels: 26.8 us -> 28.3 us  [backward(): pl.pallas_call(kernel_fn, grid=(p // t,), in_specs=in_specs, out_specs=ou...]
    ppermute x3, waiting for transfers between devices: 11.8 us -> 13.1 us  [shards(): to_hi = lambda a, k: lax.ppermute(a, 'grid', shift_hi(k))]
    ppermute x8 -> x10, waiting for transfers between devices: 3.63 us -> 2.54 us  [shards(): to_core = lambda a: lax.ppermute(a, 'mem', swap_core)]
  transfers between devices with their start and end apart: 22 -> 25, of which waited for: 12 -> 11; matrix products, arithmetic and copies ran while one was open for 1% -> 1% of each run, Pallas kernels for 37% -> 43%
where the time goes in v8:
time: 134 us; the launch traced here: 133 us
  Pallas kernels  72.7 us (54%)
  waiting for transfers between devices  28.8 us (21%)
  starting transfers between devices  25.6 us (19%)
  other arithmetic  3 us (2%)
  between operations  2.74 us (2%)
    pallas_call x4, Pallas kernels, backward(): pl.pallas_call(kernel_fn, grid=(p // t,), in_specs=in_specs, out_specs=ou...  28.3 us
    pallas_call x4, Pallas kernels, forward(): pl.pallas_call(functools.partial(forward_kernel, mloc), grid=(tiles + 1,)...  28.3 us
    pallas_call x4, Pallas kernels, input_gradient(): pl.pallas_call(input_kernel, grid=(steps,), in_specs=in_specs, out_specs=...  13.9 us
    ppermute x3, waiting for transfers between devices, shards(): to_hi = lambda a, k: lax.ppermute(a, 'grid', shift_hi(k))  13.1 us
    ppermute x7, waiting for transfers between devices, shards(): to_x = lambda a: lax.ppermute(a, 'mem', swap_x)  11.3 us
    ppermute x7, starting transfers between devices, shards(): to_x = lambda a: lax.ppermute(a, 'mem', swap_x)  8.12 us
    ppermute x10, starting transfers between devices, shards(): to_core = lambda a: lax.ppermute(a, 'mem', swap_core)  5.57 us
    ppermute x3, starting transfers between devices, gathered(): other = lax.ppermute(block, name, [(i, i ^ bit) for i in range(n)])  5.52 us
  transfers between devices with their start and end apart: 25, of which 11 were waited for; matrix products, arithmetic and copies ran while one was open for 1% of the time, Pallas kernels for 43%

profile of v8, /device:TPU:9, one launch (start us, length us, event | category | flops | bytes accessed | tf_op | source)
XLA Modules:
  0.0 133.1 jit_solution(14324364711691743392)
XLA Ops:
  0.7 7.7 %forward_part.4 = (bf16[2,2,1024,256]{3,2,1,0:T(8,128)(2,1)S(1)}, f32[2,2,1024,256]{3,2,1,0:T(8,128)S(1)}, f32[200,512]{1,0:T(8,128)S(1)}) custom-call(bf16[2,1024,2048]{2,1,0:T(8,128)(2,1)} %hid_ref.6, bf16[1024,1024]{1,0:T(8,128)(2,1)} %w_ref.8, f32[1,1024]{1,0:T(1,128)} %bitcast.75, bf16[100,1024]{1,0:T(8,128)(2,1)} %wo_ref.9, f32[1,100]{1,0:T(1,128)} %bitcast.79), custom_call_target="tpu_custom_call" | custom-call | flops 2097152 | bytes 2097152 | tf_op jit(solution)/shard_map/forward_part/pallas_call | solution.py:96
  8.4 1.3 collective-permute-start.6
  9.7 6.9 %forward_part.5 = (bf16[2,2,1024,256]{3,2,1,0:T(8,128)(2,1)S(1)}, f32[2,2,1024,256]{3,2,1,0:T(8,128)S(1)}, f32[200,512]{1,0:T(8,128)S(1)}) custom-call(bf16[2,1024,2048]{2,1,0:T(8,128)(2,1)} %hid_ref.6, bf16[1024,1024]{1,0:T(8,128)(2,1)S(1)} %copy-done, f32[1,1024]{1,0:T(1,128)} %bitcast.76, bf16[100,1024]{1,0:T(8,128)(2,1)} %wo_ref.9, f32[1,100]{1,0:T(1,128)} %bitcast.80), custom_call_target="tpu_custom_call" | custom-call | flops 2097152 | bytes 2097152 | tf_op jit(solution)/shard_map/forward_part/pallas_call | solution.py:96
  16.5 0.3 collective-permute-start.3
  16.8 1.2 collective-permute-start.5
  18.1 0.7 collective-permute-done.6.refs_2_
  18.8 2.1 %collective-permute-start.7 = (f32[200,512]{1,0:T(8,128)S(1)}, f32[200,512]{1,0:T(8,128)S(1)}, u32[]{:S(2)}, u32[]{:S(2)}) collective-permute-start(f32[200,512]{1,0:T(8,128)S(1)} %collective-permute-done.6.refs_2_), channel_id=1, source_target_pairs={{0,8},{8,0},{16,24},{24,16},{1,9},{9,1},{17,25},{25,17},{2,10},{10... | collective-permute-start | bytes 1228808 | tf_op jit(solution)/shard_map/ppermute | solution.py:408
  20.9 6.9 %forward_part.6 = (bf16[2,2,1024,256]{3,2,1,0:T(8,128)(2,1)S(1)}, f32[2,2,1024,256]{3,2,1,0:T(8,128)S(1)}, f32[200,512]{1,0:T(8,128)S(1)}) custom-call(bf16[2,1024,2048]{2,1,0:T(8,128)(2,1)} %hid_ref.6, bf16[1024,1024]{1,0:T(8,128)(2,1)S(1)} %copy-done, f32[1,1024]{1,0:T(1,128)} %bitcast.77, bf16[100,1024]{1,0:T(8,128)(2,1)} %wo_ref.9, f32[1,100]{1,0:T(1,128)} %bitcast.81), custom_call_target="tpu_custom_call" | custom-call | flops 2097152 | bytes 2097152 | tf_op jit(solution)/shard_map/forward_part/pallas_call | solution.py:96
  27.8 1.9 %collective-permute-start.10 = (f32[200,512]{1,0:T(8,128)S(1)}, f32[200,512]{1,0:T(8,128)S(1)}, u32[]{:S(2)}, u32[]{:S(2)}) collective-permute-start(f32[200,512]{1,0:T(8,128)S(1)} %get-tuple-element.66.f_ref), channel_id=1, source_target_pairs={{0,16},{8,24},{16,0},{24,8},{1,17},{9,25},{17,1},{25,9},{2,18},{10... | collective-permute-start | bytes 1228808 | tf_op jit(solution)/shard_map/ppermute | solution.py:407
  29.6 6.9 %forward_part.7 = (bf16[2,2,1024,256]{3,2,1,0:T(8,128)(2,1)S(1)}, f32[2,2,1024,256]{3,2,1,0:T(8,128)S(1)}, f32[200,512]{1,0:T(8,128)S(1)}) custom-call(bf16[2,1024,2048]{2,1,0:T(8,128)(2,1)} %hid_ref.6, bf16[1024,1024]{1,0:T(8,128)(2,1)S(1)} %copy-done, f32[1,1024]{1,0:T(1,128)} %bitcast.78, bf16[100,1024]{1,0:T(8,128)(2,1)} %wo_ref.9, f32[1,100]{1,0:T(1,128)} %bitcast.82), custom_call_target="tpu_custom_call" | custom-call | flops 2097152 | bytes 2097152 | tf_op jit(solution)/shard_map/forward_part/pallas_call | solution.py:96
  36.5 0.3 collective-permute-start.4
  36.9 2.2 %transposes.1 = (bf16[1024,1024]{1,0:T(8,128)(2,1)S(1)}, bf16[1024,128]{1,0:T(8,128)(2,1)S(1)}) custom-call(bf16[1024,1024]{1,0:T(8,128)(2,1)S(1)} %copy-done, bf16[100,1024]{1,0:T(8,128)(2,1)} %wo_ref.9), custom_call_target="tpu_custom_call" | custom-call | flops 2048 | bytes 2048 | tf_op jit(solution)/shard_map/transposes/pallas_call | solution.py:326
  39.1 0.6 collective-permute-start.9
  39.7 6.8 %backward_part.4 = (bf16[2,1024,512]{2,1,0:T(8,128)(2,1)S(1)}, f32[128,1024]{1,0:T(8,128)S(1)}, f32[1024,1024]{1,0:T(8,128)S(1)}) custom-call(f32[200,512]{1,0:T(8,128)S(1)} %get-tuple-element.62.refs_0_, f32[200,512]{1,0:T(8,128)S(1)} %collective-permute-done.5.refs_1_, f32[200,512]{1,0:T(8,128)S(1)} %collective-permute-done.6.refs_2_, ...), custom_call_target="tpu_custom_call" | custom-call | flops 2097152 | bytes 2097152 | tf_op jit(solution)/shard_map/backward_part/pallas_call | solution.py:295
  46.7 0.5 collective-permute-start.11
  47.2 6.7 %backward_part.5 = (bf16[2,1024,512]{2,1,0:T(8,128)(2,1)S(1)}, f32[128,1024]{1,0:T(8,128)S(1)}, f32[1024,1024]{1,0:T(8,128)S(1)}) custom-call(f32[200,512]{1,0:T(8,128)S(1)} %get-tuple-element.64.f_ref, f32[200,512]{1,0:T(8,128)S(1)} %collective-permute-done.2.fc_ref, ...), custom_call_target="tpu_custom_call", output_to_operand_aliasing={{2}: (11, {})} | custom-call | flops 2097152 | bytes 2097152 | tf_op jit(solution)/shard_map/backward_part/pallas_call | solution.py:295
  53.9 0.1 collective-permute-start.8
  54.0 6.7 %backward_part.6 = (bf16[2,1024,512]{2,1,0:T(8,128)(2,1)S(1)}, f32[128,1024]{1,0:T(8,128)S(1)}, f32[1024,1024]{1,0:T(8,128)S(1)}) custom-call(f32[200,512]{1,0:T(8,128)S(1)} %get-tuple-element.66.f_ref, f32[200,512]{1,0:T(8,128)S(1)} %collective-permute-done.9.fc_ref, ...), custom_call_target="tpu_custom_call", output_to_operand_aliasing={{2}: (11, {})} | custom-call | flops 2097152 | bytes 2097152 | tf_op jit(solution)/shard_map/backward_part/pallas_call | solution.py:295
  60.8 8.1 %backward_part.7 = (bf16[2,1024,512]{2,1,0:T(8,128)(2,1)S(1)}, f32[128,1024]{1,0:T(8,128)}, f32[1024,1024]{1,0:T(8,128)S(1)}, f32[2,2,4,72,256]{4,3,2,1,0:T(8,12...) custom-call(f32[200,512]{1,0:T(8,128)S(1)} %get-tuple-element.68.f_r, ...), custom_call_target="tpu_custom_call", output_to_operand_aliasing={{2}: (11, {})} | custom-call | flops 2097152 | bytes 2097152 | tf_op jit(solution)/shard_map/backward_part/pallas_call | solution.py:295
  68.8 0.4 collective-permute-start.12
  69.3 2.4 %collective-permute-done.12 = f32[2,2,4,72,256]{4,3,2,1,0:T(8,128)S(1)} collective-permute-done((f32[2,2,4,72,256]{4,3,2,1,0:T(8,128)S(1)}, f32[2,2,4,72,256]{4,3,2,1,0:T(8,128)S(1)}, u32[]{:S(2)}, u32[]{:S(2)}) %collective-permute-start.12) | collective-permute-done | bytes 1179680 | tf_op jit(solution)/shard_map/ppermute | solution.py:408
  71.8 1.5 %collective-permute-start.14 = (f32[2,4,72,256]{3,2,1,0:T(8,128)S(1)}, f32[2,4,72,256]{3,2,1,0:T(8,128)S(1)}, u32[]{:S(2)}, u32[]{:S(2)}) collective-permute-start(f32[2,4,72,256]{3,2,1,0:T(8,128)S(1)} %fusion.5), channel_id=1, source_target_pairs={{0,16},{8,24},{16,0},{24,8},{1,17},{9,25},{17,1},{25,9},{2,18},{10... | collective-permute-start | bytes 1769480 | tf_op jit(solution)/shard_map/ppermute | solution.py:407
  73.3 0.1 collective-permute-done.13
  73.5 1.3 collective-permute-start.15
  74.8 3.5 %grad_hidden_part.4.refs_0_ = bf16[2,1024,2048]{2,1,0:T(8,128)(2,1)} custom-call(bf16[1024,1024]{1,0:T(8,128)(2,1)S(1)} %get-tuple-element.70.wt_ref, bf16[2,1024,512]{2,1,0:T(8,128)(2,1)S(1)} %get-tuple-element.98.gp_ref), custom_call_target="tpu_custom_call" | custom-call | flops 2097152 | bytes 2097152 | tf_op jit(solution)/shard_map/grad_hidden_part/pallas_call | solution.py:366
  78.3 3.5 %grad_hidden_part.5.refs_0_ = bf16[2,1024,2048]{2,1,0:T(8,128)(2,1)} custom-call(bf16[1024,1024]{1,0:T(8,128)(2,1)S(1)} %get-tuple-element.70.wt_ref, bf16[2,1024,512]{2,1,0:T(8,128)(2,1)S(1)} %get-tuple-element.97.gp_ref, bf16[2,1024,2048]{2,1,0:T(8,128)(2,1)} %grad_hidden_part.4.refs_0_), custom_call_target="tpu_custom_call", output_to_operand_aliasing={{}: (2, {})} | custom-call | flops 2097152 | bytes 2097152 | tf_op jit(solution)/shard_map/grad_hidden_part/pallas_call | solution.py:366
  81.7 4.7 %collective-permute-done.14 = f32[2,4,72,256]{3,2,1,0:T(8,128)S(1)} collective-permute-done((f32[2,4,72,256]{3,2,1,0:T(8,128)S(1)}, f32[2,4,72,256]{3,2,1,0:T(8,128)S(1)}, u32[]{:S(2)}, u32[]{:S(2)}) %collective-permute-start.14) | collective-permute-done | bytes 589856 | tf_op jit(solution)/shard_map/ppermute | solution.py:407
  86.6 1.3 collective-permute-start.16
  88.1 1.6 %collective-permute-start.17 = (f32[4,72,256]{2,1,0:T(8,128)S(1)}, f32[4,72,256]{2,1,0:T(8,128)S(1)}, u32[]{:S(2)}, u32[]{:S(2)}) collective-permute-start(f32[4,72,256]{2,1,0:T(8,128)S(1)} %get-tuple-element.113), channel_id=1, source_target_pairs={{0,16},{8,24},{16,0},{24,8},{1,17},{9,25},{17,1},{25,9},{2,18},{10... | collective-permute-start | bytes 884744 | tf_op jit(solution)/shard_map/ppermute | solution.py:407
  89.7 3.5 %grad_hidden_part.6.refs_0_ = bf16[2,1024,2048]{2,1,0:T(8,128)(2,1)} custom-call(bf16[1024,1024]{1,0:T(8,128)(2,1)S(1)} %get-tuple-element.70.wt_ref, bf16[2,1024,512]{2,1,0:T(8,128)(2,1)S(1)} %get-tuple-element.104.gp_ref, bf16[2,1024,2048]{2,1,0:T(8,128)(2,1)} %grad_hidden_part.5.refs_0_), custom_call_target="tpu_custom_call", output_to_operand_aliasing={{}: (2, {})} | custom-call | flops 2097152 | bytes 2097152 | tf_op jit(solution)/shard_map/grad_hidden_part/pallas_call | solution.py:366
  93.2 0.7 collective-permute-done.16
  94.0 1.4 %collective-permute-done.17 = f32[4,72,256]{2,1,0:T(8,128)S(1)} collective-permute-done((f32[4,72,256]{2,1,0:T(8,128)S(1)}, f32[4,72,256]{2,1,0:T(8,128)S(1)}, u32[]{:S(2)}, u32[]{:S(2)}) %collective-permute-start.17) | collective-permute-done | bytes 294944 | tf_op jit(solution)/shard_map/ppermute | solution.py:407
  95.6 1.4 %collective-permute-start.18 = (f32[192,256]{1,0:T(8,128)S(1)}, f32[192,256]{1,0:T(8,128)S(1)}, u32[]{:S(2)}, u32[]{:S(2)}) collective-permute-start(f32[192,256]{1,0:T(8,128)S(1)} %get-tuple-element.135), channel_id=1, source_target_pairs={{0,2},{1,3},{2,4},{3,5},{4,6},{5,7},{6,0},{7,1},{8,10},{9,11},{10,... | collective-permute-start | bytes 589832 | tf_op jit(solution)/shard_map/ppermute | solution.py:410
  96.9 1.1 collective-permute-start.19
  98.0 1.4 %collective-permute-start.20 = (f32[192,256]{1,0:T(8,128)S(1)}, f32[192,256]{1,0:T(8,128)S(1)}, u32[]{:S(2)}, u32[]{:S(2)}) collective-permute-start(f32[192,256]{1,0:T(8,128)S(1)} %get-tuple-element.134), channel_id=1, source_target_pairs={{0,6},{1,7},{2,0},{3,1},{4,2},{5,3},{6,4},{7,5},{8,14},{9,15},{10,... | collective-permute-start | bytes 589832 | tf_op jit(solution)/shard_map/ppermute | solution.py:410
  99.4 3.5 %grad_hidden_part.7 = bf16[2,1024,2048]{2,1,0:T(8,128)(2,1)} custom-call(bf16[1024,1024]{1,0:T(8,128)(2,1)S(1)} %get-tuple-element.70.wt_ref, bf16[2,1024,512]{2,1,0:T(8,128)(2,1)S(1)} %get-tuple-element.108.gp_ref, bf16[2,1024,2048]{2,1,0:T(8,128)(2,1)} %grad_hidden_part.6.refs_0_), custom_call_target="tpu_custom_call", output_to_operand_aliasing={{}: (2, {})} | custom-call | flops 2097152 | bytes 2097152 | tf_op jit(solution)/shard_map/grad_hidden_part/pallas_call | solution.py:366
  102.9 9.0 %collective-permute-done.19 = f32[192,256]{1,0:T(8,128)S(1)} collective-permute-done((f32[192,256]{1,0:T(8,128)S(1)}, f32[192,256]{1,0:T(8,128)S(1)}, u32[]{:S(2)}, u32[]{:S(2)}) %collective-permute-start.19) | collective-permute-done | bytes 196640 | tf_op jit(solution)/shard_map/ppermute | solution.py:410
  111.9 4.1 %collective-permute-done.20 = f32[192,256]{1,0:T(8,128)S(1)} collective-permute-done((f32[192,256]{1,0:T(8,128)S(1)}, f32[192,256]{1,0:T(8,128)S(1)}, u32[]{:S(2)}, u32[]{:S(2)}) %collective-permute-start.20) | collective-permute-done | bytes 196640 | tf_op jit(solution)/shard_map/ppermute | solution.py:410
  116.1 1.6 %collective-permute-start.21 = (f32[192,256]{1,0:T(8,128)S(1)}, f32[192,256]{1,0:T(8,128)S(1)}, u32[]{:S(2)}, u32[]{:S(2)}) collective-permute-start(f32[192,256]{1,0:T(8,128)S(1)} %add_add_fusion), channel_id=1, source_target_pairs={{0,16},{8,24},{16,0},{24,8},{1,17},{9,25},{17,1},{25,9},{2,18},{10... | collective-permute-start | bytes 589832 | tf_op jit(solution)/shard_map/ppermute | solution.py:407
  117.6 4.5 %collective-permute-done.21 = f32[192,256]{1,0:T(8,128)S(1)} collective-permute-done((f32[192,256]{1,0:T(8,128)S(1)}, f32[192,256]{1,0:T(8,128)S(1)}, u32[]{:S(2)}, u32[]{:S(2)}) %collective-permute-start.21) | collective-permute-done | bytes 196640 | tf_op jit(solution)/shard_map/ppermute | solution.py:407
  122.2 1.4 %collective-permute-start.22 = (f32[1,2,64,256]{3,2,1,0:T(8,128)S(1)}, f32[1,2,64,256]{3,2,1,0:T(8,128)S(1)}, u32[]{:S(2)}, u32[]{:S(2)}) collective-permute-start(f32[1,2,64,256]{3,2,1,0:T(8,128)S(1)} %maximum_select_fusion.5), channel_id=1, source_target_pairs={{0,1},{1,0},{2,3},{3,2},{4,5},{5,4},{6,7},{7,6},{8,9},{9,8},{10,11... | collective-permute-start | bytes 393224 | tf_op jit(solution)/shard_map/ppermute | solution.py:455
  123.7 1.6 %collective-permute-start.24 = (f32[64,1024]{1,0:T(8,128)S(1)}, f32[64,1024]{1,0:T(8,128)S(1)}, u32[]{:S(2)}, u32[]{:S(2)}) collective-permute-start(f32[64,1024]{1,0:T(8,128)S(1)} %maximum_multiply_fusion), channel_id=1, source_target_pairs={{0,8},{8,0},{16,24},{24,16},{1,9},{9,1},{17,25},{25,17},{2,10},{10... | collective-permute-start | bytes 786440 | tf_op jit(solution)/shard_map/ppermute | solution.py:455
  125.3 0.8 collective-permute-done.22
  126.1 2.5 %collective-permute-start.23 = (f32[1,2,2,64,256]{4,3,2,1,0:T(8,128)S(1)}, f32[1,2,2,64,256]{4,3,2,1,0:T(8,128)S(1)}, u32[]{:S(2)}, u32[]{:S(2)}) collective-permute-start(f32[1,2,2,64,256]{4,3,2,1,0:T(8,128)S(1)} %maximum_select_fusion.3), channel_id=1, source_target_pairs={{0,8},{8,0},{16,24},{24,16},{1,9},{9,1},{17,25},{25,17},{2,10},{10... | collective-permute-start | bytes 786440 | tf_op jit(solution)/shard_map/ppermute | solution.py:455
  128.7 0.8 maximum_select_fusion.1
  129.6 0.3 collective-permute-done.23
  129.9 0.8 slice_multiply_fusion
  130.7 0.6 slice_reduce_fusion
  (51 shorter events, 1.3 us)
Async XLA Ops:
  0.6 9.0 %copy-start = (bf16[1024,1024]{1,0:T(8,128)(2,1)S(1)}, bf16[1024,1024]{1,0:T(8,128)(2,1)}, u32[]{:S(2)}) copy-start(bf16[1024,1024]{1,0:T(8,128)(2,1)} %w_ref.8) | copy-start | bytes 6291460
  8.4 10.4 %collective-permute-start.6 = (f32[200,512]{1,0:T(8,128)S(1)}, f32[200,512]{1,0:T(8,128)S(1)}, u32[]{:S(2)}, u32[]{:S(2)}) collective-permute-start(f32[200,512]{1,0:T(8,128)S(1)} %get-tuple-element.62.refs_0_), channel_id=1, source_target_pairs={{0,16},{8,24},{16,0},{24,8},{1,17},{9,25},{17,1},{25,9},{2,18},{10... | collective-permute-start | bytes 1228808 | tf_op jit(solution)/shard_map/ppermute | solution.py:407
  16.5 20.0 %collective-permute-start.3 = (f32[200,512]{1,0:T(8,128)S(1)}, f32[200,512]{1,0:T(8,128)S(1)}, u32[]{:S(2)}, u32[]{:S(2)}) collective-permute-start(f32[200,512]{1,0:T(8,128)S(1)} %get-tuple-element.64.f_ref), channel_id=1, source_target_pairs={{0,16},{8,24},{16,0},{24,8},{1,17},{9,25},{17,1},{25,9},{2,18},{10... | collective-permute-start | bytes 1228808 | tf_op jit(solution)/shard_map/ppermute | solution.py:407
  16.8 20.0 %collective-permute-start.5 = (f32[200,512]{1,0:T(8,128)S(1)}, f32[200,512]{1,0:T(8,128)S(1)}, u32[]{:S(2)}, u32[]{:S(2)}) collective-permute-start(f32[200,512]{1,0:T(8,128)S(1)} %get-tuple-element.62.refs_0_), channel_id=1, source_target_pairs={{0,8},{8,0},{16,24},{24,16},{1,9},{9,1},{17,25},{25,17},{2,10},{10... | collective-permute-start | bytes 1228808 | tf_op jit(solution)/shard_map/ppermute | solution.py:408
  18.1 28.6 %collective-permute-start.2 = (f32[200,512]{1,0:T(8,128)S(1)}, f32[200,512]{1,0:T(8,128)S(1)}, u32[]{:S(2)}, u32[]{:S(2)}) collective-permute-start(f32[200,512]{1,0:T(8,128)S(1)} %get-tuple-element.64.f_ref), channel_id=1, source_target_pairs={{0,8},{8,0},{16,24},{24,16},{1,9},{9,1},{17,25},{25,17},{2,10},{10... | collective-permute-start | bytes 1228808 | tf_op jit(solution)/shard_map/ppermute | solution.py:408
  18.8 20.3 %collective-permute-start.7 = (f32[200,512]{1,0:T(8,128)S(1)}, f32[200,512]{1,0:T(8,128)S(1)}, u32[]{:S(2)}, u32[]{:S(2)}) collective-permute-start(f32[200,512]{1,0:T(8,128)S(1)} %collective-permute-done.6.refs_2_), channel_id=1, source_target_pairs={{0,8},{8,0},{16,24},{24,16},{1,9},{9,1},{17,25},{25,17},{2,10},{10... | collective-permute-start | bytes 1228808 | tf_op jit(solution)/shard_map/ppermute | solution.py:408
  27.8 18.8 %collective-permute-start.10 = (f32[200,512]{1,0:T(8,128)S(1)}, f32[200,512]{1,0:T(8,128)S(1)}, u32[]{:S(2)}, u32[]{:S(2)}) collective-permute-start(f32[200,512]{1,0:T(8,128)S(1)} %get-tuple-element.66.f_ref), channel_id=1, source_target_pairs={{0,16},{8,24},{16,0},{24,8},{1,17},{9,25},{17,1},{25,9},{2,18},{10... | collective-permute-start | bytes 1228808 | tf_op jit(solution)/shard_map/ppermute | solution.py:407
  36.5 3.2 %copy-start.1 = (f32[100,2048]{1,0:T(8,128)S(1)}, f32[100,2048]{1,0:T(8,128)}, u32[]{:S(2)}) copy-start(f32[100,2048]{1,0:T(8,128)} %target_ref.5) | copy-start | bytes 2457604
  36.5 3.2 %copy-start.2 = (f32[2048]{0:T(1024)S(1)}, f32[2048]{0:T(1024)}, u32[]{:S(2)}) copy-start(f32[2048]{0:T(1024)} %param.10) | copy-start | bytes 24580
  36.5 3.2 %copy-start.3 = (f32[100]{0:T(128)S(1)}, f32[100]{0:T(128)}, u32[]{:S(2)}) copy-start(f32[100]{0:T(128)} %param.11) | copy-start | bytes 1204
  36.5 10.6 %collective-permute-start.4 = (f32[200,512]{1,0:T(8,128)S(1)}, f32[200,512]{1,0:T(8,128)S(1)}, u32[]{:S(2)}, u32[]{:S(2)}) collective-permute-start(f32[200,512]{1,0:T(8,128)S(1)} %collective-permute-done.3.fx_ref), channel_id=1, source_target_pairs={{0,8},{8,0},{16,24},{24,16},{1,9},{9,1},{17,25},{25,17},{2,10},{10... | collective-permute-start | bytes 1228808 | tf_op jit(solution)/shard_map/ppermute | solution.py:408
  36.9 17.0 %collective-permute-start.1 = (f32[200,512]{1,0:T(8,128)S(1)}, f32[200,512]{1,0:T(8,128)S(1)}, u32[]{:S(2)}, u32[]{:S(2)}) collective-permute-start(f32[200,512]{1,0:T(8,128)S(1)} %get-tuple-element.68.f_ref), channel_id=1, source_target_pairs={{0,16},{8,24},{16,0},{24,8},{1,17},{9,25},{17,1},{25,9},{2,18},{10... | collective-permute-start | bytes 1228808 | tf_op jit(solution)/shard_map/ppermute | solution.py:407
  39.1 14.9 %collective-permute-start.9 = (f32[200,512]{1,0:T(8,128)S(1)}, f32[200,512]{1,0:T(8,128)S(1)}, u32[]{:S(2)}, u32[]{:S(2)}) collective-permute-start(f32[200,512]{1,0:T(8,128)S(1)} %get-tuple-element.66.f_ref), channel_id=1, source_target_pairs={{0,8},{8,0},{16,24},{24,16},{1,9},{9,1},{17,25},{25,17},{2,10},{10... | collective-permute-start | bytes 1228808 | tf_op jit(solution)/shard_map/ppermute | solution.py:408
  46.6 14.2 %collective-permute-start = (f32[200,512]{1,0:T(8,128)S(1)}, f32[200,512]{1,0:T(8,128)S(1)}, u32[]{:S(2)}, u32[]{:S(2)}) collective-permute-start(f32[200,512]{1,0:T(8,128)S(1)} %get-tuple-element.68.f_ref), channel_id=1, source_target_pairs={{0,8},{8,0},{16,24},{24,16},{1,9},{9,1},{17,25},{25,17},{2,10},{10... | collective-permute-start | bytes 1228808 | tf_op jit(solution)/shard_map/ppermute | solution.py:408
  46.7 7.3 %collective-permute-start.11 = (f32[200,512]{1,0:T(8,128)S(1)}, f32[200,512]{1,0:T(8,128)S(1)}, u32[]{:S(2)}, u32[]{:S(2)}) collective-permute-start(f32[200,512]{1,0:T(8,128)S(1)} %collective-permute-done.10.fx_ref), channel_id=1, source_target_pairs={{0,8},{8,0},{16,24},{24,16},{1,9},{9,1},{17,25},{25,17},{2,10},{10... | collective-permute-start | bytes 1228808 | tf_op jit(solution)/shard_map/ppermute | solution.py:408
  53.9 6.9 %collective-permute-start.8 = (f32[200,512]{1,0:T(8,128)S(1)}, f32[200,512]{1,0:T(8,128)S(1)}, u32[]{:S(2)}, u32[]{:S(2)}) collective-permute-start(f32[200,512]{1,0:T(8,128)S(1)} %collective-permute-done.1.fx_ref), channel_id=1, source_target_pairs={{0,8},{8,0},{16,24},{24,16},{1,9},{9,1},{17,25},{25,17},{2,10},{10... | collective-permute-start | bytes 1228808 | tf_op jit(solution)/shard_map/ppermute | solution.py:408
  68.8 2.9 %collective-permute-start.12 = (f32[2,2,4,72,256]{4,3,2,1,0:T(8,128)S(1)}, f32[2,2,4,72,256]{4,3,2,1,0:T(8,128)S(1)}, u32[]{:S(2)}, u32[]{:S(2)}) collective-permute-start(f32[2,2,4,72,256]{4,3,2,1,0:T(8,128)S(1)} %get-tuple-element.94), channel_id=1, source_target_pairs={{0,8},{8,0},{16,24},{24,16},{1,9},{9,1},{17,25},{25,17},{2,10},{10... | collective-permute-start | bytes 3538952 | tf_op jit(solution)/shard_map/ppermute | solution.py:408
  69.2 4.2 %collective-permute-start.13 = (f32[2,2,4,72,256]{4,3,2,1,0:T(8,128)S(1)}, f32[2,2,4,72,256]{4,3,2,1,0:T(8,128)S(1)}, u32[]{:S(2)}, u32[]{:S(2)}) collective-permute-start(f32[2,2,4,72,256]{4,3,2,1,0:T(8,128)S(1)} %get-tuple-element.96), channel_id=1, source_target_pairs={{0,8},{8,0},{16,24},{24,16},{1,9},{9,1},{17,25},{25,17},{2,10},{10... | collective-permute-start | bytes 3538952 | tf_op jit(solution)/shard_map/ppermute | solution.py:408
  71.8 14.6 %collective-permute-start.14 = (f32[2,4,72,256]{3,2,1,0:T(8,128)S(1)}, f32[2,4,72,256]{3,2,1,0:T(8,128)S(1)}, u32[]{:S(2)}, u32[]{:S(2)}) collective-permute-start(f32[2,4,72,256]{3,2,1,0:T(8,128)S(1)} %fusion.5), channel_id=1, source_target_pairs={{0,16},{8,24},{16,0},{24,8},{1,17},{9,25},{17,1},{25,9},{2,18},{10... | collective-permute-start | bytes 1769480 | tf_op jit(solution)/shard_map/ppermute | solution.py:407
  73.5 14.4 %collective-permute-start.15 = (f32[2,4,72,256]{3,2,1,0:T(8,128)S(1)}, f32[2,4,72,256]{3,2,1,0:T(8,128)S(1)}, u32[]{:S(2)}, u32[]{:S(2)}) collective-permute-start(f32[2,4,72,256]{3,2,1,0:T(8,128)S(1)} %fusion.4), channel_id=1, source_target_pairs={{0,1},{1,0},{2,3},{3,2},{4,5},{5,4},{6,7},{7,6},{8,9},{9,8},{10,11... | collective-permute-start | bytes 1769480 | tf_op jit(solution)/shard_map/ppermute | solution.py:409
  86.6 7.4 %collective-permute-start.16 = (f32[4,72,256]{2,1,0:T(8,128)S(1)}, f32[4,72,256]{2,1,0:T(8,128)S(1)}, u32[]{:S(2)}, u32[]{:S(2)}) collective-permute-start(f32[4,72,256]{2,1,0:T(8,128)S(1)} %get-tuple-element.115), channel_id=1, source_target_pairs={{0,1},{1,0},{2,3},{3,2},{4,5},{5,4},{6,7},{7,6},{8,9},{9,8},{10,11... | collective-permute-start | bytes 884744 | tf_op jit(solution)/shard_map/ppermute | solution.py:409
  88.1 7.4 %collective-permute-start.17 = (f32[4,72,256]{2,1,0:T(8,128)S(1)}, f32[4,72,256]{2,1,0:T(8,128)S(1)}, u32[]{:S(2)}, u32[]{:S(2)}) collective-permute-start(f32[4,72,256]{2,1,0:T(8,128)S(1)} %get-tuple-element.113), channel_id=1, source_target_pairs={{0,16},{8,24},{16,0},{24,8},{1,17},{9,25},{17,1},{25,9},{2,18},{10... | collective-permute-start | bytes 884744 | tf_op jit(solution)/shard_map/ppermute | solution.py:407
  95.6 7.3 %collective-permute-start.18 = (f32[192,256]{1,0:T(8,128)S(1)}, f32[192,256]{1,0:T(8,128)S(1)}, u32[]{:S(2)}, u32[]{:S(2)}) collective-permute-start(f32[192,256]{1,0:T(8,128)S(1)} %get-tuple-element.135), channel_id=1, source_target_pairs={{0,2},{1,3},{2,4},{3,5},{4,6},{5,7},{6,0},{7,1},{8,10},{9,11},{10,... | collective-permute-start | bytes 589832 | tf_op jit(solution)/shard_map/ppermute | solution.py:410
  96.9 15.0 %collective-permute-start.19 = (f32[192,256]{1,0:T(8,128)S(1)}, f32[192,256]{1,0:T(8,128)S(1)}, u32[]{:S(2)}, u32[]{:S(2)}) collective-permute-start(f32[192,256]{1,0:T(8,128)S(1)} %get-tuple-element.133), channel_id=1, source_target_pairs={{0,4},{1,5},{2,6},{3,7},{4,0},{5,1},{6,2},{7,3},{8,12},{9,13},{10,... | collective-permute-start | bytes 589832 | tf_op jit(solution)/shard_map/ppermute | solution.py:410
  98.0 18.0 %collective-permute-start.20 = (f32[192,256]{1,0:T(8,128)S(1)}, f32[192,256]{1,0:T(8,128)S(1)}, u32[]{:S(2)}, u32[]{:S(2)}) collective-permute-start(f32[192,256]{1,0:T(8,128)S(1)} %get-tuple-element.134), channel_id=1, source_target_pairs={{0,6},{1,7},{2,0},{3,1},{4,2},{5,3},{6,4},{7,5},{8,14},{9,15},{10,... | collective-permute-start | bytes 589832 | tf_op jit(solution)/shard_map/ppermute | solution.py:410
  116.1 6.1 %collective-permute-start.21 = (f32[192,256]{1,0:T(8,128)S(1)}, f32[192,256]{1,0:T(8,128)S(1)}, u32[]{:S(2)}, u32[]{:S(2)}) collective-permute-start(f32[192,256]{1,0:T(8,128)S(1)} %add_add_fusion), channel_id=1, source_target_pairs={{0,16},{8,24},{16,0},{24,8},{1,17},{9,25},{17,1},{25,9},{2,18},{10... | collective-permute-start | bytes 589832 | tf_op jit(solution)/shard_map/ppermute | solution.py:407
  122.2 3.9 %collective-permute-start.22 = (f32[1,2,64,256]{3,2,1,0:T(8,128)S(1)}, f32[1,2,64,256]{3,2,1,0:T(8,128)S(1)}, u32[]{:S(2)}, u32[]{:S(2)}) collective-permute-start(f32[1,2,64,256]{3,2,1,0:T(8,128)S(1)} %maximum_select_fusion.5), channel_id=1, source_target_pairs={{0,1},{1,0},{2,3},{3,2},{4,5},{5,4},{6,7},{7,6},{8,9},{9,8},{10,11... | collective-permute-start | bytes 393224 | tf_op jit(solution)/shard_map/ppermute | solution.py:455
  123.7 5.0 %collective-permute-start.24 = (f32[64,1024]{1,0:T(8,128)S(1)}, f32[64,1024]{1,0:T(8,128)S(1)}, u32[]{:S(2)}, u32[]{:S(2)}) collective-permute-start(f32[64,1024]{1,0:T(8,128)S(1)} %maximum_multiply_fusion), channel_id=1, source_target_pairs={{0,8},{8,0},{16,24},{24,16},{1,9},{9,1},{17,25},{25,17},{2,10},{10... | collective-permute-start | bytes 786440 | tf_op jit(solution)/shard_map/ppermute | solution.py:455
  126.1 3.7 %collective-permute-start.23 = (f32[1,2,2,64,256]{4,3,2,1,0:T(8,128)S(1)}, f32[1,2,2,64,256]{4,3,2,1,0:T(8,128)S(1)}, u32[]{:S(2)}, u32[]{:S(2)}) collective-permute-start(f32[1,2,2,64,256]{4,3,2,1,0:T(8,128)S(1)} %maximum_select_fusion.3), channel_id=1, source_target_pairs={{0,8},{8,0},{16,24},{24,16},{1,9},{9,1},{17,25},{25,17},{2,10},{10... | collective-permute-start | bytes 786440 | tf_op jit(solution)/shard_map/ppermute | solution.py:455
